TPU v7x, 32 devices: a whole 2x2x4 slice. The times are simulated.
32 devices in a mesh: gx: 4 (over x, core), gy: 8 (over z, y).
Axes of the slice: x: 2, y: 2, z: 4, core: 2. Of those that a mesh axis runs over, the one named last changes fastest.
Arguments:
- spectrum: bfloat16 [64, 128, 1152], P('gx', 'gy'), may hold values from 0.099609375 to 1
- courant: float32 [2, 1152], replicated, may hold values from -0.45 to 0.45
- source: float32 [64, 128], P('gx', 'gy'), may hold values from 0.2 to 2
- wave_land: int32 [64, 128], P('gx', 'gy'), may hold values 0 or 1
- stokes_kernel: bfloat16 [1152, 128], replicated, may hold values from -0.1875 to 0.1875
- velocity: float32 [128, 512, 128], P('gx', 'gy'), may hold values from -6 to 6
- coriolis: float32 [128, 512], P('gx', 'gy'), may hold values from 0.5 to 1.5
- ocean_codes: int32 [128, 512, 4], P('gx', 'gy'), may hold values from 0 to 8
- ocean_weights: float32 [128, 512, 4], P('gx', 'gy'), may hold values from 0.2 to 2
- wave_codes: int32 [64, 128, 4], P('gx', 'gy'), may hold values from 0 to 23
- wave_weights: float32 [64, 128, 4], P('gx', 'gy'), may hold values from 0.2 to 2
Outputs:
- new_spectrum: bfloat16 [64, 128, 1152], P('gx', 'gy')
- new_velocity: float32 [128, 512, 128], P('gx', 'gy')
- wave_current: float32 [2, 64, 128], P(None, 'gx', 'gy')
All inputs are finite; a program needn't handle non-finite values. No bound on the sum of `wave_land` on one device may be relied on, other than what follows from the above.
Results may differ from a plain program's by a relative error of at most 0.002.
Values may be sent and summed in bfloat16 or wider, within the bound.
No kernel may reach another device: no remote copies, remote signals or barrier semaphores. Data moves between devices by JAX's collectives and lax.ppermute only.
A program may use at most 64 MiB of HBM per device.

v0:
```python
import jax
import jax.numpy as jnp
from jax import lax
from jax.sharding import PartitionSpec as P

NL = 64
K = 4
RX = 2
RY = 4


time_step = 0.5


def padded_2(value, sides, width, wrap):
    for axis, dim in sides:
        peers, length = (lax.axis_size(axis), value.shape[dim])
        up = [(i, (i + 1) % peers) for i in range(peers if wrap else peers - 1)]
        down = [(j, i) for i, j in up]
        last = lax.slice_in_dim(value, length - width, length, axis=dim)
        leading = lax.slice_in_dim(value, 0, width, axis=dim)
        before = lax.ppermute(last, axis, up)
        after = lax.ppermute(leading, axis, down)
        value = jnp.concatenate([before, value, after], axis=dim)
    return value


def shortened(value):

    def short(part):
        return part.astype(jnp.bfloat16) if part.dtype == jnp.float32 else part

    return jax.tree.map(short, value)


def clear_edges(padded, dim, width):
    index = lax.axis_index("gy")
    count = lax.axis_size("gy")
    length = padded.shape[dim]
    position = lax.broadcasted_iota(jnp.int32, (length,), 0)
    dropped = (position < width) & (index == 0) | (position >= length - width) & (
        index == count - 1
    )
    shape = [1] * padded.ndim
    shape[dim] = length
    return jnp.where(dropped.reshape(shape), jnp.zeros((), padded.dtype), padded)


def stokes_on(profiles_flat, codes, normed, wave_cols, rim):
    rows, cols = (codes.shape[0], codes.shape[1])
    ocean_x = lax.broadcasted_iota(jnp.int32, (rows, cols), 0)
    ocean_y = lax.broadcasted_iota(jnp.int32, (rows, cols), 1)
    stokes = jnp.zeros((rows, cols, profiles_flat.shape[1]), jnp.float32)
    for entry in range(K):
        code = codes[:, :, entry]
        slot = (
            (ocean_x // RX + code // 3 - 1 + rim) * (wave_cols + 2 * rim)
            + ocean_y // RY
            + code % 3
            - 1
            + rim
        )
        stokes = stokes + normed[:, :, entry : entry + 1] * jnp.take(
            profiles_flat, slot, axis=0
        ).astype(jnp.float32)
    return stokes


def stencil(along_x, along_y, coriolis_part, stokes):
    dvdx = (8.0 * (along_x[3:-1] - along_x[1:-3]) - (along_x[4:] - along_x[:-4])) / 12.0
    dudy = (8.0 * (along_y[:, 3:-1] - along_y[:, 1:-3]) - (along_y[:, 4:] - along_y[:, :-4])) / 12.0
    absolute = coriolis_part[:, :, None] + dvdx - dudy
    return jnp.concatenate([absolute * stokes[:, :, NL:], -absolute * stokes[:, :, :NL]], axis=-1)


def shards(
    spectrum,
    courant,
    source,
    wave_land,
    stokes_kernel,
    velocity,
    coriolis,
    ocean_codes,
    ocean_weights,
    wave_codes,
    wave_weights,
):
    wave_rows, wave_cols, bins = spectrum.shape
    ocean_rows, ocean_cols, levels_two = velocity.shape
    padded = padded_2(spectrum, (("gx", 0), ("gy", 1)), 1, True)
    padded = clear_edges(padded, 1, 1).astype(jnp.float32)
    center = padded[1:-1, 1:-1]
    speed_x = courant[0]
    speed_y = courant[1]
    advected = (
        center
        - jnp.maximum(speed_x, 0.0) * (center - padded[:-2, 1:-1])
        - jnp.maximum(-speed_x, 0.0) * (center - padded[2:, 1:-1])
        - jnp.maximum(speed_y, 0.0) * (center - padded[1:-1, :-2])
        - jnp.maximum(-speed_y, 0.0) * (center - padded[1:-1, 2:])
    )
    land_cells = wave_land.astype(jnp.float32)[:, :, None]
    source_cells = source[:, :, None]
    new_spectrum = (
        land_cells * (advected + 0.2 * source_cells * advected - 0.1 * advected * advected)
    ).astype(jnp.bfloat16)
    profiles = jnp.dot(
        new_spectrum.reshape(-1, bins), stokes_kernel, preferred_element_type=jnp.float32
    )
    profiles = profiles.astype(jnp.bfloat16).reshape(wave_rows, wave_cols, levels_two)
    ocean_normed = ocean_weights / jnp.sum(ocean_weights, axis=-1, keepdims=True)
    profiles_padded = padded_2(profiles, (("gx", 0), ("gy", 1)), 1, True)
    profiles_flat = clear_edges(profiles_padded, 1, 1).reshape(-1, levels_two)
    stokes = stokes_on(profiles_flat, ocean_codes, ocean_normed, wave_cols, 1)

    def tendency(state):
        along_x = padded_2(shortened(state[:, :, NL:]), (("gx", 0),), 2, True)
        along_y = padded_2(shortened(state[:, :, :NL]), (("gy", 1),), 2, False)
        return stencil(along_x, along_y, coriolis, stokes)

    first = tendency(velocity)
    middle = velocity + time_step * first
    second = tendency(middle)
    new_velocity = velocity + 0.5 * time_step * (first + second)
    means = jnp.stack(
        [jnp.mean(new_velocity[:, :, :NL], axis=-1), jnp.mean(new_velocity[:, :, NL:], axis=-1)],
        axis=0,
    )
    means_padded = padded_2(means, (("gx", 1), ("gy", 2)), 1, True)
    means_flat = clear_edges(means_padded, 2, 1).reshape(2, -1)
    grid_x = lax.broadcasted_iota(jnp.int32, (wave_rows, wave_cols), 0)
    grid_y = lax.broadcasted_iota(jnp.int32, (wave_rows, wave_cols), 1)
    wave_normed = wave_weights / jnp.sum(wave_weights, axis=-1, keepdims=True)
    current = jnp.zeros((2, wave_rows, wave_cols), jnp.float32)
    for entry in range(K):
        code = wave_codes[:, :, entry]
        slot = (RX * grid_x + code // (RY + 2)) * (ocean_cols + 2) + RY * grid_y + code % (RY + 2)
        current = current + wave_normed[None, :, :, entry] * jnp.take(means_flat, slot, axis=1)
    return (new_spectrum, new_velocity, current)


def solution(mesh):
    return jax.shard_map(
        shards,
        mesh=mesh,
        in_specs=(
            P("gx", "gy", None),
            P(),
            P("gx", "gy"),
            P("gx", "gy"),
            P(),
            P("gx", "gy", None),
            P("gx", "gy"),
            P("gx", "gy", None),
            P("gx", "gy", None),
            P("gx", "gy", None),
            P("gx", "gy", None),
        ),
        out_specs=(P("gx", "gy", None), P("gx", "gy", None), P(None, "gx", "gy")),
        check_vma=False,
    )
```

profile of v0, /device:TPU:8, one launch (start us, length us, event | category | flops | bytes accessed | tf_op | source)
XLA Modules:
  0.0 95.5 jit_solution(3237921450400184737)
XLA Ops:
  0.6 0.8 fusion.98
  1.5 1.7 %collective-permute-start.1 = (bf16[1,16,1152]{2,1,0:T(8,128)(2,1)S(1)}, bf16[1,16,1152]{2,1,0:T(8,128)(2,1)S(1)}, u32[]{:S(2)}, u32[]{:S(2)}) collective-permute-start(bf16[1,16,1152]{2,1,0:T(8,128)(2,1)S(1)} %get-tuple-element.35), channel_id=1, source_target_pairs={{8,0},{16,8},{24,16},{0,24},{9,1},{17,9},{25,17},{1,25},{10,2},{18... | collective-permute-start | bytes 110600 | tf_op jit(solution)/shard_map/ppermute | solution.py:23
  3.2 1.3 %convert.8 = bf16[32,64,128]{2,1,0:T(8,128)(2,1)S(1)} convert(f32[32,64,128]{2,1,0:T(8,128)} %param.20) | non-fusion elementwise | flops 262144 | bytes 1572864 | tf_op jit(solution)/shard_map/convert.3
  4.7 0.5 collective-permute-start.5
  5.3 3.3 %collective-permute-start.6 = (bf16[32,2,64]{2,1,0:T(2,128)(2,1)S(1)}, bf16[32,2,64]{2,1,0:T(2,128)(2,1)S(1)}, u32[]{:S(2)}, u32[]{:S(2)}) collective-permute-start(bf16[32,2,64]{2,1,0:T(2,128)(2,1)S(1)} %get-tuple-element.43), channel_id=1, source_target_pairs={{1,0},{2,1},{3,2},{4,3},{5,4},{6,5},{7,6},{9,8},{10,9},{11,10},{12... | collective-permute-start | bytes 24584 | tf_op jit(solution)/shard_map/ppermute | solution.py:23
  8.7 1.2 %fusion.103 = (bf16[32,64,64]{2,1,0:T(8,128)(2,1)}, bf16[32,64,64]{2,1,0:T(8,128)(2,1)}) fusion(bf16[32,64,128]{2,1,0:T(8,128)(2,1)S(1)} %convert.8), kind=kLoop, calls=%fused_computation.267 | loop fusion | bytes 1048576 | tf_op jit(solution)/shard_map/slice | solution.py:119
  9.9 1.3 %fusion.106 = (s32[32,64,1]{1,2,0:T(1,128)S(1)}, s32[32,64,1]{1,2,0:T(1,128)S(1)}, s32[32,64,1]{1,2,0:T(1,128)S(1)}, s32[32,64,1]{1,2,0:T(1,128)S(1)}, s32[32,64,1]{1,2,0:T(1,128)S(1)}) fusion(s32[32,64,4]{1,2,0:T(4,128)S(1)} %copy-done.10, s32[32,64,1]{1,2,0:T(1,128)S(1)} %bitcast.239), kind=kLoop, calls=%fused_computation.270 | loop fusion | flops 2048 | bytes 81920 | tf_op jit(solution)/shard_map/slice | solution.py:55
  11.8 0.7 fusion.109
  13.0 0.7 collective-permute-start.2
  13.6 2.3 %collective-permute-start.3 = (bf16[18,1,1152]{2,1,0:T(2,128)(2,1)S(1)}, bf16[18,1,1152]{2,1,0:T(2,128)(2,1)S(1)}, u32[]{:S(2)}, u32[]{:S(2)}) collective-permute-start(bf16[18,1,1152]{2,1,0:T(2,128)(2,1)S(1)} %get-tuple-element.34), channel_id=1, source_target_pairs={{1,0},{2,1},{3,2},{4,3},{5,4},{6,5},{7,6},{0,7},{9,8},{10,9},{11,1... | collective-permute-start | bytes 124424 | tf_op jit(solution)/shard_map/ppermute | solution.py:23
  16.0 3.2 %collective-permute-done.2 = bf16[18,1,1152]{2,1,0:T(2,128)(2,1)S(1)} collective-permute-done((bf16[18,1,1152]{2,1,0:T(2,128)(2,1)S(1)}, bf16[18,1,1152]{2,1,0:T(2,128)(2,1)S(1)}, u32[]{:S(2)}, u32[]{:S(2)}) %collective-permute-start.2) | collective-permute-done | bytes 41504 | tf_op jit(solution)/shard_map/ppermute | solution.py:22
  19.3 1.7 %collective-permute-done.3 = bf16[18,1,1152]{2,1,0:T(2,128)(2,1)S(1)} collective-permute-done((bf16[18,1,1152]{2,1,0:T(2,128)(2,1)S(1)}, bf16[18,1,1152]{2,1,0:T(2,128)(2,1)S(1)}, u32[]{:S(2)}, u32[]{:S(2)}) %collective-permute-start.3) | collective-permute-done | bytes 41504 | tf_op jit(solution)/shard_map/ppermute | solution.py:23
  21.0 0.5 fusion.13
  21.4 0.9 fusion.2
  22.9 1.6 %collective-permute-start.9 = (bf16[1,16,128]{2,1,0:T(8,128)(2,1)S(1)}, bf16[1,16,128]{2,1,0:T(8,128)(2,1)S(1)}, u32[]{:S(2)}, u32[]{:S(2)}) collective-permute-start(bf16[1,16,128]{2,1,0:T(8,128)(2,1)S(1)} %get-tuple-element.61), channel_id=1, source_target_pairs={{8,0},{16,8},{24,16},{0,24},{9,1},{17,9},{25,17},{1,25},{10,2},{18... | collective-permute-start | bytes 12296 | tf_op jit(solution)/shard_map/ppermute | solution.py:23
  24.7 1.1 %collective-permute-done.8 = bf16[1,16,128]{2,1,0:T(8,128)(2,1)S(1)} collective-permute-done((bf16[1,16,128]{2,1,0:T(8,128)(2,1)S(1)}, bf16[1,16,128]{2,1,0:T(8,128)(2,1)S(1)}, u32[]{:S(2)}, u32[]{:S(2)}) %collective-permute-start.8) | collective-permute-done | bytes 4128 | tf_op jit(solution)/shard_map/ppermute | solution.py:22
  25.9 1.0 %collective-permute-start.10 = (bf16[18,1,128]{2,1,0:T(2,128)(2,1)S(1)}, bf16[18,1,128]{2,1,0:T(2,128)(2,1)S(1)}, u32[]{:S(2)}, u32[]{:S(2)}) collective-permute-start(bf16[18,1,128]{2,1,0:T(2,128)(2,1)S(1)} %get-tuple-element.49), channel_id=1, source_target_pairs={{0,1},{1,2},{2,3},{3,4},{4,5},{5,6},{6,7},{7,0},{8,9},{9,10},{10,1... | collective-permute-start | bytes 13832 | tf_op jit(solution)/shard_map/ppermute | solution.py:22
  26.9 1.9 %collective-permute-start.11 = (bf16[18,1,128]{2,1,0:T(2,128)(2,1)S(1)}, bf16[18,1,128]{2,1,0:T(2,128)(2,1)S(1)}, u32[]{:S(2)}, u32[]{:S(2)}) collective-permute-start(bf16[18,1,128]{2,1,0:T(2,128)(2,1)S(1)} %get-tuple-element.50), channel_id=1, source_target_pairs={{1,0},{2,1},{3,2},{4,3},{5,4},{6,5},{7,6},{0,7},{9,8},{10,9},{11,1... | collective-permute-start | bytes 13832 | tf_op jit(solution)/shard_map/ppermute | solution.py:23
  29.1 1.4 %collective-permute-done.10 = bf16[18,1,128]{2,1,0:T(2,128)(2,1)S(1)} collective-permute-done((bf16[18,1,128]{2,1,0:T(2,128)(2,1)S(1)}, bf16[18,1,128]{2,1,0:T(2,128)(2,1)S(1)}, u32[]{:S(2)}, u32[]{:S(2)}) %collective-permute-start.10) | collective-permute-done | bytes 4640 | tf_op jit(solution)/shard_map/ppermute | solution.py:22
  30.5 2.0 %collective-permute-start.7 = (bf16[32,2,64]{2,1,0:T(2,128)(2,1)S(1)}, bf16[32,2,64]{2,1,0:T(2,128)(2,1)S(1)}, u32[]{:S(2)}, u32[]{:S(2)}) collective-permute-start(bf16[32,2,64]{2,1,0:T(2,128)(2,1)S(1)} %get-tuple-element.44), channel_id=1, source_target_pairs={{0,1},{1,2},{2,3},{3,4},{4,5},{5,6},{6,7},{8,9},{9,10},{10,11},{11... | collective-permute-start | bytes 24584 | tf_op jit(solution)/shard_map/ppermute | solution.py:22
  32.7 6.2 %gather_fusion.1 = bf16[2048,128]{1,0:T(8,128)(2,1)S(1)} fusion(bf16[324,128]{1,0:T(8,128)(2,1)S(1)} %broadcast_select_fusion.1, s32[2048]{0:T(1024)S(1)} %broadcast_clamp_fusion.2), kind=kCustom, calls=%fused_computation.2.clone | custom fusion | bytes 1056768 | tf_op jit(solution)/shard_map/jit(_take)/gather | solution.py:63
  38.9 6.2 %gather_fusion.2 = bf16[2048,128]{1,0:T(8,128)(2,1)S(1)} fusion(bf16[324,128]{1,0:T(8,128)(2,1)S(1)} %broadcast_select_fusion.1, s32[2048]{0:T(1024)S(1)} %broadcast_clamp_fusion.1), kind=kCustom, calls=%fused_computation.3.clone | custom fusion | bytes 1056768 | tf_op jit(solution)/shard_map/jit(_take)/gather | solution.py:63
  45.1 6.2 %gather_fusion = bf16[2048,128]{1,0:T(8,128)(2,1)S(1)} fusion(bf16[324,128]{1,0:T(8,128)(2,1)S(1)} %broadcast_select_fusion.1, s32[2048]{0:T(1024)S(1)} %broadcast_clamp_fusion.3), kind=kCustom, calls=%fused_computation.clone | custom fusion | bytes 1056768 | tf_op jit(solution)/shard_map/jit(_take)/gather | solution.py:63
  51.3 6.2 %gather_fusion.3 = bf16[2048,128]{1,0:T(8,128)(2,1)S(1)} fusion(bf16[324,128]{1,0:T(8,128)(2,1)S(1)} %broadcast_select_fusion.1, s32[2048]{0:T(1024)S(1)} %broadcast_clamp_fusion), kind=kCustom, calls=%fused_computation.4.clone | custom fusion | bytes 1056768 | tf_op jit(solution)/shard_map/jit(_take)/gather | solution.py:63
  57.5 2.5 %multiply_add_fusion.1 = f32[32,64,128]{2,1,0:T(8,128)S(1)} fusion(bf16[32,64,128]{2,1,0:T(8,128)(2,1)S(1)} %bitcast.228, bf16[32,64,128]{2,1,0:T(8,128)(2,1)S(1)} %bitcast.226, bf16[32,64,128]{2,1,0:T(8,128)(2,1)S(1)} %bitcast.225, bf16[32,64,128]{2,1,0:T(8,128)(2,1)S(1)} %bitcast.227, f32[32,64]{1,0:T(8,128)S(1)} %bitcast.236, f32[32,64]{1,0:T(8,128)S(1)} %bitcast.237, ...), kind=kLoop, calls=%fused_computation.36 | loop fusion | flops 3932160 | bytes 3186688 | tf_op jit(solution)/shard_map/add | solution.py:63
  60.1 2.4 %slice_multiply_fusion.1 = (f32[32,64,64]{2,1,0:T(8,128)S(1)}, bf16[32,64,64]{2,1,0:T(8,128)(2,1)S(1)}, bf16[32,64,64]{2,1,0:T(8,128)(2,1)S(1)}) fusion(f32[32,64,128]{2,1,0:T(8,128)S(1)} %multiply_add_fusion.1, f32[32,64]{1,0:T(8,128)S(1)} %copy-done.7, bf16[32,64,64]{2,1,0:T(8,128)(2,1)S(1)} %copy-done.5, ...), kind=kLoop, calls=%fused_computation.41 | loop fusion | flops 5636096 | bytes 2154496 | tf_op jit(solution)/shard_map/mul | solution.py:73
  62.5 0.4 negate_multiply_fusion.1
  62.9 0.9 copy-done.1
  64.2 0.5 collective-permute-start.12
  64.8 4.7 %collective-permute-start.14 = (bf16[32,2,64]{2,1,0:T(2,128)(2,1)S(1)}, bf16[32,2,64]{2,1,0:T(2,128)(2,1)S(1)}, u32[]{:S(2)}, u32[]{:S(2)}) collective-permute-start(bf16[32,2,64]{2,1,0:T(2,128)(2,1)S(1)} %get-tuple-element.37), channel_id=1, source_target_pairs={{1,0},{2,1},{3,2},{4,3},{5,4},{6,5},{7,6},{9,8},{10,9},{11,10},{12... | collective-permute-start | bytes 24584 | tf_op jit(solution)/shard_map/ppermute | solution.py:23
  69.5 2.2 %collective-permute-start.15 = (bf16[32,2,64]{2,1,0:T(2,128)(2,1)S(1)}, bf16[32,2,64]{2,1,0:T(2,128)(2,1)S(1)}, u32[]{:S(2)}, u32[]{:S(2)}) collective-permute-start(bf16[32,2,64]{2,1,0:T(2,128)(2,1)S(1)} %get-tuple-element.38), channel_id=1, source_target_pairs={{0,1},{1,2},{2,3},{3,4},{4,5},{5,6},{6,7},{8,9},{9,10},{10,11},{11... | collective-permute-start | bytes 24584 | tf_op jit(solution)/shard_map/ppermute | solution.py:22
  72.0 4.0 %collective-permute-done.15 = bf16[32,2,64]{2,1,0:T(2,128)(2,1)S(1)} collective-permute-done((bf16[32,2,64]{2,1,0:T(2,128)(2,1)S(1)}, bf16[32,2,64]{2,1,0:T(2,128)(2,1)S(1)}, u32[]{:S(2)}, u32[]{:S(2)}) %collective-permute-start.15) | collective-permute-done | bytes 8224 | tf_op jit(solution)/shard_map/ppermute | solution.py:22
  76.0 2.4 %slice_multiply_fusion = (f32[32,64,64]{2,1,0:T(8,128)S(1)}, bf16[32,64,64]{2,1,0:T(8,128)(2,1)S(1)}, bf16[32,64,64]{2,1,0:T(8,128)(2,1)S(1)}) fusion(f32[32,64,128]{2,1,0:T(8,128)S(1)} %multiply_add_fusion.1, f32[32,64]{1,0:T(8,128)S(1)} %copy-done.7, bf16[32,64,64]{2,1,0:T(8,128)(2,1)S(1)} %get-tuple-element.40, ...), kind=kLoop, calls=%fused_computation.40 | loop fusion | flops 5636096 | bytes 2154496 | tf_op jit(solution)/shard_map/mul | solution.py:73
  78.4 0.4 negate_multiply_fusion
  78.8 0.6 fusion.12
  79.4 0.9 slice_reduce_fusion.1
  80.4 1.7 %collective-permute-start.17 = (f32[2,1,64]{2,1,0:T(1,128)S(1)}, f32[2,1,64]{2,1,0:T(1,128)S(1)}, u32[]{:S(2)}, u32[]{:S(2)}) collective-permute-start(f32[2,1,64]{2,1,0:T(1,128)S(1)} %get-tuple-element.74), channel_id=1, source_target_pairs={{8,0},{16,8},{24,16},{0,24},{9,1},{17,9},{25,17},{1,25},{10,2},{18... | collective-permute-start | bytes 1544 | tf_op jit(solution)/shard_map/ppermute | solution.py:23
  82.2 1.2 %collective-permute-done.16 = f32[2,1,64]{2,1,0:T(1,128)S(1)} collective-permute-done((f32[2,1,64]{2,1,0:T(1,128)S(1)}, f32[2,1,64]{2,1,0:T(1,128)S(1)}, u32[]{:S(2)}, u32[]{:S(2)}) %collective-permute-start.16) | collective-permute-done | bytes 544 | tf_op jit(solution)/shard_map/ppermute | solution.py:22
  83.6 2.9 %collective-permute-start.19 = (f32[2,34,1]{2,1,0:T(8,128)S(1)}, f32[2,34,1]{2,1,0:T(8,128)S(1)}, u32[]{:S(2)}, u32[]{:S(2)}) collective-permute-start(f32[2,34,1]{2,1,0:T(8,128)S(1)} %get-tuple-element.63), channel_id=1, source_target_pairs={{1,0},{2,1},{3,2},{4,3},{5,4},{6,5},{7,6},{0,7},{9,8},{10,9},{11,1... | collective-permute-start | bytes 824 | tf_op jit(solution)/shard_map/ppermute | solution.py:23
  86.6 2.0 %collective-permute-done.18 = f32[2,34,1]{2,1,0:T(8,128)S(1)} collective-permute-done((f32[2,34,1]{2,1,0:T(8,128)S(1)}, f32[2,34,1]{2,1,0:T(8,128)S(1)}, u32[]{:S(2)}, u32[]{:S(2)}) %collective-permute-start.18) | collective-permute-done | bytes 304 | tf_op jit(solution)/shard_map/ppermute | solution.py:22
  88.6 0.8 collective-permute-done.19
  89.6 0.4 copy.38
  90.0 1.2 %broadcast_select_fusion = f32[2,2244]{0,1:T(8,128)S(1)} fusion(f32[2,2244]{0,1:T(8,128)S(1)} %copy.38, pred[2244]{0:T(1024)(128)(4,1)S(1)} %broadcast_in_dim.79), kind=kLoop, calls=%fused_computation.50 | loop fusion | flops 4488 | bytes 38148 | tf_op jit(solution)/shard_map/jit(_where)/select_n | solution.py:46
  91.3 0.7 gather_fusion.4
  92.1 0.8 gather_fusion.5
  93.0 0.7 gather_fusion.6
  93.9 0.7 gather_fusion.7
  94.8 0.6 fusion.50
  (113 shorter events, 4.4 us)
Async XLA Ops:
  0.6 21.8 %copy-start = (bf16[1152,128]{1,0:T(8,128)(2,1)S(1)}, bf16[1152,128]{1,0:T(8,128)(2,1)}, u32[]{:S(2)}) copy-start(bf16[1152,128]{1,0:T(8,128)(2,1)} %param.19) | copy-start | bytes 884740
  1.5 11.2 %collective-permute-start = (bf16[1,16,1152]{2,1,0:T(8,128)(2,1)S(1)}, bf16[1,16,1152]{2,1,0:T(8,128)(2,1)S(1)}, u32[]{:S(2)}, u32[]{:S(2)}) collective-permute-start(bf16[1,16,1152]{2,1,0:T(8,128)(2,1)S(1)} %get-tuple-element.36), channel_id=1, source_target_pairs={{0,8},{8,16},{16,24},{24,0},{1,9},{9,17},{17,25},{25,1},{2,10},{10... | collective-permute-start | bytes 110600 | tf_op jit(solution)/shard_map/ppermute | solution.py:22
  1.5 11.3 %collective-permute-start.1 = (bf16[1,16,1152]{2,1,0:T(8,128)(2,1)S(1)}, bf16[1,16,1152]{2,1,0:T(8,128)(2,1)S(1)}, u32[]{:S(2)}, u32[]{:S(2)}) collective-permute-start(bf16[1,16,1152]{2,1,0:T(8,128)(2,1)S(1)} %get-tuple-element.35), channel_id=1, source_target_pairs={{8,0},{16,8},{24,16},{0,24},{9,1},{17,9},{25,17},{1,25},{10,2},{18... | collective-permute-start | bytes 110600 | tf_op jit(solution)/shard_map/ppermute | solution.py:23
  4.5 5.3 %copy-start.13 = (f32[16,16]{1,0:T(8,128)S(1)}, f32[16,16]{1,0:T(8,128)}, u32[]{:S(2)}) copy-start(f32[16,16]{1,0:T(8,128)} %param.17) | copy-start | bytes 3076
  4.6 5.3 %copy-start.10 = (s32[32,64,4]{1,2,0:T(4,128)S(1)}, s32[32,64,4]{1,2,0:T(4,128)}, u32[]{:S(2)}) copy-start(s32[32,64,4]{1,2,0:T(4,128)} %param.22) | copy-start | bytes 98308
  4.7 55.4 %collective-permute-start.4 = (bf16[2,64,64]{2,1,0:T(8,128)(2,1)S(1)}, bf16[2,64,64]{2,1,0:T(8,128)(2,1)S(1)}, u32[]{:S(2)}, u32[]{:S(2)}) collective-permute-start(bf16[2,64,64]{2,1,0:T(8,128)(2,1)S(1)} %get-tuple-element.47), channel_id=1, source_target_pairs={{8,0},{16,8},{24,16},{0,24},{9,1},{17,9},{25,17},{1,25},{10,2},{18... | collective-permute-start | bytes 49160 | tf_op jit(solution)/shard_map/ppermute | solution.py:23
  4.7 55.3 %collective-permute-start.5 = (bf16[2,64,64]{2,1,0:T(8,128)(2,1)S(1)}, bf16[2,64,64]{2,1,0:T(8,128)(2,1)S(1)}, u32[]{:S(2)}, u32[]{:S(2)}) collective-permute-start(bf16[2,64,64]{2,1,0:T(8,128)(2,1)S(1)} %get-tuple-element.48), channel_id=1, source_target_pairs={{0,8},{8,16},{16,24},{24,0},{1,9},{9,17},{17,25},{25,1},{2,10},{10... | collective-permute-start | bytes 49160 | tf_op jit(solution)/shard_map/ppermute | solution.py:22
  5.3 54.8 %collective-permute-start.6 = (bf16[32,2,64]{2,1,0:T(2,128)(2,1)S(1)}, bf16[32,2,64]{2,1,0:T(2,128)(2,1)S(1)}, u32[]{:S(2)}, u32[]{:S(2)}) collective-permute-start(bf16[32,2,64]{2,1,0:T(2,128)(2,1)S(1)} %get-tuple-element.43), channel_id=1, source_target_pairs={{1,0},{2,1},{3,2},{4,3},{5,4},{6,5},{7,6},{9,8},{10,9},{11,10},{12... | collective-permute-start | bytes 24584 | tf_op jit(solution)/shard_map/ppermute | solution.py:23
  8.6 2.9 %copy-start.8 = (f32[32,64,4]{1,2,0:T(4,128)S(1)}, f32[32,64,4]{1,2,0:T(4,128)}, u32[]{:S(2)}) copy-start(f32[32,64,4]{1,2,0:T(4,128)} %param.23) | copy-start | bytes 98308
  8.6 3.1 %copy-start.9 = (f32[16,16,4]{1,2,0:T(4,128)S(1)}, f32[16,16,4]{1,2,0:T(4,128)}, u32[]{:S(2)}) copy-start(f32[16,16,4]{1,2,0:T(4,128)} %param.25) | copy-start | bytes 12292
  8.6 3.2 %copy-start.11 = (s32[16,16,4]{1,2,0:T(4,128)S(1)}, s32[16,16,4]{1,2,0:T(4,128)}, u32[]{:S(2)}) copy-start(s32[16,16,4]{1,2,0:T(4,128)} %param.24) | copy-start | bytes 12292
  8.7 4.0 %copy-start.12 = (f32[2,1152]{1,0:T(2,128)S(1)}, f32[2,1152]{1,0:T(2,128)}, u32[]{:S(2)}) copy-start(f32[2,1152]{1,0:T(2,128)} %param.16) | copy-start | bytes 27652
  9.8 2.9 %copy-start.6 = (bf16[16,16,1152]{2,1,0:T(8,128)(2,1)S(1)}, bf16[16,16,1152]{2,1,0:T(8,128)(2,1)}, u32[]{:S(2)}) copy-start(bf16[16,16,1152]{2,1,0:T(8,128)(2,1)} %param.15) | copy-start | bytes 1769476
  11.6 4.4 %copy-start.14 = (s32[16,16]{1,0:T(8,128)S(1)}, s32[16,16]{1,0:T(8,128)}, u32[]{:S(2)}) copy-start(s32[16,16]{1,0:T(8,128)} %param.18) | copy-start | bytes 3076
  13.0 6.3 %collective-permute-start.2 = (bf16[18,1,1152]{2,1,0:T(2,128)(2,1)S(1)}, bf16[18,1,1152]{2,1,0:T(2,128)(2,1)S(1)}, u32[]{:S(2)}, u32[]{:S(2)}) collective-permute-start(bf16[18,1,1152]{2,1,0:T(2,128)(2,1)S(1)} %get-tuple-element.33), channel_id=1, source_target_pairs={{0,1},{1,2},{2,3},{3,4},{4,5},{5,6},{6,7},{7,0},{8,9},{9,10},{10,1... | collective-permute-start | bytes 124424 | tf_op jit(solution)/shard_map/ppermute | solution.py:22
  13.6 7.3 %collective-permute-start.3 = (bf16[18,1,1152]{2,1,0:T(2,128)(2,1)S(1)}, bf16[18,1,1152]{2,1,0:T(2,128)(2,1)S(1)}, u32[]{:S(2)}, u32[]{:S(2)}) collective-permute-start(bf16[18,1,1152]{2,1,0:T(2,128)(2,1)S(1)} %get-tuple-element.34), channel_id=1, source_target_pairs={{1,0},{2,1},{3,2},{4,3},{5,4},{6,5},{7,6},{0,7},{9,8},{10,9},{11,1... | collective-permute-start | bytes 124424 | tf_op jit(solution)/shard_map/ppermute | solution.py:23
  22.4 16.5 %copy-start.3 = (bf16[16,16,1152]{2,1,0:T(8,128)(2,1)}, bf16[16,16,1152]{2,1,0:T(8,128)(2,1)S(1)}, u32[]{:S(2)}) copy-start(bf16[16,16,1152]{2,1,0:T(8,128)(2,1)S(1)} %fusion.2) | copy-start | bytes 1769476
  22.7 3.1 %collective-permute-start.8 = (bf16[1,16,128]{2,1,0:T(8,128)(2,1)S(1)}, bf16[1,16,128]{2,1,0:T(8,128)(2,1)S(1)}, u32[]{:S(2)}, u32[]{:S(2)}) collective-permute-start(bf16[1,16,128]{2,1,0:T(8,128)(2,1)S(1)} %get-tuple-element.60), channel_id=1, source_target_pairs={{0,8},{8,16},{16,24},{24,0},{1,9},{9,17},{17,25},{25,1},{2,10},{10... | collective-permute-start | bytes 12296 | tf_op jit(solution)/shard_map/ppermute | solution.py:22
  22.9 3.0 %collective-permute-start.9 = (bf16[1,16,128]{2,1,0:T(8,128)(2,1)S(1)}, bf16[1,16,128]{2,1,0:T(8,128)(2,1)S(1)}, u32[]{:S(2)}, u32[]{:S(2)}) collective-permute-start(bf16[1,16,128]{2,1,0:T(8,128)(2,1)S(1)} %get-tuple-element.61), channel_id=1, source_target_pairs={{8,0},{16,8},{24,16},{0,24},{9,1},{17,9},{25,17},{1,25},{10,2},{18... | collective-permute-start | bytes 12296 | tf_op jit(solution)/shard_map/ppermute | solution.py:23
  25.9 4.6 %collective-permute-start.10 = (bf16[18,1,128]{2,1,0:T(2,128)(2,1)S(1)}, bf16[18,1,128]{2,1,0:T(2,128)(2,1)S(1)}, u32[]{:S(2)}, u32[]{:S(2)}) collective-permute-start(bf16[18,1,128]{2,1,0:T(2,128)(2,1)S(1)} %get-tuple-element.49), channel_id=1, source_target_pairs={{0,1},{1,2},{2,3},{3,4},{4,5},{5,6},{6,7},{7,0},{8,9},{9,10},{10,1... | collective-permute-start | bytes 13832 | tf_op jit(solution)/shard_map/ppermute | solution.py:22
  26.9 5.6 %collective-permute-start.11 = (bf16[18,1,128]{2,1,0:T(2,128)(2,1)S(1)}, bf16[18,1,128]{2,1,0:T(2,128)(2,1)S(1)}, u32[]{:S(2)}, u32[]{:S(2)}) collective-permute-start(bf16[18,1,128]{2,1,0:T(2,128)(2,1)S(1)} %get-tuple-element.50), channel_id=1, source_target_pairs={{1,0},{2,1},{3,2},{4,3},{5,4},{6,5},{7,6},{0,7},{9,8},{10,9},{11,1... | collective-permute-start | bytes 13832 | tf_op jit(solution)/shard_map/ppermute | solution.py:23
  30.5 29.6 %collective-permute-start.7 = (bf16[32,2,64]{2,1,0:T(2,128)(2,1)S(1)}, bf16[32,2,64]{2,1,0:T(2,128)(2,1)S(1)}, u32[]{:S(2)}, u32[]{:S(2)}) collective-permute-start(bf16[32,2,64]{2,1,0:T(2,128)(2,1)S(1)} %get-tuple-element.44), channel_id=1, source_target_pairs={{0,1},{1,2},{2,3},{3,4},{4,5},{5,6},{6,7},{8,9},{9,10},{10,11},{11... | collective-permute-start | bytes 24584 | tf_op jit(solution)/shard_map/ppermute | solution.py:22
  57.5 2.6 %copy-start.4 = (bf16[32,64,64]{2,1,0:T(8,128)(2,1)S(1)}, bf16[32,64,64]{2,1,0:T(8,128)(2,1)}, u32[]{:S(2)}) copy-start(bf16[32,64,64]{2,1,0:T(8,128)(2,1)} %get-tuple-element.45) | copy-start | bytes 786436
  57.5 2.6 %copy-start.5 = (bf16[32,64,64]{2,1,0:T(8,128)(2,1)S(1)}, bf16[32,64,64]{2,1,0:T(8,128)(2,1)}, u32[]{:S(2)}) copy-start(bf16[32,64,64]{2,1,0:T(8,128)(2,1)} %get-tuple-element.46) | copy-start | bytes 786436
  57.5 2.6 %copy-start.7 = (f32[32,64]{1,0:T(8,128)S(1)}, f32[32,64]{1,0:T(8,128)}, u32[]{:S(2)}) copy-start(f32[32,64]{1,0:T(8,128)} %param.21) | copy-start | bytes 24580
  62.5 1.2 %copy-start.1 = (f32[32,64,128]{2,1,0:T(8,128)S(1)}, f32[32,64,128]{2,1,0:T(8,128)}, u32[]{:S(2)}) copy-start(f32[32,64,128]{2,1,0:T(8,128)} %param.20) | copy-start | bytes 3145732
  64.2 11.8 %collective-permute-start.12 = (bf16[2,64,64]{2,1,0:T(8,128)(2,1)S(1)}, bf16[2,64,64]{2,1,0:T(8,128)(2,1)S(1)}, u32[]{:S(2)}, u32[]{:S(2)}) collective-permute-start(bf16[2,64,64]{2,1,0:T(8,128)(2,1)S(1)} %get-tuple-element.41), channel_id=1, source_target_pairs={{8,0},{16,8},{24,16},{0,24},{9,1},{17,9},{25,17},{1,25},{10,2},{18... | collective-permute-start | bytes 49160 | tf_op jit(solution)/shard_map/ppermute | solution.py:23
  64.8 11.3 %collective-permute-start.13 = (bf16[2,64,64]{2,1,0:T(8,128)(2,1)S(1)}, bf16[2,64,64]{2,1,0:T(8,128)(2,1)S(1)}, u32[]{:S(2)}, u32[]{:S(2)}) collective-permute-start(bf16[2,64,64]{2,1,0:T(8,128)(2,1)S(1)} %get-tuple-element.42), channel_id=1, source_target_pairs={{0,8},{8,16},{16,24},{24,0},{1,9},{9,17},{17,25},{25,1},{2,10},{10... | collective-permute-start | bytes 49160 | tf_op jit(solution)/shard_map/ppermute | solution.py:22
  64.8 7.2 %collective-permute-start.14 = (bf16[32,2,64]{2,1,0:T(2,128)(2,1)S(1)}, bf16[32,2,64]{2,1,0:T(2,128)(2,1)S(1)}, u32[]{:S(2)}, u32[]{:S(2)}) collective-permute-start(bf16[32,2,64]{2,1,0:T(2,128)(2,1)S(1)} %get-tuple-element.37), channel_id=1, source_target_pairs={{1,0},{2,1},{3,2},{4,3},{5,4},{6,5},{7,6},{9,8},{10,9},{11,10},{12... | collective-permute-start | bytes 24584 | tf_op jit(solution)/shard_map/ppermute | solution.py:23
  69.5 6.5 %collective-permute-start.15 = (bf16[32,2,64]{2,1,0:T(2,128)(2,1)S(1)}, bf16[32,2,64]{2,1,0:T(2,128)(2,1)S(1)}, u32[]{:S(2)}, u32[]{:S(2)}) collective-permute-start(bf16[32,2,64]{2,1,0:T(2,128)(2,1)S(1)} %get-tuple-element.38), channel_id=1, source_target_pairs={{0,1},{1,2},{2,3},{3,4},{4,5},{5,6},{6,7},{8,9},{9,10},{10,11},{11... | collective-permute-start | bytes 24584 | tf_op jit(solution)/shard_map/ppermute | solution.py:22
  79.4 4.1 %copy-start.2 = (f32[32,64,128]{2,1,0:T(8,128)}, f32[32,64,128]{2,1,0:T(8,128)S(1)}, u32[]{:S(2)}) copy-start(f32[32,64,128]{2,1,0:T(8,128)S(1)} %fusion.12) | copy-start | bytes 3145732
  80.3 3.0 %collective-permute-start.16 = (f32[2,1,64]{2,1,0:T(1,128)S(1)}, f32[2,1,64]{2,1,0:T(1,128)S(1)}, u32[]{:S(2)}, u32[]{:S(2)}) collective-permute-start(f32[2,1,64]{2,1,0:T(1,128)S(1)} %get-tuple-element.73), channel_id=1, source_target_pairs={{0,8},{8,16},{16,24},{24,0},{1,9},{9,17},{17,25},{25,1},{2,10},{10... | collective-permute-start | bytes 1544 | tf_op jit(solution)/shard_map/ppermute | solution.py:22
  80.4 3.0 %collective-permute-start.17 = (f32[2,1,64]{2,1,0:T(1,128)S(1)}, f32[2,1,64]{2,1,0:T(1,128)S(1)}, u32[]{:S(2)}, u32[]{:S(2)}) collective-permute-start(f32[2,1,64]{2,1,0:T(1,128)S(1)} %get-tuple-element.74), channel_id=1, source_target_pairs={{8,0},{16,8},{24,16},{0,24},{9,1},{17,9},{25,17},{1,25},{10,2},{18... | collective-permute-start | bytes 1544 | tf_op jit(solution)/shard_map/ppermute | solution.py:23
  83.5 5.1 %collective-permute-start.18 = (f32[2,34,1]{2,1,0:T(8,128)S(1)}, f32[2,34,1]{2,1,0:T(8,128)S(1)}, u32[]{:S(2)}, u32[]{:S(2)}) collective-permute-start(f32[2,34,1]{2,1,0:T(8,128)S(1)} %get-tuple-element.62), channel_id=1, source_target_pairs={{0,1},{1,2},{2,3},{3,4},{4,5},{5,6},{6,7},{7,0},{8,9},{9,10},{10,1... | collective-permute-start | bytes 824 | tf_op jit(solution)/shard_map/ppermute | solution.py:22
  83.6 5.9 %collective-permute-start.19 = (f32[2,34,1]{2,1,0:T(8,128)S(1)}, f32[2,34,1]{2,1,0:T(8,128)S(1)}, u32[]{:S(2)}, u32[]{:S(2)}) collective-permute-start(f32[2,34,1]{2,1,0:T(8,128)S(1)} %get-tuple-element.63), channel_id=1, source_target_pairs={{1,0},{2,1},{3,2},{4,3},{5,4},{6,5},{7,6},{0,7},{9,8},{10,9},{11,1... | collective-permute-start | bytes 824 | tf_op jit(solution)/shard_map/ppermute | solution.py:23
where the time goes:
time: 96.4 us; the launch traced here: 95.5 us
  local copies, waits for them, and re-layouts  33.5 us (35%)
  starting transfers between devices  27.6 us (29%)
  other arithmetic  17.1 us (18%)
  waiting for transfers between devices  15.6 us (16%)
  between operations  1.35 us (1%)
    gather x4, local copies, waits for them, and re-layouts, stokes_on(): jnp.take(profiles_flat, slot, axis=0).astype(jnp.float32)  24.7 us
    ppermute x10, starting transfers between devices, padded_2(): after = lax.ppermute(leading, axis, down)  20.9 us
    ppermute x10, waiting for transfers between devices, padded_2(): before = lax.ppermute(last, axis, up)  13 us
    ppermute x10, starting transfers between devices, padded_2(): before = lax.ppermute(last, axis, up)  6.69 us
    mul x2, other arithmetic, stencil(): absolute * stokes[:, :, NL:]  4.76 us
    gather x8, local copies, waits for them, and re-layouts, shards(): jnp.take(means_flat, slot, axis=1)  3.57 us
    ppermute x10, waiting for transfers between devices, padded_2(): after = lax.ppermute(leading, axis, down)  2.58 us
    add x1, other arithmetic, stokes_on(): stokes + normed[:, :, entry:entry + 1] * jnp.take(profiles_flat, slot, ax...  2.49 us
  transfers between devices with their start and end apart: 20, of which 9 were waited for; matrix products, arithmetic and copies ran while one was open for 37% of the time, Pallas kernels for 0%

commit v1 on v0

v1 whole, which is shorter than its diff:
```python
import jax
import jax.numpy as jnp
from jax import lax
from jax.experimental import pallas as pl
from jax.experimental.pallas import tpu as pltpu
from jax.sharding import PartitionSpec as P

K = 4
RX = 2
RY = 4
STEP = 0.5
PAD = 8
WIDE = 24
HV, HL = 5, 3
HX, HY = 3, 2
BF = jnp.bfloat16
F32 = jnp.float32


def partners(count, parity):
    return [(i ^ 1) if parity == 0 else ((i + 1) ^ 1) - 1 for i in range(count)]


def swap_pairs(axis, parity):
    nx, ny = lax.axis_size("gx"), lax.axis_size("gy")
    pairs = []
    for x in range(nx):
        for y in range(ny):
            tx, ty = x, y
            if axis == "gx":
                tx = partners(nx, parity)[x] % nx
            else:
                ty = partners(ny, parity)[y]
                if not 0 <= ty < ny:
                    tx, ty = x ^ 1, y
            pairs.append((x * ny + y, tx * ny + ty))
    return pairs


def exchange(axis, last, first):
    even = lax.axis_index(axis) % 2 == 0
    to_a = jnp.where(even, last, first)
    to_b = jnp.where(even, first, last)
    from_b = lax.ppermute(to_b, ("gx", "gy"), swap_pairs(axis, 1))
    from_a = lax.ppermute(to_a, ("gx", "gy"), swap_pairs(axis, 0))
    return jnp.where(even, from_b, from_a), jnp.where(even, from_a, from_b)


def packed(parts):
    flat = jnp.concatenate([p.reshape(-1) for p in parts])
    return jnp.pad(flat, (0, -flat.shape[0] % 2048)).reshape(-1, 128)


def unpacked(buffer, shapes):
    flat, at, out = buffer.reshape(-1), 0, []
    for shape in shapes:
        size = 1
        for n in shape:
            size *= n
        out.append(flat[at : at + size].reshape(shape))
        at += size
    return out


def split(value):
    high = value.astype(BF)
    return high, (value - high.astype(F32)).astype(BF)


def split3(value):
    high, rest = value.astype(BF), value - value.astype(BF).astype(F32)
    middle = rest.astype(BF)
    return high, middle, (rest - middle.astype(F32)).astype(BF)


def wave_kernel(spec, west, east, south, north, courant, source, land, weights, out, profile):
    rows, cols, _ = spec.shape
    cx, cy = courant[0:1, :], courant[1:2, :]
    ax, ay = jnp.abs(cx), jnp.abs(cy)
    from_west, from_south = cx > 0.0, cy > 0.0
    keep = 1.0 - ax - ay
    sub = lax.broadcasted_iota(jnp.int32, (cols, 1), 0)
    for x in range(rows):
        center = spec[x].astype(F32)
        before = (spec[x - 1] if x else west[...]).astype(F32)
        after = (spec[x + 1] if x < rows - 1 else east[...]).astype(F32)
        below = jnp.where(sub == 0, south[x : x + 1, :].astype(F32), pltpu.roll(center, 1, 0))
        above = jnp.where(sub == cols - 1, north[x : x + 1, :].astype(F32), pltpu.roll(center, cols - 1, 0))
        advected = (
            keep * center
            + ax * jnp.where(from_west, before, after)
            + ay * jnp.where(from_south, below, above)
        )
        wind = 1.0 + 0.2 * source[:, x : x + 1]
        updated = land[:, x : x + 1] * (advected * (wind - 0.1 * advected))
        updated = updated.astype(BF)
        out[x] = updated
        profile[x] = jnp.dot(updated, weights[...], preferred_element_type=F32).astype(BF)


def ocean_kernel(
    own, before, after, before_low, after_low, left, right, left_low, right_low,
    slots, shares, coriolis, profiles, gather, wave_codes, wave_shares, spread,
    out, current,
    vel, mid, prof, drift, spin, mean, picked,
):
    rows, cols, lanes = own.shape
    half = lanes // 2
    listed = slots.shape[0]
    wide = cols + 2 * PAD
    lane = lax.broadcasted_iota(jnp.int32, (1, lanes), 1)
    is_u = lane < half
    zero = jnp.zeros((wide, lanes), F32)

    def clear(r, _):
        vel[r, 0:PAD, :] = zero[0:PAD]
        vel[r, PAD + cols :, :] = zero[0:PAD]
        return 0

    lax.fori_loop(0, rows + 2 * HV, clear, 0)

    def fill(r, _):
        vel[r + HV, PAD : PAD + cols, :] = own[r]
        return 0

    lax.fori_loop(0, rows, fill, 0)
    for r in range(HV):
        vel[r, PAD : PAD + cols, :] = before[r].astype(F32)
        vel[HV + rows + r, PAD : PAD + cols, :] = after[r].astype(F32)
    vel[HV - 1, PAD : PAD + cols, :] += before_low[0].astype(F32)
    vel[HV + rows, PAD : PAD + cols, :] += after_low[0].astype(F32)
    for j in range(HV):
        vel[:, PAD - HV + j, :] = left[j].astype(F32)
        vel[:, PAD + cols + j, :] = right[j].astype(F32)
    vel[HV - 1 : HV + rows + 1, PAD - 1, :] += left_low[...].astype(F32)
    vel[HV - 1 : HV + rows + 1, PAD + cols, :] += right_low[...].astype(F32)
    sign = jnp.where(is_u, 1.0, -1.0)
    prof[...] = pltpu.roll(profiles[...].astype(F32), half, 1) * sign
    block = 3 * WIDE
    place = lax.broadcasted_iota(jnp.int32, (block, lanes), 0)
    contract = (((0,), (0,)), ((), ()))
    ones = jnp.ones((8, lanes), BF)
    sub8 = lax.broadcasted_iota(jnp.int32, (8, lanes), 0)

    def zeta_of(ref, r):
        def at(dx, dy):
            return ref[r + dx, PAD // 2 + dy : PAD // 2 + dy + cols + PAD, :]
        d1 = jnp.where(is_u, at(0, -1), at(1, 0)) - jnp.where(is_u, at(0, 1), at(-1, 0))
        d2 = jnp.where(is_u, at(0, -2), at(2, 0)) - jnp.where(is_u, at(0, 2), at(-2, 0))
        part = 8.0 * d1 - d2
        return part + pltpu.roll(part, half, 1)

    inner = slice(PAD // 2, PAD // 2 + cols + PAD)

    def first_step(r, _):
        table = jnp.zeros((block, lanes), F32)
        for k in range(K):
            table = table + jnp.where(place == slots[r, k : k + 1, :], shares[r, k : k + 1, :], 0.0)
        start = pl.multiple_of(((r + 1) // 2) * WIDE, 8)
        names = prof[pl.ds(start, block), :].astype(BF)
        stokes = lax.dot_general(table.astype(BF), names, contract, preferred_element_type=F32)
        turn = coriolis[pl.ds(r, 1), :]
        high, middle, low = (p.astype(F32) for p in split3(turn))
        parts = jnp.where(sub8 == 0, high, jnp.where(sub8 == 1, middle, jnp.where(sub8 == 2, low, 0.0)))
        turned = lax.dot_general(parts.astype(BF), ones, contract, preferred_element_type=F32)
        drift[r] = stokes[0:wide]
        spin[r] = turned[0:wide]
        absolute = spin[r, inner, :] + zeta_of(vel, r + HV - HL) * (1.0 / 12.0)
        mid[r, 0 : PAD // 2, :] = zero[0 : PAD // 2]
        mid[r, wide - PAD // 2 :, :] = zero[0 : PAD // 2]
        mid[r, inner, :] = vel[r + HV - HL, inner, :] + STEP * absolute * drift[r, inner, :]
        return 0

    lax.fori_loop(0, listed, first_step, 0)

    mean[...] = jnp.zeros(mean.shape, F32)
    half_of = lax.broadcasted_iota(jnp.int32, (8, lanes), 0)
    lane8 = lax.broadcasted_iota(jnp.int32, (8, lanes), 1)
    averager = jnp.where(lane8 // half == half_of, 1.0 / half, 0.0).astype(BF)
    across = (((1,), (1,)), ((), ()))

    def second_step(n, _):
        r = n + HL - 1
        absolute = spin[r, inner, :] + zeta_of(mid, r) * (1.0 / 12.0)
        second = absolute * drift[r, inner, :]
        new = 0.5 * (vel[r + HV - HL, inner, :] + mid[r, inner, :]) + (0.5 * STEP) * second
        mid_new = new
        high, middle, low = split3(mid_new)
        sums = sum(
            lax.dot_general(averager, p, across, preferred_element_type=F32) for p in (high, middle, low)
        )
        mean[0, pl.ds(n, 1), 0 : cols + PAD] = sums[0:1]
        mean[1, pl.ds(n, 1), 0 : cols + PAD] = sums[1:2]

        @pl.when(jnp.logical_and(n >= 1, n <= rows))
        def _():
            out[n - 1] = new[PAD // 2 : PAD // 2 + cols]

        return 0

    lax.fori_loop(0, rows + 2, second_step, 0)

    cells_x = wave_codes.shape[1]
    lane1 = lax.broadcasted_iota(jnp.int32, (1, lanes), 1)
    group = lane1 // current.shape[2]
    for c in range(2):
        picked[...] = sum(jnp.dot(p, gather[...], preferred_element_type=F32) for p in split3(mean[c]))
        total = jnp.zeros((cells_x, lanes), F32)
        for near in range(RX + 2):
            share = jnp.zeros((cells_x, lanes), F32)
            for k in range(K):
                share = share + jnp.where(wave_codes[k] == near * (RY + 2) + group, wave_shares[k], 0.0)
            total = total + share * picked[pl.ds(near, cells_x, stride=RX), :]
        sums = sum(jnp.dot(p, spread[...], preferred_element_type=F32) for p in split3(total))
        current[c] = sums[:, 0 : current.shape[2]]


VMEM = pl.BlockSpec(memory_space=pltpu.VMEM)


def shards(
    spectrum, courant, source, wave_land, stokes_kernel, velocity, coriolis,
    ocean_codes, ocean_weights, wave_codes, wave_weights,
):
    wr, wc, bins = spectrum.shape
    rows, cols, lanes = velocity.shape
    half = lanes // 2
    gy, ny = lax.axis_index("gy"), lax.axis_size("gy")
    at_start, at_end = gy == 0, gy == ny - 1

    def clear_before(value):
        return jnp.where(at_start, jnp.zeros((), value.dtype), value)

    def clear_after(value):
        return jnp.where(at_end, jnp.zeros((), value.dtype), value)

    codes = jnp.transpose(ocean_codes, (0, 2, 1)).astype(BF)
    weights = jnp.transpose(ocean_weights, (0, 2, 1))
    shares = (weights / jnp.sum(weights, axis=1, keepdims=True)).astype(BF)
    cor_high, cor_low = split(coriolis)

    def x_edge(at_last):
        def cut(value, n):
            return value[-n:] if at_last else value[:n]
        edge = cut(velocity, HV)
        ring = velocity[-1:] if at_last else velocity[:1]
        ring_low = split(ring)[1]
        return packed([
            cut(spectrum, 1), edge.astype(BF), ring_low,
            cut(codes, HL), cut(shares, HL), cut(cor_high, HL), cut(cor_low, HL),
        ])

    shapes_x = [(wc, bins), (HV, cols, lanes), (1, cols, lanes), (HL, K, cols), (HL, K, cols), (HL, cols), (HL, cols)]
    with jax.named_scope("edges"):
        xb, xa = exchange("gx", x_edge(True), x_edge(False))
        south, north = exchange("gy", spectrum[:, -1, :], spectrum[:, 0, :])
    west, vel_b, low_b, codes_b, shares_b, ch_b, cl_b = unpacked(xb, shapes_x)
    east, vel_a, low_a, codes_a, shares_a, ch_a, cl_a = unpacked(xa, shapes_x)
    south, north = clear_before(south), clear_after(north)

    new_spectrum, profiles = pl.pallas_call(
        wave_kernel,
        out_shape=(jax.ShapeDtypeStruct(spectrum.shape, BF), jax.ShapeDtypeStruct((wr, wc, lanes), BF)),
        in_specs=[VMEM] * 9, out_specs=(VMEM, VMEM),
        compiler_params=pltpu.CompilerParams(vmem_limit_bytes=48 << 20),
        name="wave",
    )(spectrum, west, east, south, north, courant, source.T, wave_land.T.astype(F32), stokes_kernel)

    with jax.named_scope("profiles_x"):
        pb, pa = exchange("gx", profiles[-HX:], profiles[:HX])
    profiles = jnp.concatenate([pb, profiles, pa], axis=0)
    codes = jnp.concatenate([codes_b, codes, codes_a], axis=0)
    shares = jnp.concatenate([shares_b, shares, shares_a], axis=0)
    cor_high = jnp.concatenate([ch_b, cor_high, ch_a], axis=0)
    cor_low = jnp.concatenate([cl_b, cor_low, cl_a], axis=0)

    def y_edge(at_last):
        def cut(value, n, dim):
            length = value.shape[dim]
            return lax.slice_in_dim(value, length - n, length, axis=dim) if at_last else lax.slice_in_dim(value, 0, n, axis=dim)
        vel = jnp.concatenate([cut(v, HV, 1).astype(BF) for v in (vel_b, velocity, vel_a)], axis=0)
        ring = jnp.concatenate([cut(low_b, 1, 1), split(cut(velocity, 1, 1))[1], cut(low_a, 1, 1)], axis=0)
        return packed([
            cut(profiles, HY, 1), jnp.transpose(vel, (1, 0, 2)), ring[:, 0],
            cut(codes, HL, 2), cut(shares, HL, 2), cut(cor_high, HL, 1), cut(cor_low, HL, 1),
        ])

    prow, vrow, lrow = wr + 2 * HX, rows + 2 * HV, rows + 2 * HL
    shapes_y = [(prow, HY, lanes), (HV, vrow, lanes), (rows + 2, lanes), (lrow, K, HL), (lrow, K, HL), (lrow, HL), (lrow, HL)]
    with jax.named_scope("halo_y"):
        yb, ya = exchange("gy", y_edge(True), y_edge(False))
    yb, ya = clear_before(yb), clear_after(ya)
    prof_b, left, left_low, codes_b, shares_b, ch_b, cl_b = unpacked(yb, shapes_y)
    prof_a, right, right_low, codes_a, shares_a, ch_a, cl_a = unpacked(ya, shapes_y)
    profiles = jnp.concatenate([prof_b, profiles, prof_a, jnp.zeros((prow, WIDE - wc - 2 * HY, lanes), BF)], axis=1)
    profiles = profiles.reshape(prow * WIDE, lanes)

    def widened(b, own, a):
        joined = jnp.concatenate([b, own, a], axis=-1).astype(F32)
        edge = [(0, 0)] * (joined.ndim - 1)
        return jnp.pad(joined, edge + [(PAD - HL, lanes - PAD - cols - HL)])

    codes = widened(codes_b, codes, codes_a).astype(jnp.int32)
    shares = widened(shares_b, shares, shares_a)
    turn = widened(ch_b, cor_high, ch_a) + widened(cl_b, cor_low, cl_a)
    third = (codes >= 3).astype(jnp.int32) + (codes >= 6).astype(jnp.int32)
    lane = lax.broadcasted_iota(jnp.int32, codes.shape, 2)
    slots = third * (WIDE - 3) + codes + lane // RY - (PAD // RY - 1)

    reach = RY + 2
    wc_t = jnp.transpose(wave_codes, (2, 0, 1))
    ww_t = jnp.transpose(wave_weights, (2, 0, 1))
    ww_t = ww_t / jnp.sum(ww_t, axis=0, keepdims=True)
    spare = [(0, 0), (0, 0), (0, lanes - reach * wc)]
    wc_t = jnp.pad(jnp.tile(wc_t, (1, 1, reach)), spare)
    ww_t = jnp.pad(jnp.tile(ww_t, (1, 1, reach)), spare)
    at = lax.broadcasted_iota(jnp.int32, (lanes, lanes), 0)
    to = lax.broadcasted_iota(jnp.int32, (lanes, lanes), 1)
    used = to < reach * wc
    gather = (used & (at == RY * (to % wc) + to // wc + PAD // 2 - 1)).astype(BF)
    spread = ((at < reach * wc) & (at % wc == to)).astype(BF)

    scratch = [
        pltpu.VMEM((vrow, cols + 2 * PAD, lanes), F32),
        pltpu.VMEM((lrow, cols + 2 * PAD, lanes), F32),
        pltpu.VMEM((prow * WIDE, lanes), F32),
        pltpu.VMEM((lrow, cols + 2 * PAD, lanes), F32),
        pltpu.VMEM((lrow, cols + 2 * PAD, lanes), F32),
        pltpu.VMEM((2, rows + 8, lanes), F32),
        pltpu.VMEM((rows + 8, lanes), F32),
    ]
    new_velocity, current = pl.pallas_call(
        ocean_kernel,
        out_shape=(jax.ShapeDtypeStruct(velocity.shape, F32), jax.ShapeDtypeStruct((2, wr, wc), F32)),
        in_specs=[VMEM] * 17, out_specs=(VMEM, VMEM),
        scratch_shapes=scratch,
        compiler_params=pltpu.CompilerParams(vmem_limit_bytes=48 << 20),
        name="ocean",
    )(
        velocity, vel_b, vel_a, low_b, low_a, left, right, left_low, right_low,
        slots, shares, turn, profiles, gather, wc_t, ww_t, spread,
    )
    return new_spectrum, new_velocity, current


def solution(mesh):
    return jax.shard_map(
        shards,
        mesh=mesh,
        in_specs=(
            P("gx", "gy", None), P(), P("gx", "gy"), P("gx", "gy"), P(), P("gx", "gy", None),
            P("gx", "gy"), P("gx", "gy", None), P("gx", "gy", None), P("gx", "gy", None), P("gx", "gy", None),
        ),
        out_specs=(P("gx", "gy", None), P("gx", "gy", None), P(None, "gx", "gy")),
        check_vma=False,
    )
```

time: 96.4 us -> 52.9 us (0.55)
  local copies, waits for them, and re-layouts: 33.5 us -> 12.9 us
  Pallas kernels: 0 us -> 20.5 us
  starting transfers between devices: 27.6 us -> 8.04 us
  other arithmetic: 17.1 us -> 3.3 us
  waiting for transfers between devices: 15.6 us -> 6.31 us
    gather x12 -> x0, local copies, waits for them, and re-layouts: 28.3 us -> none  [the longest x4 24.7 us: stokes_on(): jnp.take(profiles_flat, slot, axis=0).astype(jnp.float32)]
    pallas_call x0 -> x2, Pallas kernels: none -> 20.5 us  [the longest x1 18.6 us: shards(): pl.pallas_call(ocean_kernel, out_shape=(jax.ShapeDtypeStruct(velocity.sha...]
    ppermute x20 -> x8, starting transfers between devices: 27.6 us -> 8.04 us  [the longest x4 4.53 us: exchange(): from_a = lax.ppermute(to_a, ('gx', 'gy'), swap_pairs(axis, 0))]
    ppermute x20 -> x8, waiting for transfers between devices: 15.6 us -> 6.31 us  [the longest x4 3.82 us: exchange(): from_a = lax.ppermute(to_a, ('gx', 'gy'), swap_pairs(axis, 0))]
    mul x7 -> x0, other arithmetic: 5.48 us -> none  [the longest x2 4.76 us: stencil(): absolute * stokes[:, :, NL:]]
    reshape x0 -> x41, local copies, waits for them, and re-layouts: none -> 4.22 us  [the longest x22 2.24 us: packed(): flat = jnp.concatenate([p.reshape(-1) for p in parts])]
    add x3 -> x2, other arithmetic: 3.74 us -> 0.1 us  [the longest x1 0.1 us: shards(): turn = widened(ch_b, cor_high, ch_a) + widened(cl_b, cor_low, cl_a)]
    unnamed x32 -> x24, local copies, waits for them, and re-layouts: 1.02 us -> 3.14 us
  transfers between devices with their start and end apart: 20 -> 8, of which waited for: 9 -> 3; matrix products, arithmetic and copies ran while one was open for 37% -> 15% of each run, Pallas kernels for 0% -> 0%
where the time goes in v1:
time: 52.9 us; the launch traced here: 52.3 us
  Pallas kernels  20.5 us (39%)
  local copies, waits for them, and re-layouts  12.9 us (24%)
  starting transfers between devices  8.04 us (15%)
  waiting for transfers between devices  6.31 us (12%)
  other arithmetic  3.3 us (6%)
  between operations  1.33 us (3%)
    pallas_call x1, Pallas kernels, shards(): pl.pallas_call(ocean_kernel, out_shape=(jax.ShapeDtypeStruct(velocity.sha...  18.6 us
    ppermute x4, starting transfers between devices, exchange(): from_a = lax.ppermute(to_a, ('gx', 'gy'), swap_pairs(axis, 0))  4.53 us
    ppermute x4, waiting for transfers between devices, exchange(): from_a = lax.ppermute(to_a, ('gx', 'gy'), swap_pairs(axis, 0))  3.82 us
    ppermute x4, starting transfers between devices, exchange(): from_b = lax.ppermute(to_b, ('gx', 'gy'), swap_pairs(axis, 1))  3.51 us
    unnamed x24, local copies, waits for them, and re-layouts  3.14 us
    ppermute x4, waiting for transfers between devices, exchange(): from_b = lax.ppermute(to_b, ('gx', 'gy'), swap_pairs(axis, 1))  2.49 us
    reshape x22, local copies, waits for them, and re-layouts, packed(): flat = jnp.concatenate([p.reshape(-1) for p in parts])  2.24 us
    concatenate x4, local copies, waits for them, and re-layouts, packed(): flat = jnp.concatenate([p.reshape(-1) for p in parts])  2.02 us
  transfers between devices with their start and end apart: 8, of which 3 were waited for; matrix products, arithmetic and copies ran while one was open for 15% of the time, Pallas kernels for 0%

profile of v1, /device:TPU:8, one launch (start us, length us, event | category | flops | bytes accessed | tf_op | source)
XLA Modules:
  0.0 52.3 jit_solution(2848645076191458854)
XLA Ops:
  0.6 1.2 %fusion.31 = (bf16[16,1,1152]{2,1,0:T(2,128)(2,1)S(1)}, bf16[16,1,1152]{2,1,0:T(2,128)(2,1)S(1)}) fusion(bf16[16,16,1152]{2,1,0:T(8,128)(2,1)} %spec.1), kind=kLoop, calls=%fused_computation.110 | loop fusion | bytes 147456 | tf_op jit(solution)/shard_map/edges/slice | solution.py:256
  1.8 1.6 %collective-permute-start.3 = (bf16[16,1152]{1,0:T(8,128)(2,1)S(1)}, bf16[16,1152]{1,0:T(8,128)(2,1)S(1)}, u32[]{:S(2)}, u32[]{:S(2)}) collective-permute-start(bf16[16,1152]{1,0:T(8,128)(2,1)S(1)} %get-tuple-element.37), channel_id=1, source_target_pairs={{0,1},{1,0},{2,3},{3,2},{4,5},{5,4},{6,7},{7,6},{8,9},{9,8},{10,11... | collective-permute-start | bytes 110600 | tf_op jit(solution)/shard_map/edges/ppermute | solution.py:45
  3.4 0.8 %fusion.32 = (bf16[1,16,1152]{2,1,0:T(8,128)(2,1)S(1)}, bf16[1,16,1152]{2,1,0:T(8,128)(2,1)S(1)}) fusion(bf16[16,16,1152]{2,1,0:T(8,128)(2,1)} %spec.1), kind=kLoop, calls=%fused_computation.111 | loop fusion | bytes 147456 | tf_op jit(solution)/shard_map/edges/slice | solution.py:244
  4.2 0.8 %fusion.15 = (bf16[8192]{0:T(1024)(128)(2,1)S(1)}, bf16[8192]{0:T(1024)(128)(2,1)S(1)}) fusion(f32[32,64,128]{2,1,0:T(8,128)} %own.1), kind=kLoop, calls=%fused_computation.55 | loop fusion | flops 65536 | bytes 98304 | tf_op jit(solution)/shard_map/edges/reshape | solution.py:50
  5.0 1.3 %convert.14 = bf16[32,64,128]{2,1,0:T(8,128)(2,1)S(1)} convert(f32[32,64,128]{2,1,0:T(8,128)} %own.1) | non-fusion elementwise | flops 262144 | bytes 1572864 | tf_op jit(solution)/shard_map/convert.11
  6.7 0.4 copy-done.4
  7.8 0.9 %concatenate.54 = bf16[69504]{0:T(1024)(128)(2,1)S(1)} concatenate(bf16[18432]{0:T(1024)(128)(2,1)S(1)} %reshape.233, bf16[40960]{0:T(1024)(128)(2,1)S(1)} %bitcast.72, bf16[8192]{0:T(1024)(128)(2,1)S(1)} %get-tuple-element.15, bf16[768]{0:T(1024)(128)(2,1)S(1)} %reshape.236, bf16[768]{0:T(1024)(128)(2,1)S(1)} %reshape.237, bf16[192]{0:T(256)(128)(2,1)S(1)} %reshape.238, ...), dimensions={0} | concatenate | bytes 278016 | tf_op jit(solution)/shard_map/edges/concatenate | solution.py:50
  8.7 0.9 %concatenate.55 = bf16[69504]{0:T(1024)(128)(2,1)S(1)} concatenate(bf16[18432]{0:T(1024)(128)(2,1)S(1)} %reshape.240, bf16[40960]{0:T(1024)(128)(2,1)S(1)} %bitcast.71, bf16[8192]{0:T(1024)(128)(2,1)S(1)} %get-tuple-element.16, bf16[768]{0:T(1024)(128)(2,1)S(1)} %reshape.243, bf16[768]{0:T(1024)(128)(2,1)S(1)} %reshape.244, bf16[192]{0:T(256)(128)(2,1)S(1)} %reshape.245, ...), dimensions={0} | concatenate | bytes 278016 | tf_op jit(solution)/shard_map/edges/concatenate | solution.py:50
  9.8 2.0 %collective-permute-start = (bf16[544,128]{1,0:T(8,128)(2,1)S(1)}, bf16[544,128]{1,0:T(8,128)(2,1)S(1)}, u32[]{:S(2)}, u32[]{:S(2)}) collective-permute-start(bf16[544,128]{1,0:T(8,128)(2,1)S(1)} %get-tuple-element.32), channel_id=1, source_target_pairs={{0,24},{1,25},{2,26},{3,27},{4,28},{5,29},{6,30},{7,31},{8,16},{9,... | collective-permute-start | bytes 417800 | tf_op jit(solution)/shard_map/edges/ppermute | solution.py:44
  11.9 0.6 %copy-done.7 = s32[16,16]{1,0:T(8,128)S(1)} copy-done((s32[16,16]{1,0:T(8,128)S(1)}, s32[16,16]{1,0:T(8,128)}, u32[]{:S(2)}) %copy-start.7) | copy-done | bytes 1048
  12.6 0.7 %copy-done.10 = f32[16,16,4]{1,2,0:T(4,128)S(1)} copy-done((f32[16,16,4]{1,2,0:T(4,128)S(1)}, f32[16,16,4]{1,2,0:T(4,128)}, u32[]{:S(2)}) %copy-start.10) | copy-done | bytes 4120
  13.4 0.1 fusion.6
  13.5 0.5 copy-done.8
  14.2 0.1 tile.21
  14.3 0.1 tile.9
  14.6 1.0 %collective-permute-done = bf16[544,128]{1,0:T(8,128)(2,1)S(1)} collective-permute-done((bf16[544,128]{1,0:T(8,128)(2,1)S(1)}, bf16[544,128]{1,0:T(8,128)(2,1)S(1)}, u32[]{:S(2)}, u32[]{:S(2)}) %collective-permute-start) | collective-permute-done | bytes 139296 | tf_op jit(solution)/shard_map/edges/ppermute | solution.py:44
  15.7 0.1 slice.269
  15.9 0.1 slice.271
  17.1 0.5 copy-done.2
  17.6 0.1 copy-done.3
  17.7 1.8 %wave.1 = (bf16[16,16,1152]{2,1,0:T(8,128)(2,1)}, bf16[16,16,128]{2,1,0:T(8,128)(2,1)S(1)}) custom-call(bf16[16,16,1152]{2,1,0:T(8,128)(2,1)S(1)} %copy-done.1, bf16[16,1152]{1,0:T(8,128)(2,1)S(1)} %reshape.247.west, bf16[16,1152]{1,0:T(8,128)(2,1)S(1)} %reshape.248.east, bf16[16,1152]{1,0:T(8,128)(2,1)S(1)} %get-tuple-element.58.south, ...), custom_call_target="tpu_custom_call" | custom-call | tf_op jit(solution)/shard_map/wave/pallas_call | solution.py:261
  19.6 1.5 %collective-permute-start.4 = (bf16[3,16,128]{2,1,0:T(8,128)(2,1)S(1)}, bf16[3,16,128]{2,1,0:T(8,128)(2,1)S(1)}, u32[]{:S(2)}, u32[]{:S(2)}) collective-permute-start(bf16[3,16,128]{2,1,0:T(8,128)(2,1)S(1)} %get-tuple-element.59), channel_id=1, source_target_pairs={{0,24},{1,25},{2,26},{3,27},{4,28},{5,29},{6,30},{7,31},{8,16},{9,... | collective-permute-start | bytes 36872 | tf_op jit(solution)/shard_map/profiles_x/ppermute | solution.py:44
  21.1 0.1 collective-permute-start.5
  21.3 0.2 reshape.257
  21.5 0.2 reshape.265
  21.7 0.2 reshape.260
  21.9 0.2 reshape.266
  22.3 0.1 reshape.261
  22.4 0.1 reshape.267
  22.5 0.1 reshape.262
  22.6 0.1 reshape.268
  22.9 0.1 concatenate.63
  23.0 0.1 concatenate.66
  23.2 2.7 %collective-permute-start.7 = (bf16[304,128]{1,0:T(8,128)(2,1)S(1)}, bf16[304,128]{1,0:T(8,128)(2,1)S(1)}, u32[]{:S(2)}, u32[]{:S(2)}) collective-permute-start(bf16[304,128]{1,0:T(8,128)(2,1)S(1)} %get-tuple-element.35), channel_id=1, source_target_pairs={{0,1},{1,0},{2,3},{3,2},{4,5},{5,4},{6,7},{7,6},{8,9},{9,8},{10,11... | collective-permute-start | bytes 233480 | tf_op jit(solution)/shard_map/halo_y/ppermute | solution.py:45
  25.9 3.8 %collective-permute-done.7 = bf16[304,128]{1,0:T(8,128)(2,1)S(1)} collective-permute-done((bf16[304,128]{1,0:T(8,128)(2,1)S(1)}, bf16[304,128]{1,0:T(8,128)(2,1)S(1)}, u32[]{:S(2)}, u32[]{:S(2)}) %collective-permute-start.7) | collective-permute-done | bytes 77856 | tf_op jit(solution)/shard_map/halo_y/ppermute | solution.py:45
  29.7 1.5 %collective-permute-done.6 = bf16[304,128]{1,0:T(8,128)(2,1)S(1)} collective-permute-done((bf16[304,128]{1,0:T(8,128)(2,1)S(1)}, bf16[304,128]{1,0:T(8,128)(2,1)S(1)}, u32[]{:S(2)}, u32[]{:S(2)}) %collective-permute-start.6) | collective-permute-done | bytes 77856 | tf_op jit(solution)/shard_map/halo_y/ppermute | solution.py:44
  31.6 0.1 reshape.278
  31.7 0.1 reshape.277
  31.8 0.1 reshape.280
  32.0 0.1 reshape.279
  32.2 0.2 reshape.276
  32.4 0.2 reshape.275
  32.7 0.2 reshape.274
  32.9 0.2 reshape.272
  33.1 0.1 fusion.7.shares
  33.4 0.1 convert_add_fusion.coriolis
  33.5 0.2 add_add_fusion.slots
  33.7 18.6 %ocean.1 = (f32[32,64,128]{2,1,0:T(8,128)}, f32[2,16,16]{2,1,0:T(8,128)}) custom-call(f32[32,64,128]{2,1,0:T(8,128)S(1)} %copy-done, bf16[5,64,128]{2,1,0:T(8,128)(2,1)S(1)} %bitcast.69, bf16[5,64,128]{2,1,0:T(8,128)(2,1)S(1)} %bitcast.67, bf16[1,64,128]{2,1,0:T(8,128)(2,1)S(1)} %get-tuple-element.88.before_low, ...), custom_call_target="tpu_custom_call" | custom-call | tf_op jit(solution)/shard_map/ocean/pallas_call | solution.py:332
  (122 shorter events, 3.4 us)
Async XLA Ops:
  1.8 12.7 %collective-permute-start.3 = (bf16[16,1152]{1,0:T(8,128)(2,1)S(1)}, bf16[16,1152]{1,0:T(8,128)(2,1)S(1)}, u32[]{:S(2)}, u32[]{:S(2)}) collective-permute-start(bf16[16,1152]{1,0:T(8,128)(2,1)S(1)} %get-tuple-element.37), channel_id=1, source_target_pairs={{0,1},{1,0},{2,3},{3,2},{4,5},{5,4},{6,7},{7,6},{8,9},{9,8},{10,11... | collective-permute-start | bytes 110600 | tf_op jit(solution)/shard_map/edges/ppermute | solution.py:45
  3.4 11.1 %collective-permute-start.2 = (bf16[16,1152]{1,0:T(8,128)(2,1)S(1)}, bf16[16,1152]{1,0:T(8,128)(2,1)S(1)}, u32[]{:S(2)}, u32[]{:S(2)}) collective-permute-start(bf16[16,1152]{1,0:T(8,128)(2,1)S(1)} %get-tuple-element.38), channel_id=1, source_target_pairs={{0,8},{1,2},{2,1},{3,4},{4,3},{5,6},{6,5},{7,15},{8,0},{9,10},{10,... | collective-permute-start | bytes 110600 | tf_op jit(solution)/shard_map/edges/ppermute | solution.py:44
  5.0 1.3 %copy-start.6 = (f32[32,64]{1,0:T(8,128)S(1)}, f32[32,64]{1,0:T(8,128)}, u32[]{:S(2)}) copy-start(f32[32,64]{1,0:T(8,128)} %param.17) | copy-start | bytes 24580
  6.3 0.8 %copy-start.4 = (s32[32,64,4]{1,2,0:T(4,128)S(1)}, s32[32,64,4]{1,2,0:T(4,128)}, u32[]{:S(2)}) copy-start(s32[32,64,4]{1,2,0:T(4,128)} %param.18) | copy-start | bytes 98308
  6.6 0.8 %copy-start.9 = (f32[32,64,4]{1,2,0:T(4,128)S(1)}, f32[32,64,4]{1,2,0:T(4,128)}, u32[]{:S(2)}) copy-start(f32[32,64,4]{1,2,0:T(4,128)} %param.19) | copy-start | bytes 98308
  7.4 4.4 %copy-start = (f32[32,64,128]{2,1,0:T(8,128)S(1)}, f32[32,64,128]{2,1,0:T(8,128)}, u32[]{:S(2)}) copy-start(f32[32,64,128]{2,1,0:T(8,128)} %own.1) | copy-start | bytes 3145732
  9.7 4.9 %collective-permute-start.1 = (bf16[544,128]{1,0:T(8,128)(2,1)S(1)}, bf16[544,128]{1,0:T(8,128)(2,1)S(1)}, u32[]{:S(2)}, u32[]{:S(2)}) collective-permute-start(bf16[544,128]{1,0:T(8,128)(2,1)S(1)} %get-tuple-element.31), channel_id=1, source_target_pairs={{0,8},{1,9},{2,10},{3,11},{4,12},{5,13},{6,14},{7,15},{8,0},{9,1},... | collective-permute-start | bytes 417800 | tf_op jit(solution)/shard_map/edges/ppermute | solution.py:45
  9.8 5.8 %collective-permute-start = (bf16[544,128]{1,0:T(8,128)(2,1)S(1)}, bf16[544,128]{1,0:T(8,128)(2,1)S(1)}, u32[]{:S(2)}, u32[]{:S(2)}) collective-permute-start(bf16[544,128]{1,0:T(8,128)(2,1)S(1)} %get-tuple-element.32), channel_id=1, source_target_pairs={{0,24},{1,25},{2,26},{3,27},{4,28},{5,29},{6,30},{7,31},{8,16},{9,... | collective-permute-start | bytes 417800 | tf_op jit(solution)/shard_map/edges/ppermute | solution.py:44
  11.8 0.7 %copy-start.7 = (s32[16,16]{1,0:T(8,128)S(1)}, s32[16,16]{1,0:T(8,128)}, u32[]{:S(2)}) copy-start(s32[16,16]{1,0:T(8,128)} %param.14) | copy-start | bytes 3076
  12.5 0.8 %copy-start.10 = (f32[16,16,4]{1,2,0:T(4,128)S(1)}, f32[16,16,4]{1,2,0:T(4,128)}, u32[]{:S(2)}) copy-start(f32[16,16,4]{1,2,0:T(4,128)} %param.21) | copy-start | bytes 12292
  13.3 0.7 %copy-start.8 = (f32[16,16]{1,0:T(8,128)S(1)}, f32[16,16]{1,0:T(8,128)}, u32[]{:S(2)}) copy-start(f32[16,16]{1,0:T(8,128)} %param.13) | copy-start | bytes 3076
  13.4 0.8 %copy-start.5 = (s32[16,16,4]{1,2,0:T(4,128)S(1)}, s32[16,16,4]{1,2,0:T(4,128)}, u32[]{:S(2)}) copy-start(s32[16,16,4]{1,2,0:T(4,128)} %param.20) | copy-start | bytes 12292
  15.9 1.2 %copy-start.1 = (bf16[16,16,1152]{2,1,0:T(8,128)(2,1)S(1)}, bf16[16,16,1152]{2,1,0:T(8,128)(2,1)}, u32[]{:S(2)}) copy-start(bf16[16,16,1152]{2,1,0:T(8,128)(2,1)} %spec.1) | copy-start | bytes 1769476
  16.6 1.0 %copy-start.2 = (bf16[1152,128]{1,0:T(8,128)(2,1)S(1)}, bf16[1152,128]{1,0:T(8,128)(2,1)}, u32[]{:S(2)}) copy-start(bf16[1152,128]{1,0:T(8,128)(2,1)} %weights.1) | copy-start | bytes 884740
  17.0 0.7 %copy-start.3 = (f32[2,1152]{1,0:T(2,128)S(1)}, f32[2,1152]{1,0:T(2,128)}, u32[]{:S(2)}) copy-start(f32[2,1152]{1,0:T(2,128)} %courant.1) | copy-start | bytes 27652
  19.6 3.2 %collective-permute-start.4 = (bf16[3,16,128]{2,1,0:T(8,128)(2,1)S(1)}, bf16[3,16,128]{2,1,0:T(8,128)(2,1)S(1)}, u32[]{:S(2)}, u32[]{:S(2)}) collective-permute-start(bf16[3,16,128]{2,1,0:T(8,128)(2,1)S(1)} %get-tuple-element.59), channel_id=1, source_target_pairs={{0,24},{1,25},{2,26},{3,27},{4,28},{5,29},{6,30},{7,31},{8,16},{9,... | collective-permute-start | bytes 36872 | tf_op jit(solution)/shard_map/profiles_x/ppermute | solution.py:44
  21.1 1.7 %collective-permute-start.5 = (bf16[3,16,128]{2,1,0:T(8,128)(2,1)S(1)}, bf16[3,16,128]{2,1,0:T(8,128)(2,1)S(1)}, u32[]{:S(2)}, u32[]{:S(2)}) collective-permute-start(bf16[3,16,128]{2,1,0:T(8,128)(2,1)S(1)} %get-tuple-element.60), channel_id=1, source_target_pairs={{0,8},{1,9},{2,10},{3,11},{4,12},{5,13},{6,14},{7,15},{8,0},{9,1},... | collective-permute-start | bytes 36872 | tf_op jit(solution)/shard_map/profiles_x/ppermute | solution.py:45
  23.2 6.6 %collective-permute-start.7 = (bf16[304,128]{1,0:T(8,128)(2,1)S(1)}, bf16[304,128]{1,0:T(8,128)(2,1)S(1)}, u32[]{:S(2)}, u32[]{:S(2)}) collective-permute-start(bf16[304,128]{1,0:T(8,128)(2,1)S(1)} %get-tuple-element.35), channel_id=1, source_target_pairs={{0,1},{1,0},{2,3},{3,2},{4,5},{5,4},{6,7},{7,6},{8,9},{9,8},{10,11... | collective-permute-start | bytes 233480 | tf_op jit(solution)/shard_map/halo_y/ppermute | solution.py:45
  25.9 5.3 %collective-permute-start.6 = (bf16[304,128]{1,0:T(8,128)(2,1)S(1)}, bf16[304,128]{1,0:T(8,128)(2,1)S(1)}, u32[]{:S(2)}, u32[]{:S(2)}) collective-permute-start(bf16[304,128]{1,0:T(8,128)(2,1)S(1)} %get-tuple-element.36), channel_id=1, source_target_pairs={{0,8},{1,2},{2,1},{3,4},{4,3},{5,6},{6,5},{7,15},{8,0},{9,10},{10,... | collective-permute-start | bytes 233480 | tf_op jit(solution)/shard_map/halo_y/ppermute | solution.py:44

commit v2 on v0

v2 whole, which is shorter than its diff:
```python
import jax
import jax.numpy as jnp
from jax import lax
from jax.experimental import pallas as pl
from jax.experimental.pallas import tpu as pltpu
from jax.sharding import PartitionSpec as P

K = 4
RX = 2
RY = 4
STEP = 0.5
WIDE = 24
LEAD = 4
HV, HL = 5, 3
HX, HY = 3, 2
EDGE = 8
BF = jnp.bfloat16
F32 = jnp.float32
ROWS_DOT = (((0,), (0,)), ((), ()))


def partner(i, count, parity):
    return (i ^ 1) if parity == 0 else ((i + 1) ^ 1) - 1


def swap(value, axis, parity):
    nx, ny = lax.axis_size("gx"), lax.axis_size("gy")
    pairs = []
    for x in range(nx):
        for y in range(ny):
            tx, ty = x, y
            if axis == "gx":
                tx = partner(x, nx, parity) % nx
            else:
                ty = partner(y, ny, parity)
                if not 0 <= ty < ny:
                    tx, ty = x ^ 1, y
            pairs.append((x * ny + y, tx * ny + ty))
    return lax.ppermute(value, ("gx", "gy"), pairs)


def exchange(axis, to_a, to_b):
    from_b = swap(to_b, axis, 1)
    from_a = swap(to_a, axis, 0)
    return from_a, from_b


def is_even(axis):
    return lax.axis_index(axis) % 2 == 0


def inside(axis):
    index = lax.axis_index(axis)
    before = jnp.where(index == 0, 0.0, 1.0).astype(F32)
    after = jnp.where(index == lax.axis_size(axis) - 1, 0.0, 1.0).astype(F32)
    return before, after


def pick(cond, one, other):
    return jnp.where(cond, one.astype(F32), other.astype(F32))


def split(value):
    high = value.astype(BF)
    return high, (value - high.astype(F32)).astype(BF)


def split3(value):
    high = value.astype(BF)
    rest = value - high.astype(F32)
    middle = rest.astype(BF)
    return high, middle, (rest - middle.astype(F32)).astype(BF)


def iota(shape, dim):
    return lax.broadcasted_iota(jnp.int32, shape, dim)


def edges_kernel(spec, xa, xb, ya, yb):
    rows, cols, bins = spec.shape
    even_x, even_y = is_even("gx"), is_even("gy")
    first, last = spec[0].astype(F32), spec[rows - 1].astype(F32)
    xa[...] = jnp.where(even_x, last, first).astype(BF)
    xb[...] = jnp.where(even_x, first, last).astype(BF)
    at, cell = iota((2 * rows, rows * cols), 0), iota((2 * rows, rows * cols), 1)
    wanted = jnp.where(at < rows, at * cols, (at - rows) * cols + cols - 1)
    chosen = (cell == wanted).astype(F32).astype(BF)
    sides = jnp.dot(chosen, spec[...].reshape(rows * cols, bins), preferred_element_type=F32)
    first, last = sides[0:rows], sides[rows:]
    ya[...] = jnp.where(even_y, last, first).astype(BF)
    yb[...] = jnp.where(even_y, first, last).astype(BF)


def ocean_edges_kernel(vel, lists, xa, xb):
    rows, cols, lanes = vel.shape
    even = is_even("gx")

    def put(at, last, first):
        n = last.shape[0]
        xa[at : at + n] = jnp.where(even, last, first).astype(BF)
        xb[at : at + n] = jnp.where(even, first, last).astype(BF)

    for i in range(HV):
        put(i * cols, vel[rows - HV + i], vel[i])
    last, first = vel[rows - 1], vel[0]
    put(HV * cols, last - last.astype(BF).astype(F32), first - first.astype(BF).astype(F32))
    for i in range(HL):
        put((HV + 1) * cols + i * 16, lists[rows - HL + i].astype(F32), lists[i].astype(F32))


def wave_kernel(spec, xa, xb, ya, yb, courant, source, land, weights, out, profile, pa, pb):
    rows, cols, _ = spec.shape
    even_x, even_y = is_even("gx"), is_even("gy")
    has_south, has_north = inside("gy")
    west, east = pick(even_x, xb[...], xa[...]), pick(even_x, xa[...], xb[...])
    south = pick(even_y, yb[...], ya[...]) * has_south
    north = pick(even_y, ya[...], yb[...]) * has_north
    cx, cy = courant[0:1, :], courant[1:2, :]
    ax, ay = jnp.abs(cx), jnp.abs(cy)
    from_west, from_south = cx > 0.0, cy > 0.0
    keep = 1.0 - ax - ay
    sub = iota((cols, 1), 0)
    parts = []
    for x in range(rows):
        center = spec[x].astype(F32)
        before = spec[x - 1].astype(F32) if x else west
        after = spec[x + 1].astype(F32) if x < rows - 1 else east
        below = jnp.where(sub == 0, south[x : x + 1, :], pltpu.roll(center, 1, 0))
        above = jnp.where(sub == cols - 1, north[x : x + 1, :], pltpu.roll(center, cols - 1, 0))
        advected = (
            keep * center
            + ax * jnp.where(from_west, before, after)
            + ay * jnp.where(from_south, below, above)
        )
        wind = 1.0 + 0.2 * source[:, x : x + 1]
        updated = land[:, x : x + 1] * (advected * (wind - 0.1 * advected))
        updated = updated.astype(BF)
        out[x] = updated
        part = jnp.dot(updated, weights[...], preferred_element_type=F32).astype(BF)
        profile[x] = part
        parts.append(part.astype(F32))
    for i in range(HX):
        first, last = parts[i], parts[rows - HX + i]
        pa[i] = jnp.where(even_x, last, first).astype(BF)
        pb[i] = jnp.where(even_x, first, last).astype(BF)


def halo_kernel(vel, oa, ob, lists, profile, pa, pb, ya, yb):
    rows, cols, lanes = vel.shape
    even_x, even_y = is_even("gx"), is_even("gy")
    wr, wc = profile.shape[0], profile.shape[1]

    def put(at, last, first):
        n = last.shape[0]
        ya[at : at + n] = jnp.where(even_y, last, first).astype(BF)
        yb[at : at + n] = jnp.where(even_y, first, last).astype(BF)

    before, after = pick(even_x, pb[...], pa[...]), pick(even_x, pa[...], pb[...])
    joined = jnp.concatenate([before.astype(BF), profile[...], after.astype(BF)], axis=0)
    count = (wr + 2 * HX) * wc
    slots = 24 * HY
    at, cell = iota((2 * slots, count), 0), iota((2 * slots, count), 1)
    side, rest = at // slots, at % slots
    column = rest // 24 + jnp.where(side == 0, wc - HY, 0)
    row = rest % 24
    chosen = ((row < wr + 2 * HX) & (cell == row * wc + column)).astype(F32).astype(BF)
    sides = jnp.dot(chosen, joined.reshape(count, lanes), preferred_element_type=F32)
    put(0, sides[0:slots], sides[slots:])

    sub = iota((EDGE, 1), 0)
    blocks = []
    low_at = HV * cols
    for r in range(rows + 2 * HV):
        if HV <= r < HV + rows:
            last, first = vel[r - HV, cols - EDGE : cols, :], vel[r - HV, 0:EDGE, :]
            low_last = last - last.astype(BF).astype(F32)
            low_first = first - first.astype(BF).astype(F32)
        else:
            i = r if r < HV else r - HV - rows
            ref_one, ref_two = (ob, oa) if r < HV else (oa, ob)

            def tail(start):
                both = pick(even_x, ref_one[start : start + cols, :], ref_two[start : start + cols, :])
                return both[cols - EDGE :], both[0:EDGE]

            last, first = tail(i * cols)
            if r in (HV - 1, HV + rows):
                low_last, low_first = tail(low_at)
            else:
                low_last = low_first = jnp.zeros((EDGE, lanes), F32)
        last = jnp.where(sub == 0, pltpu.roll(low_last, 1, 0), last)
        first = jnp.where(sub == EDGE - 1, pltpu.roll(low_first, EDGE - 1, 0), first)
        blocks.append((last, first))
    for r in range(0, rows + 2 * HV, 2):
        put(
            slots + r * EDGE,
            jnp.concatenate([blocks[r][0], blocks[r + 1][0]], axis=0),
            jnp.concatenate([blocks[r][1], blocks[r + 1][1]], axis=0),
        )

    lane = iota((1, lanes), 1)
    group = lane // LEAD
    per = lanes // LEAD
    acc = None
    start = slots + (rows + 2 * HV) * EDGE
    for r in range(rows + 2 * HL):
        if r % per == 0:
            acc = [jnp.zeros((16, lanes), F32)] * 2
        if HL <= r < HL + rows:
            own = lists[r - HL].astype(F32)
        else:
            i = r if r < HL else r - HL - rows
            at = (HV + 1) * cols + i * 16
            one, two = (ob, oa) if r < HL else (oa, ob)
            own = pick(even_x, one[at : at + 16, :], two[at : at + 16, :])
        to = (r % per) * LEAD
        acc = [
            jnp.where(group == r % per, pltpu.roll(own, (to - where) % lanes, 1), a)
            for a, where in zip(acc, (cols, LEAD))
        ]
        if r % per == per - 1 or r == rows + 2 * HL - 1:
            put(start + (r // per) * 16, acc[0], acc[1])


def ocean_kernel(
    own, oa, ob, lists, profile, pa, pb, ya, yb, wave_codes, wave_shares,
    out, current,
    vel, mid, prof, names, table, drift, spin, mean, picked,
):
    rows, cols, lanes = own.shape
    wr, wc = profile.shape[0], profile.shape[1]
    half = lanes // 2
    listed = rows + 2 * HL
    inner = cols + 2 * LEAD
    even_x, even_y = is_even("gx"), is_even("gy")
    has_south, has_north = inside("gy")
    lane = iota((1, lanes), 1)
    is_u = lane < half
    slots = 24 * HY

    def from_x(r, halo, start, n):
        one, two = (ob, oa) if r < halo else (oa, ob)
        return pick(even_x, one[start : start + n, :], two[start : start + n, :])

    def from_y(start, n):
        a, b = ya[start : start + n, :], yb[start : start + n, :]
        return pick(even_y, b, a) * has_south, pick(even_y, a, b) * has_north

    def fill(r, _):
        vel[r + HV, EDGE : EDGE + cols, :] = own[r]
        return 0

    lax.fori_loop(0, rows, fill, 0, unroll=4)
    for r in range(HV):
        vel[r, EDGE : EDGE + cols, :] = from_x(r, HV, r * cols, cols)
        vel[HV + rows + r, EDGE : EDGE + cols, :] = from_x(HV + rows, HV, r * cols, cols)
    vel[HV - 1, EDGE : EDGE + cols, :] += from_x(0, HV, HV * cols, cols)
    vel[HV + rows, EDGE : EDGE + cols, :] += from_x(HV, HV, HV * cols, cols)
    sub = iota((EDGE, 1), 0)
    for r in range(0, rows + 2 * HV, 2):
        south, north = from_y(slots + r * EDGE, 2 * EDGE)
        for i in range(2):
            low, high = south[i * EDGE : i * EDGE + EDGE], north[i * EDGE : i * EDGE + EDGE]
            low = jnp.where(sub == 0, 0.0, low) + jnp.where(sub == EDGE - 1, pltpu.roll(low, EDGE - 1, 0), 0.0)
            high = jnp.where(sub == EDGE - 1, 0.0, high) + jnp.where(sub == 0, pltpu.roll(high, 1, 0), 0.0)
            vel[r + i, 0:EDGE, :] = low
            vel[r + i, EDGE + cols :, :] = high

    group = lane // LEAD
    per = lanes // LEAD
    sub16 = iota((16, 1), 0)
    start = slots + (rows + 2 * HV) * EDGE
    place_of = (lane // RY).astype(F32)
    for r in range(listed):
        if r % per == 0:
            south, north = from_y(start + (r // per) * 16, 16)
        if HL <= r < HL + rows:
            full = lists[r - HL].astype(F32)
        else:
            i = r if r < HL else r - HL - rows
            full = from_x(0 if r < HL else HL, HL, (HV + 1) * cols + i * 16, 16)
        at = (r % per) * LEAD
        full = jnp.where(group == 0, pltpu.roll(south, (-at) % lanes, 1), full)
        full = jnp.where(group == 1 + cols // LEAD, pltpu.roll(north, (LEAD + cols - at) % lanes, 1), full)
        third = jnp.where(full >= 6.0, 2.0, jnp.where(full >= 3.0, 1.0, 0.0))
        table[r] = jnp.where(sub16 < K, third * (WIDE - 3.0) + full + place_of, full)

    prof[...] = jnp.zeros(prof.shape, F32)
    for x in range(wr + 2 * HX):
        if HX <= x < HX + wr:
            part = profile[x - HX].astype(F32)
        elif x < HX:
            part = pick(even_x, pb[x], pa[x])
        else:
            part = pick(even_x, pa[x - HX - wr], pb[x - HX - wr])
        prof[x * WIDE + HY : x * WIDE + HY + wc, :] = part
    south, north = from_y(0, slots)
    for c in range(HY):
        prof[pl.ds(c, wr + 2 * HX, stride=WIDE), :] = south[24 * c : 24 * c + wr + 2 * HX]
        prof[pl.ds(HY + wc + c, wr + 2 * HX, stride=WIDE), :] = north[24 * c : 24 * c + wr + 2 * HX]
    sign = jnp.where(is_u, 1.0, -1.0)
    block = 3 * WIDE
    for x in range(wr + 2 * HX - 2):
        part = pltpu.roll(prof[x * WIDE : x * WIDE + block, :], half, 1) * sign
        none = jnp.zeros((8, lanes), F32)
        names[x, :, 0:lanes] = jnp.concatenate([part, none], axis=0).astype(BF)
        names[x, :, lanes:] = jnp.concatenate([jnp.zeros((block, lanes), F32), none + 1.0], axis=0).astype(BF)

    place = iota((block, lanes), 0).astype(F32)

    def stokes(m, _):
        for u in range(UNROLL):
            r = m * UNROLL + u
            hot = jnp.where(place == table[r, 0:1, :], table[r, K : K + 1, :], 0.0)
            for k in range(1, K):
                hot = hot + jnp.where(place == table[r, k : k + 1, :], table[r, K + k : K + k + 1, :], 0.0)
            left = jnp.concatenate([hot, table[r, 8:16, :]], axis=0).astype(BF)
            both = lax.dot_general(left, names[(r + 1) // 2], ROWS_DOT, preferred_element_type=F32)
            drift[r] = both[0:inner, 0:lanes]
            spin[r] = both[0:inner, lanes:]
        return 0

    lax.fori_loop(0, listed // UNROLL, stokes, 0)

    def zeta(ref, r, base):
        def at(dx, dy):
            return ref[r + dx, base + dy : base + dy + inner, :]

        near = jnp.where(is_u, at(0, -1), at(1, 0)) - jnp.where(is_u, at(0, 1), at(-1, 0))
        far = jnp.where(is_u, at(0, -2), at(2, 0)) - jnp.where(is_u, at(0, 2), at(-2, 0))
        part = (8.0 / 12.0) * near - (1.0 / 12.0) * far
        return part + pltpu.roll(part, half, 1)

    base = EDGE - LEAD
    lift = HV - HL
    none = jnp.zeros((8, lanes), F32)

    def first_step(m, _):
        for u in range(UNROLL):
            r = m * UNROLL + u
            absolute = spin[r] + zeta(vel, r + lift, base)
            mid[r, 0:8, :] = none
            mid[r, 8 + inner :, :] = none
            mid[r, 8 : 8 + inner, :] = vel[r + lift, base : base + inner, :] + STEP * (absolute * drift[r])
        return 0

    lax.fori_loop(0, listed // UNROLL, first_step, 0)

    at = iota((2 * lanes, lanes), 0)
    to = iota((2 * lanes, lanes), 1)
    average = jnp.where((at % lanes) // half == to % 2, 1.0 / half, 0.0).astype(BF)
    total = jnp.zeros((inner, lanes), F32)
    for n in range(rows + 2):
        r = n + HL - 1
        absolute = spin[r] + zeta(mid, r, 8)
        old = vel[r + lift, base : base + inner, :] + mid[r, 8 : 8 + inner, :]
        new = 0.5 * old + (0.5 * STEP) * (absolute * drift[r])
        sums = jnp.dot(jnp.concatenate(split(new), axis=1), average, preferred_element_type=F32)
        total = jnp.where(lane // 2 == n, sums, total)
        if 1 <= n <= rows:
            out[n - 1] = new[LEAD : LEAD + cols]

    at, to = iota((inner, lanes), 0), iota((inner, lanes), 1)
    reach = (RY + 2) * wc
    chosen = ((to < reach) & (at == RY * (to % wc) + to // wc + LEAD - 1)).astype(F32).astype(BF)
    picked[...] = sum(
        lax.dot_general(p, chosen, ROWS_DOT, preferred_element_type=F32) for p in split3(total)
    )
    at, to = iota((lanes, lanes), 0), iota((lanes, lanes), 1)
    spread = ((at < reach) & (at % wc == to)).astype(F32).astype(BF)
    offset = lane // wc
    for c in range(2):
        summed = jnp.zeros((wr, lanes), F32)
        for near in range(RX + 2):
            share = jnp.zeros((wr, lanes), F32)
            for k in range(K):
                share = share + jnp.where(wave_codes[k] == near * (RY + 2) + offset, wave_shares[k], 0.0)
            summed = summed + share * picked[pl.ds(2 * near + c, wr, stride=2 * RX), :]
        sums = sum(jnp.dot(p, spread, preferred_element_type=F32) for p in split3(summed))
        current[c] = sums[:, 0:wc]


UNROLL = 19
VMEM = pl.BlockSpec(memory_space=pltpu.VMEM)
PARAMS = pltpu.CompilerParams(vmem_limit_bytes=40 << 20)


def call(kernel, name, outs, *args, scratch=()):
    return pl.pallas_call(
        kernel,
        out_shape=tuple(jax.ShapeDtypeStruct(shape, dtype) for shape, dtype in outs),
        in_specs=[VMEM] * len(args),
        out_specs=tuple([VMEM] * len(outs)),
        scratch_shapes=list(scratch),
        compiler_params=PARAMS,
        name=name,
    )(*args)


def shards(
    spectrum, courant, source, wave_land, stokes_kernel, velocity, coriolis,
    ocean_codes, ocean_weights, wave_codes, wave_weights,
):
    wr, wc, bins = spectrum.shape
    rows, cols, lanes = velocity.shape
    listed = rows + 2 * HL

    with jax.named_scope("spectrum_edges"):
        edge = ((wc, bins), BF)
        xa, xb, ya, yb = call(edges_kernel, "edges", [edge] * 2 + [((wr, bins), BF)] * 2, spectrum)
        xa, xb = exchange("gx", xa, xb)
        ya, yb = exchange("gy", ya, yb)

    with jax.named_scope("lists"):
        codes = jnp.transpose(ocean_codes, (0, 2, 1)).astype(BF)
        weights = jnp.transpose(ocean_weights, (0, 2, 1))
        shares = (weights / jnp.sum(weights, axis=1, keepdims=True)).astype(BF)
        high, low = split(coriolis)
        spare = jnp.zeros((rows, 16 - 2 * K - 2, cols), BF)
        lists = jnp.concatenate([codes, shares, high[:, None], low[:, None], spare], axis=1)
        lists = jnp.pad(lists, ((0, 0), (0, 0), (LEAD, lanes - LEAD - cols)))

    with jax.named_scope("ocean_edges"):
        size = (HV + 1) * cols + HL * 16
        oa, ob = call(ocean_edges_kernel, "ocean_edges", [((size, lanes), BF)] * 2, velocity, lists)
        oa, ob = exchange("gx", oa, ob)

    with jax.named_scope("wave"):
        new_spectrum, profiles, pa, pb = call(
            wave_kernel, "wave",
            [(spectrum.shape, BF), ((wr, wc, lanes), BF), ((HX, wc, lanes), BF), ((HX, wc, lanes), BF)],
            spectrum, xa, xb, ya, yb, courant, source.T, wave_land.T.astype(F32), stokes_kernel,
        )
        pa, pb = exchange("gx", pa, pb)

    with jax.named_scope("halo"):
        per = lanes // LEAD
        size = 24 * HY + (rows + 2 * HV) * EDGE + -(-listed // per) * 16
        ya, yb = call(
            halo_kernel, "halo", [((size, lanes), BF)] * 2, velocity, oa, ob, lists, profiles, pa, pb
        )
        ya, yb = exchange("gy", ya, yb)

    with jax.named_scope("wave_lists"):
        reach = RY + 2
        wc_t = jnp.transpose(wave_codes, (2, 0, 1))
        ww_t = jnp.transpose(wave_weights, (2, 0, 1))
        ww_t = ww_t / jnp.sum(ww_t, axis=0, keepdims=True)
        spare = [(0, 0), (0, 0), (0, lanes - reach * wc)]
        wc_t = jnp.pad(jnp.tile(wc_t, (1, 1, reach)), spare)
        ww_t = jnp.pad(jnp.tile(ww_t, (1, 1, reach)), spare)

    with jax.named_scope("ocean"):
        wide = cols + 2 * EDGE
        inner = cols + 2 * LEAD
        prow = wr + 2 * HX
        scratch = [
            pltpu.VMEM((rows + 2 * HV, wide, lanes), F32),
            pltpu.VMEM((listed, inner + 16, lanes), F32),
            pltpu.VMEM((prow * WIDE, lanes), F32),
            pltpu.VMEM((prow - 2, 3 * WIDE + 8, 2 * lanes), BF),
            pltpu.VMEM((listed, 16, lanes), F32),
            pltpu.VMEM((listed, inner, lanes), F32),
            pltpu.VMEM((listed, inner, lanes), F32),
            pltpu.VMEM((8, lanes), F32),
            pltpu.VMEM((lanes, lanes), F32),
        ]
        new_velocity, current = call(
            ocean_kernel, "ocean", [(velocity.shape, F32), ((2, wr, wc), F32)],
            velocity, oa, ob, lists, profiles, pa, pb, ya, yb, wc_t, ww_t, scratch=scratch,
        )
    return new_spectrum, new_velocity, current


def solution(mesh):
    return jax.shard_map(
        shards,
        mesh=mesh,
        in_specs=(
            P("gx", "gy", None), P(), P("gx", "gy"), P("gx", "gy"), P(), P("gx", "gy", None),
            P("gx", "gy"), P("gx", "gy", None), P("gx", "gy", None), P("gx", "gy", None), P("gx", "gy", None),
        ),
        out_specs=(P("gx", "gy", None), P("gx", "gy", None), P(None, "gx", "gy")),
        check_vma=False,
    )
```

time: 96.4 us -> 29.8 us (0.31)
  the two profiles are of different devices: /device:TPU:8 before, /device:TPU:0 now
where the time goes in v2:
time: 29.8 us; the launch traced here: 29.4 us
  starting transfers between devices  10.3 us (35%)
  Pallas kernels  7.44 us (25%)
  waiting for transfers between devices  6.19 us (21%)
  local copies, waits for them, and re-layouts  3.7 us (12%)
  other arithmetic  0.95 us (3%)
  between operations  0.84 us (3%)
    ppermute x10, starting transfers between devices, swap(): return lax.ppermute(value, ('gx', 'gy'), pairs)  10.3 us
    pallas_call x5, Pallas kernels, call(): pl.pallas_call(kernel, out_shape=tuple((jax.ShapeDtypeStruct(shape, dtype...  7.44 us
    ppermute x10, waiting for transfers between devices, swap(): return lax.ppermute(value, ('gx', 'gy'), pairs)  6.19 us
    unnamed x24, local copies, waits for them, and re-layouts  3.14 us
    convert_element_type x1, other arithmetic, shards(): codes = jnp.transpose(ocean_codes, (0, 2, 1)).astype(BF)  0.85 us
  transfers between devices with their start and end apart: 10, of which 2 were waited for; matrix products, arithmetic and copies ran while one was open for 6% of the time, Pallas kernels for 7%

profile of v2, /device:TPU:0, one launch (start us, length us, event | category | flops | bytes accessed | tf_op | source)
XLA Modules:
  0.0 29.4 jit_solution(13766776584672324624)
XLA Ops:
  0.6 0.0 copy-start
  0.6 0.0 copy-start.1
  0.7 0.0 copy-start.2
  0.7 1.1 %copy-done.2 = bf16[16,16,1152]{2,1,0:T(8,128)(2,1)S(1)} copy-done((bf16[16,16,1152]{2,1,0:T(8,128)(2,1)S(1)}, bf16[16,16,1152]{2,1,0:T(8,128)(2,1)}, u32[]{:S(2)}) %copy-start.2) | copy-done | bytes 589848
  1.8 0.2 edges.1
  2.0 0.5 %collective-permute-start = (bf16[16,1152]{1,0:T(8,128)(2,1)S(1)}, bf16[16,1152]{1,0:T(8,128)(2,1)S(1)}, u32[]{:S(2)}, u32[]{:S(2)}) collective-permute-start(bf16[16,1152]{1,0:T(8,128)(2,1)S(1)} %get-tuple-element.17), channel_id=1, source_target_pairs={{0,8},{1,9},{2,10},{3,11},{4,12},{5,13},{6,14},{7,15},{8,0},{9,1},... | collective-permute-start | bytes 110600 | tf_op jit(solution)/shard_map/spectrum_edges/ppermute | solution.py:39
  2.5 2.6 %collective-permute-start.1 = (bf16[16,1152]{1,0:T(8,128)(2,1)S(1)}, bf16[16,1152]{1,0:T(8,128)(2,1)S(1)}, u32[]{:S(2)}, u32[]{:S(2)}) collective-permute-start(bf16[16,1152]{1,0:T(8,128)(2,1)S(1)} %get-tuple-element.18), channel_id=1, source_target_pairs={{0,24},{1,25},{2,26},{3,27},{4,28},{5,29},{6,30},{7,31},{8,16},{9,... | collective-permute-start | bytes 110600 | tf_op jit(solution)/shard_map/spectrum_edges/ppermute | solution.py:39
  5.2 1.5 %collective-permute-start.2 = (bf16[16,1152]{1,0:T(8,128)(2,1)S(1)}, bf16[16,1152]{1,0:T(8,128)(2,1)S(1)}, u32[]{:S(2)}, u32[]{:S(2)}) collective-permute-start(bf16[16,1152]{1,0:T(8,128)(2,1)S(1)} %get-tuple-element.19), channel_id=1, source_target_pairs={{0,1},{1,0},{2,3},{3,2},{4,5},{5,4},{6,7},{7,6},{8,9},{9,8},{10,11... | collective-permute-start | bytes 110600 | tf_op jit(solution)/shard_map/spectrum_edges/ppermute | solution.py:39
  6.7 0.0 collective-permute-start.3
  6.7 0.9 %convert_bitcast_fusion = bf16[32,4,64]{2,1,0:T(4,128)(2,1)S(1)} fusion(s32[32,64,4]{1,2,0:T(4,128)} %param.18), kind=kLoop, calls=%fused_computation.7 | loop fusion | flops 8192 | bytes 49152 | tf_op jit(solution)/shard_map/lists/convert_element_type | solution.py:415
  7.5 0.0 copy-start.7
  7.6 0.1 fusion.2
  7.6 0.6 %copy-done.7 = f32[32,64]{1,0:T(8,128)S(1)} copy-done((f32[32,64]{1,0:T(8,128)S(1)}, f32[32,64]{1,0:T(8,128)}, u32[]{:S(2)}) %copy-start.7) | copy-done | bytes 8216
  8.3 0.1 concatenate.3
  8.5 0.1 pad.12.lists
  8.6 0.0 copy-start.8
  8.6 0.0 copy-start.3
  8.6 0.0 copy-start.4
  8.7 0.6 %collective-permute-start.4 = (bf16[432,128]{1,0:T(8,128)(2,1)S(1)}, bf16[432,128]{1,0:T(8,128)(2,1)S(1)}, u32[]{:S(2)}, u32[]{:S(2)}) collective-permute-start(bf16[432,128]{1,0:T(8,128)(2,1)S(1)} %get-tuple-element.22), channel_id=1, source_target_pairs={{0,8},{1,9},{2,10},{3,11},{4,12},{5,13},{6,14},{7,15},{8,0},{9,1},... | collective-permute-start | bytes 331784 | tf_op jit(solution)/shard_map/ocean_edges/ppermute | solution.py:39
  9.3 0.0 copy-done.8
  9.3 0.1 copy.25
  9.4 0.0 collective-permute-done.xa
  9.4 0.7 %collective-permute-start.5 = (bf16[432,128]{1,0:T(8,128)(2,1)S(1)}, bf16[432,128]{1,0:T(8,128)(2,1)S(1)}, u32[]{:S(2)}, u32[]{:S(2)}) collective-permute-start(bf16[432,128]{1,0:T(8,128)(2,1)S(1)} %get-tuple-element.23), channel_id=1, source_target_pairs={{0,24},{1,25},{2,26},{3,27},{4,28},{5,29},{6,30},{7,31},{8,16},{9,... | collective-permute-start | bytes 331784 | tf_op jit(solution)/shard_map/ocean_edges/ppermute | solution.py:39
  10.0 0.0 copy-done.9
  10.1 0.1 copy.24
  10.1 0.0 collective-permute-done.1.xb
  10.1 0.0 collective-permute-done.2.ya
  10.1 0.0 collective-permute-done.3.yb
  10.2 0.0 copy-done.3
  10.2 0.0 copy-done.4
  10.2 0.6 %copy-done.5 = f32[2,1152]{1,0:T(2,128)S(1)} copy-done((f32[2,1152]{1,0:T(2,128)S(1)}, f32[2,1152]{1,0:T(2,128)}, u32[]{:S(2)}) %copy-start.5) | copy-done | bytes 9240
  10.8 1.9 %wave.1 = (bf16[16,16,1152]{2,1,0:T(8,128)(2,1)}, bf16[16,16,128]{2,1,0:T(8,128)(2,1)S(1)}, bf16[3,16,128]{2,1,0:T(8,128)(2,1)S(1)}, bf16[3,16,128]{2,1,0:T(8,128)(2,1)S(1)}) custom-call(bf16[16,16,1152]{2,1,0:T(8,128)(2,1)S(1)} %copy-done.3, bf16[16,1152]{1,0:T(8,128)(2,1)S(1)} %collective-permute-done.xa, bf16[16,1152]{1,0:T(8,128)(2,1)S(1)} %collective-permute-done.1.xb, ...), custom_call_target="tpu_custom_call" | custom-call | tf_op jit(solution)/shard_map/wave/wave/pallas_call | solution.py:389
  12.7 0.5 %collective-permute-start.6 = (bf16[3,16,128]{2,1,0:T(8,128)(2,1)S(1)}, bf16[3,16,128]{2,1,0:T(8,128)(2,1)S(1)}, u32[]{:S(2)}, u32[]{:S(2)}) collective-permute-start(bf16[3,16,128]{2,1,0:T(8,128)(2,1)S(1)} %get-tuple-element.25), channel_id=1, source_target_pairs={{0,8},{1,9},{2,10},{3,11},{4,12},{5,13},{6,14},{7,15},{8,0},{9,1},... | collective-permute-start | bytes 36872 | tf_op jit(solution)/shard_map/wave/ppermute | solution.py:39
  13.2 1.1 %collective-permute-start.7 = (bf16[3,16,128]{2,1,0:T(8,128)(2,1)S(1)}, bf16[3,16,128]{2,1,0:T(8,128)(2,1)S(1)}, u32[]{:S(2)}, u32[]{:S(2)}) collective-permute-start(bf16[3,16,128]{2,1,0:T(8,128)(2,1)S(1)} %get-tuple-element.26), channel_id=1, source_target_pairs={{0,24},{1,25},{2,26},{3,27},{4,28},{5,29},{6,30},{7,31},{8,16},{9,... | collective-permute-start | bytes 36872 | tf_op jit(solution)/shard_map/wave/ppermute | solution.py:39
  14.3 0.0 collective-permute-done.6.pa
  14.3 2.1 %collective-permute-done.7.pb = bf16[3,16,128]{2,1,0:T(8,128)(2,1)S(1)} collective-permute-done((bf16[3,16,128]{2,1,0:T(8,128)(2,1)S(1)}, bf16[3,16,128]{2,1,0:T(8,128)(2,1)S(1)}, u32[]{:S(2)}, u32[]{:S(2)}) %collective-permute-start.7) | collective-permute-done | bytes 12320 | tf_op jit(solution)/shard_map/wave/ppermute | solution.py:39
  16.3 0.0 collective-permute-done.4.oa
  16.3 0.0 collective-permute-done.5.ob
  16.3 0.3 halo.1
  16.6 2.6 %collective-permute-start.8 = (bf16[416,128]{1,0:T(8,128)(2,1)S(1)}, bf16[416,128]{1,0:T(8,128)(2,1)S(1)}, u32[]{:S(2)}, u32[]{:S(2)}) collective-permute-start(bf16[416,128]{1,0:T(8,128)(2,1)S(1)} %get-tuple-element.27), channel_id=1, source_target_pairs={{0,1},{1,0},{2,3},{3,2},{4,5},{5,4},{6,7},{7,6},{8,9},{9,8},{10,11... | collective-permute-start | bytes 319496 | tf_op jit(solution)/shard_map/halo/ppermute | solution.py:39
  19.2 0.2 collective-permute-start.9
  19.4 0.0 copy-done.10
  19.5 0.5 %copy-done.6 = s32[16,16,4]{1,2,0:T(4,128)S(1)} copy-done((s32[16,16,4]{1,2,0:T(4,128)S(1)}, s32[16,16,4]{1,2,0:T(4,128)}, u32[]{:S(2)}) %copy-start.6) | copy-done | bytes 4120
  20.0 0.1 tile.21
  20.1 0.1 tile.9
  20.3 4.1 %collective-permute-done.8.ya = bf16[416,128]{1,0:T(8,128)(2,1)S(1)} collective-permute-done((bf16[416,128]{1,0:T(8,128)(2,1)S(1)}, bf16[416,128]{1,0:T(8,128)(2,1)S(1)}, u32[]{:S(2)}, u32[]{:S(2)}) %collective-permute-start.8) | collective-permute-done | bytes 106528 | tf_op jit(solution)/shard_map/halo/ppermute | solution.py:39
  24.4 0.0 collective-permute-done.9.yb
  24.4 5.0 %ocean.1 = (f32[32,64,128]{2,1,0:T(8,128)}, f32[2,16,16]{2,1,0:T(8,128)}) custom-call(f32[32,64,128]{2,1,0:T(8,128)S(1)} %copy-done.1, bf16[432,128]{1,0:T(8,128)(2,1)S(1)} %collective-permute-done.4.oa, bf16[432,128]{1,0:T(8,128)(2,1)S(1)} %collective-permute-done.5.ob, bf16[32,16,128]{2,1,0:T(8,128)(2,1)S(1)} %pad.12.lists, ...), custom_call_target="tpu_custom_call" | custom-call | tf_op jit(solution)/shard_map/ocean/ocean/pallas_call | solution.py:389
  (19 shorter events, 0.2 us)
Async XLA Ops:
  0.6 6.9 %copy-start = (f32[32,64,4]{1,2,0:T(4,128)S(1)}, f32[32,64,4]{1,2,0:T(4,128)}, u32[]{:S(2)}) copy-start(f32[32,64,4]{1,2,0:T(4,128)} %param.19) | copy-start | bytes 98308
  0.6 7.9 %copy-start.1 = (f32[32,64,128]{2,1,0:T(8,128)S(1)}, f32[32,64,128]{2,1,0:T(8,128)}, u32[]{:S(2)}) copy-start(f32[32,64,128]{2,1,0:T(8,128)} %own.1) | copy-start | bytes 3145732
  0.7 1.2 %copy-start.2 = (bf16[16,16,1152]{2,1,0:T(8,128)(2,1)S(1)}, bf16[16,16,1152]{2,1,0:T(8,128)(2,1)}, u32[]{:S(2)}) copy-start(bf16[16,16,1152]{2,1,0:T(8,128)(2,1)} %spec.3) | copy-start | bytes 1769476
  2.0 7.3 %collective-permute-start = (bf16[16,1152]{1,0:T(8,128)(2,1)S(1)}, bf16[16,1152]{1,0:T(8,128)(2,1)S(1)}, u32[]{:S(2)}, u32[]{:S(2)}) collective-permute-start(bf16[16,1152]{1,0:T(8,128)(2,1)S(1)} %get-tuple-element.17), channel_id=1, source_target_pairs={{0,8},{1,9},{2,10},{3,11},{4,12},{5,13},{6,14},{7,15},{8,0},{9,1},... | collective-permute-start | bytes 110600 | tf_op jit(solution)/shard_map/spectrum_edges/ppermute | solution.py:39
  2.5 7.6 %collective-permute-start.1 = (bf16[16,1152]{1,0:T(8,128)(2,1)S(1)}, bf16[16,1152]{1,0:T(8,128)(2,1)S(1)}, u32[]{:S(2)}, u32[]{:S(2)}) collective-permute-start(bf16[16,1152]{1,0:T(8,128)(2,1)S(1)} %get-tuple-element.18), channel_id=1, source_target_pairs={{0,24},{1,25},{2,26},{3,27},{4,28},{5,29},{6,30},{7,31},{8,16},{9,... | collective-permute-start | bytes 110600 | tf_op jit(solution)/shard_map/spectrum_edges/ppermute | solution.py:39
  5.2 5.0 %collective-permute-start.2 = (bf16[16,1152]{1,0:T(8,128)(2,1)S(1)}, bf16[16,1152]{1,0:T(8,128)(2,1)S(1)}, u32[]{:S(2)}, u32[]{:S(2)}) collective-permute-start(bf16[16,1152]{1,0:T(8,128)(2,1)S(1)} %get-tuple-element.19), channel_id=1, source_target_pairs={{0,1},{1,0},{2,3},{3,2},{4,5},{5,4},{6,7},{7,6},{8,9},{9,8},{10,11... | collective-permute-start | bytes 110600 | tf_op jit(solution)/shard_map/spectrum_edges/ppermute | solution.py:39
  6.7 3.5 %collective-permute-start.3 = (bf16[16,1152]{1,0:T(8,128)(2,1)S(1)}, bf16[16,1152]{1,0:T(8,128)(2,1)S(1)}, u32[]{:S(2)}, u32[]{:S(2)}) collective-permute-start(bf16[16,1152]{1,0:T(8,128)(2,1)S(1)} %get-tuple-element.20), channel_id=1, source_target_pairs={{0,8},{1,2},{2,1},{3,4},{4,3},{5,6},{6,5},{7,15},{8,0},{9,10},{10,... | collective-permute-start | bytes 110600 | tf_op jit(solution)/shard_map/spectrum_edges/ppermute | solution.py:39
  7.5 0.7 %copy-start.7 = (f32[32,64]{1,0:T(8,128)S(1)}, f32[32,64]{1,0:T(8,128)}, u32[]{:S(2)}) copy-start(f32[32,64]{1,0:T(8,128)} %param.17) | copy-start | bytes 24580
  8.6 0.7 %copy-start.8 = (s32[16,16]{1,0:T(8,128)S(1)}, s32[16,16]{1,0:T(8,128)}, u32[]{:S(2)}) copy-start(s32[16,16]{1,0:T(8,128)} %param.14) | copy-start | bytes 3076
  8.6 1.5 %copy-start.3 = (bf16[16,16,1152]{2,1,0:T(8,128)(2,1)S(1)}, bf16[16,16,1152]{2,1,0:T(8,128)(2,1)}, u32[]{:S(2)}) copy-start(bf16[16,16,1152]{2,1,0:T(8,128)(2,1)} %spec.3) | copy-start | bytes 1769476
  8.6 1.5 %copy-start.4 = (bf16[1152,128]{1,0:T(8,128)(2,1)S(1)}, bf16[1152,128]{1,0:T(8,128)(2,1)}, u32[]{:S(2)}) copy-start(bf16[1152,128]{1,0:T(8,128)(2,1)} %weights.1) | copy-start | bytes 884740
  8.7 7.6 %collective-permute-start.4 = (bf16[432,128]{1,0:T(8,128)(2,1)S(1)}, bf16[432,128]{1,0:T(8,128)(2,1)S(1)}, u32[]{:S(2)}, u32[]{:S(2)}) collective-permute-start(bf16[432,128]{1,0:T(8,128)(2,1)S(1)} %get-tuple-element.22), channel_id=1, source_target_pairs={{0,8},{1,9},{2,10},{3,11},{4,12},{5,13},{6,14},{7,15},{8,0},{9,1},... | collective-permute-start | bytes 331784 | tf_op jit(solution)/shard_map/ocean_edges/ppermute | solution.py:39
  9.4 0.7 %copy-start.9 = (f32[16,16]{1,0:T(8,128)S(1)}, f32[16,16]{1,0:T(8,128)}, u32[]{:S(2)}) copy-start(f32[16,16]{1,0:T(8,128)} %param.13) | copy-start | bytes 3076
  9.4 7.0 %collective-permute-start.5 = (bf16[432,128]{1,0:T(8,128)(2,1)S(1)}, bf16[432,128]{1,0:T(8,128)(2,1)S(1)}, u32[]{:S(2)}, u32[]{:S(2)}) collective-permute-start(bf16[432,128]{1,0:T(8,128)(2,1)S(1)} %get-tuple-element.23), channel_id=1, source_target_pairs={{0,24},{1,25},{2,26},{3,27},{4,28},{5,29},{6,30},{7,31},{8,16},{9,... | collective-permute-start | bytes 331784 | tf_op jit(solution)/shard_map/ocean_edges/ppermute | solution.py:39
  10.1 0.7 %copy-start.5 = (f32[2,1152]{1,0:T(2,128)S(1)}, f32[2,1152]{1,0:T(2,128)}, u32[]{:S(2)}) copy-start(f32[2,1152]{1,0:T(2,128)} %courant.1) | copy-start | bytes 27652
  12.7 1.6 %collective-permute-start.6 = (bf16[3,16,128]{2,1,0:T(8,128)(2,1)S(1)}, bf16[3,16,128]{2,1,0:T(8,128)(2,1)S(1)}, u32[]{:S(2)}, u32[]{:S(2)}) collective-permute-start(bf16[3,16,128]{2,1,0:T(8,128)(2,1)S(1)} %get-tuple-element.25), channel_id=1, source_target_pairs={{0,8},{1,9},{2,10},{3,11},{4,12},{5,13},{6,14},{7,15},{8,0},{9,1},... | collective-permute-start | bytes 36872 | tf_op jit(solution)/shard_map/wave/ppermute | solution.py:39
  13.2 3.1 %collective-permute-start.7 = (bf16[3,16,128]{2,1,0:T(8,128)(2,1)S(1)}, bf16[3,16,128]{2,1,0:T(8,128)(2,1)S(1)}, u32[]{:S(2)}, u32[]{:S(2)}) collective-permute-start(bf16[3,16,128]{2,1,0:T(8,128)(2,1)S(1)} %get-tuple-element.26), channel_id=1, source_target_pairs={{0,24},{1,25},{2,26},{3,27},{4,28},{5,29},{6,30},{7,31},{8,16},{9,... | collective-permute-start | bytes 36872 | tf_op jit(solution)/shard_map/wave/ppermute | solution.py:39
  16.3 3.1 %copy-start.10 = (f32[16,16,4]{1,2,0:T(4,128)S(1)}, f32[16,16,4]{1,2,0:T(4,128)}, u32[]{:S(2)}) copy-start(f32[16,16,4]{1,2,0:T(4,128)} %param.21) | copy-start | bytes 12292
  16.6 7.8 %collective-permute-start.8 = (bf16[416,128]{1,0:T(8,128)(2,1)S(1)}, bf16[416,128]{1,0:T(8,128)(2,1)S(1)}, u32[]{:S(2)}, u32[]{:S(2)}) collective-permute-start(bf16[416,128]{1,0:T(8,128)(2,1)S(1)} %get-tuple-element.27), channel_id=1, source_target_pairs={{0,1},{1,0},{2,3},{3,2},{4,5},{5,4},{6,7},{7,6},{8,9},{9,8},{10,11... | collective-permute-start | bytes 319496 | tf_op jit(solution)/shard_map/halo/ppermute | solution.py:39
  19.2 0.8 %copy-start.6 = (s32[16,16,4]{1,2,0:T(4,128)S(1)}, s32[16,16,4]{1,2,0:T(4,128)}, u32[]{:S(2)}) copy-start(s32[16,16,4]{1,2,0:T(4,128)} %param.20) | copy-start | bytes 12292
  19.2 5.2 %collective-permute-start.9 = (bf16[416,128]{1,0:T(8,128)(2,1)S(1)}, bf16[416,128]{1,0:T(8,128)(2,1)S(1)}, u32[]{:S(2)}, u32[]{:S(2)}) collective-permute-start(bf16[416,128]{1,0:T(8,128)(2,1)S(1)} %get-tuple-element.28), channel_id=1, source_target_pairs={{0,8},{1,2},{2,1},{3,4},{4,3},{5,6},{6,5},{7,15},{8,0},{9,10},{10,... | collective-permute-start | bytes 319496 | tf_op jit(solution)/shard_map/halo/ppermute | solution.py:39

commit v3 on v2

v3 whole, which is shorter than its diff:
```python
import jax
import jax.numpy as jnp
from jax import lax
from jax.experimental import pallas as pl
from jax.experimental.pallas import tpu as pltpu
from jax.sharding import PartitionSpec as P

K = 4
RX = 2
RY = 4
STEP = 0.5
TALL = 24
RIM = 4
HV, HL = 5, 3
HX, HY = 3, 2
EDGE = 8
BF = jnp.bfloat16
F32 = jnp.float32
ROWS_DOT = (((0,), (0,)), ((), ()))


def partner(i, count, parity):
    return (i ^ 1) if parity == 0 else ((i + 1) ^ 1) - 1


def swap(value, axis, parity):
    nx, ny = lax.axis_size("gx"), lax.axis_size("gy")
    pairs = []
    for x in range(nx):
        for y in range(ny):
            tx, ty = x, y
            if axis == "gx":
                tx = partner(x, nx, parity) % nx
            else:
                ty = partner(y, ny, parity)
                if not 0 <= ty < ny:
                    tx, ty = x ^ 1, y
            pairs.append((x * ny + y, tx * ny + ty))
    return lax.ppermute(value, ("gx", "gy"), pairs)


def exchange(axis, to_a, to_b):
    from_b = swap(to_b, axis, 1)
    from_a = swap(to_a, axis, 0)
    return from_a, from_b


def is_even(axis):
    return lax.axis_index(axis) % 2 == 0


def inside(axis):
    index = lax.axis_index(axis)
    before = jnp.where(index == 0, 0.0, 1.0).astype(F32)
    after = jnp.where(index == lax.axis_size(axis) - 1, 0.0, 1.0).astype(F32)
    return before, after


def pick(cond, one, other):
    return jnp.where(cond, one.astype(F32), other.astype(F32))


def split(value):
    high = value.astype(BF)
    return high, (value - high.astype(F32)).astype(BF)


def split3(value):
    high = value.astype(BF)
    rest = value - high.astype(F32)
    middle = rest.astype(BF)
    return high, middle, (rest - middle.astype(F32)).astype(BF)


def iota(shape, dim):
    return lax.broadcasted_iota(jnp.int32, shape, dim)


def edges_kernel(*refs):
    count = (len(refs) - 5) // 2
    given, (xa, xb, ya, yb), kept, sems = refs[:count], refs[count : count + 4], refs[count + 4 : -1], refs[-1]
    copies = [pltpu.make_async_copy(v, k, sems.at[i]) for i, (v, k) in enumerate(zip(given, kept))]
    for copy in copies:
        copy.start()
    copies[0].wait()
    spec = kept[0]
    rows, cols, bins = spec.shape
    even_x, even_y = is_even("gx"), is_even("gy")
    first, last = spec[0].astype(F32), spec[rows - 1].astype(F32)
    xa[...] = jnp.where(even_x, last, first).astype(BF)
    xb[...] = jnp.where(even_x, first, last).astype(BF)
    at, cell = iota((2 * rows, rows * cols), 0), iota((2 * rows, rows * cols), 1)
    wanted = jnp.where(at < rows, at * cols, (at - rows) * cols + cols - 1)
    chosen = (cell == wanted).astype(F32).astype(BF)
    sides = jnp.dot(chosen, spec[...].reshape(rows * cols, bins), preferred_element_type=F32)
    first, last = sides[0:rows], sides[rows:]
    ya[...] = jnp.where(even_y, last, first).astype(BF)
    yb[...] = jnp.where(even_y, first, last).astype(BF)
    for copy in copies[1:]:
        copy.wait()


def ocean_edges_kernel(vel_far, given, codes, weights, coriolis, xa, xb, lists, vel, kept, sems):
    rows, cols, lanes = vel.shape
    copies = [pltpu.make_async_copy(vel_far, vel, sems.at[0]), pltpu.make_async_copy(given, kept, sems.at[1])]
    for copy in copies:
        copy.start()
    even = is_even("gx")
    for r in range(rows):
        lists[r] = jnp.zeros((16, lanes), F32)
        weight = weights[r]
        turn = coriolis[r : r + 1, :]
        high = turn.astype(BF).astype(F32)
        lists[r, 0:K, 0:cols] = codes[r].astype(F32)
        lists[r, K : 2 * K, 0:cols] = weight / jnp.sum(weight, axis=0, keepdims=True)
        lists[r, 2 * K : 2 * K + 1, 0:cols] = high
        lists[r, 2 * K + 1 : 2 * K + 2, 0:cols] = turn - high

    copies[0].wait()

    def put(at, last, first):
        n = last.shape[0]
        xa[at : at + n] = jnp.where(even, last, first).astype(BF)
        xb[at : at + n] = jnp.where(even, first, last).astype(BF)

    for i in range(HV):
        put(i * cols, vel[rows - HV + i], vel[i])
    last, first = vel[rows - 1], vel[0]
    put(HV * cols, last - last.astype(BF).astype(F32), first - first.astype(BF).astype(F32))
    for i in range(HL):
        put((HV + 1) * cols + i * 16, lists[rows - HL + i], lists[i])
    copies[1].wait()


def wave_kernel(spec, xa, xb, ya, yb, courant, source, land, weights, out, profile, pa, pb):
    rows, cols, _ = spec.shape
    even_x, even_y = is_even("gx"), is_even("gy")
    has_south, has_north = inside("gy")
    west, east = pick(even_x, xb[...], xa[...]), pick(even_x, xa[...], xb[...])
    south = pick(even_y, yb[...], ya[...]) * has_south
    north = pick(even_y, ya[...], yb[...]) * has_north
    cx, cy = courant[0:1, :], courant[1:2, :]
    ax, ay = jnp.abs(cx), jnp.abs(cy)
    from_west, from_south = cx > 0.0, cy > 0.0
    keep = 1.0 - ax - ay
    sub = iota((cols, 1), 0)
    parts = []
    for x in range(rows):
        center = spec[x].astype(F32)
        before = spec[x - 1].astype(F32) if x else west
        after = spec[x + 1].astype(F32) if x < rows - 1 else east
        below = jnp.where(sub == 0, south[x : x + 1, :], pltpu.roll(center, 1, 0))
        above = jnp.where(sub == cols - 1, north[x : x + 1, :], pltpu.roll(center, cols - 1, 0))
        advected = (
            keep * center
            + ax * jnp.where(from_west, before, after)
            + ay * jnp.where(from_south, below, above)
        )
        wind = 1.0 + 0.2 * source[:, x : x + 1]
        updated = land[:, x : x + 1] * (advected * (wind - 0.1 * advected))
        updated = updated.astype(BF)
        out[x] = updated
        part = jnp.dot(updated, weights[...], preferred_element_type=F32).astype(BF)
        profile[x] = part
        parts.append(part.astype(F32))
    for i in range(HX):
        first, last = parts[i], parts[rows - HX + i]
        pa[i] = jnp.where(even_x, last, first).astype(BF)
        pb[i] = jnp.where(even_x, first, last).astype(BF)


def list_place(r, lanes):
    per = lanes // 16
    return r // (4 * per), (r % per) * 16 + RIM * ((r // per) % 4)


def halo_kernel(vel, oa, ob, lists, profile, pa, pb, ya, yb):
    rows, cols, lanes = vel.shape
    even_x, even_y = is_even("gx"), is_even("gy")
    wr, wc = profile.shape[0], profile.shape[1]

    def put(at, last, first):
        n = last.shape[0]
        ya[at : at + n] = jnp.where(even_y, last, first).astype(BF)
        yb[at : at + n] = jnp.where(even_y, first, last).astype(BF)

    before, after = pick(even_x, pb[...], pa[...]), pick(even_x, pa[...], pb[...])
    joined = jnp.concatenate([before.astype(BF), profile[...], after.astype(BF)], axis=0)
    count = (wr + 2 * HX) * wc
    slots = TALL * HY
    at, cell = iota((2 * slots, count), 0), iota((2 * slots, count), 1)
    side, rest = at // slots, at % slots
    column = rest // TALL + jnp.where(side == 0, wc - HY, 0)
    row = rest % TALL
    chosen = ((row < wr + 2 * HX) & (cell == row * wc + column)).astype(F32).astype(BF)
    sides = jnp.dot(chosen, joined.reshape(count, lanes), preferred_element_type=F32)
    put(0, sides[0:slots], sides[slots:])

    sub = iota((EDGE, 1), 0)
    blocks = []
    low_at = HV * cols
    for r in range(rows + 2 * HV):
        if HV <= r < HV + rows:
            last, first = vel[r - HV, cols - EDGE : cols, :], vel[r - HV, 0:EDGE, :]
            low_last = last - last.astype(BF).astype(F32)
            low_first = first - first.astype(BF).astype(F32)
        else:
            i = r if r < HV else r - HV - rows
            one, two = (ob, oa) if r < HV else (oa, ob)

            def ends(start):
                both = pick(even_x, one[start : start + cols, :], two[start : start + cols, :])
                return both[cols - EDGE :], both[0:EDGE]

            last, first = ends(i * cols)
            if r in (HV - 1, HV + rows):
                low_last, low_first = ends(low_at)
            else:
                low_last = low_first = jnp.zeros((EDGE, lanes), F32)
        last = jnp.where(sub == 0, pltpu.roll(low_last, 1, 0), last)
        first = jnp.where(sub == EDGE - 1, pltpu.roll(low_first, EDGE - 1, 0), first)
        blocks.append((last, first))
    for r in range(0, rows + 2 * HV, 2):
        put(
            slots + r * EDGE,
            jnp.concatenate([blocks[r][0], blocks[r + 1][0]], axis=0),
            jnp.concatenate([blocks[r][1], blocks[r + 1][1]], axis=0),
        )

    group = iota((1, lanes), 1) // RIM
    start = slots + (rows + 2 * HV) * EDGE
    tiles = list_place(rows + 2 * HL - 1, lanes)[0] + 1
    acc = [[jnp.zeros((16, lanes), F32)] * 2 for _ in range(tiles)]
    for r in range(rows + 2 * HL):
        if HL <= r < HL + rows:
            own = lists[r - HL]
        else:
            i = r if r < HL else r - HL - rows
            at = (HV + 1) * cols + i * 16
            one, two = (ob, oa) if r < HL else (oa, ob)
            own = pick(even_x, one[at : at + 16, :], two[at : at + 16, :])
        tile, to = list_place(r, lanes)
        acc[tile] = [
            jnp.where(group == to // RIM, pltpu.roll(own, (to - where) % lanes, 1), a)
            for a, where in zip(acc[tile], (cols - RIM, 0))
        ]
    for tile in range(tiles):
        put(start + tile * 16, acc[tile][0], acc[tile][1])


def vorticity(ref, r, base, count):
    half = ref.shape[-1] // 2
    is_u = iota((1, 2 * half), 1) < half

    def at(dx, dy):
        return ref[r + dx, base + dy : base + dy + count, :]

    near = jnp.where(is_u, at(0, -1), at(1, 0)) - jnp.where(is_u, at(0, 1), at(-1, 0))
    far = jnp.where(is_u, at(0, -2), at(2, 0)) - jnp.where(is_u, at(0, 2), at(-2, 0))
    part = (8.0 / 12.0) * near - (1.0 / 12.0) * far
    return part + pltpu.roll(part, half, 1)


def averager(lanes):
    at = iota((2 * lanes, lanes), 0)
    to = iota((2 * lanes, lanes), 1)
    half = lanes // 2
    return jnp.where((at % lanes) // half == to % 2, 1.0 / half, 0.0).astype(BF)


def turned(value):
    half = value.shape[-1] // 2
    sign = jnp.where(iota((1, 2 * half), 1) < half, 1.0, -1.0)
    return pltpu.roll(value, half, 1) * sign


def prepare_kernel(own, oa, ob, lists, vel, spin, turn, table, list_rim):
    rows, cols, lanes = own.shape
    wc = cols // RY
    listed = rows + 2 * HL
    unroll = listed // 2
    even_x = is_even("gx")
    lane = iota((1, lanes), 1)

    def from_x(r, halo, start, n):
        one, two = (ob, oa) if r < halo else (oa, ob)
        return pick(even_x, one[start : start + n, :], two[start : start + n, :])

    blank = jnp.zeros((EDGE, lanes), F32)

    def fill(r, _):
        vel[r + HV, EDGE : EDGE + cols, :] = own[r]
        return 0

    lax.fori_loop(0, rows, fill, 0, unroll=4)
    for r in range(rows + 2 * HV):
        vel[r, 0:EDGE, :] = blank
        vel[r, EDGE + cols :, :] = blank
    for r in range(HV):
        vel[r, EDGE : EDGE + cols, :] = from_x(r, HV, r * cols, cols)
        vel[HV + rows + r, EDGE : EDGE + cols, :] = from_x(HV, HV, r * cols, cols)
    vel[HV - 1, EDGE : EDGE + cols, :] += from_x(0, HV, HV * cols, cols)
    vel[HV + rows, EDGE : EDGE + cols, :] += from_x(HV, HV, HV * cols, cols)

    sub16 = iota((16, 1), 0)
    place_of = (lane // RY).astype(F32) - 1.0
    per = lanes // 16
    rim = jnp.zeros((16, lanes), F32)
    for r in range(listed):
        if HL <= r < HL + rows:
            full = lists[r - HL]
        else:
            i = r if r < HL else r - HL - rows
            full = from_x(0 if r < HL else HL, HL, (HV + 1) * cols + i * 16, 16)
        third = jnp.where(full >= 6.0, 2.0, jnp.where(full >= 3.0, 1.0, 0.0))
        table[r] = jnp.where(sub16 < K, third * (wc - 3.0) + full + place_of, full)
        to = (r % per) * 16
        rim = jnp.where(lane // RIM == to // RIM + 1, pltpu.roll(full, (to + RIM) % lanes, 1), rim)
        rim = jnp.where(lane // RIM == to // RIM + 2, pltpu.roll(full, (to + 3 * RIM - cols) % lanes, 1), rim)
        if r % per == per - 1 or r == listed - 1:
            list_rim[r // per] = rim
            rim = jnp.zeros((16, lanes), F32)

    ones = jnp.ones((8, lanes), BF)

    def absolute(m, _):
        for u in range(unroll):
            r = m * unroll + u
            wide = lax.dot_general(table[r, 2 * K :, :].astype(BF), ones, ROWS_DOT, preferred_element_type=F32)
            spin[r] = wide[0:cols]
            turn[r] = wide[0:cols] + vorticity(vel, r + HV - HL, EDGE, cols)
        return 0

    lax.fori_loop(0, listed // unroll, absolute, 0)


def inner_kernel(
    vel, spin, turn, table, profile, pa, pb,
    out, mid_rim, drift_rim, spin_rim, total, prof_rim,
    mid, names, prof, drift,
):
    rows, cols, lanes = out.shape
    wr, wc = profile.shape[0], profile.shape[1]
    listed = rows + 2 * HL
    prow = wr + 2 * HX
    unroll = listed // 2
    even_x = is_even("gx")
    lane = iota((1, lanes), 1)
    blank = jnp.zeros((EDGE, lanes), F32)
    for x in range(prow):
        if HX <= x < HX + wr:
            part = profile[x - HX].astype(F32)
        elif x < HX:
            part = pick(even_x, pb[x], pa[x])
        else:
            part = pick(even_x, pa[x - HX - wr], pb[x - HX - wr])
        part = turned(part)
        prof[x * wc : (x + 1) * wc, :] = part
        names[x * wc : (x + 1) * wc, :] = part.astype(BF)
    prof_rim[...] = jnp.zeros(prof_rim.shape, F32)
    for c in range(HY):
        prof_rim[0, pl.ds(HY + c, prow, stride=2 * HY), :] = prof[pl.ds(c, prow, stride=wc), :]
        prof_rim[1, pl.ds(c, prow, stride=2 * HY), :] = prof[pl.ds(wc - HY + c, prow, stride=wc), :]

    block = 3 * wc
    place = iota((block, lanes), 0).astype(F32)
    lift = HV - HL

    def first_step(m, _):
        for u in range(unroll):
            r = m * unroll + u
            hot = jnp.where(place == table[r, 0:1, :], table[r, K : K + 1, :], 0.0)
            for k in range(1, K):
                hot = hot + jnp.where(place == table[r, k : k + 1, :], table[r, K + k : K + k + 1, :], 0.0)
            named = names[pl.ds(pl.multiple_of((r + 1) // 2 * wc, wc), block), :]
            stokes = lax.dot_general(hot.astype(BF), named, ROWS_DOT, preferred_element_type=F32)[0:cols]
            drift[r] = stokes
            new = vel[r + lift, EDGE : EDGE + cols, :] + STEP * (turn[r] * stokes)
            mid[r, 0:EDGE, :] = blank
            mid[r, EDGE + cols :, :] = blank
            mid[r, EDGE : EDGE + cols, :] = new
            mid_rim[r, 0] = new[0 : 2 * EDGE]
            mid_rim[r, 1] = new[cols - 2 * EDGE :]
            for where in range(2):
                begin = RIM if where == 0 else cols - RIM - EDGE
                drift_rim[r, where] = drift[r, begin : begin + EDGE, :]
                spin_rim[r, where] = spin[r, begin : begin + EDGE, :]
        return 0

    lax.fori_loop(0, listed // unroll, first_step, 0)

    average = averager(lanes)
    means = jnp.zeros((cols, lanes), F32)
    for n in range(rows + 2):
        r = n + HL - 1
        absolute = spin[r] + vorticity(mid, r, EDGE, cols)
        old = vel[r + lift, EDGE : EDGE + cols, :] + mid[r, EDGE : EDGE + cols, :]
        new = 0.5 * old + (0.5 * STEP) * (absolute * drift[r])
        sums = jnp.dot(jnp.concatenate(split(new), axis=1), average, preferred_element_type=F32)
        means = jnp.where(lane // 2 == n, sums, means)
        if 1 <= n <= rows:
            out[n - 1] = new
    total[...] = means


def rim_kernel(
    own, oa, ob, ya, yb, mid_rim, drift_rim, spin_rim, total, list_rim, prof_rim,
    wave_codes, wave_shares, velocity_in,
    velocity_out, current,
    vel, mid, prof, drift, spin, picked, means, strips, sems,
):
    rows, cols, lanes = own.shape
    wr, wc = wave_codes.shape[1], current.shape[2]
    listed = rows + 2 * HL
    prow = wr + 2 * HX
    wide = 3 * EDGE
    even_x, even_y = is_even("gx"), is_even("gy")
    has_south, has_north = inside("gy")
    lane = iota((1, lanes), 1)
    sub = iota((EDGE, 1), 0)
    slots = TALL * HY

    def from_x(r, halo, start, n):
        one, two = (ob, oa) if r < halo else (oa, ob)
        return pick(even_x, one[start : start + n, :], two[start : start + n, :])

    def from_y(start, n):
        a, b = ya[start : start + n, :], yb[start : start + n, :]
        return pick(even_y, b, a) * has_south, pick(even_y, a, b) * has_north

    for r in range(rows + 2 * HV):
        if HV <= r < HV + rows:
            near, far = own[r - HV, 0 : 2 * EDGE, :], own[r - HV, cols - 2 * EDGE :, :]
        else:
            i = r if r < HV else r - HV - rows
            at = 0 if r < HV else HV
            near = from_x(at, HV, i * cols, 2 * EDGE)
            far = from_x(at, HV, (i + 1) * cols - 2 * EDGE, 2 * EDGE)
            if r in (HV - 1, HV + rows):
                near = near + from_x(at, HV, HV * cols, 2 * EDGE)
                far = far + from_x(at, HV, (HV + 1) * cols - 2 * EDGE, 2 * EDGE)
        vel[0, r, EDGE:, :] = near
        vel[1, r, 0 : 2 * EDGE, :] = far
    for r in range(0, rows + 2 * HV, 2):
        south, north = from_y(slots + r * EDGE, 2 * EDGE)
        for i in range(2):
            low, high = south[i * EDGE : i * EDGE + EDGE], north[i * EDGE : i * EDGE + EDGE]
            low = jnp.where(sub == 0, 0.0, low) + jnp.where(sub == EDGE - 1, pltpu.roll(low, EDGE - 1, 0), 0.0)
            high = jnp.where(sub == EDGE - 1, 0.0, high) + jnp.where(sub == 0, pltpu.roll(high, 1, 0), 0.0)
            vel[0, r + i, 0:EDGE, :] = low
            vel[1, r + i, 2 * EDGE :, :] = high

    prof[...] = prof_rim[...]
    south, north = from_y(0, slots)
    south, north = turned(south), turned(north)
    for c in range(HY):
        prof[0, pl.ds(c, TALL, stride=2 * HY), :] = south[TALL * c : TALL * (c + 1)]
        prof[1, pl.ds(HY + c, TALL, stride=2 * HY), :] = north[TALL * c : TALL * (c + 1)]

    per = lanes // 16
    start = slots + (rows + 2 * HV) * EDGE
    span = 2 * per * HY
    place = iota((2 * span, lanes), 0).astype(F32)
    part = lane % 16
    offset = (part // EDGE) * span + ((lane // 16 + 1) // 2) * (2 * HY) + (part % EDGE) // RIM
    sub16 = iota((16, 1), 0)
    ones = jnp.ones((8, lanes), F32)
    none = jnp.zeros((2 * span, lanes), F32)
    blank = jnp.zeros((8, lanes), F32)
    for g in range(-(-listed // per)):
        tile, to = list_place(g * per, lanes)
        south, north = from_y(start + tile * 16, 16)
        full = list_rim[g]
        full = jnp.where(part // RIM == 0, pltpu.roll(south, (-to) % lanes, 1), full)
        full = jnp.where(part // RIM == 3, pltpu.roll(north, (3 * RIM - to) % lanes, 1), full)
        third = jnp.where(full >= 6.0, 2.0, jnp.where(full >= 3.0, 1.0, 0.0))
        full = jnp.where(sub16 < K, third + full + offset.astype(F32), full)
        hot = jnp.zeros((2 * span, lanes), F32)
        for k in range(K):
            hot = hot + jnp.where(place == full[k : k + 1], full[K + k : K + k + 1], 0.0)
        left = jnp.concatenate([hot, full[2 * K :], blank], axis=0).astype(BF)
        begin = g * (per // 2) * 2 * HY
        named = jnp.concatenate([prof[0, begin : begin + span, :], prof[1, begin : begin + span, :]], axis=0)
        right = jnp.concatenate([
            jnp.concatenate([named, blank, blank], axis=0),
            jnp.concatenate([none, ones, blank], axis=0),
        ], axis=1).astype(BF)
        both = lax.dot_general(left, right, ROWS_DOT, preferred_element_type=F32)
        for i in range(min(per, listed - g * per)):
            for side in range(2):
                at = i * 16 + side * EDGE
                drift[side, g * per + i, side * EDGE : side * EDGE + EDGE, :] = both[at : at + EDGE, 0:lanes]
                spin[side, g * per + i, side * EDGE : side * EDGE + EDGE, :] = both[at : at + EDGE, lanes:]

    lift = HV - HL
    for r in range(listed):
        for side in range(2):
            base = RIM + side * EDGE
            drift[side, r, EDGE - side * EDGE : 2 * EDGE - side * EDGE, :] = drift_rim[r, side]
            spin[side, r, EDGE - side * EDGE : 2 * EDGE - side * EDGE, :] = spin_rim[r, side]
            mid[side, r, 2 * EDGE * side : 2 * EDGE * side + EDGE, :] = blank
            mid[side, r, EDGE - side * EDGE : wide - side * EDGE, :] = mid_rim[r, side]
            tile = slice(side * EDGE, side * EDGE + EDGE)
            absolute = spin[side, r, tile, :] + vorticity(vel.at[side], r + lift, base, EDGE)
            new = vel[side, r + lift, base : base + EDGE, :] + STEP * (absolute * drift[side, r, tile, :])
            mid[side, r, base : base + EDGE, :] = new

    average = averager(lanes)
    acc = jnp.zeros((4 * EDGE, lanes), F32)
    for n in range(rows + 2):
        r = n + HL - 1
        both = []
        for side in range(2):
            absolute = spin[side, r] + vorticity(mid.at[side], r, RIM, 2 * EDGE)
            tile = slice(RIM, RIM + 2 * EDGE)
            old = vel[side, r + lift, tile, :] + mid[side, r, tile, :]
            new = 0.5 * old + (0.5 * STEP) * (absolute * drift[side, r])
            both.append(new)
            if 1 <= n <= rows:
                strips[side, n - 1] = new[RIM : RIM + EDGE]
        sums = jnp.dot(
            jnp.concatenate(split(jnp.concatenate(both, axis=0)), axis=1), average, preferred_element_type=F32
        )
        acc = jnp.where(lane // 2 == n, sums, acc)
    copies = [
        pltpu.make_async_copy(strips.at[side], velocity_out.at[:, pl.ds(at, EDGE), :], sems.at[side])
        for side, at in ((0, 0), (1, cols - EDGE))
    ]
    for copy in copies:
        copy.start()
    means[0 : 2 * EDGE] = acc[0 : 2 * EDGE]
    means[2 * EDGE : 2 * RIM + cols - 2 * EDGE] = total[2 * EDGE - RIM : cols - 2 * EDGE + RIM, :]
    means[2 * RIM + cols - 2 * EDGE :] = acc[2 * EDGE :]

    count = cols + 2 * RIM
    at, to = iota((count, lanes), 0), iota((count, lanes), 1)
    reach = (RY + 2) * wc
    chosen = ((to < reach) & (at == RY * (to % wc) + to // wc + RIM - 1)).astype(F32).astype(BF)
    picked[...] = sum(
        lax.dot_general(p, chosen, ROWS_DOT, preferred_element_type=F32) for p in split3(means[...])
    )
    at, to = iota((lanes, lanes), 0), iota((lanes, lanes), 1)
    spread = ((at < reach) & (at % wc == to)).astype(F32).astype(BF)
    shift = lane // wc
    for c in range(2):
        summed = jnp.zeros((wr, lanes), F32)
        for near in range(RX + 2):
            share = jnp.zeros((wr, lanes), F32)
            for k in range(K):
                share = share + jnp.where(wave_codes[k] == near * (RY + 2) + shift, wave_shares[k], 0.0)
            summed = summed + share * picked[pl.ds(2 * near + c, wr, stride=2 * RX), :]
        sums = sum(jnp.dot(p, spread, preferred_element_type=F32) for p in split3(summed))
        current[c] = sums[:, 0:wc]
    for copy in copies:
        copy.wait()


VMEM = pl.BlockSpec(memory_space=pltpu.VMEM)
ANY = pl.BlockSpec(memory_space=pltpu.HBM)


def call(kernel, name, outs, *args, scratch=(), any_in=(), any_out=(), aliases=None):
    args = [pltpu.with_memory_space_constraint(v, pltpu.HBM) if i in any_in else v for i, v in enumerate(args)]
    return pl.pallas_call(
        kernel,
        out_shape=tuple(jax.ShapeDtypeStruct(shape, dtype) for shape, dtype in outs),
        in_specs=[ANY if i in any_in else VMEM for i in range(len(args))],
        out_specs=tuple(ANY if i in any_out else VMEM for i in range(len(outs))),
        scratch_shapes=list(scratch),
        input_output_aliases=aliases or {},
        compiler_params=pltpu.CompilerParams(vmem_limit_bytes=28 << 20),
        name=name,
    )(*args)


def shards(
    spectrum, courant, source, wave_land, stokes_kernel, velocity, coriolis,
    ocean_codes, ocean_weights, wave_codes, wave_weights,
):
    wr, wc, bins = spectrum.shape
    rows, cols, lanes = velocity.shape
    listed = rows + 2 * HL
    prow = wr + 2 * HX

    with jax.named_scope("spectrum_edges"):
        edge = ((wc, bins), BF)
        raw = [
            spectrum, courant, source, wave_land, coriolis,
            jnp.transpose(ocean_codes, (0, 2, 1)), jnp.transpose(ocean_weights, (0, 2, 1)),
        ]
        xa, xb, ya, yb, spectrum, courant, source, wave_land, coriolis, codes, weights = call(
            edges_kernel, "edges",
            [edge] * 2 + [((wr, bins), BF)] * 2 + [(v.shape, v.dtype) for v in raw],
            *raw, any_in=range(len(raw)), scratch=[pltpu.SemaphoreType.DMA((len(raw),))],
        )
        xa, xb = exchange("gx", xa, xb)
        ya, yb = exchange("gy", ya, yb)

    with jax.named_scope("ocean_edges"):
        size = (HV + 1) * cols + HL * 16
        oa, ob, lists, velocity, stokes_kernel = call(
            ocean_edges_kernel, "ocean_edges",
            [((size, lanes), BF)] * 2
            + [((rows, 16, lanes), F32), (velocity.shape, F32), (stokes_kernel.shape, BF)],
            velocity, stokes_kernel, codes, weights, coriolis,
            any_in=(0, 1), scratch=[pltpu.SemaphoreType.DMA((2,))],
        )
        oa, ob = exchange("gx", oa, ob)

    with jax.named_scope("wave"):
        new_spectrum, profiles, pa, pb = call(
            wave_kernel, "wave",
            [(spectrum.shape, BF), ((wr, wc, lanes), BF), ((HX, wc, lanes), BF), ((HX, wc, lanes), BF)],
            spectrum, xa, xb, ya, yb, courant, source.T, wave_land.T.astype(F32), stokes_kernel,
        )
        pa, pb = exchange("gx", pa, pb)

    with jax.named_scope("halo"):
        size = TALL * HY + (rows + 2 * HV) * EDGE + (list_place(listed - 1, lanes)[0] + 1) * 16
        ya, yb = call(
            halo_kernel, "halo", [((size, lanes), BF)] * 2, velocity, oa, ob, lists, profiles, pa, pb
        )
        ya, yb = exchange("gy", ya, yb)

    with jax.named_scope("wave_lists"):
        reach = RY + 2
        wc_t = jnp.transpose(wave_codes, (2, 0, 1))
        ww_t = jnp.transpose(wave_weights, (2, 0, 1))
        ww_t = ww_t / jnp.sum(ww_t, axis=0, keepdims=True)
        spare = [(0, 0), (0, 0), (0, lanes - reach * wc)]
        wc_t = jnp.pad(jnp.tile(wc_t, (1, 1, reach)), spare)
        ww_t = jnp.pad(jnp.tile(ww_t, (1, 1, reach)), spare)

    with jax.named_scope("prepare"):
        wide = cols + 2 * EDGE
        groups = -(-listed // (lanes // 16))
        vel, spin, turn, table, list_rim = call(
            prepare_kernel, "prepare",
            [
                ((rows + 2 * HV, wide, lanes), F32),
                ((listed, cols, lanes), F32),
                ((listed, cols, lanes), F32),
                ((listed, 16, lanes), F32),
                ((groups, 16, lanes), F32),
            ],
            velocity, oa, ob, lists,
        )

    with jax.named_scope("inner"):
        scratch = [
            pltpu.VMEM((listed, wide, lanes), F32),
            pltpu.VMEM((prow * wc, lanes), BF),
            pltpu.VMEM((prow * wc, lanes), F32),
            pltpu.VMEM((listed, cols, lanes), F32),
        ]
        new_velocity, mid_rim, drift_rim, spin_rim, total, prof_rim = call(
            inner_kernel, "inner",
            [
                (velocity.shape, F32),
                ((listed, 2, 2 * EDGE, lanes), F32),
                ((listed, 2, EDGE, lanes), F32),
                ((listed, 2, EDGE, lanes), F32),
                ((cols, lanes), F32),
                ((2, 2 * HY * (TALL + 4), lanes), F32),
            ],
            vel, spin, turn, table, profiles, pa, pb, scratch=scratch,
        )

    with jax.named_scope("rim"):
        scratch = [
            pltpu.VMEM((2, rows + 2 * HV, 3 * EDGE, lanes), F32),
            pltpu.VMEM((2, listed, 3 * EDGE, lanes), F32),
            pltpu.VMEM((2, 2 * HY * (TALL + 4), lanes), F32),
            pltpu.VMEM((2, listed, 2 * EDGE, lanes), F32),
            pltpu.VMEM((2, listed, 2 * EDGE, lanes), F32),
            pltpu.VMEM((lanes, lanes), F32),
            pltpu.VMEM((cols + 2 * RIM, lanes), F32),
            pltpu.VMEM((2, rows, EDGE, lanes), F32),
            pltpu.SemaphoreType.DMA((2,)),
        ]
        new_velocity, current = call(
            rim_kernel, "rim", [(velocity.shape, F32), ((2, wr, wc), F32)],
            velocity, oa, ob, ya, yb, mid_rim, drift_rim, spin_rim, total, list_rim, prof_rim, wc_t, ww_t, new_velocity,
            scratch=scratch, any_in=(13,), any_out=(0,), aliases={13: 0},
        )
    return new_spectrum, new_velocity, current


def solution(mesh):
    return jax.shard_map(
        shards,
        mesh=mesh,
        in_specs=(
            P("gx", "gy", None), P(), P("gx", "gy"), P("gx", "gy"), P(), P("gx", "gy", None),
            P("gx", "gy"), P("gx", "gy", None), P("gx", "gy", None), P("gx", "gy", None), P("gx", "gy", None),
        ),
        out_specs=(P("gx", "gy", None), P("gx", "gy", None), P(None, "gx", "gy")),
        check_vma=False,
    )
```

time: 29.8 us -> 26 us (0.87)
  the two profiles are of different devices: /device:TPU:0 before, /device:TPU:8 now
where the time goes in v3:
time: 26 us; the launch traced here: 25.8 us
  Pallas kernels  11.9 us (46%)
  waiting for transfers between devices  7.57 us (29%)
  starting transfers between devices  5.13 us (20%)
  between operations  0.76 us (3%)
  local copies, waits for them, and re-layouts  0.42 us (2%)
    pallas_call x7, Pallas kernels, call(): pl.pallas_call(kernel, out_shape=tuple((jax.ShapeDtypeStruct(shape, dtype...  11.9 us
    ppermute x10, waiting for transfers between devices, swap(): return lax.ppermute(value, ('gx', 'gy'), pairs)  7.57 us
    ppermute x10, starting transfers between devices, swap(): return lax.ppermute(value, ('gx', 'gy'), pairs)  5.13 us
  transfers between devices with their start and end apart: 10, of which 5 were waited for; matrix products, arithmetic and copies ran while one was open for 2% of the time, Pallas kernels for 29%

profile of v3, /device:TPU:8, one launch (start us, length us, event | category | flops | bytes accessed | tf_op | source)
XLA Modules:
  0.0 25.8 jit_solution(12187546561957798906)
XLA Ops:
  0.6 1.4 %edges.1 = (bf16[16,1152]{1,0:T(8,128)(2,1)S(1)}, bf16[16,1152]{1,0:T(8,128)(2,1)S(1)}, bf16[16,1152]{1,0:T(8,128)(2,1)S(1)}, bf16[16,1152]{1,0:T(8,128)(2,1)S(1...) custom-call(bf16[16,16,1152]{2,1,0:T(8,128)(2,1)} %refs_0_.1, ...), custom_call_target="tpu_custom_call" | custom-call | tf_op jit(solution)/shard_map/spectrum_edges/edges/pallas_call | solution.py:564
  2.0 0.1 collective-permute-start
  2.1 1.6 %collective-permute-start.1 = (bf16[16,1152]{1,0:T(8,128)(2,1)S(1)}, bf16[16,1152]{1,0:T(8,128)(2,1)S(1)}, u32[]{:S(2)}, u32[]{:S(2)}) collective-permute-start(bf16[16,1152]{1,0:T(8,128)(2,1)S(1)} %get-tuple-element.40), channel_id=1, source_target_pairs={{0,24},{1,25},{2,26},{3,27},{4,28},{5,29},{6,30},{7,31},{8,16},{9,... | collective-permute-start | bytes 110600 | tf_op jit(solution)/shard_map/spectrum_edges/ppermute | solution.py:39
  3.7 1.5 %collective-permute-start.2 = (bf16[16,1152]{1,0:T(8,128)(2,1)S(1)}, bf16[16,1152]{1,0:T(8,128)(2,1)S(1)}, u32[]{:S(2)}, u32[]{:S(2)}) collective-permute-start(bf16[16,1152]{1,0:T(8,128)(2,1)S(1)} %get-tuple-element.41), channel_id=1, source_target_pairs={{0,1},{1,0},{2,3},{3,2},{4,5},{5,4},{6,7},{7,6},{8,9},{9,8},{10,11... | collective-permute-start | bytes 110600 | tf_op jit(solution)/shard_map/spectrum_edges/ppermute | solution.py:39
  5.2 0.4 %collective-permute-start.3 = (bf16[16,1152]{1,0:T(8,128)(2,1)S(1)}, bf16[16,1152]{1,0:T(8,128)(2,1)S(1)}, u32[]{:S(2)}, u32[]{:S(2)}) collective-permute-start(bf16[16,1152]{1,0:T(8,128)(2,1)S(1)} %get-tuple-element.42), channel_id=1, source_target_pairs={{0,8},{1,2},{2,1},{3,4},{4,3},{5,6},{6,5},{7,15},{8,0},{9,10},{10,... | collective-permute-start | bytes 110600 | tf_op jit(solution)/shard_map/spectrum_edges/ppermute | solution.py:39
  5.6 1.3 %ocean_edges.1 = (bf16[432,128]{1,0:T(8,128)(2,1)S(1)}, bf16[432,128]{1,0:T(8,128)(2,1)S(1)}, f32[32,16,128]{2,1,0:T(8,128)S(1)}, f32[32,64,128]{2,1,0:T(8,128)S(1)}, bf16[1152,128]{1,0:T(8,128)(2,1)S(1)}) custom-call(f32[32,64,128]{2,1,0:T(8,128)} %vel_far.1, bf16[1152,128]{1,0:T(8,128)(2,1)} %given.1, s32[32,4,64]{2,1,0:T(4,128)S(1)} %get-tuple-element.46.codes, ...), custom_call_target="tpu_custom_call" | custom-call | tf_op jit(solution)/shard_map/ocean_edges/ocean_edges/pallas_call | solution.py:564
  6.9 0.1 collective-permute-start.4
  7.0 0.1 copy.20
  7.1 0.0 collective-permute-done.xa
  7.1 0.2 collective-permute-start.5
  7.3 0.1 copy.19
  7.4 0.0 collective-permute-done.1.xb
  7.4 0.3 %collective-permute-done.2.ya = bf16[16,1152]{1,0:T(8,128)(2,1)S(1)} collective-permute-done((bf16[16,1152]{1,0:T(8,128)(2,1)S(1)}, bf16[16,1152]{1,0:T(8,128)(2,1)S(1)}, u32[]{:S(2)}, u32[]{:S(2)}) %collective-permute-start.2) | collective-permute-done | bytes 36896 | tf_op jit(solution)/shard_map/spectrum_edges/ppermute | solution.py:39
  7.7 2.4 %collective-permute-done.3.yb = bf16[16,1152]{1,0:T(8,128)(2,1)S(1)} collective-permute-done((bf16[16,1152]{1,0:T(8,128)(2,1)S(1)}, bf16[16,1152]{1,0:T(8,128)(2,1)S(1)}, u32[]{:S(2)}, u32[]{:S(2)}) %collective-permute-start.3) | collective-permute-done | bytes 36896 | tf_op jit(solution)/shard_map/spectrum_edges/ppermute | solution.py:39
  10.1 0.0 copy-start.1
  10.1 0.0 copy-start
  10.1 1.9 %wave.1 = (bf16[16,16,1152]{2,1,0:T(8,128)(2,1)}, bf16[16,16,128]{2,1,0:T(8,128)(2,1)S(1)}, bf16[3,16,128]{2,1,0:T(8,128)(2,1)S(1)}, bf16[3,16,128]{2,1,0:T(8,128)(2,1)S(1)}) custom-call(bf16[16,16,1152]{2,1,0:T(8,128)(2,1)S(1)} %get-tuple-element.38.spec, bf16[16,1152]{1,0:T(8,128)(2,1)S(1)} %collective-permute-done.xa, ...), custom_call_target="tpu_custom_call" | custom-call | tf_op jit(solution)/shard_map/wave/wave/pallas_call | solution.py:564
  12.0 0.0 collective-permute-start.6
  12.0 0.6 %collective-permute-start.7 = (bf16[3,16,128]{2,1,0:T(8,128)(2,1)S(1)}, bf16[3,16,128]{2,1,0:T(8,128)(2,1)S(1)}, u32[]{:S(2)}, u32[]{:S(2)}) collective-permute-start(bf16[3,16,128]{2,1,0:T(8,128)(2,1)S(1)} %get-tuple-element.57), channel_id=1, source_target_pairs={{0,24},{1,25},{2,26},{3,27},{4,28},{5,29},{6,30},{7,31},{8,16},{9,... | collective-permute-start | bytes 36872 | tf_op jit(solution)/shard_map/wave/ppermute | solution.py:39
  12.6 0.5 %collective-permute-done.6.pa = bf16[3,16,128]{2,1,0:T(8,128)(2,1)S(1)} collective-permute-done((bf16[3,16,128]{2,1,0:T(8,128)(2,1)S(1)}, bf16[3,16,128]{2,1,0:T(8,128)(2,1)S(1)}, u32[]{:S(2)}, u32[]{:S(2)}) %collective-permute-start.6) | collective-permute-done | bytes 12320 | tf_op jit(solution)/shard_map/wave/ppermute | solution.py:39
  13.2 1.9 %collective-permute-done.7.pb = bf16[3,16,128]{2,1,0:T(8,128)(2,1)S(1)} collective-permute-done((bf16[3,16,128]{2,1,0:T(8,128)(2,1)S(1)}, bf16[3,16,128]{2,1,0:T(8,128)(2,1)S(1)}, u32[]{:S(2)}, u32[]{:S(2)}) %collective-permute-start.7) | collective-permute-done | bytes 12320 | tf_op jit(solution)/shard_map/wave/ppermute | solution.py:39
  15.1 0.0 collective-permute-done.4.oa
  15.1 0.0 collective-permute-done.5.ob
  15.1 0.3 %halo.1 = (bf16[416,128]{1,0:T(8,128)(2,1)S(1)}, bf16[416,128]{1,0:T(8,128)(2,1)S(1)}) custom-call(f32[32,64,128]{2,1,0:T(8,128)S(1)} %get-tuple-element.51.vel.own, bf16[432,128]{1,0:T(8,128)(2,1)S(1)} %collective-permute-done.4.oa, bf16[432,128]{1,0:T(8,128)(2,1)S(1)} %collective-permute-done.5.ob, f32[32,16,128]{2,1,0:T(8,128)S(1)} %get-tuple-element.54.lists, ...), custom_call_target="tpu_custom_call" | custom-call | tf_op jit(solution)/shard_map/halo/halo/pallas_call | solution.py:564
  15.4 0.6 %collective-permute-start.8 = (bf16[416,128]{1,0:T(8,128)(2,1)S(1)}, bf16[416,128]{1,0:T(8,128)(2,1)S(1)}, u32[]{:S(2)}, u32[]{:S(2)}) collective-permute-start(bf16[416,128]{1,0:T(8,128)(2,1)S(1)} %get-tuple-element.58), channel_id=1, source_target_pairs={{0,1},{1,0},{2,3},{3,2},{4,5},{5,4},{6,7},{7,6},{8,9},{9,8},{10,11... | collective-permute-start | bytes 319496 | tf_op jit(solution)/shard_map/halo/ppermute | solution.py:39
  16.0 0.0 collective-permute-start.9
  16.0 0.0 copy-done.1
  16.0 0.0 copy-done
  16.1 0.1 tile.9
  16.2 0.1 tile.21
  16.4 1.5 %prepare.1 = (f32[42,80,128]{2,1,0:T(8,128)S(1)}, f32[38,64,128]{2,1,0:T(8,128)S(1)}, f32[38,64,128]{2,1,0:T(8,128)S(1)}, f32[38,16,128]{2,1,0:T(8,128)S(1)}, f32[5,16,128]{2,1,0:T(8,128)S(1)}) custom-call(f32[32,64,128]{2,1,0:T(8,128)S(1)} %get-tuple-element.51.vel.own, bf16[432,128]{1,0:T(8,128)(2,1)S(1)} %collective-permute-done.4.oa, ...), custom_call_target="tpu_custom_call" | custom-call | tf_op jit(solution)/shard_map/prepare/prepare/pallas_call | solution.py:564
  17.8 2.9 %inner.1 = (f32[32,64,128]{2,1,0:T(8,128)}, f32[38,2,16,128]{3,2,1,0:T(8,128)S(1)}, f32[38,2,8,128]{3,2,1,0:T(8,128)S(1)}, f32[38,2,8,128]{3,2,1,0:T(8,128)S(1)}...) custom-call(f32[42,80,128]{2,1,0:T(8,128)S(1)} %get-tuple-element.60.vel, f32[38,64,128]{2,1,0:T(8,128)S(1)} %get-tuple-element.61.spin, ...), custom_call_target="tpu_custom_call" | custom-call | tf_op jit(solution)/shard_map/inner/inner/pallas_call | solution.py:564
  20.7 2.4 %collective-permute-done.8.ya = bf16[416,128]{1,0:T(8,128)(2,1)S(1)} collective-permute-done((bf16[416,128]{1,0:T(8,128)(2,1)S(1)}, bf16[416,128]{1,0:T(8,128)(2,1)S(1)}, u32[]{:S(2)}, u32[]{:S(2)}) %collective-permute-start.8) | collective-permute-done | bytes 106528 | tf_op jit(solution)/shard_map/halo/ppermute | solution.py:39
  23.1 0.0 collective-permute-done.9.yb
  23.1 2.7 %rim.1 = (f32[32,64,128]{2,1,0:T(8,128)}, f32[2,16,16]{2,1,0:T(8,128)}) custom-call(f32[32,64,128]{2,1,0:T(8,128)S(1)} %get-tuple-element.51.vel.own, bf16[432,128]{1,0:T(8,128)(2,1)S(1)} %collective-permute-done.4.oa, bf16[432,128]{1,0:T(8,128)(2,1)S(1)} %collective-permute-done.5.ob, ...), custom_call_target="tpu_custom_call", output_to_operand_aliasing={{0}: (13, {})} | custom-call | tf_op jit(solution)/shard_map/rim/rim/pallas_call | solution.py:564
  (8 shorter events, 0.1 us)
Async XLA Ops:
  2.0 5.1 %collective-permute-start = (bf16[16,1152]{1,0:T(8,128)(2,1)S(1)}, bf16[16,1152]{1,0:T(8,128)(2,1)S(1)}, u32[]{:S(2)}, u32[]{:S(2)}) collective-permute-start(bf16[16,1152]{1,0:T(8,128)(2,1)S(1)} %get-tuple-element.39), channel_id=1, source_target_pairs={{0,8},{1,9},{2,10},{3,11},{4,12},{5,13},{6,14},{7,15},{8,0},{9,1},... | collective-permute-start | bytes 110600 | tf_op jit(solution)/shard_map/spectrum_edges/ppermute | solution.py:39
  2.1 5.3 %collective-permute-start.1 = (bf16[16,1152]{1,0:T(8,128)(2,1)S(1)}, bf16[16,1152]{1,0:T(8,128)(2,1)S(1)}, u32[]{:S(2)}, u32[]{:S(2)}) collective-permute-start(bf16[16,1152]{1,0:T(8,128)(2,1)S(1)} %get-tuple-element.40), channel_id=1, source_target_pairs={{0,24},{1,25},{2,26},{3,27},{4,28},{5,29},{6,30},{7,31},{8,16},{9,... | collective-permute-start | bytes 110600 | tf_op jit(solution)/shard_map/spectrum_edges/ppermute | solution.py:39
  3.7 4.0 %collective-permute-start.2 = (bf16[16,1152]{1,0:T(8,128)(2,1)S(1)}, bf16[16,1152]{1,0:T(8,128)(2,1)S(1)}, u32[]{:S(2)}, u32[]{:S(2)}) collective-permute-start(bf16[16,1152]{1,0:T(8,128)(2,1)S(1)} %get-tuple-element.41), channel_id=1, source_target_pairs={{0,1},{1,0},{2,3},{3,2},{4,5},{5,4},{6,7},{7,6},{8,9},{9,8},{10,11... | collective-permute-start | bytes 110600 | tf_op jit(solution)/shard_map/spectrum_edges/ppermute | solution.py:39
  5.2 4.9 %collective-permute-start.3 = (bf16[16,1152]{1,0:T(8,128)(2,1)S(1)}, bf16[16,1152]{1,0:T(8,128)(2,1)S(1)}, u32[]{:S(2)}, u32[]{:S(2)}) collective-permute-start(bf16[16,1152]{1,0:T(8,128)(2,1)S(1)} %get-tuple-element.42), channel_id=1, source_target_pairs={{0,8},{1,2},{2,1},{3,4},{4,3},{5,6},{6,5},{7,15},{8,0},{9,10},{10,... | collective-permute-start | bytes 110600 | tf_op jit(solution)/shard_map/spectrum_edges/ppermute | solution.py:39
  6.9 8.2 %collective-permute-start.4 = (bf16[432,128]{1,0:T(8,128)(2,1)S(1)}, bf16[432,128]{1,0:T(8,128)(2,1)S(1)}, u32[]{:S(2)}, u32[]{:S(2)}) collective-permute-start(bf16[432,128]{1,0:T(8,128)(2,1)S(1)} %get-tuple-element.52), channel_id=1, source_target_pairs={{0,8},{1,9},{2,10},{3,11},{4,12},{5,13},{6,14},{7,15},{8,0},{9,1},... | collective-permute-start | bytes 331784 | tf_op jit(solution)/shard_map/ocean_edges/ppermute | solution.py:39
  7.1 8.0 %collective-permute-start.5 = (bf16[432,128]{1,0:T(8,128)(2,1)S(1)}, bf16[432,128]{1,0:T(8,128)(2,1)S(1)}, u32[]{:S(2)}, u32[]{:S(2)}) collective-permute-start(bf16[432,128]{1,0:T(8,128)(2,1)S(1)} %get-tuple-element.53), channel_id=1, source_target_pairs={{0,24},{1,25},{2,26},{3,27},{4,28},{5,29},{6,30},{7,31},{8,16},{9,... | collective-permute-start | bytes 331784 | tf_op jit(solution)/shard_map/ocean_edges/ppermute | solution.py:39
  10.1 5.9 %copy-start.1 = (f32[16,16,4]{1,2,0:T(4,128)S(1)}, f32[16,16,4]{1,2,0:T(4,128)}, u32[]{:S(2)}) copy-start(f32[16,16,4]{1,2,0:T(4,128)} %param.21) | copy-start | bytes 12292
  10.1 5.9 %copy-start = (s32[16,16,4]{1,2,0:T(4,128)S(1)}, s32[16,16,4]{1,2,0:T(4,128)}, u32[]{:S(2)}) copy-start(s32[16,16,4]{1,2,0:T(4,128)} %param.20) | copy-start | bytes 12292
  12.0 1.2 %collective-permute-start.6 = (bf16[3,16,128]{2,1,0:T(8,128)(2,1)S(1)}, bf16[3,16,128]{2,1,0:T(8,128)(2,1)S(1)}, u32[]{:S(2)}, u32[]{:S(2)}) collective-permute-start(bf16[3,16,128]{2,1,0:T(8,128)(2,1)S(1)} %get-tuple-element.56), channel_id=1, source_target_pairs={{0,8},{1,9},{2,10},{3,11},{4,12},{5,13},{6,14},{7,15},{8,0},{9,1},... | collective-permute-start | bytes 36872 | tf_op jit(solution)/shard_map/wave/ppermute | solution.py:39
  12.0 3.1 %collective-permute-start.7 = (bf16[3,16,128]{2,1,0:T(8,128)(2,1)S(1)}, bf16[3,16,128]{2,1,0:T(8,128)(2,1)S(1)}, u32[]{:S(2)}, u32[]{:S(2)}) collective-permute-start(bf16[3,16,128]{2,1,0:T(8,128)(2,1)S(1)} %get-tuple-element.57), channel_id=1, source_target_pairs={{0,24},{1,25},{2,26},{3,27},{4,28},{5,29},{6,30},{7,31},{8,16},{9,... | collective-permute-start | bytes 36872 | tf_op jit(solution)/shard_map/wave/ppermute | solution.py:39
  15.4 7.7 %collective-permute-start.8 = (bf16[416,128]{1,0:T(8,128)(2,1)S(1)}, bf16[416,128]{1,0:T(8,128)(2,1)S(1)}, u32[]{:S(2)}, u32[]{:S(2)}) collective-permute-start(bf16[416,128]{1,0:T(8,128)(2,1)S(1)} %get-tuple-element.58), channel_id=1, source_target_pairs={{0,1},{1,0},{2,3},{3,2},{4,5},{5,4},{6,7},{7,6},{8,9},{9,8},{10,11... | collective-permute-start | bytes 319496 | tf_op jit(solution)/shard_map/halo/ppermute | solution.py:39
  16.0 7.2 %collective-permute-start.9 = (bf16[416,128]{1,0:T(8,128)(2,1)S(1)}, bf16[416,128]{1,0:T(8,128)(2,1)S(1)}, u32[]{:S(2)}, u32[]{:S(2)}) collective-permute-start(bf16[416,128]{1,0:T(8,128)(2,1)S(1)} %get-tuple-element.59), channel_id=1, source_target_pairs={{0,8},{1,2},{2,1},{3,4},{4,3},{5,6},{6,5},{7,15},{8,0},{9,10},{10,... | collective-permute-start | bytes 319496 | tf_op jit(solution)/shard_map/halo/ppermute | solution.py:39

commit v4 on v3

--- a/solution.py
+++ b/solution.py
@@ -76,64 +76,72 @@
     return lax.broadcasted_iota(jnp.int32, shape, dim)
 
 
+def x_rows(cols):
+    return (HV - 1) * cols, cols, HL * 16
+
+
 def edges_kernel(*refs):
-    count = (len(refs) - 5) // 2
-    given, (xa, xb, ya, yb), kept, sems = refs[:count], refs[count : count + 4], refs[count + 4 : -1], refs[-1]
-    copies = [pltpu.make_async_copy(v, k, sems.at[i]) for i, (v, k) in enumerate(zip(given, kept))]
+    (spec_far, courant_far, source_far, land_far, codes_far, weights_far, coriolis_far, vel_far) = refs[:8]
+    (xa, xb, ya, yb, oa, ob, lists, spec, courant, source, land, codes, weights, coriolis, vel, sems) = refs[8:]
+    rows, cols, bins = spec.shape
+    lanes = vel.shape[-1]
+    pairs = [(spec_far, spec)]
+    pairs += [(vel_far.at[pl.ds(at, HV)], vel.at[i]) for i, at in ((0, 0), (1, vel_far.shape[0] - HV))]
+    pairs += [(codes_far, codes), (weights_far, weights), (coriolis_far, coriolis)]
+    pairs += [(courant_far, courant), (source_far, source), (land_far, land)]
+    copies = [pltpu.make_async_copy(one, two, sems.at[i]) for i, (one, two) in enumerate(pairs)]
     for copy in copies:
         copy.start()
+    even_x, even_y = is_even("gx"), is_even("gy")
+
+    def put(at, last, first):
+        n = last.shape[0]
+        oa[at : at + n] = jnp.where(even_x, last, first).astype(BF)
+        ob[at : at + n] = jnp.where(even_x, first, last).astype(BF)
+
+    at, cell = iota((2 * rows, rows * cols), 0), iota((2 * rows, rows * cols), 1)
+    wanted = jnp.where(at < rows, at * cols, (at - rows) * cols + cols - 1)
+    chosen = (cell == wanted).astype(F32).astype(BF)
     copies[0].wait()
-    spec = kept[0]
-    rows, cols, bins = spec.shape
-    even_x, even_y = is_even("gx"), is_even("gy")
+    sides = jnp.dot(chosen, spec[...].reshape(rows * cols, bins), preferred_element_type=F32)
     first, last = spec[0].astype(F32), spec[rows - 1].astype(F32)
     xa[...] = jnp.where(even_x, last, first).astype(BF)
     xb[...] = jnp.where(even_x, first, last).astype(BF)
-    at, cell = iota((2 * rows, rows * cols), 0), iota((2 * rows, rows * cols), 1)
-    wanted = jnp.where(at < rows, at * cols, (at - rows) * cols + cols - 1)
-    chosen = (cell == wanted).astype(F32).astype(BF)
-    sides = jnp.dot(chosen, spec[...].reshape(rows * cols, bins), preferred_element_type=F32)
     first, last = sides[0:rows], sides[rows:]
     ya[...] = jnp.where(even_y, last, first).astype(BF)
     yb[...] = jnp.where(even_y, first, last).astype(BF)
+
     for copy in copies[1:]:
         copy.wait()
-
-
-def ocean_edges_kernel(vel_far, given, codes, weights, coriolis, xa, xb, lists, vel, kept, sems):
-    rows, cols, lanes = vel.shape
-    copies = [pltpu.make_async_copy(vel_far, vel, sems.at[0]), pltpu.make_async_copy(given, kept, sems.at[1])]
-    for copy in copies:
-        copy.start()
-    even = is_even("gx")
-    for r in range(rows):
+    listed, wide = codes.shape[0], codes.shape[2]
+    is_u = iota((1, lanes), 1) < lanes // 2
+    outer = [
+        jnp.where(is_u, pltpu.roll(vel[side, one], lanes // 2, 1), vel[side, two])
+        for side, one, two in ((1, 0, 1), (0, HV - 1, HV - 2))
+    ]
+    put(0, *outer)
+    for i in range(1, HV - 1):
+        put(i * wide, vel[1, i + 1], vel[0, i - 1])
+    last, first = vel[1, HV - 1], vel[0, 0]
+    put((HV - 1) * wide, last - last.astype(BF).astype(F32), first - first.astype(BF).astype(F32))
+    for r in range(listed):
         lists[r] = jnp.zeros((16, lanes), F32)
         weight = weights[r]
         turn = coriolis[r : r + 1, :]
         high = turn.astype(BF).astype(F32)
-        lists[r, 0:K, 0:cols] = codes[r].astype(F32)
-        lists[r, K : 2 * K, 0:cols] = weight / jnp.sum(weight, axis=0, keepdims=True)
-        lists[r, 2 * K : 2 * K + 1, 0:cols] = high
-        lists[r, 2 * K + 1 : 2 * K + 2, 0:cols] = turn - high
-
-    copies[0].wait()
-
-    def put(at, last, first):
-        n = last.shape[0]
-        xa[at : at + n] = jnp.where(even, last, first).astype(BF)
-        xb[at : at + n] = jnp.where(even, first, last).astype(BF)
-
-    for i in range(HV):
-        put(i * cols, vel[rows - HV + i], vel[i])
-    last, first = vel[rows - 1], vel[0]
-    put(HV * cols, last - last.astype(BF).astype(F32), first - first.astype(BF).astype(F32))
+        lists[r, 0:K, 0:wide] = codes[r].astype(F32)
+        lists[r, K : 2 * K, 0:wide] = weight / jnp.sum(weight, axis=0, keepdims=True)
+        lists[r, 2 * K : 2 * K + 1, 0:wide] = high
+        lists[r, 2 * K + 1 : 2 * K + 2, 0:wide] = turn - high
     for i in range(HL):
-        put((HV + 1) * cols + i * 16, lists[rows - HL + i], lists[i])
-    copies[1].wait()
-
-
-def wave_kernel(spec, xa, xb, ya, yb, courant, source, land, weights, out, profile, pa, pb):
-    rows, cols, _ = spec.shape
+        put(HV * wide + i * 16, lists[listed - HL + i], lists[i])
+
+
+def wave_kernel(spec, xa, xb, ya, yb, courant, source, land, weights_far, vel_far, out, profile, pa, pb, vel, weights, sems):
+    rows, cols, bins = spec.shape
+    copies = [pltpu.make_async_copy(weights_far, weights, sems.at[0]), pltpu.make_async_copy(vel_far, vel, sems.at[1])]
+    for copy in copies:
+        copy.start()
     even_x, even_y = is_even("gx"), is_even("gy")
     has_south, has_north = inside("gy")
     west, east = pick(even_x, xb[...], xa[...]), pick(even_x, xa[...], xb[...])
@@ -144,7 +152,7 @@
     from_west, from_south = cx > 0.0, cy > 0.0
     keep = 1.0 - ax - ay
     sub = iota((cols, 1), 0)
-    parts = []
+    cells, parts = [], []
     for x in range(rows):
         center = spec[x].astype(F32)
         before = spec[x - 1].astype(F32) if x else west
@@ -160,13 +168,20 @@
         updated = land[:, x : x + 1] * (advected * (wind - 0.1 * advected))
         updated = updated.astype(BF)
         out[x] = updated
-        part = jnp.dot(updated, weights[...], preferred_element_type=F32).astype(BF)
-        profile[x] = part
-        parts.append(part.astype(F32))
+        cells.append(updated)
+        if x == 3 * rows // 4 - 1:
+            copies[0].wait()
+        if x in (3 * rows // 4 - 1, rows - 1):
+            part = jnp.dot(jnp.concatenate(cells, axis=0), weights[...], preferred_element_type=F32)
+            parts += [part[i * cols : (i + 1) * cols] for i in range(len(cells))]
+            cells = []
+    for x in range(rows):
+        profile[x] = parts[x].astype(BF)
     for i in range(HX):
         first, last = parts[i], parts[rows - HX + i]
         pa[i] = jnp.where(even_x, last, first).astype(BF)
         pb[i] = jnp.where(even_x, first, last).astype(BF)
+    copies[1].wait()
 
 
 def list_place(r, lanes):
@@ -174,8 +189,14 @@
     return r // (4 * per), (r % per) * 16 + RIM * ((r // per) % 4)
 
 
+def y_rows(rows):
+    pairs = (rows + 2 * HV + 1) // 2
+    return TALL * HY, (pairs + pairs % 2) * EDGE, -(-(rows + 2) // 16) * 16
+
+
 def halo_kernel(vel, oa, ob, lists, profile, pa, pb, ya, yb):
-    rows, cols, lanes = vel.shape
+    vrow, lanes = vel.shape[0], vel.shape[2]
+    rows, cols = vrow - 2 * HV, vel.shape[1] - 2 * EDGE
     even_x, even_y = is_even("gx"), is_even("gy")
     wr, wc = profile.shape[0], profile.shape[1]
 
@@ -197,38 +218,30 @@
     put(0, sides[0:slots], sides[slots:])
 
     sub = iota((EDGE, 1), 0)
+    is_u = iota((1, lanes), 1) < lanes // 2
+    end = EDGE + cols
     blocks = []
-    low_at = HV * cols
-    for r in range(rows + 2 * HV):
-        if HV <= r < HV + rows:
-            last, first = vel[r - HV, cols - EDGE : cols, :], vel[r - HV, 0:EDGE, :]
-            low_last = last - last.astype(BF).astype(F32)
-            low_first = first - first.astype(BF).astype(F32)
-        else:
-            i = r if r < HV else r - HV - rows
-            one, two = (ob, oa) if r < HV else (oa, ob)
-
-            def ends(start):
-                both = pick(even_x, one[start : start + cols, :], two[start : start + cols, :])
-                return both[cols - EDGE :], both[0:EDGE]
-
-            last, first = ends(i * cols)
-            if r in (HV - 1, HV + rows):
-                low_last, low_first = ends(low_at)
-            else:
-                low_last = low_first = jnp.zeros((EDGE, lanes), F32)
-        last = jnp.where(sub == 0, pltpu.roll(low_last, 1, 0), last)
-        first = jnp.where(sub == EDGE - 1, pltpu.roll(low_first, EDGE - 1, 0), first)
+    for r in range(vrow):
+        to = RIM * (r % 2)
+        one, two = vel[r, end - RIM - to : end + RIM - to, :], vel[r, end - RIM - 1 - to : end + RIM - 1 - to, :]
+        last = jnp.where(sub == to, jnp.where(is_u, two, pltpu.roll(one, lanes // 2, 1)), one)
+        one, two = vel[r, EDGE - to : 2 * EDGE - to, :], vel[r, EDGE + 1 - to : 2 * EDGE + 1 - to, :]
+        first = jnp.where(sub == to + RIM - 1, jnp.where(is_u, one, pltpu.roll(two, lanes // 2, 1)), one)
         blocks.append((last, first))
-    for r in range(0, rows + 2 * HV, 2):
-        put(
-            slots + r * EDGE,
-            jnp.concatenate([blocks[r][0], blocks[r + 1][0]], axis=0),
-            jnp.concatenate([blocks[r][1], blocks[r + 1][1]], axis=0),
-        )
+    pairs = [
+        [jnp.where(sub < RIM, blocks[r][i], blocks[r + 1][i]) for i in range(2)] for r in range(0, vrow, 2)
+    ]
+    pairs += [[jnp.zeros((EDGE, lanes), F32)] * 2] * (len(pairs) % 2)
+    for i in range(0, len(pairs), 2):
+        put(slots + i * EDGE, *[jnp.concatenate([pairs[i][j], pairs[i + 1][j]], axis=0) for j in range(2)])
+    start = slots + len(pairs) * EDGE
+    edge = [vel[HV - 1 : HV + rows + 1, at, :] for at in (end - 1, EDGE)]
+    spare = jnp.zeros((-(rows + 2) % 16, lanes), F32)
+    put(start, *[jnp.concatenate([v - v.astype(BF).astype(F32), spare], axis=0) for v in edge])
+    start += rows + 2 + spare.shape[0]
 
     group = iota((1, lanes), 1) // RIM
-    start = slots + (rows + 2 * HV) * EDGE
+    x_start = oa.shape[0] - HL * 16
     tiles = list_place(rows + 2 * HL - 1, lanes)[0] + 1
     acc = [[jnp.zeros((16, lanes), F32)] * 2 for _ in range(tiles)]
     for r in range(rows + 2 * HL):
@@ -236,7 +249,7 @@
             own = lists[r - HL]
         else:
             i = r if r < HL else r - HL - rows
-            at = (HV + 1) * cols + i * 16
+            at = x_start + i * 16
             one, two = (ob, oa) if r < HL else (oa, ob)
             own = pick(even_x, one[at : at + 16, :], two[at : at + 16, :])
         tile, to = list_place(r, lanes)
@@ -292,15 +305,24 @@
         vel[r + HV, EDGE : EDGE + cols, :] = own[r]
         return 0
 
-    lax.fori_loop(0, rows, fill, 0, unroll=4)
+    lax.fori_loop(0, rows, fill, 0, unroll=8)
     for r in range(rows + 2 * HV):
         vel[r, 0:EDGE, :] = blank
         vel[r, EDGE + cols :, :] = blank
-    for r in range(HV):
-        vel[r, EDGE : EDGE + cols, :] = from_x(r, HV, r * cols, cols)
-        vel[HV + rows + r, EDGE : EDGE + cols, :] = from_x(HV, HV, r * cols, cols)
-    vel[HV - 1, EDGE : EDGE + cols, :] += from_x(0, HV, HV * cols, cols)
-    vel[HV + rows, EDGE : EDGE + cols, :] += from_x(HV, HV, HV * cols, cols)
+    for i in range(HV - 1):
+        near, far = from_x(0, HV, i * cols, cols), from_x(HV, HV, i * cols, cols)
+        if i == 0:
+            vel[0, EDGE : EDGE + cols, :] = pltpu.roll(near, lanes // 2, 1)
+            vel[2 * HV + rows - 1, EDGE : EDGE + cols, :] = pltpu.roll(far, lanes // 2, 1)
+            vel[1, EDGE : EDGE + cols, :] = near
+            vel[2 * HV + rows - 2, EDGE : EDGE + cols, :] = far
+        else:
+            if i == HV - 2:
+                near = near + from_x(0, HV, (HV - 1) * cols, cols)
+            if i == 1:
+                far = far + from_x(HV, HV, (HV - 1) * cols, cols)
+            vel[i + 1, EDGE : EDGE + cols, :] = near
+            vel[HV + rows + i - 1, EDGE : EDGE + cols, :] = far
 
     sub16 = iota((16, 1), 0)
     place_of = (lane // RY).astype(F32) - 1.0
@@ -311,7 +333,7 @@
             full = lists[r - HL]
         else:
             i = r if r < HL else r - HL - rows
-            full = from_x(0 if r < HL else HL, HL, (HV + 1) * cols + i * 16, 16)
+            full = from_x(0 if r < HL else HL, HL, HV * cols + i * 16, 16)
         third = jnp.where(full >= 6.0, 2.0, jnp.where(full >= 3.0, 1.0, 0.0))
         table[r] = jnp.where(sub16 < K, third * (wc - 3.0) + full + place_of, full)
         to = (r % per) * 16
@@ -335,11 +357,18 @@
 
 
 def inner_kernel(
-    vel, spin, turn, table, profile, pa, pb,
-    out, mid_rim, drift_rim, spin_rim, total, prof_rim,
-    mid, names, prof, drift,
+    vel, spin, turn, table, profile, pa, pb, codes_far, weights_far, cells,
+    out_far, cells_far, mid_rim, drift_rim, spin_rim, total, prof_rim, wave_shares, chosen, spread,
+    mid, names, prof, drift, out, codes, weights, sems,
 ):
     rows, cols, lanes = out.shape
+    copies = [
+        pltpu.make_async_copy(codes_far, codes, sems.at[0]),
+        pltpu.make_async_copy(weights_far, weights, sems.at[1]),
+        pltpu.make_async_copy(cells, cells_far, sems.at[2]),
+    ]
+    for copy in copies:
+        copy.start()
     wr, wc = profile.shape[0], profile.shape[1]
     listed = rows + 2 * HL
     prow = wr + 2 * HX
@@ -400,55 +429,77 @@
         means = jnp.where(lane // 2 == n, sums, means)
         if 1 <= n <= rows:
             out[n - 1] = new
+            if n % (rows // 4) == 0:
+                part = pl.ds(n - rows // 4, rows // 4)
+                copies.append(pltpu.make_async_copy(out.at[part], out_far.at[part], sems.at[len(copies)]))
+                copies[-1].start()
     total[...] = means
 
+    at, to = iota(chosen.shape, 0), iota(chosen.shape, 1)
+    reach = (RY + 2) * wc
+    chosen[...] = ((to < reach) & (at == RY * (to % wc) + to // wc + RIM - 1)).astype(F32)
+    at, to = iota((lanes, lanes), 0), iota((lanes, lanes), 1)
+    spread[...] = ((at < reach) & (at % wc == to)).astype(F32).astype(BF)
+
+    copies[0].wait()
+    copies[1].wait()
+    at, to = iota((wc, lanes), 0), iota((wc, lanes), 1)
+    repeat = ((to < reach) & (to % wc == at)).astype(F32).astype(BF)
+    shift = (lane // wc).astype(F32)
+    weight = [weights[:, k, :] for k in range(K)]
+    whole = sum(weight[1:], weight[0])
+    code = [jnp.dot(codes[:, k, :].astype(F32).astype(BF), repeat, preferred_element_type=F32) for k in range(K)]
+    share = [
+        sum(jnp.dot(p, repeat, preferred_element_type=F32) for p in split3(weight[k] / whole)) for k in range(K)
+    ]
+    for near in range(RX + 2):
+        wave_shares[near] = sum(
+            jnp.where(code[k] == near * (RY + 2.0) + shift, share[k], 0.0) for k in range(K)
+        )
+    for copy in copies[2:]:
+        copy.wait()
+
 
 def rim_kernel(
-    own, oa, ob, ya, yb, mid_rim, drift_rim, spin_rim, total, list_rim, prof_rim,
-    wave_codes, wave_shares, velocity_in,
+    wide, ya, yb, mid_rim, drift_rim, spin_rim, total, list_rim, prof_rim, wave_shares, chosen, spread, velocity_in,
     velocity_out, current,
     vel, mid, prof, drift, spin, picked, means, strips, sems,
 ):
-    rows, cols, lanes = own.shape
-    wr, wc = wave_codes.shape[1], current.shape[2]
+    vrow, lanes = wide.shape[0], wide.shape[2]
+    rows, cols = vrow - 2 * HV, wide.shape[1] - 2 * EDGE
+    wr, wc = current.shape[1], current.shape[2]
     listed = rows + 2 * HL
     prow = wr + 2 * HX
-    wide = 3 * EDGE
-    even_x, even_y = is_even("gx"), is_even("gy")
+    even_y = is_even("gy")
     has_south, has_north = inside("gy")
     lane = iota((1, lanes), 1)
     sub = iota((EDGE, 1), 0)
-    slots = TALL * HY
-
-    def from_x(r, halo, start, n):
-        one, two = (ob, oa) if r < halo else (oa, ob)
-        return pick(even_x, one[start : start + n, :], two[start : start + n, :])
+    slots, vel_rows, low_rows = y_rows(rows)
 
     def from_y(start, n):
         a, b = ya[start : start + n, :], yb[start : start + n, :]
         return pick(even_y, b, a) * has_south, pick(even_y, a, b) * has_north
 
-    for r in range(rows + 2 * HV):
-        if HV <= r < HV + rows:
-            near, far = own[r - HV, 0 : 2 * EDGE, :], own[r - HV, cols - 2 * EDGE :, :]
-        else:
-            i = r if r < HV else r - HV - rows
-            at = 0 if r < HV else HV
-            near = from_x(at, HV, i * cols, 2 * EDGE)
-            far = from_x(at, HV, (i + 1) * cols - 2 * EDGE, 2 * EDGE)
-            if r in (HV - 1, HV + rows):
-                near = near + from_x(at, HV, HV * cols, 2 * EDGE)
-                far = far + from_x(at, HV, (HV + 1) * cols - 2 * EDGE, 2 * EDGE)
-        vel[0, r, EDGE:, :] = near
-        vel[1, r, 0 : 2 * EDGE, :] = far
-    for r in range(0, rows + 2 * HV, 2):
-        south, north = from_y(slots + r * EDGE, 2 * EDGE)
+    blank = jnp.zeros((EDGE, lanes), F32)
+    for r in range(vrow):
+        vel[0, r, 0:EDGE, :] = blank
+        vel[1, r, 2 * EDGE :, :] = blank
+        vel[0, r, EDGE:, :] = wide[r, EDGE : 3 * EDGE, :]
+        vel[1, r, 0 : 2 * EDGE, :] = wide[r, cols - EDGE : cols + EDGE, :]
+    for start in range(0, vel_rows, 2 * EDGE):
+        pieces = from_y(slots + start, 2 * EDGE)
         for i in range(2):
-            low, high = south[i * EDGE : i * EDGE + EDGE], north[i * EDGE : i * EDGE + EDGE]
-            low = jnp.where(sub == 0, 0.0, low) + jnp.where(sub == EDGE - 1, pltpu.roll(low, EDGE - 1, 0), 0.0)
-            high = jnp.where(sub == EDGE - 1, 0.0, high) + jnp.where(sub == 0, pltpu.roll(high, 1, 0), 0.0)
-            vel[0, r + i, 0:EDGE, :] = low
-            vel[1, r + i, 2 * EDGE :, :] = high
+            low, high = (p[i * EDGE : i * EDGE + EDGE] for p in pieces)
+            low_moved, high_moved = pltpu.roll(low, lanes // 2, 1), pltpu.roll(high, lanes // 2, 1)
+            low_in = jnp.where(sub % RIM == 0, low_moved, low)
+            for j in range(2):
+                r = (start + i * EDGE) // RIM + j
+                if r < vrow:
+                    at = j * RIM
+                    vel[0, r, EDGE - RIM : EDGE, :] = low_in[at : at + RIM]
+                    vel[0, r, EDGE - RIM - 1 : EDGE - RIM, :] = low[at : at + 1]
+                    vel[1, r, 2 * EDGE : 2 * EDGE + RIM, :] = high[at : at + RIM]
+                    vel[1, r, 2 * EDGE + RIM : 2 * EDGE + RIM + 1, :] = high_moved[at + RIM - 1 : at + RIM]
 
     prof[...] = prof_rim[...]
     south, north = from_y(0, slots)
@@ -458,7 +509,7 @@
         prof[1, pl.ds(HY + c, TALL, stride=2 * HY), :] = north[TALL * c : TALL * (c + 1)]
 
     per = lanes // 16
-    start = slots + (rows + 2 * HV) * EDGE
+    start = slots + vel_rows + low_rows
     span = 2 * per * HY
     place = iota((2 * span, lanes), 0).astype(F32)
     part = lane % 16
@@ -466,7 +517,6 @@
     sub16 = iota((16, 1), 0)
     ones = jnp.ones((8, lanes), F32)
     none = jnp.zeros((2 * span, lanes), F32)
-    blank = jnp.zeros((8, lanes), F32)
     for g in range(-(-listed // per)):
         tile, to = list_place(g * per, lanes)
         south, north = from_y(start + tile * 16, 16)
@@ -489,20 +539,17 @@
         for i in range(min(per, listed - g * per)):
             for side in range(2):
                 at = i * 16 + side * EDGE
-                drift[side, g * per + i, side * EDGE : side * EDGE + EDGE, :] = both[at : at + EDGE, 0:lanes]
-                spin[side, g * per + i, side * EDGE : side * EDGE + EDGE, :] = both[at : at + EDGE, lanes:]
+                drift[side, g * per + i] = both[at : at + EDGE, 0:lanes]
+                spin[side, g * per + i] = both[at : at + EDGE, lanes:]
 
     lift = HV - HL
     for r in range(listed):
         for side in range(2):
             base = RIM + side * EDGE
-            drift[side, r, EDGE - side * EDGE : 2 * EDGE - side * EDGE, :] = drift_rim[r, side]
-            spin[side, r, EDGE - side * EDGE : 2 * EDGE - side * EDGE, :] = spin_rim[r, side]
             mid[side, r, 2 * EDGE * side : 2 * EDGE * side + EDGE, :] = blank
-            mid[side, r, EDGE - side * EDGE : wide - side * EDGE, :] = mid_rim[r, side]
-            tile = slice(side * EDGE, side * EDGE + EDGE)
-            absolute = spin[side, r, tile, :] + vorticity(vel.at[side], r + lift, base, EDGE)
-            new = vel[side, r + lift, base : base + EDGE, :] + STEP * (absolute * drift[side, r, tile, :])
+            mid[side, r, EDGE - side * EDGE : 3 * EDGE - side * EDGE, :] = mid_rim[r, side]
+            absolute = spin[side, r] + vorticity(vel.at[side], r + lift, base, EDGE)
+            new = vel[side, r + lift, base : base + EDGE, :] + STEP * (absolute * drift[side, r])
             mid[side, r, base : base + EDGE, :] = new
 
     average = averager(lanes)
@@ -511,10 +558,12 @@
         r = n + HL - 1
         both = []
         for side in range(2):
-            absolute = spin[side, r] + vorticity(mid.at[side], r, RIM, 2 * EDGE)
+            turns, drifts = (spin[side, r], spin_rim[r, side]), (drift[side, r], drift_rim[r, side])
+            order = 1 - 2 * side
+            absolute = jnp.concatenate(turns[::order], axis=0) + vorticity(mid.at[side], r, RIM, 2 * EDGE)
             tile = slice(RIM, RIM + 2 * EDGE)
             old = vel[side, r + lift, tile, :] + mid[side, r, tile, :]
-            new = 0.5 * old + (0.5 * STEP) * (absolute * drift[side, r])
+            new = 0.5 * old + (0.5 * STEP) * (absolute * jnp.concatenate(drifts[::order], axis=0))
             both.append(new)
             if 1 <= n <= rows:
                 strips[side, n - 1] = new[RIM : RIM + EDGE]
@@ -522,6 +571,11 @@
             jnp.concatenate(split(jnp.concatenate(both, axis=0)), axis=1), average, preferred_element_type=F32
         )
         acc = jnp.where(lane // 2 == n, sums, acc)
+    where = iota((4 * EDGE, 1), 0)
+    own_lane = lane // 2 == iota((low_rows, 1), 0)
+    for low, at in zip(from_y(slots + vel_rows, low_rows), (RIM - 1, 4 * EDGE - RIM)):
+        sums = jnp.dot(low.astype(BF), average[0:lanes], preferred_element_type=F32)
+        acc = acc + jnp.where(where == at, jnp.sum(jnp.where(own_lane, sums, 0.0), axis=0, keepdims=True), 0.0)
     copies = [
         pltpu.make_async_copy(strips.at[side], velocity_out.at[:, pl.ds(at, EDGE), :], sems.at[side])
         for side, at in ((0, 0), (1, cols - EDGE))
@@ -532,25 +586,19 @@
     means[2 * EDGE : 2 * RIM + cols - 2 * EDGE] = total[2 * EDGE - RIM : cols - 2 * EDGE + RIM, :]
     means[2 * RIM + cols - 2 * EDGE :] = acc[2 * EDGE :]
 
-    count = cols + 2 * RIM
-    at, to = iota((count, lanes), 0), iota((count, lanes), 1)
-    reach = (RY + 2) * wc
-    chosen = ((to < reach) & (at == RY * (to % wc) + to // wc + RIM - 1)).astype(F32).astype(BF)
+    named = chosen[...].astype(BF)
     picked[...] = sum(
-        lax.dot_general(p, chosen, ROWS_DOT, preferred_element_type=F32) for p in split3(means[...])
+        lax.dot_general(p, named, ROWS_DOT, preferred_element_type=F32) for p in split3(means[...])
     )
-    at, to = iota((lanes, lanes), 0), iota((lanes, lanes), 1)
-    spread = ((at < reach) & (at % wc == to)).astype(F32).astype(BF)
-    shift = lane // wc
-    for c in range(2):
-        summed = jnp.zeros((wr, lanes), F32)
-        for near in range(RX + 2):
-            share = jnp.zeros((wr, lanes), F32)
-            for k in range(K):
-                share = share + jnp.where(wave_codes[k] == near * (RY + 2) + shift, wave_shares[k], 0.0)
-            summed = summed + share * picked[pl.ds(2 * near + c, wr, stride=2 * RX), :]
-        sums = sum(jnp.dot(p, spread, preferred_element_type=F32) for p in split3(summed))
-        current[c] = sums[:, 0:wc]
+    summed = [
+        sum(wave_shares[near] * picked[pl.ds(2 * near + c, wr, stride=2 * RX), :] for near in range(RX + 2))
+        for c in range(2)
+    ]
+    sums = sum(
+        jnp.dot(p, spread[...], preferred_element_type=F32) for p in split3(jnp.concatenate(summed, axis=0))
+    )
+    current[0] = sums[0:wr, 0:wc]
+    current[1] = sums[wr:, 0:wc]
     for copy in copies:
         copy.wait()
 
@@ -568,7 +616,7 @@
         out_specs=tuple(ANY if i in any_out else VMEM for i in range(len(outs))),
         scratch_shapes=list(scratch),
         input_output_aliases=aliases or {},
-        compiler_params=pltpu.CompilerParams(vmem_limit_bytes=28 << 20),
+        compiler_params=pltpu.CompilerParams(vmem_limit_bytes=14 << 20),
         name=name,
     )(*args)
 
@@ -583,53 +631,34 @@
     prow = wr + 2 * HX
 
     with jax.named_scope("spectrum_edges"):
-        edge = ((wc, bins), BF)
-        raw = [
-            spectrum, courant, source, wave_land, coriolis,
-            jnp.transpose(ocean_codes, (0, 2, 1)), jnp.transpose(ocean_weights, (0, 2, 1)),
-        ]
-        xa, xb, ya, yb, spectrum, courant, source, wave_land, coriolis, codes, weights = call(
-            edges_kernel, "edges",
-            [edge] * 2 + [((wr, bins), BF)] * 2 + [(v.shape, v.dtype) for v in raw],
-            *raw, any_in=range(len(raw)), scratch=[pltpu.SemaphoreType.DMA((len(raw),))],
+        codes, weights = jnp.transpose(ocean_codes, (0, 2, 1)), jnp.transpose(ocean_weights, (0, 2, 1))
+        size = sum(x_rows(cols))
+        outs = [((wc, bins), BF)] * 2 + [((wr, bins), BF)] * 2 + [((size, lanes), BF)] * 2 + [((rows, 16, lanes), F32)]
+        kept = [spectrum, courant, source, wave_land]
+        xa, xb, ya, yb, oa, ob, lists, spectrum, courant, source, wave_land = call(
+            edges_kernel, "edges", outs + [(v.shape, v.dtype) for v in kept],
+            *kept, codes, weights, coriolis, velocity, any_in=range(8),
+            scratch=[
+                pltpu.VMEM(codes.shape, codes.dtype),
+                pltpu.VMEM(weights.shape, F32),
+                pltpu.VMEM(coriolis.shape, F32),
+                pltpu.VMEM((2, HV, cols, lanes), F32),
+                pltpu.SemaphoreType.DMA((9,)),
+            ],
         )
         xa, xb = exchange("gx", xa, xb)
         ya, yb = exchange("gy", ya, yb)
-
-    with jax.named_scope("ocean_edges"):
-        size = (HV + 1) * cols + HL * 16
-        oa, ob, lists, velocity, stokes_kernel = call(
-            ocean_edges_kernel, "ocean_edges",
-            [((size, lanes), BF)] * 2
-            + [((rows, 16, lanes), F32), (velocity.shape, F32), (stokes_kernel.shape, BF)],
-            velocity, stokes_kernel, codes, weights, coriolis,
-            any_in=(0, 1), scratch=[pltpu.SemaphoreType.DMA((2,))],
-        )
         oa, ob = exchange("gx", oa, ob)
 
     with jax.named_scope("wave"):
-        new_spectrum, profiles, pa, pb = call(
+        new_spectrum, profiles, pa, pb, velocity = call(
             wave_kernel, "wave",
-            [(spectrum.shape, BF), ((wr, wc, lanes), BF), ((HX, wc, lanes), BF), ((HX, wc, lanes), BF)],
-            spectrum, xa, xb, ya, yb, courant, source.T, wave_land.T.astype(F32), stokes_kernel,
+            [(spectrum.shape, BF), ((wr, wc, lanes), BF), ((HX, wc, lanes), BF), ((HX, wc, lanes), BF), (velocity.shape, F32)],
+            spectrum, xa, xb, ya, yb, courant, source.T, wave_land.T.astype(F32),
+            stokes_kernel, velocity,
+            any_in=(8, 9), scratch=[pltpu.VMEM(stokes_kernel.shape, BF), pltpu.SemaphoreType.DMA((2,))],
         )
         pa, pb = exchange("gx", pa, pb)
-
-    with jax.named_scope("halo"):
-        size = TALL * HY + (rows + 2 * HV) * EDGE + (list_place(listed - 1, lanes)[0] + 1) * 16
-        ya, yb = call(
-            halo_kernel, "halo", [((size, lanes), BF)] * 2, velocity, oa, ob, lists, profiles, pa, pb
-        )
-        ya, yb = exchange("gy", ya, yb)
-
-    with jax.named_scope("wave_lists"):
-        reach = RY + 2
-        wc_t = jnp.transpose(wave_codes, (2, 0, 1))
-        ww_t = jnp.transpose(wave_weights, (2, 0, 1))
-        ww_t = ww_t / jnp.sum(ww_t, axis=0, keepdims=True)
-        spare = [(0, 0), (0, 0), (0, lanes - reach * wc)]
-        wc_t = jnp.pad(jnp.tile(wc_t, (1, 1, reach)), spare)
-        ww_t = jnp.pad(jnp.tile(ww_t, (1, 1, reach)), spare)
 
     with jax.named_scope("prepare"):
         wide = cols + 2 * EDGE
@@ -646,24 +675,41 @@
             velocity, oa, ob, lists,
         )
 
+    with jax.named_scope("halo"):
+        size = sum(y_rows(rows)) + (list_place(listed - 1, lanes)[0] + 1) * 16
+        ya, yb = call(
+            halo_kernel, "halo", [((size, lanes), BF)] * 2, vel, oa, ob, lists, profiles, pa, pb
+        )
+        ya, yb = exchange("gy", ya, yb)
+
     with jax.named_scope("inner"):
         scratch = [
             pltpu.VMEM((listed, wide, lanes), F32),
             pltpu.VMEM((prow * wc, lanes), BF),
             pltpu.VMEM((prow * wc, lanes), F32),
             pltpu.VMEM((listed, cols, lanes), F32),
+            pltpu.VMEM(velocity.shape, F32),
+            pltpu.VMEM((wr, K, wc), jnp.int32),
+            pltpu.VMEM((wr, K, wc), F32),
+            pltpu.SemaphoreType.DMA((7,)),
         ]
-        new_velocity, mid_rim, drift_rim, spin_rim, total, prof_rim = call(
+        new_velocity, new_spectrum, mid_rim, drift_rim, spin_rim, total, prof_rim, wave_shares, chosen, spread = call(
             inner_kernel, "inner",
             [
                 (velocity.shape, F32),
+                (spectrum.shape, BF),
                 ((listed, 2, 2 * EDGE, lanes), F32),
                 ((listed, 2, EDGE, lanes), F32),
                 ((listed, 2, EDGE, lanes), F32),
                 ((cols, lanes), F32),
                 ((2, 2 * HY * (TALL + 4), lanes), F32),
+                ((RX + 2, wr, lanes), F32),
+                ((cols + 2 * RIM, lanes), F32),
+                ((lanes, lanes), BF),
             ],
-            vel, spin, turn, table, profiles, pa, pb, scratch=scratch,
+            vel, spin, turn, table, profiles, pa, pb,
+            jnp.transpose(wave_codes, (0, 2, 1)), jnp.transpose(wave_weights, (0, 2, 1)),
+            new_spectrum, scratch=scratch, any_in=(7, 8), any_out=(0, 1),
         )
 
     with jax.named_scope("rim"):
@@ -671,8 +717,8 @@
             pltpu.VMEM((2, rows + 2 * HV, 3 * EDGE, lanes), F32),
             pltpu.VMEM((2, listed, 3 * EDGE, lanes), F32),
             pltpu.VMEM((2, 2 * HY * (TALL + 4), lanes), F32),
-            pltpu.VMEM((2, listed, 2 * EDGE, lanes), F32),
-            pltpu.VMEM((2, listed, 2 * EDGE, lanes), F32),
+            pltpu.VMEM((2, listed, EDGE, lanes), F32),
+            pltpu.VMEM((2, listed, EDGE, lanes), F32),
             pltpu.VMEM((lanes, lanes), F32),
             pltpu.VMEM((cols + 2 * RIM, lanes), F32),
             pltpu.VMEM((2, rows, EDGE, lanes), F32),
@@ -680,8 +726,8 @@
         ]
         new_velocity, current = call(
             rim_kernel, "rim", [(velocity.shape, F32), ((2, wr, wc), F32)],
-            velocity, oa, ob, ya, yb, mid_rim, drift_rim, spin_rim, total, list_rim, prof_rim, wc_t, ww_t, new_velocity,
-            scratch=scratch, any_in=(13,), any_out=(0,), aliases={13: 0},
+            vel, ya, yb, mid_rim, drift_rim, spin_rim, total, list_rim, prof_rim, wave_shares, chosen, spread,
+            new_velocity, scratch=scratch, any_in=(12,), any_out=(0,), aliases={12: 0},
         )
     return new_spectrum, new_velocity, current
 

time: 26 us -> 24.5 us (0.942)
  Pallas kernels: 11.9 us -> 10.2 us
  waiting for transfers between devices: 7.57 us -> 8.23 us
  local copies, waits for them, and re-layouts: 0.42 us -> 0.14 us
    pallas_call x7 -> x6, Pallas kernels: 11.9 us -> 10.2 us  [call(): pl.pallas_call(kernel, out_shape=tuple((jax.ShapeDtypeStruct(shape, dtype...]
    ppermute x10, waiting for transfers between devices: 7.57 us -> 8.23 us  [swap(): return lax.ppermute(value, ('gx', 'gy'), pairs)]
  transfers between devices with their start and end apart: 10 -> 10, of which waited for: 5 -> 4; matrix products, arithmetic and copies ran while one was open for 2% -> 1% of each run, Pallas kernels for 29% -> 23%
where the time goes in v4:
time: 24.5 us; the launch traced here: 24.4 us
  Pallas kernels  10.2 us (42%)
  waiting for transfers between devices  8.23 us (34%)
  starting transfers between devices  5.15 us (21%)
  between operations  0.7 us (3%)
    pallas_call x6, Pallas kernels, call(): pl.pallas_call(kernel, out_shape=tuple((jax.ShapeDtypeStruct(shape, dtype...  10.2 us
    ppermute x10, waiting for transfers between devices, swap(): return lax.ppermute(value, ('gx', 'gy'), pairs)  8.23 us
    ppermute x10, starting transfers between devices, swap(): return lax.ppermute(value, ('gx', 'gy'), pairs)  5.15 us
  transfers between devices with their start and end apart: 10, of which 4 were waited for; matrix products, arithmetic and copies ran while one was open for 1% of the time, Pallas kernels for 23%

profile of v4, /device:TPU:8, one launch (start us, length us, event | category | flops | bytes accessed | tf_op | source)
XLA Modules:
  0.0 24.4 jit_solution(7743560197908196602)
XLA Ops:
  0.6 1.5 %edges.1 = (bf16[16,1152]{1,0:T(8,128)(2,1)S(1)}, bf16[16,1152]{1,0:T(8,128)(2,1)S(1)}, bf16[16,1152]{1,0:T(8,128)(2,1)S(1)}, bf16[16,1152]{1,0:T(8,128)(2,1)S(1...) custom-call(bf16[16,16,1152]{2,1,0:T(8,128)(2,1)} %refs_0_.1, ...), custom_call_target="tpu_custom_call" | custom-call | tf_op jit(solution)/shard_map/spectrum_edges/edges/pallas_call | solution.py:612
  2.2 0.1 collective-permute-start
  2.2 1.6 %collective-permute-start.1 = (bf16[16,1152]{1,0:T(8,128)(2,1)S(1)}, bf16[16,1152]{1,0:T(8,128)(2,1)S(1)}, u32[]{:S(2)}, u32[]{:S(2)}) collective-permute-start(bf16[16,1152]{1,0:T(8,128)(2,1)S(1)} %get-tuple-element.40), channel_id=1, source_target_pairs={{0,24},{1,25},{2,26},{3,27},{4,28},{5,29},{6,30},{7,31},{8,16},{9,... | collective-permute-start | bytes 110600 | tf_op jit(solution)/shard_map/spectrum_edges/ppermute | solution.py:39
  3.8 1.5 %collective-permute-start.2 = (bf16[16,1152]{1,0:T(8,128)(2,1)S(1)}, bf16[16,1152]{1,0:T(8,128)(2,1)S(1)}, u32[]{:S(2)}, u32[]{:S(2)}) collective-permute-start(bf16[16,1152]{1,0:T(8,128)(2,1)S(1)} %get-tuple-element.41), channel_id=1, source_target_pairs={{0,1},{1,0},{2,3},{3,2},{4,5},{5,4},{6,7},{7,6},{8,9},{9,8},{10,11... | collective-permute-start | bytes 110600 | tf_op jit(solution)/shard_map/spectrum_edges/ppermute | solution.py:39
  5.4 0.4 %collective-permute-start.3 = (bf16[16,1152]{1,0:T(8,128)(2,1)S(1)}, bf16[16,1152]{1,0:T(8,128)(2,1)S(1)}, u32[]{:S(2)}, u32[]{:S(2)}) collective-permute-start(bf16[16,1152]{1,0:T(8,128)(2,1)S(1)} %get-tuple-element.42), channel_id=1, source_target_pairs={{0,8},{1,2},{2,1},{3,4},{4,3},{5,6},{6,5},{7,15},{8,0},{9,10},{10,... | collective-permute-start | bytes 110600 | tf_op jit(solution)/shard_map/spectrum_edges/ppermute | solution.py:39
  5.8 0.0 collective-permute-start.4
  5.8 0.1 copy.16
  5.8 0.0 collective-permute-done.xa
  5.8 0.3 %collective-permute-start.5 = (bf16[368,128]{1,0:T(8,128)(2,1)S(1)}, bf16[368,128]{1,0:T(8,128)(2,1)S(1)}, u32[]{:S(2)}, u32[]{:S(2)}) collective-permute-start(bf16[368,128]{1,0:T(8,128)(2,1)S(1)} %get-tuple-element.48), channel_id=1, source_target_pairs={{0,24},{1,25},{2,26},{3,27},{4,28},{5,29},{6,30},{7,31},{8,16},{9,... | collective-permute-start | bytes 282632 | tf_op jit(solution)/shard_map/spectrum_edges/ppermute | solution.py:39
  6.1 0.1 copy.15
  6.2 0.0 collective-permute-done.1.xb
  6.2 1.6 %collective-permute-done.2.ya = bf16[16,1152]{1,0:T(8,128)(2,1)S(1)} collective-permute-done((bf16[16,1152]{1,0:T(8,128)(2,1)S(1)}, bf16[16,1152]{1,0:T(8,128)(2,1)S(1)}, u32[]{:S(2)}, u32[]{:S(2)}) %collective-permute-start.2) | collective-permute-done | bytes 36896 | tf_op jit(solution)/shard_map/spectrum_edges/ppermute | solution.py:39
  7.8 2.4 %collective-permute-done.3.yb = bf16[16,1152]{1,0:T(8,128)(2,1)S(1)} collective-permute-done((bf16[16,1152]{1,0:T(8,128)(2,1)S(1)}, bf16[16,1152]{1,0:T(8,128)(2,1)S(1)}, u32[]{:S(2)}, u32[]{:S(2)}) %collective-permute-start.3) | collective-permute-done | bytes 36896 | tf_op jit(solution)/shard_map/spectrum_edges/ppermute | solution.py:39
  10.2 1.4 %wave.1 = (bf16[16,16,1152]{2,1,0:T(8,128)(2,1)S(1)}, bf16[16,16,128]{2,1,0:T(8,128)(2,1)S(1)}, bf16[3,16,128]{2,1,0:T(8,128)(2,1)S(1)}, bf16[3,16,128]{2,1,0:T(8,128)(2,1)S(1)}, f32[32,64,128]{2,1,0:T(8,128)S(1)}) custom-call(bf16[16,16,1152]{2,1,0:T(8,128)(2,1)S(1)} %get-tuple-element.38.spec, bf16[16,1152]{1,0:T(8,128)(2,1)S(1)} %collective-permute-done.xa, ...), custom_call_target="tpu_custom_call" | custom-call | tf_op jit(solution)/shard_map/wave/wave/pallas_call | solution.py:612
  11.6 0.1 collective-permute-start.6
  11.7 0.6 %collective-permute-start.7 = (bf16[3,16,128]{2,1,0:T(8,128)(2,1)S(1)}, bf16[3,16,128]{2,1,0:T(8,128)(2,1)S(1)}, u32[]{:S(2)}, u32[]{:S(2)}) collective-permute-start(bf16[3,16,128]{2,1,0:T(8,128)(2,1)S(1)} %get-tuple-element.56), channel_id=1, source_target_pairs={{0,24},{1,25},{2,26},{3,27},{4,28},{5,29},{6,30},{7,31},{8,16},{9,... | collective-permute-start | bytes 36872 | tf_op jit(solution)/shard_map/wave/ppermute | solution.py:39
  12.4 0.0 collective-permute-done.4.oa
  12.4 0.0 collective-permute-done.5.ob
  12.4 1.5 %prepare.1 = (f32[42,80,128]{2,1,0:T(8,128)S(1)}, f32[38,64,128]{2,1,0:T(8,128)S(1)}, f32[38,64,128]{2,1,0:T(8,128)S(1)}, f32[38,16,128]{2,1,0:T(8,128)S(1)}, f32[5,16,128]{2,1,0:T(8,128)S(1)}) custom-call(f32[32,64,128]{2,1,0:T(8,128)S(1)} %get-tuple-element.46.own, bf16[368,128]{1,0:T(8,128)(2,1)S(1)} %collective-permute-done.4.oa, ...), custom_call_target="tpu_custom_call" | custom-call | tf_op jit(solution)/shard_map/prepare/prepare/pallas_call | solution.py:612
  13.8 0.0 collective-permute-done.6.pa
  13.9 1.0 %collective-permute-done.7.pb = bf16[3,16,128]{2,1,0:T(8,128)(2,1)S(1)} collective-permute-done((bf16[3,16,128]{2,1,0:T(8,128)(2,1)S(1)}, bf16[3,16,128]{2,1,0:T(8,128)(2,1)S(1)}, u32[]{:S(2)}, u32[]{:S(2)}) %collective-permute-start.7) | collective-permute-done | bytes 12320 | tf_op jit(solution)/shard_map/wave/ppermute | solution.py:39
  14.9 0.3 %halo.1 = (bf16[304,128]{1,0:T(8,128)(2,1)S(1)}, bf16[304,128]{1,0:T(8,128)(2,1)S(1)}) custom-call(f32[42,80,128]{2,1,0:T(8,128)S(1)} %get-tuple-element.50.vel.wide, bf16[368,128]{1,0:T(8,128)(2,1)S(1)} %collective-permute-done.4.oa, bf16[368,128]{1,0:T(8,128)(2,1)S(1)} %collective-permute-done.5.ob, f32[32,16,128]{2,1,0:T(8,128)S(1)} %get-tuple-element.49.lists, ...), custom_call_target="tpu_custom_call" | custom-call | tf_op jit(solution)/shard_map/halo/halo/pallas_call | solution.py:612
  15.2 0.6 %collective-permute-start.8 = (bf16[304,128]{1,0:T(8,128)(2,1)S(1)}, bf16[304,128]{1,0:T(8,128)(2,1)S(1)}, u32[]{:S(2)}, u32[]{:S(2)}) collective-permute-start(bf16[304,128]{1,0:T(8,128)(2,1)S(1)} %get-tuple-element.59), channel_id=1, source_target_pairs={{0,1},{1,0},{2,3},{3,2},{4,5},{5,4},{6,7},{7,6},{8,9},{9,8},{10,11... | collective-permute-start | bytes 233480 | tf_op jit(solution)/shard_map/halo/ppermute | solution.py:39
  15.8 0.0 collective-permute-start.9
  15.8 2.7 %inner.1 = (f32[32,64,128]{2,1,0:T(8,128)}, bf16[16,16,1152]{2,1,0:T(8,128)(2,1)}, f32[38,2,16,128]{3,2,1,0:T(8,128)S(1)}, f32[38,2,8,128]{3,2,1,0:T(8,128)S(1)}...) custom-call(f32[42,80,128]{2,1,0:T(8,128)S(1)} %get-tuple-element.50, ...), custom_call_target="tpu_custom_call" | custom-call | tf_op jit(solution)/shard_map/inner/inner/pallas_call | solution.py:612
  18.5 3.1 %collective-permute-done.8.ya = bf16[304,128]{1,0:T(8,128)(2,1)S(1)} collective-permute-done((bf16[304,128]{1,0:T(8,128)(2,1)S(1)}, bf16[304,128]{1,0:T(8,128)(2,1)S(1)}, u32[]{:S(2)}, u32[]{:S(2)}) %collective-permute-start.8) | collective-permute-done | bytes 77856 | tf_op jit(solution)/shard_map/halo/ppermute | solution.py:39
  21.7 0.0 collective-permute-done.9.yb
  21.7 2.7 %rim.1 = (f32[32,64,128]{2,1,0:T(8,128)}, f32[2,16,16]{2,1,0:T(8,128)}) custom-call(f32[42,80,128]{2,1,0:T(8,128)S(1)} %get-tuple-element.50.vel.wide, bf16[304,128]{1,0:T(8,128)(2,1)S(1)} %collective-permute-done.8.ya, bf16[304,128]{1,0:T(8,128)(2,1)S(1)} %collective-permute-done.9.yb, ...), custom_call_target="tpu_custom_call", output_to_operand_aliasing={{0}: (12, {})} | custom-call | tf_op jit(solution)/shard_map/rim/rim/pallas_call | solution.py:612
  (1 shorter events, 0.0 us)
Async XLA Ops:
  2.2 3.7 %collective-permute-start = (bf16[16,1152]{1,0:T(8,128)(2,1)S(1)}, bf16[16,1152]{1,0:T(8,128)(2,1)S(1)}, u32[]{:S(2)}, u32[]{:S(2)}) collective-permute-start(bf16[16,1152]{1,0:T(8,128)(2,1)S(1)} %get-tuple-element.39), channel_id=1, source_target_pairs={{0,8},{1,9},{2,10},{3,11},{4,12},{5,13},{6,14},{7,15},{8,0},{9,1},... | collective-permute-start | bytes 110600 | tf_op jit(solution)/shard_map/spectrum_edges/ppermute | solution.py:39
  2.2 3.9 %collective-permute-start.1 = (bf16[16,1152]{1,0:T(8,128)(2,1)S(1)}, bf16[16,1152]{1,0:T(8,128)(2,1)S(1)}, u32[]{:S(2)}, u32[]{:S(2)}) collective-permute-start(bf16[16,1152]{1,0:T(8,128)(2,1)S(1)} %get-tuple-element.40), channel_id=1, source_target_pairs={{0,24},{1,25},{2,26},{3,27},{4,28},{5,29},{6,30},{7,31},{8,16},{9,... | collective-permute-start | bytes 110600 | tf_op jit(solution)/shard_map/spectrum_edges/ppermute | solution.py:39
  3.8 4.0 %collective-permute-start.2 = (bf16[16,1152]{1,0:T(8,128)(2,1)S(1)}, bf16[16,1152]{1,0:T(8,128)(2,1)S(1)}, u32[]{:S(2)}, u32[]{:S(2)}) collective-permute-start(bf16[16,1152]{1,0:T(8,128)(2,1)S(1)} %get-tuple-element.41), channel_id=1, source_target_pairs={{0,1},{1,0},{2,3},{3,2},{4,5},{5,4},{6,7},{7,6},{8,9},{9,8},{10,11... | collective-permute-start | bytes 110600 | tf_op jit(solution)/shard_map/spectrum_edges/ppermute | solution.py:39
  5.4 4.9 %collective-permute-start.3 = (bf16[16,1152]{1,0:T(8,128)(2,1)S(1)}, bf16[16,1152]{1,0:T(8,128)(2,1)S(1)}, u32[]{:S(2)}, u32[]{:S(2)}) collective-permute-start(bf16[16,1152]{1,0:T(8,128)(2,1)S(1)} %get-tuple-element.42), channel_id=1, source_target_pairs={{0,8},{1,2},{2,1},{3,4},{4,3},{5,6},{6,5},{7,15},{8,0},{9,10},{10,... | collective-permute-start | bytes 110600 | tf_op jit(solution)/shard_map/spectrum_edges/ppermute | solution.py:39
  5.8 6.6 %collective-permute-start.4 = (bf16[368,128]{1,0:T(8,128)(2,1)S(1)}, bf16[368,128]{1,0:T(8,128)(2,1)S(1)}, u32[]{:S(2)}, u32[]{:S(2)}) collective-permute-start(bf16[368,128]{1,0:T(8,128)(2,1)S(1)} %get-tuple-element.47), channel_id=1, source_target_pairs={{0,8},{1,9},{2,10},{3,11},{4,12},{5,13},{6,14},{7,15},{8,0},{9,1},... | collective-permute-start | bytes 282632 | tf_op jit(solution)/shard_map/spectrum_edges/ppermute | solution.py:39
  5.8 6.5 %collective-permute-start.5 = (bf16[368,128]{1,0:T(8,128)(2,1)S(1)}, bf16[368,128]{1,0:T(8,128)(2,1)S(1)}, u32[]{:S(2)}, u32[]{:S(2)}) collective-permute-start(bf16[368,128]{1,0:T(8,128)(2,1)S(1)} %get-tuple-element.48), channel_id=1, source_target_pairs={{0,24},{1,25},{2,26},{3,27},{4,28},{5,29},{6,30},{7,31},{8,16},{9,... | collective-permute-start | bytes 282632 | tf_op jit(solution)/shard_map/spectrum_edges/ppermute | solution.py:39
  11.6 2.2 %collective-permute-start.6 = (bf16[3,16,128]{2,1,0:T(8,128)(2,1)S(1)}, bf16[3,16,128]{2,1,0:T(8,128)(2,1)S(1)}, u32[]{:S(2)}, u32[]{:S(2)}) collective-permute-start(bf16[3,16,128]{2,1,0:T(8,128)(2,1)S(1)} %get-tuple-element.55), channel_id=1, source_target_pairs={{0,8},{1,9},{2,10},{3,11},{4,12},{5,13},{6,14},{7,15},{8,0},{9,1},... | collective-permute-start | bytes 36872 | tf_op jit(solution)/shard_map/wave/ppermute | solution.py:39
  11.7 3.2 %collective-permute-start.7 = (bf16[3,16,128]{2,1,0:T(8,128)(2,1)S(1)}, bf16[3,16,128]{2,1,0:T(8,128)(2,1)S(1)}, u32[]{:S(2)}, u32[]{:S(2)}) collective-permute-start(bf16[3,16,128]{2,1,0:T(8,128)(2,1)S(1)} %get-tuple-element.56), channel_id=1, source_target_pairs={{0,24},{1,25},{2,26},{3,27},{4,28},{5,29},{6,30},{7,31},{8,16},{9,... | collective-permute-start | bytes 36872 | tf_op jit(solution)/shard_map/wave/ppermute | solution.py:39
  15.2 6.4 %collective-permute-start.8 = (bf16[304,128]{1,0:T(8,128)(2,1)S(1)}, bf16[304,128]{1,0:T(8,128)(2,1)S(1)}, u32[]{:S(2)}, u32[]{:S(2)}) collective-permute-start(bf16[304,128]{1,0:T(8,128)(2,1)S(1)} %get-tuple-element.59), channel_id=1, source_target_pairs={{0,1},{1,0},{2,3},{3,2},{4,5},{5,4},{6,7},{7,6},{8,9},{9,8},{10,11... | collective-permute-start | bytes 233480 | tf_op jit(solution)/shard_map/halo/ppermute | solution.py:39
  15.8 5.9 %collective-permute-start.9 = (bf16[304,128]{1,0:T(8,128)(2,1)S(1)}, bf16[304,128]{1,0:T(8,128)(2,1)S(1)}, u32[]{:S(2)}, u32[]{:S(2)}) collective-permute-start(bf16[304,128]{1,0:T(8,128)(2,1)S(1)} %get-tuple-element.60), channel_id=1, source_target_pairs={{0,8},{1,2},{2,1},{3,4},{4,3},{5,6},{6,5},{7,15},{8,0},{9,10},{10,... | collective-permute-start | bytes 233480 | tf_op jit(solution)/shard_map/halo/ppermute | solution.py:39

commit v5 on v4

--- a/solution.py
+++ b/solution.py
@@ -9,6 +9,7 @@
 RX = 2
 RY = 4
 STEP = 0.5
+PARTS = 1
 TALL = 24
 RIM = 4
 HV, HL = 5, 3
@@ -77,18 +78,24 @@
 
 
 def x_rows(cols):
-    return (HV - 1) * cols, cols, HL * 16
+    return (HV - 1) * cols, HL * 16
+
+
+def cut_rows(one, two):
+    step = one.shape[0] // PARTS
+    return [(one.at[pl.ds(i * step, step)], two.at[pl.ds(i * step, step)]) for i in range(PARTS)]
 
 
 def edges_kernel(*refs):
-    (spec_far, courant_far, source_far, land_far, codes_far, weights_far, coriolis_far, vel_far) = refs[:8]
-    (xa, xb, ya, yb, oa, ob, lists, spec, courant, source, land, codes, weights, coriolis, vel, sems) = refs[8:]
+    (spec_far, courant_far, source_far, land_far, basis_far, codes_far, weights_far, coriolis_far, vel_far) = refs[:9]
+    (xa, xb, ya, yb, oa, ob, lists, spec, courant, source, land, basis) = refs[9:21]
+    (codes, weights, coriolis, vel, sems) = refs[21:]
     rows, cols, bins = spec.shape
     lanes = vel.shape[-1]
-    pairs = [(spec_far, spec)]
+    pairs = cut_rows(spec_far, spec)
     pairs += [(vel_far.at[pl.ds(at, HV)], vel.at[i]) for i, at in ((0, 0), (1, vel_far.shape[0] - HV))]
     pairs += [(codes_far, codes), (weights_far, weights), (coriolis_far, coriolis)]
-    pairs += [(courant_far, courant), (source_far, source), (land_far, land)]
+    pairs += [(courant_far, courant), (source_far, source), (land_far, land), (basis_far, basis)]
     copies = [pltpu.make_async_copy(one, two, sems.at[i]) for i, (one, two) in enumerate(pairs)]
     for copy in copies:
         copy.start()
@@ -102,7 +109,8 @@
     at, cell = iota((2 * rows, rows * cols), 0), iota((2 * rows, rows * cols), 1)
     wanted = jnp.where(at < rows, at * cols, (at - rows) * cols + cols - 1)
     chosen = (cell == wanted).astype(F32).astype(BF)
-    copies[0].wait()
+    for copy in copies[:PARTS]:
+        copy.wait()
     sides = jnp.dot(chosen, spec[...].reshape(rows * cols, bins), preferred_element_type=F32)
     first, last = spec[0].astype(F32), spec[rows - 1].astype(F32)
     xa[...] = jnp.where(even_x, last, first).astype(BF)
@@ -111,7 +119,7 @@
     ya[...] = jnp.where(even_y, last, first).astype(BF)
     yb[...] = jnp.where(even_y, first, last).astype(BF)
 
-    for copy in copies[1:]:
+    for copy in copies[PARTS:]:
         copy.wait()
     listed, wide = codes.shape[0], codes.shape[2]
     is_u = iota((1, lanes), 1) < lanes // 2
@@ -122,8 +130,6 @@
     put(0, *outer)
     for i in range(1, HV - 1):
         put(i * wide, vel[1, i + 1], vel[0, i - 1])
-    last, first = vel[1, HV - 1], vel[0, 0]
-    put((HV - 1) * wide, last - last.astype(BF).astype(F32), first - first.astype(BF).astype(F32))
     for r in range(listed):
         lists[r] = jnp.zeros((16, lanes), F32)
         weight = weights[r]
@@ -134,17 +140,13 @@
         lists[r, 2 * K : 2 * K + 1, 0:wide] = high
         lists[r, 2 * K + 1 : 2 * K + 2, 0:wide] = turn - high
     for i in range(HL):
-        put(HV * wide + i * 16, lists[listed - HL + i], lists[i])
-
-
-def wave_kernel(spec, xa, xb, ya, yb, courant, source, land, weights_far, vel_far, out, profile, pa, pb, vel, weights, sems):
-    rows, cols, bins = spec.shape
-    copies = [pltpu.make_async_copy(weights_far, weights, sems.at[0]), pltpu.make_async_copy(vel_far, vel, sems.at[1])]
-    for copy in copies:
-        copy.start()
-    even_x, even_y = is_even("gx"), is_even("gy")
+        put((HV - 1) * wide + i * 16, lists[listed - HL + i], lists[i])
+
+
+def advance(chosen, spec, sides, ya, yb, courant, source, land, weights, at_once, put):
+    rows, cols, _ = spec.shape
+    even_y = is_even("gy")
     has_south, has_north = inside("gy")
-    west, east = pick(even_x, xb[...], xa[...]), pick(even_x, xa[...], xb[...])
     south = pick(even_y, yb[...], ya[...]) * has_south
     north = pick(even_y, ya[...], yb[...]) * has_north
     cx, cy = courant[0:1, :], courant[1:2, :]
@@ -152,11 +154,11 @@
     from_west, from_south = cx > 0.0, cy > 0.0
     keep = 1.0 - ax - ay
     sub = iota((cols, 1), 0)
-    cells, parts = [], []
-    for x in range(rows):
+    cells = []
+    for x in chosen:
         center = spec[x].astype(F32)
-        before = spec[x - 1].astype(F32) if x else west
-        after = spec[x + 1].astype(F32) if x < rows - 1 else east
+        before = spec[x - 1].astype(F32) if x else sides[0]
+        after = spec[x + 1].astype(F32) if x < rows - 1 else sides[1]
         below = jnp.where(sub == 0, south[x : x + 1, :], pltpu.roll(center, 1, 0))
         above = jnp.where(sub == cols - 1, north[x : x + 1, :], pltpu.roll(center, cols - 1, 0))
         advected = (
@@ -166,22 +168,41 @@
         )
         wind = 1.0 + 0.2 * source[:, x : x + 1]
         updated = land[:, x : x + 1] * (advected * (wind - 0.1 * advected))
-        updated = updated.astype(BF)
-        out[x] = updated
-        cells.append(updated)
-        if x == 3 * rows // 4 - 1:
-            copies[0].wait()
-        if x in (3 * rows // 4 - 1, rows - 1):
-            part = jnp.dot(jnp.concatenate(cells, axis=0), weights[...], preferred_element_type=F32)
-            parts += [part[i * cols : (i + 1) * cols] for i in range(len(cells))]
+        cells.append(updated.astype(BF))
+        if len(cells) == at_once:
+            parts = jnp.dot(jnp.concatenate(cells, axis=0), weights[...], preferred_element_type=F32)
+            for i, value in enumerate(cells):
+                put(x - at_once + 1 + i, value, parts[i * cols : (i + 1) * cols])
             cells = []
-    for x in range(rows):
-        profile[x] = parts[x].astype(BF)
+
+
+def wave_ends_kernel(spec, xa, xb, ya, yb, courant, source, land, weights, out, profile, pa, pb):
+    rows, cols, bins = spec.shape
+    even_x = is_even("gx")
+    west, east = pick(even_x, xb[...], xa[...]), pick(even_x, xa[...], xb[...])
+
+    parts = []
+
+    def put(x, value, part):
+        i = len(parts)
+        out[i], profile[i] = value, part.astype(BF)
+        parts.append(part)
+
+    ends = list(range(HX)) + list(range(rows - HX, rows))
+    advance(ends, spec, (west, east), ya, yb, courant, source, land, weights, HX, put)
     for i in range(HX):
-        first, last = parts[i], parts[rows - HX + i]
+        first, last = parts[i], parts[HX + i]
         pa[i] = jnp.where(even_x, last, first).astype(BF)
         pb[i] = jnp.where(even_x, first, last).astype(BF)
-    copies[1].wait()
+
+
+def wave_rest_kernel(spec, ya, yb, courant, source, land, weights, ends, out, profile):
+    rows = spec.shape[0]
+
+    def put(x, value, part):
+        out[x - HX], profile[x - HX] = value, part.astype(BF)
+
+    advance(range(HX, rows - HX), spec, None, ya, yb, courant, source, land, weights, (rows - 2 * HX) // 2, put)
 
 
 def list_place(r, lanes):
@@ -191,14 +212,14 @@
 
 def y_rows(rows):
     pairs = (rows + 2 * HV + 1) // 2
-    return TALL * HY, (pairs + pairs % 2) * EDGE, -(-(rows + 2) // 16) * 16
-
-
-def halo_kernel(vel, oa, ob, lists, profile, pa, pb, ya, yb):
+    return TALL * HY, (pairs + pairs % 2) * EDGE
+
+
+def halo_kernel(vel, oa, ob, lists, ends, rest, pa, pb, ya, yb):
     vrow, lanes = vel.shape[0], vel.shape[2]
     rows, cols = vrow - 2 * HV, vel.shape[1] - 2 * EDGE
     even_x, even_y = is_even("gx"), is_even("gy")
-    wr, wc = profile.shape[0], profile.shape[1]
+    wr, wc = rest.shape[0] + 2 * HX, rest.shape[1]
 
     def put(at, last, first):
         n = last.shape[0]
@@ -206,7 +227,7 @@
         yb[at : at + n] = jnp.where(even_y, first, last).astype(BF)
 
     before, after = pick(even_x, pb[...], pa[...]), pick(even_x, pa[...], pb[...])
-    joined = jnp.concatenate([before.astype(BF), profile[...], after.astype(BF)], axis=0)
+    joined = jnp.concatenate([before.astype(BF), ends[0:HX], rest[...], ends[HX:], after.astype(BF)], axis=0)
     count = (wr + 2 * HX) * wc
     slots = TALL * HY
     at, cell = iota((2 * slots, count), 0), iota((2 * slots, count), 1)
@@ -235,10 +256,6 @@
     for i in range(0, len(pairs), 2):
         put(slots + i * EDGE, *[jnp.concatenate([pairs[i][j], pairs[i + 1][j]], axis=0) for j in range(2)])
     start = slots + len(pairs) * EDGE
-    edge = [vel[HV - 1 : HV + rows + 1, at, :] for at in (end - 1, EDGE)]
-    spare = jnp.zeros((-(rows + 2) % 16, lanes), F32)
-    put(start, *[jnp.concatenate([v - v.astype(BF).astype(F32), spare], axis=0) for v in edge])
-    start += rows + 2 + spare.shape[0]
 
     group = iota((1, lanes), 1) // RIM
     x_start = oa.shape[0] - HL * 16
@@ -317,10 +334,6 @@
             vel[1, EDGE : EDGE + cols, :] = near
             vel[2 * HV + rows - 2, EDGE : EDGE + cols, :] = far
         else:
-            if i == HV - 2:
-                near = near + from_x(0, HV, (HV - 1) * cols, cols)
-            if i == 1:
-                far = far + from_x(HV, HV, (HV - 1) * cols, cols)
             vel[i + 1, EDGE : EDGE + cols, :] = near
             vel[HV + rows + i - 1, EDGE : EDGE + cols, :] = far
 
@@ -333,7 +346,7 @@
             full = lists[r - HL]
         else:
             i = r if r < HL else r - HL - rows
-            full = from_x(0 if r < HL else HL, HL, HV * cols + i * 16, 16)
+            full = from_x(0 if r < HL else HL, HL, (HV - 1) * cols + i * 16, 16)
         third = jnp.where(full >= 6.0, 2.0, jnp.where(full >= 3.0, 1.0, 0.0))
         table[r] = jnp.where(sub16 < K, third * (wc - 3.0) + full + place_of, full)
         to = (r % per) * 16
@@ -357,7 +370,7 @@
 
 
 def inner_kernel(
-    vel, spin, turn, table, profile, pa, pb, codes_far, weights_far, cells,
+    vel, spin, turn, table, ends, rest, pa, pb, codes_far, weights_far, cells_ends, cells_rest,
     out_far, cells_far, mid_rim, drift_rim, spin_rim, total, prof_rim, wave_shares, chosen, spread,
     mid, names, prof, drift, out, codes, weights, sems,
 ):
@@ -365,11 +378,16 @@
     copies = [
         pltpu.make_async_copy(codes_far, codes, sems.at[0]),
         pltpu.make_async_copy(weights_far, weights, sems.at[1]),
-        pltpu.make_async_copy(cells, cells_far, sems.at[2]),
     ]
+    wr, wc = rest.shape[0] + 2 * HX, rest.shape[1]
+    for part, to in (
+        (cells_ends.at[pl.ds(0, HX)], cells_far.at[pl.ds(0, HX)]),
+        (cells_rest, cells_far.at[pl.ds(HX, wr - 2 * HX)]),
+        (cells_ends.at[pl.ds(HX, HX)], cells_far.at[pl.ds(wr - HX, HX)]),
+    ):
+        copies.append(pltpu.make_async_copy(part, to, sems.at[len(copies)]))
     for copy in copies:
         copy.start()
-    wr, wc = profile.shape[0], profile.shape[1]
     listed = rows + 2 * HL
     prow = wr + 2 * HX
     unroll = listed // 2
@@ -378,7 +396,9 @@
     blank = jnp.zeros((EDGE, lanes), F32)
     for x in range(prow):
         if HX <= x < HX + wr:
-            part = profile[x - HX].astype(F32)
+            i = x - HX
+            own = ends[i] if i < HX else rest[i - HX] if i < wr - HX else ends[i - wr + 2 * HX]
+            part = own.astype(F32)
         elif x < HX:
             part = pick(even_x, pb[x], pa[x])
         else:
@@ -474,7 +494,7 @@
     has_south, has_north = inside("gy")
     lane = iota((1, lanes), 1)
     sub = iota((EDGE, 1), 0)
-    slots, vel_rows, low_rows = y_rows(rows)
+    slots, vel_rows = y_rows(rows)
 
     def from_y(start, n):
         a, b = ya[start : start + n, :], yb[start : start + n, :]
@@ -509,7 +529,7 @@
         prof[1, pl.ds(HY + c, TALL, stride=2 * HY), :] = north[TALL * c : TALL * (c + 1)]
 
     per = lanes // 16
-    start = slots + vel_rows + low_rows
+    start = slots + vel_rows
     span = 2 * per * HY
     place = iota((2 * span, lanes), 0).astype(F32)
     part = lane % 16
@@ -571,11 +591,6 @@
             jnp.concatenate(split(jnp.concatenate(both, axis=0)), axis=1), average, preferred_element_type=F32
         )
         acc = jnp.where(lane // 2 == n, sums, acc)
-    where = iota((4 * EDGE, 1), 0)
-    own_lane = lane // 2 == iota((low_rows, 1), 0)
-    for low, at in zip(from_y(slots + vel_rows, low_rows), (RIM - 1, 4 * EDGE - RIM)):
-        sums = jnp.dot(low.astype(BF), average[0:lanes], preferred_element_type=F32)
-        acc = acc + jnp.where(where == at, jnp.sum(jnp.where(own_lane, sums, 0.0), axis=0, keepdims=True), 0.0)
     copies = [
         pltpu.make_async_copy(strips.at[side], velocity_out.at[:, pl.ds(at, EDGE), :], sems.at[side])
         for side, at in ((0, 0), (1, cols - EDGE))
@@ -634,16 +649,16 @@
         codes, weights = jnp.transpose(ocean_codes, (0, 2, 1)), jnp.transpose(ocean_weights, (0, 2, 1))
         size = sum(x_rows(cols))
         outs = [((wc, bins), BF)] * 2 + [((wr, bins), BF)] * 2 + [((size, lanes), BF)] * 2 + [((rows, 16, lanes), F32)]
-        kept = [spectrum, courant, source, wave_land]
-        xa, xb, ya, yb, oa, ob, lists, spectrum, courant, source, wave_land = call(
+        kept = [spectrum, courant, source, wave_land, stokes_kernel]
+        xa, xb, ya, yb, oa, ob, lists, spectrum, courant, source, wave_land, stokes_kernel = call(
             edges_kernel, "edges", outs + [(v.shape, v.dtype) for v in kept],
-            *kept, codes, weights, coriolis, velocity, any_in=range(8),
+            *kept, codes, weights, coriolis, velocity, any_in=range(9),
             scratch=[
                 pltpu.VMEM(codes.shape, codes.dtype),
                 pltpu.VMEM(weights.shape, F32),
                 pltpu.VMEM(coriolis.shape, F32),
                 pltpu.VMEM((2, HV, cols, lanes), F32),
-                pltpu.SemaphoreType.DMA((9,)),
+                pltpu.SemaphoreType.DMA((9 + PARTS,)),
             ],
         )
         xa, xb = exchange("gx", xa, xb)
@@ -651,14 +666,19 @@
         oa, ob = exchange("gx", oa, ob)
 
     with jax.named_scope("wave"):
-        new_spectrum, profiles, pa, pb, velocity = call(
-            wave_kernel, "wave",
-            [(spectrum.shape, BF), ((wr, wc, lanes), BF), ((HX, wc, lanes), BF), ((HX, wc, lanes), BF), (velocity.shape, F32)],
-            spectrum, xa, xb, ya, yb, courant, source.T, wave_land.T.astype(F32),
-            stokes_kernel, velocity,
-            any_in=(8, 9), scratch=[pltpu.VMEM(stokes_kernel.shape, BF), pltpu.SemaphoreType.DMA((2,))],
+        source, land = source.T, wave_land.T.astype(F32)
+        edge = (HX, wc, lanes)
+        cells_ends, ends, pa, pb = call(
+            wave_ends_kernel, "wave_ends",
+            [((2 * HX, wc, bins), BF), ((2 * HX, wc, lanes), BF), (edge, BF), (edge, BF)],
+            spectrum, xa, xb, ya, yb, courant, source, land, stokes_kernel,
         )
         pa, pb = exchange("gx", pa, pb)
+        cells_rest, rest = call(
+            wave_rest_kernel, "wave_rest",
+            [((wr - 2 * HX, wc, bins), BF), ((wr - 2 * HX, wc, lanes), BF)],
+            spectrum, ya, yb, courant, source, land, stokes_kernel, ends,
+        )
 
     with jax.named_scope("prepare"):
         wide = cols + 2 * EDGE
@@ -678,7 +698,7 @@
     with jax.named_scope("halo"):
         size = sum(y_rows(rows)) + (list_place(listed - 1, lanes)[0] + 1) * 16
         ya, yb = call(
-            halo_kernel, "halo", [((size, lanes), BF)] * 2, vel, oa, ob, lists, profiles, pa, pb
+            halo_kernel, "halo", [((size, lanes), BF)] * 2, vel, oa, ob, lists, ends, rest, pa, pb
         )
         ya, yb = exchange("gy", ya, yb)
 
@@ -691,7 +711,7 @@
             pltpu.VMEM(velocity.shape, F32),
             pltpu.VMEM((wr, K, wc), jnp.int32),
             pltpu.VMEM((wr, K, wc), F32),
-            pltpu.SemaphoreType.DMA((7,)),
+            pltpu.SemaphoreType.DMA((9,)),
         ]
         new_velocity, new_spectrum, mid_rim, drift_rim, spin_rim, total, prof_rim, wave_shares, chosen, spread = call(
             inner_kernel, "inner",
@@ -707,9 +727,9 @@
                 ((cols + 2 * RIM, lanes), F32),
                 ((lanes, lanes), BF),
             ],
-            vel, spin, turn, table, profiles, pa, pb,
+            vel, spin, turn, table, ends, rest, pa, pb,
             jnp.transpose(wave_codes, (0, 2, 1)), jnp.transpose(wave_weights, (0, 2, 1)),
-            new_spectrum, scratch=scratch, any_in=(7, 8), any_out=(0, 1),
+            cells_ends, cells_rest, scratch=scratch, any_in=(8, 9), any_out=(0, 1),
         )
 
     with jax.named_scope("rim"):

time: 24.5 us -> 23.1 us (0.943)
  waiting for transfers between devices: 8.23 us -> 6.99 us
  Pallas kernels: 10.2 us -> 9.9 us
    ppermute x10, waiting for transfers between devices: 8.23 us -> 6.99 us  [swap(): return lax.ppermute(value, ('gx', 'gy'), pairs)]
    pallas_call x6 -> x7, Pallas kernels: 10.2 us -> 9.9 us  [call(): pl.pallas_call(kernel, out_shape=tuple((jax.ShapeDtypeStruct(shape, dtype...]
where the time goes in v5:
time: 23.1 us; the launch traced here: 22.9 us
  Pallas kernels  9.9 us (43%)
  waiting for transfers between devices  6.99 us (30%)
  starting transfers between devices  5.15 us (22%)
  between operations  0.74 us (3%)
    pallas_call x7, Pallas kernels, call(): pl.pallas_call(kernel, out_shape=tuple((jax.ShapeDtypeStruct(shape, dtype...  9.9 us
    ppermute x10, waiting for transfers between devices, swap(): return lax.ppermute(value, ('gx', 'gy'), pairs)  6.99 us
    ppermute x10, starting transfers between devices, swap(): return lax.ppermute(value, ('gx', 'gy'), pairs)  5.15 us
  transfers between devices with their start and end apart: 10, of which 4 were waited for; matrix products, arithmetic and copies ran while one was open for 1% of the time, Pallas kernels for 23%

profile of v5, /device:TPU:8, one launch (start us, length us, event | category | flops | bytes accessed | tf_op | source)
XLA Modules:
  0.0 22.9 jit_solution(6361686144351348488)
XLA Ops:
  0.6 1.6 %edges.1 = (bf16[16,1152]{1,0:T(8,128)(2,1)S(1)}, bf16[16,1152]{1,0:T(8,128)(2,1)S(1)}, bf16[16,1152]{1,0:T(8,128)(2,1)S(1)}, bf16[16,1152]{1,0:T(8,128)(2,1)S(1...) custom-call(bf16[16,16,1152]{2,1,0:T(8,128)(2,1)} %refs_0_.1, ...), custom_call_target="tpu_custom_call" | custom-call | tf_op jit(solution)/shard_map/spectrum_edges/edges/pallas_call | solution.py:627
  2.2 0.0 copy-start
  2.2 0.1 collective-permute-start.2
  2.3 1.6 %collective-permute-start.3 = (bf16[16,1152]{1,0:T(8,128)(2,1)S(1)}, bf16[16,1152]{1,0:T(8,128)(2,1)S(1)}, u32[]{:S(2)}, u32[]{:S(2)}) collective-permute-start(bf16[16,1152]{1,0:T(8,128)(2,1)S(1)} %get-tuple-element.49), channel_id=1, source_target_pairs={{0,24},{1,25},{2,26},{3,27},{4,28},{5,29},{6,30},{7,31},{8,16},{9,... | collective-permute-start | bytes 110600 | tf_op jit(solution)/shard_map/spectrum_edges/ppermute | solution.py:40
  3.9 1.5 %collective-permute-start.4 = (bf16[16,1152]{1,0:T(8,128)(2,1)S(1)}, bf16[16,1152]{1,0:T(8,128)(2,1)S(1)}, u32[]{:S(2)}, u32[]{:S(2)}) collective-permute-start(bf16[16,1152]{1,0:T(8,128)(2,1)S(1)} %get-tuple-element.50), channel_id=1, source_target_pairs={{0,1},{1,0},{2,3},{3,2},{4,5},{5,4},{6,7},{7,6},{8,9},{9,8},{10,11... | collective-permute-start | bytes 110600 | tf_op jit(solution)/shard_map/spectrum_edges/ppermute | solution.py:40
  5.4 0.4 %collective-permute-start.5 = (bf16[16,1152]{1,0:T(8,128)(2,1)S(1)}, bf16[16,1152]{1,0:T(8,128)(2,1)S(1)}, u32[]{:S(2)}, u32[]{:S(2)}) collective-permute-start(bf16[16,1152]{1,0:T(8,128)(2,1)S(1)} %get-tuple-element.51), channel_id=1, source_target_pairs={{0,8},{1,2},{2,1},{3,4},{4,3},{5,6},{6,5},{7,15},{8,0},{9,10},{10,... | collective-permute-start | bytes 110600 | tf_op jit(solution)/shard_map/spectrum_edges/ppermute | solution.py:40
  5.8 0.0 collective-permute-start
  5.8 0.1 copy.16
  5.9 0.0 collective-permute-done.2.xa
  5.9 0.3 %collective-permute-start.1 = (bf16[304,128]{1,0:T(8,128)(2,1)S(1)}, bf16[304,128]{1,0:T(8,128)(2,1)S(1)}, u32[]{:S(2)}, u32[]{:S(2)}) collective-permute-start(bf16[304,128]{1,0:T(8,128)(2,1)S(1)} %get-tuple-element.41), channel_id=1, source_target_pairs={{0,24},{1,25},{2,26},{3,27},{4,28},{5,29},{6,30},{7,31},{8,16},{9,... | collective-permute-start | bytes 233480 | tf_op jit(solution)/shard_map/spectrum_edges/ppermute | solution.py:40
  6.2 0.1 copy.15
  6.2 0.0 collective-permute-done.3.xb
  6.2 1.6 %collective-permute-done.4.ya = bf16[16,1152]{1,0:T(8,128)(2,1)S(1)} collective-permute-done((bf16[16,1152]{1,0:T(8,128)(2,1)S(1)}, bf16[16,1152]{1,0:T(8,128)(2,1)S(1)}, u32[]{:S(2)}, u32[]{:S(2)}) %collective-permute-start.4) | collective-permute-done | bytes 36896 | tf_op jit(solution)/shard_map/spectrum_edges/ppermute | solution.py:40
  7.9 2.4 %collective-permute-done.5.yb = bf16[16,1152]{1,0:T(8,128)(2,1)S(1)} collective-permute-done((bf16[16,1152]{1,0:T(8,128)(2,1)S(1)}, bf16[16,1152]{1,0:T(8,128)(2,1)S(1)}, u32[]{:S(2)}, u32[]{:S(2)}) %collective-permute-start.5) | collective-permute-done | bytes 36896 | tf_op jit(solution)/shard_map/spectrum_edges/ppermute | solution.py:40
  10.3 0.5 %wave_ends.1 = (bf16[6,16,1152]{2,1,0:T(8,128)(2,1)S(1)}, bf16[6,16,128]{2,1,0:T(8,128)(2,1)S(1)}, bf16[3,16,128]{2,1,0:T(8,128)(2,1)S(1)}, bf16[3,16,128]{2,1,0:T(8,128)(2,1)S(1)}) custom-call(bf16[16,16,1152]{2,1,0:T(8,128)(2,1)S(1)} %get-tuple-element.47.spec, bf16[16,1152]{1,0:T(8,128)(2,1)S(1)} %collective-permute-done.2.xa, ...), custom_call_target="tpu_custom_call" | custom-call | tf_op jit(solution)/shard_map/wave/wave_ends/pallas_call | solution.py:627
  10.8 0.1 collective-permute-start.6
  10.9 0.7 %collective-permute-start.7 = (bf16[3,16,128]{2,1,0:T(8,128)(2,1)S(1)}, bf16[3,16,128]{2,1,0:T(8,128)(2,1)S(1)}, u32[]{:S(2)}, u32[]{:S(2)}) collective-permute-start(bf16[3,16,128]{2,1,0:T(8,128)(2,1)S(1)} %get-tuple-element.59), channel_id=1, source_target_pairs={{0,24},{1,25},{2,26},{3,27},{4,28},{5,29},{6,30},{7,31},{8,16},{9,... | collective-permute-start | bytes 36872 | tf_op jit(solution)/shard_map/wave/ppermute | solution.py:40
  11.5 0.6 %wave_rest.1 = (bf16[10,16,1152]{2,1,0:T(8,128)(2,1)S(1)}, bf16[10,16,128]{2,1,0:T(8,128)(2,1)S(1)}) custom-call(bf16[16,16,1152]{2,1,0:T(8,128)(2,1)S(1)} %get-tuple-element.47.spec, bf16[16,1152]{1,0:T(8,128)(2,1)S(1)} %collective-permute-done.4.ya, bf16[16,1152]{1,0:T(8,128)(2,1)S(1)} %collective-permute-done.5.yb, ...), custom_call_target="tpu_custom_call" | custom-call | tf_op jit(solution)/shard_map/wave/wave_rest/pallas_call | solution.py:627
  12.2 0.0 collective-permute-done.oa
  12.2 0.0 collective-permute-done.1.ob
  12.2 0.0 copy-done
  12.2 1.5 %prepare.1 = (f32[42,80,128]{2,1,0:T(8,128)S(1)}, f32[38,64,128]{2,1,0:T(8,128)S(1)}, f32[38,64,128]{2,1,0:T(8,128)S(1)}, f32[38,16,128]{2,1,0:T(8,128)S(1)}, f32[5,16,128]{2,1,0:T(8,128)S(1)}) custom-call(f32[32,64,128]{2,1,0:T(8,128)S(1)} %copy-done, bf16[304,128]{1,0:T(8,128)(2,1)S(1)} %collective-permute-done.oa, ...), custom_call_target="tpu_custom_call" | custom-call | tf_op jit(solution)/shard_map/prepare/prepare/pallas_call | solution.py:627
  13.7 0.0 collective-permute-done.6.pa
  13.7 0.3 %collective-permute-done.7.pb = bf16[3,16,128]{2,1,0:T(8,128)(2,1)S(1)} collective-permute-done((bf16[3,16,128]{2,1,0:T(8,128)(2,1)S(1)}, bf16[3,16,128]{2,1,0:T(8,128)(2,1)S(1)}, u32[]{:S(2)}, u32[]{:S(2)}) %collective-permute-start.7) | collective-permute-done | bytes 12320 | tf_op jit(solution)/shard_map/wave/ppermute | solution.py:40
  14.0 0.3 %halo.1 = (bf16[256,128]{1,0:T(8,128)(2,1)S(1)}, bf16[256,128]{1,0:T(8,128)(2,1)S(1)}) custom-call(f32[42,80,128]{2,1,0:T(8,128)S(1)} %get-tuple-element.43.vel.wide, bf16[304,128]{1,0:T(8,128)(2,1)S(1)} %collective-permute-done.oa, bf16[304,128]{1,0:T(8,128)(2,1)S(1)} %collective-permute-done.1.ob, f32[32,16,128]{2,1,0:T(8,128)S(1)} %get-tuple-element.42.lists, ...), custom_call_target="tpu_custom_call" | custom-call | tf_op jit(solution)/shard_map/halo/halo/pallas_call | solution.py:627
  14.3 0.6 %collective-permute-start.8 = (bf16[256,128]{1,0:T(8,128)(2,1)S(1)}, bf16[256,128]{1,0:T(8,128)(2,1)S(1)}, u32[]{:S(2)}, u32[]{:S(2)}) collective-permute-start(bf16[256,128]{1,0:T(8,128)(2,1)S(1)} %get-tuple-element.63), channel_id=1, source_target_pairs={{0,1},{1,0},{2,3},{3,2},{4,5},{5,4},{6,7},{7,6},{8,9},{9,8},{10,11... | collective-permute-start | bytes 196616 | tf_op jit(solution)/shard_map/halo/ppermute | solution.py:40
  14.9 0.0 collective-permute-start.9
  14.9 2.8 %inner.1 = (f32[32,64,128]{2,1,0:T(8,128)}, bf16[16,16,1152]{2,1,0:T(8,128)(2,1)}, f32[38,2,16,128]{3,2,1,0:T(8,128)S(1)}, f32[38,2,8,128]{3,2,1,0:T(8,128)S(1)}...) custom-call(f32[42,80,128]{2,1,0:T(8,128)S(1)} %get-tuple-element.43, ...), custom_call_target="tpu_custom_call" | custom-call | tf_op jit(solution)/shard_map/inner/inner/pallas_call | solution.py:627
  17.6 2.6 %collective-permute-done.8.ya = bf16[256,128]{1,0:T(8,128)(2,1)S(1)} collective-permute-done((bf16[256,128]{1,0:T(8,128)(2,1)S(1)}, bf16[256,128]{1,0:T(8,128)(2,1)S(1)}, u32[]{:S(2)}, u32[]{:S(2)}) %collective-permute-start.8) | collective-permute-done | bytes 65568 | tf_op jit(solution)/shard_map/halo/ppermute | solution.py:40
  20.2 0.0 collective-permute-done.9.yb
  20.2 2.7 %rim.1 = (f32[32,64,128]{2,1,0:T(8,128)}, f32[2,16,16]{2,1,0:T(8,128)}) custom-call(f32[42,80,128]{2,1,0:T(8,128)S(1)} %get-tuple-element.43.vel.wide, bf16[256,128]{1,0:T(8,128)(2,1)S(1)} %collective-permute-done.8.ya, bf16[256,128]{1,0:T(8,128)(2,1)S(1)} %collective-permute-done.9.yb, ...), custom_call_target="tpu_custom_call", output_to_operand_aliasing={{0}: (12, {})} | custom-call | tf_op jit(solution)/shard_map/rim/rim/pallas_call | solution.py:627
  (1 shorter events, 0.0 us)
Async XLA Ops:
  2.2 10.0 %copy-start = (f32[32,64,128]{2,1,0:T(8,128)S(1)}, f32[32,64,128]{2,1,0:T(8,128)}, u32[]{:S(2)}) copy-start(f32[32,64,128]{2,1,0:T(8,128)} %own.1) | copy-start | bytes 3145732
  2.2 3.7 %collective-permute-start.2 = (bf16[16,1152]{1,0:T(8,128)(2,1)S(1)}, bf16[16,1152]{1,0:T(8,128)(2,1)S(1)}, u32[]{:S(2)}, u32[]{:S(2)}) collective-permute-start(bf16[16,1152]{1,0:T(8,128)(2,1)S(1)} %get-tuple-element.48), channel_id=1, source_target_pairs={{0,8},{1,9},{2,10},{3,11},{4,12},{5,13},{6,14},{7,15},{8,0},{9,1},... | collective-permute-start | bytes 110600 | tf_op jit(solution)/shard_map/spectrum_edges/ppermute | solution.py:40
  2.3 3.9 %collective-permute-start.3 = (bf16[16,1152]{1,0:T(8,128)(2,1)S(1)}, bf16[16,1152]{1,0:T(8,128)(2,1)S(1)}, u32[]{:S(2)}, u32[]{:S(2)}) collective-permute-start(bf16[16,1152]{1,0:T(8,128)(2,1)S(1)} %get-tuple-element.49), channel_id=1, source_target_pairs={{0,24},{1,25},{2,26},{3,27},{4,28},{5,29},{6,30},{7,31},{8,16},{9,... | collective-permute-start | bytes 110600 | tf_op jit(solution)/shard_map/spectrum_edges/ppermute | solution.py:40
  3.9 4.0 %collective-permute-start.4 = (bf16[16,1152]{1,0:T(8,128)(2,1)S(1)}, bf16[16,1152]{1,0:T(8,128)(2,1)S(1)}, u32[]{:S(2)}, u32[]{:S(2)}) collective-permute-start(bf16[16,1152]{1,0:T(8,128)(2,1)S(1)} %get-tuple-element.50), channel_id=1, source_target_pairs={{0,1},{1,0},{2,3},{3,2},{4,5},{5,4},{6,7},{7,6},{8,9},{9,8},{10,11... | collective-permute-start | bytes 110600 | tf_op jit(solution)/shard_map/spectrum_edges/ppermute | solution.py:40
  5.4 4.9 %collective-permute-start.5 = (bf16[16,1152]{1,0:T(8,128)(2,1)S(1)}, bf16[16,1152]{1,0:T(8,128)(2,1)S(1)}, u32[]{:S(2)}, u32[]{:S(2)}) collective-permute-start(bf16[16,1152]{1,0:T(8,128)(2,1)S(1)} %get-tuple-element.51), channel_id=1, source_target_pairs={{0,8},{1,2},{2,1},{3,4},{4,3},{5,6},{6,5},{7,15},{8,0},{9,10},{10,... | collective-permute-start | bytes 110600 | tf_op jit(solution)/shard_map/spectrum_edges/ppermute | solution.py:40
  5.8 6.3 %collective-permute-start = (bf16[304,128]{1,0:T(8,128)(2,1)S(1)}, bf16[304,128]{1,0:T(8,128)(2,1)S(1)}, u32[]{:S(2)}, u32[]{:S(2)}) collective-permute-start(bf16[304,128]{1,0:T(8,128)(2,1)S(1)} %get-tuple-element.40), channel_id=1, source_target_pairs={{0,8},{1,9},{2,10},{3,11},{4,12},{5,13},{6,14},{7,15},{8,0},{9,1},... | collective-permute-start | bytes 233480 | tf_op jit(solution)/shard_map/spectrum_edges/ppermute | solution.py:40
  5.9 6.3 %collective-permute-start.1 = (bf16[304,128]{1,0:T(8,128)(2,1)S(1)}, bf16[304,128]{1,0:T(8,128)(2,1)S(1)}, u32[]{:S(2)}, u32[]{:S(2)}) collective-permute-start(bf16[304,128]{1,0:T(8,128)(2,1)S(1)} %get-tuple-element.41), channel_id=1, source_target_pairs={{0,24},{1,25},{2,26},{3,27},{4,28},{5,29},{6,30},{7,31},{8,16},{9,... | collective-permute-start | bytes 233480 | tf_op jit(solution)/shard_map/spectrum_edges/ppermute | solution.py:40
  10.8 2.9 %collective-permute-start.6 = (bf16[3,16,128]{2,1,0:T(8,128)(2,1)S(1)}, bf16[3,16,128]{2,1,0:T(8,128)(2,1)S(1)}, u32[]{:S(2)}, u32[]{:S(2)}) collective-permute-start(bf16[3,16,128]{2,1,0:T(8,128)(2,1)S(1)} %get-tuple-element.58), channel_id=1, source_target_pairs={{0,8},{1,9},{2,10},{3,11},{4,12},{5,13},{6,14},{7,15},{8,0},{9,1},... | collective-permute-start | bytes 36872 | tf_op jit(solution)/shard_map/wave/ppermute | solution.py:40
  10.9 3.2 %collective-permute-start.7 = (bf16[3,16,128]{2,1,0:T(8,128)(2,1)S(1)}, bf16[3,16,128]{2,1,0:T(8,128)(2,1)S(1)}, u32[]{:S(2)}, u32[]{:S(2)}) collective-permute-start(bf16[3,16,128]{2,1,0:T(8,128)(2,1)S(1)} %get-tuple-element.59), channel_id=1, source_target_pairs={{0,24},{1,25},{2,26},{3,27},{4,28},{5,29},{6,30},{7,31},{8,16},{9,... | collective-permute-start | bytes 36872 | tf_op jit(solution)/shard_map/wave/ppermute | solution.py:40
  14.3 5.9 %collective-permute-start.8 = (bf16[256,128]{1,0:T(8,128)(2,1)S(1)}, bf16[256,128]{1,0:T(8,128)(2,1)S(1)}, u32[]{:S(2)}, u32[]{:S(2)}) collective-permute-start(bf16[256,128]{1,0:T(8,128)(2,1)S(1)} %get-tuple-element.63), channel_id=1, source_target_pairs={{0,1},{1,0},{2,3},{3,2},{4,5},{5,4},{6,7},{7,6},{8,9},{9,8},{10,11... | collective-permute-start | bytes 196616 | tf_op jit(solution)/shard_map/halo/ppermute | solution.py:40
  14.9 5.3 %collective-permute-start.9 = (bf16[256,128]{1,0:T(8,128)(2,1)S(1)}, bf16[256,128]{1,0:T(8,128)(2,1)S(1)}, u32[]{:S(2)}, u32[]{:S(2)}) collective-permute-start(bf16[256,128]{1,0:T(8,128)(2,1)S(1)} %get-tuple-element.64), channel_id=1, source_target_pairs={{0,8},{1,2},{2,1},{3,4},{4,3},{5,6},{6,5},{7,15},{8,0},{9,10},{10,... | collective-permute-start | bytes 196616 | tf_op jit(solution)/shard_map/halo/ppermute | solution.py:40

commit v6 on v5

--- a/solution.py
+++ b/solution.py
@@ -9,7 +9,7 @@
 RX = 2
 RY = 4
 STEP = 0.5
-PARTS = 1
+PARTS = 4
 TALL = 24
 RIM = 4
 HV, HL = 5, 3
@@ -41,8 +41,8 @@
 
 
 def exchange(axis, to_a, to_b):
+    from_a = swap(to_a, axis, 0)
     from_b = swap(to_b, axis, 1)
-    from_a = swap(to_a, axis, 0)
     return from_a, from_b
 
 
@@ -81,21 +81,18 @@
     return (HV - 1) * cols, HL * 16
 
 
-def cut_rows(one, two):
-    step = one.shape[0] // PARTS
-    return [(one.at[pl.ds(i * step, step)], two.at[pl.ds(i * step, step)]) for i in range(PARTS)]
-
-
 def edges_kernel(*refs):
-    (spec_far, courant_far, source_far, land_far, basis_far, codes_far, weights_far, coriolis_far, vel_far) = refs[:9]
-    (xa, xb, ya, yb, oa, ob, lists, spec, courant, source, land, basis) = refs[9:21]
-    (codes, weights, coriolis, vel, sems) = refs[21:]
+    (spec_far, courant_far, source_far, land_far, codes_far, weights_far, coriolis_far, vel_far, basis_far) = refs[:9]
+    (wave_codes_far, wave_weights_far) = refs[9:11]
+    (oa, ob, ya, yb, lists, spec, courant, source_t, land_t, basis, wave_codes, wave_weights) = refs[11:23]
+    (source, land, codes, weights, coriolis, vel, sems) = refs[23:]
     rows, cols, bins = spec.shape
     lanes = vel.shape[-1]
-    pairs = cut_rows(spec_far, spec)
+    pairs = [(spec_far, spec)]
     pairs += [(vel_far.at[pl.ds(at, HV)], vel.at[i]) for i, at in ((0, 0), (1, vel_far.shape[0] - HV))]
     pairs += [(codes_far, codes), (weights_far, weights), (coriolis_far, coriolis)]
     pairs += [(courant_far, courant), (source_far, source), (land_far, land), (basis_far, basis)]
+    pairs += [(wave_codes_far, wave_codes), (wave_weights_far, wave_weights)]
     copies = [pltpu.make_async_copy(one, two, sems.at[i]) for i, (one, two) in enumerate(pairs)]
     for copy in copies:
         copy.start()
@@ -109,18 +106,20 @@
     at, cell = iota((2 * rows, rows * cols), 0), iota((2 * rows, rows * cols), 1)
     wanted = jnp.where(at < rows, at * cols, (at - rows) * cols + cols - 1)
     chosen = (cell == wanted).astype(F32).astype(BF)
-    for copy in copies[:PARTS]:
-        copy.wait()
+    copies[0].wait()
     sides = jnp.dot(chosen, spec[...].reshape(rows * cols, bins), preferred_element_type=F32)
-    first, last = spec[0].astype(F32), spec[rows - 1].astype(F32)
-    xa[...] = jnp.where(even_x, last, first).astype(BF)
-    xb[...] = jnp.where(even_x, first, last).astype(BF)
+    start = sum(x_rows(codes.shape[2]))
+    for i in range(bins // lanes):
+        part = slice(i * lanes, (i + 1) * lanes)
+        put(start + i * cols, spec[rows - 1, :, part].astype(F32), spec[0, :, part].astype(F32))
     first, last = sides[0:rows], sides[rows:]
     ya[...] = jnp.where(even_y, last, first).astype(BF)
     yb[...] = jnp.where(even_y, first, last).astype(BF)
 
-    for copy in copies[PARTS:]:
+    for copy in copies[1:]:
         copy.wait()
+    source_t[...] = source[...].T
+    land_t[...] = land[...].astype(F32).T
     listed, wide = codes.shape[0], codes.shape[2]
     is_u = iota((1, lanes), 1) < lanes // 2
     outer = [
@@ -176,11 +175,20 @@
             cells = []
 
 
-def wave_ends_kernel(spec, xa, xb, ya, yb, courant, source, land, weights, out, profile, pa, pb):
+def sides_kernel(xb, xa, after, sides):
+    even_x = is_even("gx")
+    cols, bins = sides.shape[1], sides.shape[2]
+    lanes = xa.shape[1]
+    start = xa.shape[0] - cols * bins // lanes
+    for i in range(bins // lanes):
+        a, b = (ref[start + i * cols : start + (i + 1) * cols, :] for ref in (xa, xb))
+        part = slice(i * lanes, (i + 1) * lanes)
+        sides[0, :, part], sides[1, :, part] = pick(even_x, b, a).astype(BF), pick(even_x, a, b).astype(BF)
+
+
+def wave_ends_kernel(spec, sides, yb, ya, courant, source, land, weights, out, profile, pa, pb):
     rows, cols, bins = spec.shape
     even_x = is_even("gx")
-    west, east = pick(even_x, xb[...], xa[...]), pick(even_x, xa[...], xb[...])
-
     parts = []
 
     def put(x, value, part):
@@ -189,14 +197,14 @@
         parts.append(part)
 
     ends = list(range(HX)) + list(range(rows - HX, rows))
-    advance(ends, spec, (west, east), ya, yb, courant, source, land, weights, HX, put)
+    advance(ends, spec, [sides[i].astype(F32) for i in range(2)], ya, yb, courant, source, land, weights, HX, put)
     for i in range(HX):
         first, last = parts[i], parts[HX + i]
         pa[i] = jnp.where(even_x, last, first).astype(BF)
         pb[i] = jnp.where(even_x, first, last).astype(BF)
 
 
-def wave_rest_kernel(spec, ya, yb, courant, source, land, weights, ends, out, profile):
+def wave_rest_kernel(spec, yb, ya, courant, source, land, weights, ends, out, profile):
     rows = spec.shape[0]
 
     def put(x, value, part):
@@ -215,9 +223,13 @@
     return TALL * HY, (pairs + pairs % 2) * EDGE
 
 
-def halo_kernel(vel, oa, ob, lists, ends, rest, pa, pb, ya, yb):
-    vrow, lanes = vel.shape[0], vel.shape[2]
-    rows, cols = vrow - 2 * HV, vel.shape[1] - 2 * EDGE
+def row_of(i, rows, own, ends, reach):
+    return own[i] if 0 <= i < rows else ends[i + reach if i < 0 else i - rows + reach]
+
+
+def halo_kernel(vel, vel_halo, ob, oa, lists, ends, rest, pb, pa, ya, yb):
+    rows, cols, lanes = vel.shape
+    vrow = rows + 2 * HV
     even_x, even_y = is_even("gx"), is_even("gy")
     wr, wc = rest.shape[0] + 2 * HX, rest.shape[1]
 
@@ -240,13 +252,25 @@
 
     sub = iota((EDGE, 1), 0)
     is_u = iota((1, lanes), 1) < lanes // 2
-    end = EDGE + cols
     blocks = []
     for r in range(vrow):
         to = RIM * (r % 2)
-        one, two = vel[r, end - RIM - to : end + RIM - to, :], vel[r, end - RIM - 1 - to : end + RIM - 1 - to, :]
+
+        def ends_of(ref, k):
+            return ref[k, cols - EDGE : cols, :], ref[k, 0:EDGE, :]
+
+        i = r - HV
+        if 0 <= i < rows:
+            last, first = ends_of(vel, i)
+        else:
+            last, first = ends_of(vel_halo, r if i < 0 else r - rows)
+
+        def moved(value, one, two):
+            return pltpu.roll(value, (two - one) % EDGE, 0) if one != two else value
+
+        one, two = moved(last, EDGE - RIM, to), moved(last, EDGE - RIM - 1, to)
         last = jnp.where(sub == to, jnp.where(is_u, two, pltpu.roll(one, lanes // 2, 1)), one)
-        one, two = vel[r, EDGE - to : 2 * EDGE - to, :], vel[r, EDGE + 1 - to : 2 * EDGE + 1 - to, :]
+        one, two = moved(first, 0, to), moved(first, RIM, to + RIM - 1)
         first = jnp.where(sub == to + RIM - 1, jnp.where(is_u, one, pltpu.roll(two, lanes // 2, 1)), one)
         blocks.append((last, first))
     pairs = [
@@ -258,7 +282,7 @@
     start = slots + len(pairs) * EDGE
 
     group = iota((1, lanes), 1) // RIM
-    x_start = oa.shape[0] - HL * 16
+    x_start = (HV - 1) * cols
     tiles = list_place(rows + 2 * HL - 1, lanes)[0] + 1
     acc = [[jnp.zeros((16, lanes), F32)] * 2 for _ in range(tiles)]
     for r in range(rows + 2 * HL):
@@ -304,81 +328,133 @@
     return pltpu.roll(value, half, 1) * sign
 
 
-def prepare_kernel(own, oa, ob, lists, vel, spin, turn, table, list_rim):
+def one_hot(full, cols):
+    lanes = full.shape[1]
+    wave_cols = cols // RY
+    codes = full[0:EDGE]
+    third = jnp.where(codes >= 6.0, 2.0, jnp.where(codes >= 3.0, 1.0, 0.0))
+    slot = third * (wave_cols - 3.0) + codes + (iota((1, lanes), 1) // RY).astype(F32) - 1.0
+    place = iota((3 * wave_cols, lanes), 0).astype(F32)
+    hot = jnp.where(place == slot[0:1], full[K : K + 1], 0.0)
+    for k in range(1, K):
+        hot = hot + jnp.where(place == slot[k : k + 1], full[K + k : K + k + 1], 0.0)
+    return hot.astype(BF)
+
+
+def rim_lists(full, rim, r, cols):
+    lanes = full.shape[1]
+    lane = iota((1, lanes), 1)
+    to = (r % (lanes // 16)) * 16
+    rim = jnp.where(lane // RIM == to // RIM + 1, pltpu.roll(full, (to + RIM) % lanes, 1), rim)
+    return jnp.where(lane // RIM == to // RIM + 2, pltpu.roll(full, (to + 3 * RIM - cols) % lanes, 1), rim)
+
+
+def prepare_own_kernel(
+    own, lists, codes, weights, spin, turn, table, list_rim, wave_shares, chosen, spread, vel
+):
     rows, cols, lanes = own.shape
+    per = lanes // 16
+    blank = jnp.zeros((EDGE, lanes), F32)
+
+    def fill(i, _):
+        vel[i, 0:EDGE, :] = blank
+        vel[i, EDGE + cols :, :] = blank
+        vel[i, EDGE : EDGE + cols, :] = own[i]
+        return 0
+
+    lax.fori_loop(0, rows, fill, 0, unroll=8)
+    rim = [jnp.zeros((16, lanes), F32)] * list_rim.shape[0]
+    for i in range(rows):
+        g = (i + HL) // per
+        full = lists[i]
+        table[i], rim[g] = one_hot(full, cols), rim_lists(full, rim[g], i + HL, cols)
+    for g, value in enumerate(rim):
+        list_rim[g] = value
+
+    ones = jnp.ones((8, lanes), BF)
+
+    def widened(i):
+        return lax.dot_general(lists[i, 2 * K :, :].astype(BF), ones, ROWS_DOT, preferred_element_type=F32)[0:cols]
+
+    for i in (0, 1, rows - 2, rows - 1):
+        spin[i] = widened(i)
+    half = (rows - 4) // 2
+
+    def absolute(m, _):
+        for u in range(half):
+            i = m * half + u + 2
+            wide = widened(i)
+            spin[i] = wide
+            turn[i - 2] = wide + vorticity(vel, i, EDGE, cols)
+        return 0
+
+    lax.fori_loop(0, 2, absolute, 0)
+
     wc = cols // RY
-    listed = rows + 2 * HL
-    unroll = listed // 2
+    lane = iota((1, lanes), 1)
+    at, to = iota(chosen.shape, 0), iota(chosen.shape, 1)
+    reach = (RY + 2) * wc
+    chosen[...] = ((to < reach) & (at == RY * (to % wc) + to // wc + RIM - 1)).astype(F32)
+    at, to = iota((lanes, lanes), 0), iota((lanes, lanes), 1)
+    spread[...] = ((at < reach) & (at % wc == to)).astype(F32).astype(BF)
+
+    at, to = iota((wc, lanes), 0), iota((wc, lanes), 1)
+    repeat = ((to < reach) & (to % wc == at)).astype(F32).astype(BF)
+    shift = (lane // wc).astype(F32)
+    weight = [weights[:, k, :] for k in range(K)]
+    whole = sum(weight[1:], weight[0])
+    code = [jnp.dot(codes[:, k, :].astype(F32).astype(BF), repeat, preferred_element_type=F32) for k in range(K)]
+    share = [
+        sum(jnp.dot(p, repeat, preferred_element_type=F32) for p in split3(weight[k] / whole)) for k in range(K)
+    ]
+    for near in range(RX + 2):
+        wave_shares[near] = sum(
+            jnp.where(code[k] == near * (RY + 2.0) + shift, share[k], 0.0) for k in range(K)
+        )
+
+
+def prepare_ends_kernel(own, ob, oa, spin_own, list_own, vel_halo, spin, turn, table, list_rim, vel):
+    rows, cols, lanes = own.shape
+    per = lanes // 16
     even_x = is_even("gx")
-    lane = iota((1, lanes), 1)
-
-    def from_x(r, halo, start, n):
-        one, two = (ob, oa) if r < halo else (oa, ob)
-        return pick(even_x, one[start : start + n, :], two[start : start + n, :])
-
     blank = jnp.zeros((EDGE, lanes), F32)
-
-    def fill(r, _):
-        vel[r + HV, EDGE : EDGE + cols, :] = own[r]
-        return 0
-
-    lax.fori_loop(0, rows, fill, 0, unroll=8)
-    for r in range(rows + 2 * HV):
-        vel[r, 0:EDGE, :] = blank
-        vel[r, EDGE + cols :, :] = blank
-    for i in range(HV - 1):
-        near, far = from_x(0, HV, i * cols, cols), from_x(HV, HV, i * cols, cols)
-        if i == 0:
-            vel[0, EDGE : EDGE + cols, :] = pltpu.roll(near, lanes // 2, 1)
-            vel[2 * HV + rows - 1, EDGE : EDGE + cols, :] = pltpu.roll(far, lanes // 2, 1)
-            vel[1, EDGE : EDGE + cols, :] = near
-            vel[2 * HV + rows - 2, EDGE : EDGE + cols, :] = far
-        else:
-            vel[i + 1, EDGE : EDGE + cols, :] = near
-            vel[HV + rows + i - 1, EDGE : EDGE + cols, :] = far
-
-    sub16 = iota((16, 1), 0)
-    place_of = (lane // RY).astype(F32) - 1.0
-    per = lanes // 16
-    rim = jnp.zeros((16, lanes), F32)
-    for r in range(listed):
-        if HL <= r < HL + rows:
-            full = lists[r - HL]
-        else:
-            i = r if r < HL else r - HL - rows
-            full = from_x(0 if r < HL else HL, HL, (HV - 1) * cols + i * 16, 16)
-        third = jnp.where(full >= 6.0, 2.0, jnp.where(full >= 3.0, 1.0, 0.0))
-        table[r] = jnp.where(sub16 < K, third * (wc - 3.0) + full + place_of, full)
-        to = (r % per) * 16
-        rim = jnp.where(lane // RIM == to // RIM + 1, pltpu.roll(full, (to + RIM) % lanes, 1), rim)
-        rim = jnp.where(lane // RIM == to // RIM + 2, pltpu.roll(full, (to + 3 * RIM - cols) % lanes, 1), rim)
-        if r % per == per - 1 or r == listed - 1:
-            list_rim[r // per] = rim
-            rim = jnp.zeros((16, lanes), F32)
-
+    list_rim[...] = list_own[...]
     ones = jnp.ones((8, lanes), BF)
-
-    def absolute(m, _):
-        for u in range(unroll):
-            r = m * unroll + u
-            wide = lax.dot_general(table[r, 2 * K :, :].astype(BF), ones, ROWS_DOT, preferred_element_type=F32)
-            spin[r] = wide[0:cols]
-            turn[r] = wide[0:cols] + vorticity(vel, r + HV - HL, EDGE, cols)
-        return 0
-
-    lax.fori_loop(0, listed // unroll, absolute, 0)
+    for side in range(2):
+        one, two = (oa, ob) if side else (ob, oa)
+
+        def from_x(start, n):
+            return pick(even_x, one[start : start + n, :], two[start : start + n, :])
+
+        parts = [from_x(i * cols, cols) for i in range(HV - 1)]
+        outer = pltpu.roll(parts[0], lanes // 2, 1)
+        parts = parts[1:] + [parts[0], outer] if side else [outer] + parts
+        for k in range(HV):
+            vel_halo[side * HV + k] = parts[k]
+        near = [own[i] for i in (range(rows - HV + 1, rows) if side else range(HV - 1))]
+        for k, value in enumerate(near + parts if side else parts + near):
+            vel[side, k, 0:EDGE, :] = blank
+            vel[side, k, EDGE + cols :, :] = blank
+            vel[side, k, EDGE : EDGE + cols, :] = value
+        for k in range(HL):
+            at = side * HL + k
+            r = k + side * (rows + HL)
+            full = from_x((HV - 1) * cols + k * 16, 16)
+            table[at], list_rim[r // per] = one_hot(full, cols), rim_lists(full, list_rim[r // per], r, cols)
+            spin[at] = lax.dot_general(full[2 * K :].astype(BF), ones, ROWS_DOT, preferred_element_type=F32)[0:cols]
+        for k in range(HL + 2):
+            i = k + (rows - 2 if side else -HL)
+            turn[side * (HL + 2) + k] = row_of(i, rows, spin_own, spin, HL) + vorticity(vel.at[side], k + 2, EDGE, cols)
 
 
 def inner_kernel(
-    vel, spin, turn, table, ends, rest, pa, pb, codes_far, weights_far, cells_ends, cells_rest,
-    out_far, cells_far, mid_rim, drift_rim, spin_rim, total, prof_rim, wave_shares, chosen, spread,
-    mid, names, prof, drift, out, codes, weights, sems,
+    vel, vel_halo, spin_own, spin_ends, turn_own, turn_ends, table_own, table_ends,
+    ends, rest, pb, pa, cells_ends, cells_rest,
+    out, cells_far, mid_rim, drift_rim, spin_rim, total, prof_rim,
+    mid, names, prof, drift, sems,
 ):
     rows, cols, lanes = out.shape
-    copies = [
-        pltpu.make_async_copy(codes_far, codes, sems.at[0]),
-        pltpu.make_async_copy(weights_far, weights, sems.at[1]),
-    ]
+    copies = []
     wr, wc = rest.shape[0] + 2 * HX, rest.shape[1]
     for part, to in (
         (cells_ends.at[pl.ds(0, HX)], cells_far.at[pl.ds(0, HX)]),
@@ -390,7 +466,6 @@
         copy.start()
     listed = rows + 2 * HL
     prow = wr + 2 * HX
-    unroll = listed // 2
     even_x = is_even("gx")
     lane = iota((1, lanes), 1)
     blank = jnp.zeros((EDGE, lanes), F32)
@@ -412,81 +487,63 @@
         prof_rim[1, pl.ds(c, prow, stride=2 * HY), :] = prof[pl.ds(wc - HY + c, prow, stride=wc), :]
 
     block = 3 * wc
-    place = iota((block, lanes), 0).astype(F32)
-    lift = HV - HL
+
+    def first(r, vel_ref, table_ref, turn_ref, spin_ref, vk, tk, uk):
+        named = names[pl.ds(pl.multiple_of((r + 1) // 2 * wc, wc), block), :]
+        stokes = lax.dot_general(table_ref[tk], named, ROWS_DOT, preferred_element_type=F32)[0:cols]
+        drift[r] = stokes
+        new = vel_ref[vk] + STEP * (turn_ref[uk] * stokes)
+        mid[r, 0:EDGE, :] = blank
+        mid[r, EDGE + cols :, :] = blank
+        mid[r, EDGE : EDGE + cols, :] = new
+        mid_rim[r, 0] = new[0 : 2 * EDGE]
+        mid_rim[r, 1] = new[cols - 2 * EDGE :]
+        for where in range(2):
+            begin = RIM if where == 0 else cols - RIM - EDGE
+            drift_rim[r, where] = drift[r, begin : begin + EDGE, :]
+            spin_rim[r, where] = spin_ref[tk, begin : begin + EDGE, :]
+
+    for i in [*range(-HL, 2), *range(rows - 2, rows + HL)]:
+        end = i + HL if i < 2 else i - rows + HL + 4
+        if 0 <= i < rows:
+            first(i + HL, vel, table_own, turn_ends, spin_own, i, i, end)
+        else:
+            far = 0 if i < 0 else rows
+            first(i + HL, vel_halo, table_ends, turn_ends, spin_ends, i - far + HV, i - far + HL, end)
+    unroll = (rows - 4) // 2
 
     def first_step(m, _):
         for u in range(unroll):
-            r = m * unroll + u
-            hot = jnp.where(place == table[r, 0:1, :], table[r, K : K + 1, :], 0.0)
-            for k in range(1, K):
-                hot = hot + jnp.where(place == table[r, k : k + 1, :], table[r, K + k : K + k + 1, :], 0.0)
-            named = names[pl.ds(pl.multiple_of((r + 1) // 2 * wc, wc), block), :]
-            stokes = lax.dot_general(hot.astype(BF), named, ROWS_DOT, preferred_element_type=F32)[0:cols]
-            drift[r] = stokes
-            new = vel[r + lift, EDGE : EDGE + cols, :] + STEP * (turn[r] * stokes)
-            mid[r, 0:EDGE, :] = blank
-            mid[r, EDGE + cols :, :] = blank
-            mid[r, EDGE : EDGE + cols, :] = new
-            mid_rim[r, 0] = new[0 : 2 * EDGE]
-            mid_rim[r, 1] = new[cols - 2 * EDGE :]
-            for where in range(2):
-                begin = RIM if where == 0 else cols - RIM - EDGE
-                drift_rim[r, where] = drift[r, begin : begin + EDGE, :]
-                spin_rim[r, where] = spin[r, begin : begin + EDGE, :]
+            i = m * unroll + u + 2
+            first(i + HL, vel, table_own, turn_own, spin_own, i, i, i - 2)
         return 0
 
-    lax.fori_loop(0, listed // unroll, first_step, 0)
+    lax.fori_loop(0, 2, first_step, 0)
 
     average = averager(lanes)
     means = jnp.zeros((cols, lanes), F32)
     for n in range(rows + 2):
         r = n + HL - 1
-        absolute = spin[r] + vorticity(mid, r, EDGE, cols)
-        old = vel[r + lift, EDGE : EDGE + cols, :] + mid[r, EDGE : EDGE + cols, :]
+        absolute = row_of(n - 1, rows, spin_own, spin_ends, HL) + vorticity(mid, r, EDGE, cols)
+        old = row_of(n - 1, rows, vel, vel_halo, HV) + mid[r, EDGE : EDGE + cols, :]
         new = 0.5 * old + (0.5 * STEP) * (absolute * drift[r])
         sums = jnp.dot(jnp.concatenate(split(new), axis=1), average, preferred_element_type=F32)
         means = jnp.where(lane // 2 == n, sums, means)
         if 1 <= n <= rows:
             out[n - 1] = new
-            if n % (rows // 4) == 0:
-                part = pl.ds(n - rows // 4, rows // 4)
-                copies.append(pltpu.make_async_copy(out.at[part], out_far.at[part], sems.at[len(copies)]))
-                copies[-1].start()
     total[...] = means
 
-    at, to = iota(chosen.shape, 0), iota(chosen.shape, 1)
-    reach = (RY + 2) * wc
-    chosen[...] = ((to < reach) & (at == RY * (to % wc) + to // wc + RIM - 1)).astype(F32)
-    at, to = iota((lanes, lanes), 0), iota((lanes, lanes), 1)
-    spread[...] = ((at < reach) & (at % wc == to)).astype(F32).astype(BF)
-
-    copies[0].wait()
-    copies[1].wait()
-    at, to = iota((wc, lanes), 0), iota((wc, lanes), 1)
-    repeat = ((to < reach) & (to % wc == at)).astype(F32).astype(BF)
-    shift = (lane // wc).astype(F32)
-    weight = [weights[:, k, :] for k in range(K)]
-    whole = sum(weight[1:], weight[0])
-    code = [jnp.dot(codes[:, k, :].astype(F32).astype(BF), repeat, preferred_element_type=F32) for k in range(K)]
-    share = [
-        sum(jnp.dot(p, repeat, preferred_element_type=F32) for p in split3(weight[k] / whole)) for k in range(K)
-    ]
-    for near in range(RX + 2):
-        wave_shares[near] = sum(
-            jnp.where(code[k] == near * (RY + 2.0) + shift, share[k], 0.0) for k in range(K)
-        )
-    for copy in copies[2:]:
+    for copy in copies:
         copy.wait()
 
 
 def rim_kernel(
-    wide, ya, yb, mid_rim, drift_rim, spin_rim, total, list_rim, prof_rim, wave_shares, chosen, spread, velocity_in,
-    velocity_out, current,
+    own, vel_halo, yb, ya, mid_rim, drift_rim, spin_rim, total, list_rim, prof_rim, wave_shares, chosen, spread, inner,
+    out, current,
     vel, mid, prof, drift, spin, picked, means, strips, sems,
 ):
-    vrow, lanes = wide.shape[0], wide.shape[2]
-    rows, cols = vrow - 2 * HV, wide.shape[1] - 2 * EDGE
+    rows, cols, lanes = own.shape
+    vrow = rows + 2 * HV
     wr, wc = current.shape[1], current.shape[2]
     listed = rows + 2 * HL
     prow = wr + 2 * HX
@@ -500,12 +557,17 @@
         a, b = ya[start : start + n, :], yb[start : start + n, :]
         return pick(even_y, b, a) * has_south, pick(even_y, a, b) * has_north
 
+    middle = pl.ds(EDGE, cols - 2 * EDGE)
+    copies = [pltpu.make_async_copy(inner.at[:, middle, :], out.at[:, middle, :], sems.at[0])]
+    copies[0].start()
+
     blank = jnp.zeros((EDGE, lanes), F32)
     for r in range(vrow):
         vel[0, r, 0:EDGE, :] = blank
         vel[1, r, 2 * EDGE :, :] = blank
-        vel[0, r, EDGE:, :] = wide[r, EDGE : 3 * EDGE, :]
-        vel[1, r, 0 : 2 * EDGE, :] = wide[r, cols - EDGE : cols + EDGE, :]
+        ref, k = (own, r - HV) if HV <= r < HV + rows else (vel_halo, r if r < HV else r - rows)
+        vel[0, r, EDGE:, :] = ref[k, 0 : 2 * EDGE, :]
+        vel[1, r, 0 : 2 * EDGE, :] = ref[k, cols - 2 * EDGE : cols, :]
     for start in range(0, vel_rows, 2 * EDGE):
         pieces = from_y(slots + start, 2 * EDGE)
         for i in range(2):
@@ -574,6 +636,7 @@
 
     average = averager(lanes)
     acc = jnp.zeros((4 * EDGE, lanes), F32)
+    step = rows // PARTS
     for n in range(rows + 2):
         r = n + HL - 1
         both = []
@@ -591,12 +654,12 @@
             jnp.concatenate(split(jnp.concatenate(both, axis=0)), axis=1), average, preferred_element_type=F32
         )
         acc = jnp.where(lane // 2 == n, sums, acc)
-    copies = [
-        pltpu.make_async_copy(strips.at[side], velocity_out.at[:, pl.ds(at, EDGE), :], sems.at[side])
-        for side, at in ((0, 0), (1, cols - EDGE))
-    ]
-    for copy in copies:
-        copy.start()
+        if n and n % step == 0:
+            part = pl.ds(n - step, step)
+            for side, at in ((0, 0), (1, cols - EDGE)):
+                one, two = strips.at[side, part], out.at[part, pl.ds(at, EDGE), :]
+                copies.append(pltpu.make_async_copy(one, two, sems.at[len(copies)]))
+                copies[-1].start()
     means[0 : 2 * EDGE] = acc[0 : 2 * EDGE]
     means[2 * EDGE : 2 * RIM + cols - 2 * EDGE] = total[2 * EDGE - RIM : cols - 2 * EDGE + RIM, :]
     means[2 * RIM + cols - 2 * EDGE :] = acc[2 * EDGE :]
@@ -622,7 +685,7 @@
 ANY = pl.BlockSpec(memory_space=pltpu.HBM)
 
 
-def call(kernel, name, outs, *args, scratch=(), any_in=(), any_out=(), aliases=None):
+def call(kernel, name, outs, *args, scratch=(), any_in=(), any_out=()):
     args = [pltpu.with_memory_space_constraint(v, pltpu.HBM) if i in any_in else v for i, v in enumerate(args)]
     return pl.pallas_call(
         kernel,
@@ -630,7 +693,6 @@
         in_specs=[ANY if i in any_in else VMEM for i in range(len(args))],
         out_specs=tuple(ANY if i in any_out else VMEM for i in range(len(outs))),
         scratch_shapes=list(scratch),
-        input_output_aliases=aliases or {},
         compiler_params=pltpu.CompilerParams(vmem_limit_bytes=14 << 20),
         name=name,
     )(*args)
@@ -647,73 +709,82 @@
 
     with jax.named_scope("spectrum_edges"):
         codes, weights = jnp.transpose(ocean_codes, (0, 2, 1)), jnp.transpose(ocean_weights, (0, 2, 1))
-        size = sum(x_rows(cols))
-        outs = [((wc, bins), BF)] * 2 + [((wr, bins), BF)] * 2 + [((size, lanes), BF)] * 2 + [((rows, 16, lanes), F32)]
-        kept = [spectrum, courant, source, wave_land, stokes_kernel]
-        xa, xb, ya, yb, oa, ob, lists, spectrum, courant, source, wave_land, stokes_kernel = call(
-            edges_kernel, "edges", outs + [(v.shape, v.dtype) for v in kept],
-            *kept, codes, weights, coriolis, velocity, any_in=range(9),
+        size = sum(x_rows(cols)) + wc * bins // lanes
+        outs = [((size, lanes), BF)] * 2 + [((wr, bins), BF)] * 2 + [((rows, 16, lanes), F32)]
+        outs += [(spectrum.shape, BF), (courant.shape, F32), ((wc, wr), F32), ((wc, wr), F32), (stokes_kernel.shape, BF)]
+        outs += [((wr, K, wc), wave_codes.dtype), ((wr, K, wc), F32)]
+        oa, ob, ya, yb, lists, spectrum, courant, source, land, stokes_kernel, wave_codes, wave_weights = call(
+            edges_kernel, "edges", outs,
+            spectrum, courant, source, wave_land, codes, weights, coriolis, velocity, stokes_kernel,
+            jnp.transpose(wave_codes, (0, 2, 1)), jnp.transpose(wave_weights, (0, 2, 1)), any_in=range(11),
             scratch=[
+                pltpu.VMEM(source.shape, F32),
+                pltpu.VMEM(wave_land.shape, wave_land.dtype),
                 pltpu.VMEM(codes.shape, codes.dtype),
                 pltpu.VMEM(weights.shape, F32),
                 pltpu.VMEM(coriolis.shape, F32),
                 pltpu.VMEM((2, HV, cols, lanes), F32),
-                pltpu.SemaphoreType.DMA((9 + PARTS,)),
+                pltpu.SemaphoreType.DMA((12,)),
             ],
         )
-        xa, xb = exchange("gx", xa, xb)
+        oa, ob = exchange("gx", oa, ob)
         ya, yb = exchange("gy", ya, yb)
-        oa, ob = exchange("gx", oa, ob)
+
+    with jax.named_scope("prepare_own"):
+        groups = -(-listed // (lanes // 16))
+        level = (cols, lanes)
+        spin_own, turn_own, table_own, list_own, wave_shares, chosen, spread = call(
+            prepare_own_kernel, "prepare_own",
+            [
+                ((rows, *level), F32), ((rows - 4, *level), F32), ((rows, 3 * wc, lanes), BF), ((groups, 16, lanes), F32),
+                ((RX + 2, wr, lanes), F32), ((cols + 2 * RIM, lanes), F32), ((lanes, lanes), BF),
+            ],
+            velocity, lists, wave_codes, wave_weights, scratch=[pltpu.VMEM((rows, cols + 2 * EDGE, lanes), F32)],
+        )
 
     with jax.named_scope("wave"):
-        source, land = source.T, wave_land.T.astype(F32)
         edge = (HX, wc, lanes)
+        sides = call(sides_kernel, "sides", [((2, wc, bins), BF)], ob, oa, list_own)[0]
         cells_ends, ends, pa, pb = call(
             wave_ends_kernel, "wave_ends",
             [((2 * HX, wc, bins), BF), ((2 * HX, wc, lanes), BF), (edge, BF), (edge, BF)],
-            spectrum, xa, xb, ya, yb, courant, source, land, stokes_kernel,
+            spectrum, sides, yb, ya, courant, source, land, stokes_kernel,
         )
         pa, pb = exchange("gx", pa, pb)
         cells_rest, rest = call(
             wave_rest_kernel, "wave_rest",
             [((wr - 2 * HX, wc, bins), BF), ((wr - 2 * HX, wc, lanes), BF)],
-            spectrum, ya, yb, courant, source, land, stokes_kernel, ends,
-        )
-
-    with jax.named_scope("prepare"):
-        wide = cols + 2 * EDGE
-        groups = -(-listed // (lanes // 16))
-        vel, spin, turn, table, list_rim = call(
-            prepare_kernel, "prepare",
+            spectrum, yb, ya, courant, source, land, stokes_kernel, ends,
+        )
+
+    with jax.named_scope("prepare_ends"):
+        vel_halo, spin_ends, turn_ends, table_ends, list_rim = call(
+            prepare_ends_kernel, "prepare_ends",
             [
-                ((rows + 2 * HV, wide, lanes), F32),
-                ((listed, cols, lanes), F32),
-                ((listed, cols, lanes), F32),
-                ((listed, 16, lanes), F32),
-                ((groups, 16, lanes), F32),
+                ((2 * HV, *level), F32), ((2 * HL, *level), F32), ((2 * HL + 4, *level), F32),
+                ((2 * HL, 3 * wc, lanes), BF), ((groups, 16, lanes), F32),
             ],
-            velocity, oa, ob, lists,
+            velocity, ob, oa, spin_own, list_own,
+            scratch=[pltpu.VMEM((2, 2 * HV - 1, cols + 2 * EDGE, lanes), F32)],
         )
 
     with jax.named_scope("halo"):
         size = sum(y_rows(rows)) + (list_place(listed - 1, lanes)[0] + 1) * 16
         ya, yb = call(
-            halo_kernel, "halo", [((size, lanes), BF)] * 2, vel, oa, ob, lists, ends, rest, pa, pb
+            halo_kernel, "halo", [((size, lanes), BF)] * 2,
+            velocity, vel_halo, ob, oa, lists, ends, rest, pb, pa,
         )
         ya, yb = exchange("gy", ya, yb)
 
     with jax.named_scope("inner"):
         scratch = [
-            pltpu.VMEM((listed, wide, lanes), F32),
+            pltpu.VMEM((listed, cols + 2 * EDGE, lanes), F32),
             pltpu.VMEM((prow * wc, lanes), BF),
             pltpu.VMEM((prow * wc, lanes), F32),
             pltpu.VMEM((listed, cols, lanes), F32),
-            pltpu.VMEM(velocity.shape, F32),
-            pltpu.VMEM((wr, K, wc), jnp.int32),
-            pltpu.VMEM((wr, K, wc), F32),
-            pltpu.SemaphoreType.DMA((9,)),
+            pltpu.SemaphoreType.DMA((3,)),
         ]
-        new_velocity, new_spectrum, mid_rim, drift_rim, spin_rim, total, prof_rim, wave_shares, chosen, spread = call(
+        result, new_spectrum, mid_rim, drift_rim, spin_rim, total, prof_rim = call(
             inner_kernel, "inner",
             [
                 (velocity.shape, F32),
@@ -723,13 +794,10 @@
                 ((listed, 2, EDGE, lanes), F32),
                 ((cols, lanes), F32),
                 ((2, 2 * HY * (TALL + 4), lanes), F32),
-                ((RX + 2, wr, lanes), F32),
-                ((cols + 2 * RIM, lanes), F32),
-                ((lanes, lanes), BF),
             ],
-            vel, spin, turn, table, ends, rest, pa, pb,
-            jnp.transpose(wave_codes, (0, 2, 1)), jnp.transpose(wave_weights, (0, 2, 1)),
-            cells_ends, cells_rest, scratch=scratch, any_in=(8, 9), any_out=(0, 1),
+            velocity, vel_halo, spin_own, spin_ends, turn_own, turn_ends, table_own, table_ends,
+            ends, rest, pb, pa,
+            cells_ends, cells_rest, scratch=scratch, any_out=(1,),
         )
 
     with jax.named_scope("rim"):
@@ -742,12 +810,12 @@
             pltpu.VMEM((lanes, lanes), F32),
             pltpu.VMEM((cols + 2 * RIM, lanes), F32),
             pltpu.VMEM((2, rows, EDGE, lanes), F32),
-            pltpu.SemaphoreType.DMA((2,)),
+            pltpu.SemaphoreType.DMA((1 + 2 * PARTS,)),
         ]
         new_velocity, current = call(
             rim_kernel, "rim", [(velocity.shape, F32), ((2, wr, wc), F32)],
-            vel, ya, yb, mid_rim, drift_rim, spin_rim, total, list_rim, prof_rim, wave_shares, chosen, spread,
-            new_velocity, scratch=scratch, any_in=(12,), any_out=(0,), aliases={12: 0},
+            velocity, vel_halo, yb, ya, mid_rim, drift_rim, spin_rim, total, list_rim, prof_rim, wave_shares, chosen, spread,
+            result, scratch=scratch, any_out=(0,),
         )
     return new_spectrum, new_velocity, current
 

time: 23.1 us -> 22.7 us (0.983)
  the two profiles are of different devices: /device:TPU:8 before, /device:TPU:0 now
where the time goes in v6:
time: 22.7 us; the launch traced here: 22.6 us
  starting transfers between devices  10.4 us (46%)
  Pallas kernels  9.56 us (42%)
  waiting for transfers between devices  1.92 us (8%)
  between operations  0.72 us (3%)
    ppermute x8, starting transfers between devices, swap(): return lax.ppermute(value, ('gx', 'gy'), pairs)  10.4 us
    pallas_call x9, Pallas kernels, call(): pl.pallas_call(kernel, out_shape=tuple((jax.ShapeDtypeStruct(shape, dtype...  9.56 us
    ppermute x8, waiting for transfers between devices, swap(): return lax.ppermute(value, ('gx', 'gy'), pairs)  1.92 us
  transfers between devices with their start and end apart: 8, of which 3 were waited for; matrix products, arithmetic and copies ran while one was open for 0% of the time, Pallas kernels for 21%

profile of v6, /device:TPU:0, one launch (start us, length us, event | category | flops | bytes accessed | tf_op | source)
XLA Modules:
  0.0 22.6 jit_solution(16865056713840599687)
XLA Ops:
  0.6 0.0 copy-start
  0.6 1.7 %edges.1 = (bf16[448,128]{1,0:T(8,128)(2,1)S(1)}, bf16[448,128]{1,0:T(8,128)(2,1)S(1)}, bf16[16,1152]{1,0:T(8,128)(2,1)S(1)}, bf16[16,1152]{1,0:T(8,128)(2,1)S(1...) custom-call(bf16[16,16,1152]{2,1,0:T(8,128)(2,1)} %refs_0_.1, ...), custom_call_target="tpu_custom_call" | custom-call | tf_op jit(solution)/shard_map/spectrum_edges/edges/pallas_call | solution.py:690
  2.3 2.4 %collective-permute-start = (bf16[448,128]{1,0:T(8,128)(2,1)S(1)}, bf16[448,128]{1,0:T(8,128)(2,1)S(1)}, u32[]{:S(2)}, u32[]{:S(2)}) collective-permute-start(bf16[448,128]{1,0:T(8,128)(2,1)S(1)} %get-tuple-element.44), channel_id=1, source_target_pairs={{0,24},{1,25},{2,26},{3,27},{4,28},{5,29},{6,30},{7,31},{8,16},{9,... | collective-permute-start | bytes 344072 | tf_op jit(solution)/shard_map/spectrum_edges/ppermute | solution.py:40
  4.8 0.7 %collective-permute-start.1 = (bf16[448,128]{1,0:T(8,128)(2,1)S(1)}, bf16[448,128]{1,0:T(8,128)(2,1)S(1)}, u32[]{:S(2)}, u32[]{:S(2)}) collective-permute-start(bf16[448,128]{1,0:T(8,128)(2,1)S(1)} %get-tuple-element.45), channel_id=1, source_target_pairs={{0,8},{1,9},{2,10},{3,11},{4,12},{5,13},{6,14},{7,15},{8,0},{9,1},... | collective-permute-start | bytes 344072 | tf_op jit(solution)/shard_map/spectrum_edges/ppermute | solution.py:40
  5.5 0.0 collective-permute-start.2
  5.5 3.0 %collective-permute-start.3 = (bf16[16,1152]{1,0:T(8,128)(2,1)S(1)}, bf16[16,1152]{1,0:T(8,128)(2,1)S(1)}, u32[]{:S(2)}, u32[]{:S(2)}) collective-permute-start(bf16[16,1152]{1,0:T(8,128)(2,1)S(1)} %get-tuple-element.59), channel_id=1, source_target_pairs={{0,1},{1,0},{2,3},{3,2},{4,5},{5,4},{6,7},{7,6},{8,9},{9,8},{10,11... | collective-permute-start | bytes 110600 | tf_op jit(solution)/shard_map/spectrum_edges/ppermute | solution.py:40
  8.5 0.0 copy-done
  8.5 1.5 %prepare_own.1 = (f32[32,64,128]{2,1,0:T(8,128)S(1)}, f32[28,64,128]{2,1,0:T(8,128)S(1)}, bf16[32,48,128]{2,1,0:T(8,128)(2,1)S(1)}, f32[5,16,128]{2,1,0:T(8,128)...) custom-call(f32[32,64,128]{2,1,0:T(8,128)S(1)} %copy-done, ...), custom_call_target="tpu_custom_call" | custom-call | tf_op jit(solution)/shard_map/prepare_own/prepare_own/pallas_call | solution.py:690
  10.0 0.0 collective-permute-done.ob.xb
  10.1 0.0 collective-permute-done.1.oa.xa
  10.1 0.0 collective-permute-done.2.yb
  10.1 0.3 %collective-permute-done.3.ya = bf16[16,1152]{1,0:T(8,128)(2,1)S(1)} collective-permute-done((bf16[16,1152]{1,0:T(8,128)(2,1)S(1)}, bf16[16,1152]{1,0:T(8,128)(2,1)S(1)}, u32[]{:S(2)}, u32[]{:S(2)}) %collective-permute-start.3) | collective-permute-done | bytes 36896 | tf_op jit(solution)/shard_map/spectrum_edges/ppermute | solution.py:40
  10.4 0.5 %wave_ends.1 = (bf16[6,16,1152]{2,1,0:T(8,128)(2,1)S(1)}, bf16[6,16,128]{2,1,0:T(8,128)(2,1)S(1)}, bf16[3,16,128]{2,1,0:T(8,128)(2,1)S(1)}, bf16[3,16,128]{2,1,0:T(8,128)(2,1)S(1)}) custom-call(bf16[16,16,1152]{2,1,0:T(8,128)(2,1)S(1)} %get-tuple-element.57.spec, bf16[2,16,1152]{2,1,0:T(8,128)(2,1)S(1)} %sides.1, ...), custom_call_target="tpu_custom_call" | custom-call | tf_op jit(solution)/shard_map/wave/wave_ends/pallas_call | solution.py:690
  10.9 0.2 collective-permute-start.4
  11.1 0.5 %collective-permute-start.5 = (bf16[3,16,128]{2,1,0:T(8,128)(2,1)S(1)}, bf16[3,16,128]{2,1,0:T(8,128)(2,1)S(1)}, u32[]{:S(2)}, u32[]{:S(2)}) collective-permute-start(bf16[3,16,128]{2,1,0:T(8,128)(2,1)S(1)} %get-tuple-element.67), channel_id=1, source_target_pairs={{0,8},{1,9},{2,10},{3,11},{4,12},{5,13},{6,14},{7,15},{8,0},{9,1},... | collective-permute-start | bytes 36872 | tf_op jit(solution)/shard_map/wave/ppermute | solution.py:40
  11.6 0.7 %wave_rest.1 = (bf16[10,16,1152]{2,1,0:T(8,128)(2,1)S(1)}, bf16[10,16,128]{2,1,0:T(8,128)(2,1)S(1)}) custom-call(bf16[16,16,1152]{2,1,0:T(8,128)(2,1)S(1)} %get-tuple-element.57.spec, bf16[16,1152]{1,0:T(8,128)(2,1)S(1)} %collective-permute-done.2.yb, bf16[16,1152]{1,0:T(8,128)(2,1)S(1)} %collective-permute-done.3.ya, ...), custom_call_target="tpu_custom_call" | custom-call | tf_op jit(solution)/shard_map/wave/wave_rest/pallas_call | solution.py:690
  12.3 0.4 %prepare_ends.1 = (f32[10,64,128]{2,1,0:T(8,128)S(1)}, f32[6,64,128]{2,1,0:T(8,128)S(1)}, f32[10,64,128]{2,1,0:T(8,128)S(1)}, bf16[6,48,128]{2,1,0:T(8,128)(2,1)S(1)}, f32[5,16,128]{2,1,0:T(8,128)S(1)}) custom-call(f32[32,64,128]{2,1,0:T(8,128)S(1)} %copy-done, bf16[448,128]{1,0:T(8,128)(2,1)S(1)} %collective-permute-done.ob.xb, ...), custom_call_target="tpu_custom_call" | custom-call | tf_op jit(solution)/shard_map/prepare_ends/prepare_ends/pallas_call | solution.py:690
  12.7 1.4 %collective-permute-done.4.pb = bf16[3,16,128]{2,1,0:T(8,128)(2,1)S(1)} collective-permute-done((bf16[3,16,128]{2,1,0:T(8,128)(2,1)S(1)}, bf16[3,16,128]{2,1,0:T(8,128)(2,1)S(1)}, u32[]{:S(2)}, u32[]{:S(2)}) %collective-permute-start.4) | collective-permute-done | bytes 12320 | tf_op jit(solution)/shard_map/wave/ppermute | solution.py:40
  14.1 0.0 collective-permute-done.5.pa
  14.1 0.3 %halo.1 = (bf16[256,128]{1,0:T(8,128)(2,1)S(1)}, bf16[256,128]{1,0:T(8,128)(2,1)S(1)}) custom-call(f32[32,64,128]{2,1,0:T(8,128)S(1)} %copy-done, f32[10,64,128]{2,1,0:T(8,128)S(1)} %get-tuple-element.51.vel_halo, bf16[448,128]{1,0:T(8,128)(2,1)S(1)} %collective-permute-done.ob.xb, bf16[448,128]{1,0:T(8,128)(2,1)S(1)} %collective-permute-done.1.oa.xa, ...), custom_call_target="tpu_custom_call" | custom-call | tf_op jit(solution)/shard_map/halo/halo/pallas_call | solution.py:690
  14.4 0.1 collective-permute-start.6
  14.5 3.4 %collective-permute-start.7 = (bf16[256,128]{1,0:T(8,128)(2,1)S(1)}, bf16[256,128]{1,0:T(8,128)(2,1)S(1)}, u32[]{:S(2)}, u32[]{:S(2)}) collective-permute-start(bf16[256,128]{1,0:T(8,128)(2,1)S(1)} %get-tuple-element.72), channel_id=1, source_target_pairs={{0,1},{1,0},{2,3},{3,2},{4,5},{5,4},{6,7},{7,6},{8,9},{9,8},{10,11... | collective-permute-start | bytes 196616 | tf_op jit(solution)/shard_map/halo/ppermute | solution.py:40
  17.9 2.1 %inner.1 = (f32[32,64,128]{2,1,0:T(8,128)S(1)}, bf16[16,16,1152]{2,1,0:T(8,128)(2,1)}, f32[38,2,16,128]{3,2,1,0:T(8,128)S(1)}, f32[38,2,8,128]{3,2,1,0:T(8,128)S...) custom-call(f32[32,64,128]{2,1,0:T(8,128)S(1)} %copy-done, ...), custom_call_target="tpu_custom_call" | custom-call | tf_op jit(solution)/shard_map/inner/inner/pallas_call | solution.py:690
  20.0 0.0 collective-permute-done.6.yb
  20.0 0.2 collective-permute-done.7.ya
  20.1 2.4 %rim.1 = (f32[32,64,128]{2,1,0:T(8,128)}, f32[2,16,16]{2,1,0:T(8,128)}) custom-call(f32[32,64,128]{2,1,0:T(8,128)S(1)} %copy-done, f32[10,64,128]{2,1,0:T(8,128)S(1)} %get-tuple-element.51.vel_halo, bf16[256,128]{1,0:T(8,128)(2,1)S(1)} %collective-permute-done.6.yb, bf16[256,128]{1,0:T(8,128)(2,1)S(1)} %collective-permute-done.7.ya, ...), custom_call_target="tpu_custom_call" | custom-call | tf_op jit(solution)/shard_map/rim/rim/pallas_call | solution.py:690
  (1 shorter events, 0.0 us)
Async XLA Ops:
  0.6 7.9 %copy-start = (f32[32,64,128]{2,1,0:T(8,128)S(1)}, f32[32,64,128]{2,1,0:T(8,128)}, u32[]{:S(2)}) copy-start(f32[32,64,128]{2,1,0:T(8,128)} %own.5) | copy-start | bytes 3145732
  2.3 7.7 %collective-permute-start = (bf16[448,128]{1,0:T(8,128)(2,1)S(1)}, bf16[448,128]{1,0:T(8,128)(2,1)S(1)}, u32[]{:S(2)}, u32[]{:S(2)}) collective-permute-start(bf16[448,128]{1,0:T(8,128)(2,1)S(1)} %get-tuple-element.44), channel_id=1, source_target_pairs={{0,24},{1,25},{2,26},{3,27},{4,28},{5,29},{6,30},{7,31},{8,16},{9,... | collective-permute-start | bytes 344072 | tf_op jit(solution)/shard_map/spectrum_edges/ppermute | solution.py:40
  4.8 5.3 %collective-permute-start.1 = (bf16[448,128]{1,0:T(8,128)(2,1)S(1)}, bf16[448,128]{1,0:T(8,128)(2,1)S(1)}, u32[]{:S(2)}, u32[]{:S(2)}) collective-permute-start(bf16[448,128]{1,0:T(8,128)(2,1)S(1)} %get-tuple-element.45), channel_id=1, source_target_pairs={{0,8},{1,9},{2,10},{3,11},{4,12},{5,13},{6,14},{7,15},{8,0},{9,1},... | collective-permute-start | bytes 344072 | tf_op jit(solution)/shard_map/spectrum_edges/ppermute | solution.py:40
  5.5 4.6 %collective-permute-start.2 = (bf16[16,1152]{1,0:T(8,128)(2,1)S(1)}, bf16[16,1152]{1,0:T(8,128)(2,1)S(1)}, u32[]{:S(2)}, u32[]{:S(2)}) collective-permute-start(bf16[16,1152]{1,0:T(8,128)(2,1)S(1)} %get-tuple-element.58), channel_id=1, source_target_pairs={{0,8},{1,2},{2,1},{3,4},{4,3},{5,6},{6,5},{7,15},{8,0},{9,10},{10,... | collective-permute-start | bytes 110600 | tf_op jit(solution)/shard_map/spectrum_edges/ppermute | solution.py:40
  5.5 5.0 %collective-permute-start.3 = (bf16[16,1152]{1,0:T(8,128)(2,1)S(1)}, bf16[16,1152]{1,0:T(8,128)(2,1)S(1)}, u32[]{:S(2)}, u32[]{:S(2)}) collective-permute-start(bf16[16,1152]{1,0:T(8,128)(2,1)S(1)} %get-tuple-element.59), channel_id=1, source_target_pairs={{0,1},{1,0},{2,3},{3,2},{4,5},{5,4},{6,7},{7,6},{8,9},{9,8},{10,11... | collective-permute-start | bytes 110600 | tf_op jit(solution)/shard_map/spectrum_edges/ppermute | solution.py:40
  10.9 3.2 %collective-permute-start.4 = (bf16[3,16,128]{2,1,0:T(8,128)(2,1)S(1)}, bf16[3,16,128]{2,1,0:T(8,128)(2,1)S(1)}, u32[]{:S(2)}, u32[]{:S(2)}) collective-permute-start(bf16[3,16,128]{2,1,0:T(8,128)(2,1)S(1)} %get-tuple-element.66), channel_id=1, source_target_pairs={{0,24},{1,25},{2,26},{3,27},{4,28},{5,29},{6,30},{7,31},{8,16},{9,... | collective-permute-start | bytes 36872 | tf_op jit(solution)/shard_map/wave/ppermute | solution.py:40
  11.1 3.0 %collective-permute-start.5 = (bf16[3,16,128]{2,1,0:T(8,128)(2,1)S(1)}, bf16[3,16,128]{2,1,0:T(8,128)(2,1)S(1)}, u32[]{:S(2)}, u32[]{:S(2)}) collective-permute-start(bf16[3,16,128]{2,1,0:T(8,128)(2,1)S(1)} %get-tuple-element.67), channel_id=1, source_target_pairs={{0,8},{1,9},{2,10},{3,11},{4,12},{5,13},{6,14},{7,15},{8,0},{9,1},... | collective-permute-start | bytes 36872 | tf_op jit(solution)/shard_map/wave/ppermute | solution.py:40
  14.4 5.6 %collective-permute-start.6 = (bf16[256,128]{1,0:T(8,128)(2,1)S(1)}, bf16[256,128]{1,0:T(8,128)(2,1)S(1)}, u32[]{:S(2)}, u32[]{:S(2)}) collective-permute-start(bf16[256,128]{1,0:T(8,128)(2,1)S(1)} %get-tuple-element.71), channel_id=1, source_target_pairs={{0,8},{1,2},{2,1},{3,4},{4,3},{5,6},{6,5},{7,15},{8,0},{9,10},{10,... | collective-permute-start | bytes 196616 | tf_op jit(solution)/shard_map/halo/ppermute | solution.py:40
  14.5 5.7 %collective-permute-start.7 = (bf16[256,128]{1,0:T(8,128)(2,1)S(1)}, bf16[256,128]{1,0:T(8,128)(2,1)S(1)}, u32[]{:S(2)}, u32[]{:S(2)}) collective-permute-start(bf16[256,128]{1,0:T(8,128)(2,1)S(1)} %get-tuple-element.72), channel_id=1, source_target_pairs={{0,1},{1,0},{2,3},{3,2},{4,5},{5,4},{6,7},{7,6},{8,9},{9,8},{10,11... | collective-permute-start | bytes 196616 | tf_op jit(solution)/shard_map/halo/ppermute | solution.py:40

commit v7 on v6

--- a/solution.py
+++ b/solution.py
@@ -186,7 +186,7 @@
         sides[0, :, part], sides[1, :, part] = pick(even_x, b, a).astype(BF), pick(even_x, a, b).astype(BF)
 
 
-def wave_ends_kernel(spec, sides, yb, ya, courant, source, land, weights, out, profile, pa, pb):
+def wave_ends_kernel(spec, sides, ya, yb, courant, source, land, weights, out, profile, pa, pb):
     rows, cols, bins = spec.shape
     even_x = is_even("gx")
     parts = []
@@ -204,7 +204,7 @@
         pb[i] = jnp.where(even_x, first, last).astype(BF)
 
 
-def wave_rest_kernel(spec, yb, ya, courant, source, land, weights, ends, out, profile):
+def wave_rest_kernel(spec, ya, yb, courant, source, land, weights, ends, out, profile):
     rows = spec.shape[0]
 
     def put(x, value, part):
@@ -227,28 +227,16 @@
     return own[i] if 0 <= i < rows else ends[i + reach if i < 0 else i - rows + reach]
 
 
-def halo_kernel(vel, vel_halo, ob, oa, lists, ends, rest, pb, pa, ya, yb):
+def pack_rows(vel, vel_halo, ob, oa, lists, ya, yb):
     rows, cols, lanes = vel.shape
     vrow = rows + 2 * HV
+    slots = 0
     even_x, even_y = is_even("gx"), is_even("gy")
-    wr, wc = rest.shape[0] + 2 * HX, rest.shape[1]
 
     def put(at, last, first):
         n = last.shape[0]
         ya[at : at + n] = jnp.where(even_y, last, first).astype(BF)
         yb[at : at + n] = jnp.where(even_y, first, last).astype(BF)
-
-    before, after = pick(even_x, pb[...], pa[...]), pick(even_x, pa[...], pb[...])
-    joined = jnp.concatenate([before.astype(BF), ends[0:HX], rest[...], ends[HX:], after.astype(BF)], axis=0)
-    count = (wr + 2 * HX) * wc
-    slots = TALL * HY
-    at, cell = iota((2 * slots, count), 0), iota((2 * slots, count), 1)
-    side, rest = at // slots, at % slots
-    column = rest // TALL + jnp.where(side == 0, wc - HY, 0)
-    row = rest % TALL
-    chosen = ((row < wr + 2 * HX) & (cell == row * wc + column)).astype(F32).astype(BF)
-    sides = jnp.dot(chosen, joined.reshape(count, lanes), preferred_element_type=F32)
-    put(0, sides[0:slots], sides[slots:])
 
     sub = iota((EDGE, 1), 0)
     is_u = iota((1, lanes), 1) < lanes // 2
@@ -302,6 +290,30 @@
         put(start + tile * 16, acc[tile][0], acc[tile][1])
 
 
+def halo_kernel(fixed_a, fixed_b, ends, rest, pb, pa, ya, yb):
+    lanes = rest.shape[2]
+    even_x, even_y = is_even("gx"), is_even("gy")
+    wr, wc = rest.shape[0] + 2 * HX, rest.shape[1]
+
+    def put(at, last, first):
+        n = last.shape[0]
+        ya[at : at + n] = jnp.where(even_y, last, first).astype(BF)
+        yb[at : at + n] = jnp.where(even_y, first, last).astype(BF)
+
+    before, after = pick(even_x, pb[...], pa[...]), pick(even_x, pa[...], pb[...])
+    joined = jnp.concatenate([before.astype(BF), ends[0:HX], rest[...], ends[HX:], after.astype(BF)], axis=0)
+    count = (wr + 2 * HX) * wc
+    slots = TALL * HY
+    at, cell = iota((2 * slots, count), 0), iota((2 * slots, count), 1)
+    side, rest = at // slots, at % slots
+    column = rest // TALL + jnp.where(side == 0, wc - HY, 0)
+    row = rest % TALL
+    chosen = ((row < wr + 2 * HX) & (cell == row * wc + column)).astype(F32).astype(BF)
+    sides = jnp.dot(chosen, joined.reshape(count, lanes), preferred_element_type=F32)
+    put(0, sides[0:slots], sides[slots:])
+    ya[slots:], yb[slots:] = fixed_a[...], fixed_b[...]
+
+
 def vorticity(ref, r, base, count):
     half = ref.shape[-1] // 2
     is_u = iota((1, 2 * half), 1) < half
@@ -413,7 +425,9 @@
         )
 
 
-def prepare_ends_kernel(own, ob, oa, spin_own, list_own, vel_halo, spin, turn, table, list_rim, vel):
+def prepare_ends_kernel(
+    own, ob, oa, lists, spin_own, list_own, vel_halo, spin, turn, table, list_rim, fixed_a, fixed_b, vel
+):
     rows, cols, lanes = own.shape
     per = lanes // 16
     even_x = is_even("gx")
@@ -445,6 +459,7 @@
         for k in range(HL + 2):
             i = k + (rows - 2 if side else -HL)
             turn[side * (HL + 2) + k] = row_of(i, rows, spin_own, spin, HL) + vorticity(vel.at[side], k + 2, EDGE, cols)
+    pack_rows(own, vel_halo, ob, oa, lists, fixed_a, fixed_b)
 
 
 def inner_kernel(
@@ -538,7 +553,7 @@
 
 
 def rim_kernel(
-    own, vel_halo, yb, ya, mid_rim, drift_rim, spin_rim, total, list_rim, prof_rim, wave_shares, chosen, spread, inner,
+    own, vel_halo, ya, yb, mid_rim, drift_rim, spin_rim, total, list_rim, prof_rim, wave_shares, chosen, spread, inner,
     out, current,
     vel, mid, prof, drift, spin, picked, means, strips, sems,
 ):
@@ -635,21 +650,26 @@
             mid[side, r, base : base + EDGE, :] = new
 
     average = averager(lanes)
-    acc = jnp.zeros((4 * EDGE, lanes), F32)
+    acc = jnp.zeros((2 * EDGE, lanes), F32)
     step = rows // PARTS
+    begins = (EDGE - 1, EDGE + 1)
     for n in range(rows + 2):
         r = n + HL - 1
         both = []
-        for side in range(2):
-            turns, drifts = (spin[side, r], spin_rim[r, side]), (drift[side, r], drift_rim[r, side])
+        for side, begin in enumerate(begins):
             order = 1 - 2 * side
-            absolute = jnp.concatenate(turns[::order], axis=0) + vorticity(mid.at[side], r, RIM, 2 * EDGE)
-            tile = slice(RIM, RIM + 2 * EDGE)
-            old = vel[side, r + lift, tile, :] + mid[side, r, tile, :]
-            new = 0.5 * old + (0.5 * STEP) * (absolute * jnp.concatenate(drifts[::order], axis=0))
+
+            def joined(here, there):
+                return jnp.concatenate([here, there][::order], axis=0)[begin - RIM : begin - RIM + EDGE]
+
+            absolute = joined(spin[side, r], spin_rim[r, side]) + vorticity(mid.at[side], r, begin, EDGE)
+            old = vel[side, r + lift, begin : begin + EDGE, :] + mid[side, r, begin : begin + EDGE, :]
+            new = 0.5 * old + (0.5 * STEP) * (absolute * joined(drift[side, r], drift_rim[r, side]))
             both.append(new)
             if 1 <= n <= rows:
-                strips[side, n - 1] = new[RIM : RIM + EDGE]
+                kept = inner[n - 1, side * (cols - EDGE) : side * (cols - EDGE) + EDGE, :]
+                moved = pltpu.roll(new, EDGE - 1 if side == 0 else 1, 0)
+                strips[side, n - 1] = jnp.where(sub == (EDGE - 1 if side == 0 else 0), kept, moved)
         sums = jnp.dot(
             jnp.concatenate(split(jnp.concatenate(both, axis=0)), axis=1), average, preferred_element_type=F32
         )
@@ -660,9 +680,12 @@
                 one, two = strips.at[side, part], out.at[part, pl.ds(at, EDGE), :]
                 copies.append(pltpu.make_async_copy(one, two, sems.at[len(copies)]))
                 copies[-1].start()
-    means[0 : 2 * EDGE] = acc[0 : 2 * EDGE]
-    means[2 * EDGE : 2 * RIM + cols - 2 * EDGE] = total[2 * EDGE - RIM : cols - 2 * EDGE + RIM, :]
-    means[2 * RIM + cols - 2 * EDGE :] = acc[2 * EDGE :]
+    count = cols + 2 * RIM
+    means[0:EDGE] = blank
+    means[count - EDGE :] = blank
+    means[RIM - 1 : RIM - 1 + EDGE] = acc[0:EDGE]
+    means[RIM - 1 + EDGE : count - RIM + 1 - EDGE] = total[EDGE - 1 : cols - EDGE + 1, :]
+    means[count - RIM + 1 - EDGE : count - RIM + 1] = acc[EDGE:]
 
     named = chosen[...].astype(BF)
     picked[...] = sum(
@@ -748,31 +771,32 @@
         cells_ends, ends, pa, pb = call(
             wave_ends_kernel, "wave_ends",
             [((2 * HX, wc, bins), BF), ((2 * HX, wc, lanes), BF), (edge, BF), (edge, BF)],
-            spectrum, sides, yb, ya, courant, source, land, stokes_kernel,
+            spectrum, sides, ya, yb, courant, source, land, stokes_kernel,
         )
         pa, pb = exchange("gx", pa, pb)
         cells_rest, rest = call(
             wave_rest_kernel, "wave_rest",
             [((wr - 2 * HX, wc, bins), BF), ((wr - 2 * HX, wc, lanes), BF)],
-            spectrum, yb, ya, courant, source, land, stokes_kernel, ends,
+            spectrum, ya, yb, courant, source, land, stokes_kernel, ends,
         )
 
     with jax.named_scope("prepare_ends"):
-        vel_halo, spin_ends, turn_ends, table_ends, list_rim = call(
+        size = y_rows(rows)[1] + (list_place(listed - 1, lanes)[0] + 1) * 16
+        vel_halo, spin_ends, turn_ends, table_ends, list_rim, fixed_a, fixed_b = call(
             prepare_ends_kernel, "prepare_ends",
             [
                 ((2 * HV, *level), F32), ((2 * HL, *level), F32), ((2 * HL + 4, *level), F32),
                 ((2 * HL, 3 * wc, lanes), BF), ((groups, 16, lanes), F32),
+                ((size, lanes), BF), ((size, lanes), BF),
             ],
-            velocity, ob, oa, spin_own, list_own,
+            velocity, ob, oa, lists, spin_own, list_own,
             scratch=[pltpu.VMEM((2, 2 * HV - 1, cols + 2 * EDGE, lanes), F32)],
         )
 
     with jax.named_scope("halo"):
-        size = sum(y_rows(rows)) + (list_place(listed - 1, lanes)[0] + 1) * 16
+        size += y_rows(rows)[0]
         ya, yb = call(
-            halo_kernel, "halo", [((size, lanes), BF)] * 2,
-            velocity, vel_halo, ob, oa, lists, ends, rest, pb, pa,
+            halo_kernel, "halo", [((size, lanes), BF)] * 2, fixed_a, fixed_b, ends, rest, pb, pa
         )
         ya, yb = exchange("gy", ya, yb)
 
@@ -814,7 +838,7 @@
         ]
         new_velocity, current = call(
             rim_kernel, "rim", [(velocity.shape, F32), ((2, wr, wc), F32)],
-            velocity, vel_halo, yb, ya, mid_rim, drift_rim, spin_rim, total, list_rim, prof_rim, wave_shares, chosen, spread,
+            velocity, vel_halo, ya, yb, mid_rim, drift_rim, spin_rim, total, list_rim, prof_rim, wave_shares, chosen, spread,
             result, scratch=scratch, any_out=(0,),
         )
     return new_spectrum, new_velocity, current

time: 22.7 us -> 22.4 us (0.987)
  the two profiles are of different devices: /device:TPU:0 before, /device:TPU:8 now
where the time goes in v7:
time: 22.4 us; the launch traced here: 22.3 us
  Pallas kernels  9.41 us (42%)
  waiting for transfers between devices  7.29 us (33%)
  starting transfers between devices  4.86 us (22%)
  between operations  0.71 us (3%)
    pallas_call x9, Pallas kernels, call(): pl.pallas_call(kernel, out_shape=tuple((jax.ShapeDtypeStruct(shape, dtype...  9.41 us
    ppermute x8, waiting for transfers between devices, swap(): return lax.ppermute(value, ('gx', 'gy'), pairs)  7.29 us
    ppermute x8, starting transfers between devices, swap(): return lax.ppermute(value, ('gx', 'gy'), pairs)  4.86 us
  transfers between devices with their start and end apart: 8, of which 6 were waited for; matrix products, arithmetic and copies ran while one was open for 0% of the time, Pallas kernels for 21%

profile of v7, /device:TPU:8, one launch (start us, length us, event | category | flops | bytes accessed | tf_op | source)
XLA Modules:
  0.0 22.3 jit_solution(2483831251941050725)
XLA Ops:
  0.6 0.0 copy-start
  0.6 1.7 %edges.1 = (bf16[448,128]{1,0:T(8,128)(2,1)S(1)}, bf16[448,128]{1,0:T(8,128)(2,1)S(1)}, bf16[16,1152]{1,0:T(8,128)(2,1)S(1)}, bf16[16,1152]{1,0:T(8,128)(2,1)S(1...) custom-call(bf16[16,16,1152]{2,1,0:T(8,128)(2,1)} %refs_0_.1, ...), custom_call_target="tpu_custom_call" | custom-call | tf_op jit(solution)/shard_map/spectrum_edges/edges/pallas_call | solution.py:713
  2.3 1.0 %collective-permute-start = (bf16[448,128]{1,0:T(8,128)(2,1)S(1)}, bf16[448,128]{1,0:T(8,128)(2,1)S(1)}, u32[]{:S(2)}, u32[]{:S(2)}) collective-permute-start(bf16[448,128]{1,0:T(8,128)(2,1)S(1)} %get-tuple-element.46), channel_id=1, source_target_pairs={{0,24},{1,25},{2,26},{3,27},{4,28},{5,29},{6,30},{7,31},{8,16},{9,... | collective-permute-start | bytes 344072 | tf_op jit(solution)/shard_map/spectrum_edges/ppermute | solution.py:40
  3.3 0.7 %collective-permute-start.1 = (bf16[448,128]{1,0:T(8,128)(2,1)S(1)}, bf16[448,128]{1,0:T(8,128)(2,1)S(1)}, u32[]{:S(2)}, u32[]{:S(2)}) collective-permute-start(bf16[448,128]{1,0:T(8,128)(2,1)S(1)} %get-tuple-element.47), channel_id=1, source_target_pairs={{0,8},{1,9},{2,10},{3,11},{4,12},{5,13},{6,14},{7,15},{8,0},{9,1},... | collective-permute-start | bytes 344072 | tf_op jit(solution)/shard_map/spectrum_edges/ppermute | solution.py:40
  4.0 1.5 %collective-permute-start.2 = (bf16[16,1152]{1,0:T(8,128)(2,1)S(1)}, bf16[16,1152]{1,0:T(8,128)(2,1)S(1)}, u32[]{:S(2)}, u32[]{:S(2)}) collective-permute-start(bf16[16,1152]{1,0:T(8,128)(2,1)S(1)} %get-tuple-element.60), channel_id=1, source_target_pairs={{0,1},{1,0},{2,3},{3,2},{4,5},{5,4},{6,7},{7,6},{8,9},{9,8},{10,11... | collective-permute-start | bytes 110600 | tf_op jit(solution)/shard_map/spectrum_edges/ppermute | solution.py:40
  5.5 0.4 %collective-permute-start.3 = (bf16[16,1152]{1,0:T(8,128)(2,1)S(1)}, bf16[16,1152]{1,0:T(8,128)(2,1)S(1)}, u32[]{:S(2)}, u32[]{:S(2)}) collective-permute-start(bf16[16,1152]{1,0:T(8,128)(2,1)S(1)} %get-tuple-element.61), channel_id=1, source_target_pairs={{0,8},{1,2},{2,1},{3,4},{4,3},{5,6},{6,5},{7,15},{8,0},{9,10},{10,... | collective-permute-start | bytes 110600 | tf_op jit(solution)/shard_map/spectrum_edges/ppermute | solution.py:40
  5.9 0.0 copy-done
  5.9 1.5 %prepare_own.1 = (f32[32,64,128]{2,1,0:T(8,128)S(1)}, f32[28,64,128]{2,1,0:T(8,128)S(1)}, bf16[32,48,128]{2,1,0:T(8,128)(2,1)S(1)}, f32[5,16,128]{2,1,0:T(8,128)...) custom-call(f32[32,64,128]{2,1,0:T(8,128)S(1)} %copy-done, ...), custom_call_target="tpu_custom_call" | custom-call | tf_op jit(solution)/shard_map/prepare_own/prepare_own/pallas_call | solution.py:713
  7.5 0.3 %collective-permute-done.ob.xb = bf16[448,128]{1,0:T(8,128)(2,1)S(1)} collective-permute-done((bf16[448,128]{1,0:T(8,128)(2,1)S(1)}, bf16[448,128]{1,0:T(8,128)(2,1)S(1)}, u32[]{:S(2)}, u32[]{:S(2)}) %collective-permute-start) | collective-permute-done | bytes 114720 | tf_op jit(solution)/shard_map/spectrum_edges/ppermute | solution.py:40
  7.8 0.0 collective-permute-done.1.oa.xa
  7.8 0.1 collective-permute-done.2.ya
  8.0 2.4 %collective-permute-done.3.yb = bf16[16,1152]{1,0:T(8,128)(2,1)S(1)} collective-permute-done((bf16[16,1152]{1,0:T(8,128)(2,1)S(1)}, bf16[16,1152]{1,0:T(8,128)(2,1)S(1)}, u32[]{:S(2)}, u32[]{:S(2)}) %collective-permute-start.3) | collective-permute-done | bytes 36896 | tf_op jit(solution)/shard_map/spectrum_edges/ppermute | solution.py:40
  10.4 0.5 %wave_ends.1 = (bf16[6,16,1152]{2,1,0:T(8,128)(2,1)S(1)}, bf16[6,16,128]{2,1,0:T(8,128)(2,1)S(1)}, bf16[3,16,128]{2,1,0:T(8,128)(2,1)S(1)}, bf16[3,16,128]{2,1,0:T(8,128)(2,1)S(1)}) custom-call(bf16[16,16,1152]{2,1,0:T(8,128)(2,1)S(1)} %get-tuple-element.59.spec, bf16[2,16,1152]{2,1,0:T(8,128)(2,1)S(1)} %sides.1, ...), custom_call_target="tpu_custom_call" | custom-call | tf_op jit(solution)/shard_map/wave/wave_ends/pallas_call | solution.py:713
  10.9 0.1 collective-permute-start.4
  11.0 0.6 %collective-permute-start.5 = (bf16[3,16,128]{2,1,0:T(8,128)(2,1)S(1)}, bf16[3,16,128]{2,1,0:T(8,128)(2,1)S(1)}, u32[]{:S(2)}, u32[]{:S(2)}) collective-permute-start(bf16[3,16,128]{2,1,0:T(8,128)(2,1)S(1)} %get-tuple-element.69), channel_id=1, source_target_pairs={{0,8},{1,9},{2,10},{3,11},{4,12},{5,13},{6,14},{7,15},{8,0},{9,1},... | collective-permute-start | bytes 36872 | tf_op jit(solution)/shard_map/wave/ppermute | solution.py:40
  11.6 0.7 %wave_rest.1 = (bf16[10,16,1152]{2,1,0:T(8,128)(2,1)S(1)}, bf16[10,16,128]{2,1,0:T(8,128)(2,1)S(1)}) custom-call(bf16[16,16,1152]{2,1,0:T(8,128)(2,1)S(1)} %get-tuple-element.59.spec, bf16[16,1152]{1,0:T(8,128)(2,1)S(1)} %collective-permute-done.2.ya, bf16[16,1152]{1,0:T(8,128)(2,1)S(1)} %collective-permute-done.3.yb, ...), custom_call_target="tpu_custom_call" | custom-call | tf_op jit(solution)/shard_map/wave/wave_rest/pallas_call | solution.py:713
  12.3 0.5 %prepare_ends.1 = (f32[10,64,128]{2,1,0:T(8,128)S(1)}, f32[6,64,128]{2,1,0:T(8,128)S(1)}, f32[10,64,128]{2,1,0:T(8,128)S(1)}, bf16[6,48,128]{2,1,0:T(8,128)(2,1)...) custom-call(f32[32,64,128]{2,1,0:T(8,128)S(1)} %copy-done, ...), custom_call_target="tpu_custom_call" | custom-call | tf_op jit(solution)/shard_map/prepare_ends/prepare_ends/pallas_call | solution.py:713
  12.8 1.3 %collective-permute-done.4.pb = bf16[3,16,128]{2,1,0:T(8,128)(2,1)S(1)} collective-permute-done((bf16[3,16,128]{2,1,0:T(8,128)(2,1)S(1)}, bf16[3,16,128]{2,1,0:T(8,128)(2,1)S(1)}, u32[]{:S(2)}, u32[]{:S(2)}) %collective-permute-start.4) | collective-permute-done | bytes 12320 | tf_op jit(solution)/shard_map/wave/ppermute | solution.py:40
  14.1 0.0 collective-permute-done.5.pa
  14.1 0.2 halo.1
  14.3 0.6 %collective-permute-start.6 = (bf16[256,128]{1,0:T(8,128)(2,1)S(1)}, bf16[256,128]{1,0:T(8,128)(2,1)S(1)}, u32[]{:S(2)}, u32[]{:S(2)}) collective-permute-start(bf16[256,128]{1,0:T(8,128)(2,1)S(1)} %get-tuple-element.75), channel_id=1, source_target_pairs={{0,1},{1,0},{2,3},{3,2},{4,5},{5,4},{6,7},{7,6},{8,9},{9,8},{10,11... | collective-permute-start | bytes 196616 | tf_op jit(solution)/shard_map/halo/ppermute | solution.py:40
  14.8 0.0 collective-permute-start.7
  14.8 2.0 %inner.1 = (f32[32,64,128]{2,1,0:T(8,128)S(1)}, bf16[16,16,1152]{2,1,0:T(8,128)(2,1)}, f32[38,2,16,128]{3,2,1,0:T(8,128)S(1)}, f32[38,2,8,128]{3,2,1,0:T(8,128)S...) custom-call(f32[32,64,128]{2,1,0:T(8,128)S(1)} %copy-done, ...), custom_call_target="tpu_custom_call" | custom-call | tf_op jit(solution)/shard_map/inner/inner/pallas_call | solution.py:713
  16.9 1.7 %collective-permute-done.6.ya = bf16[256,128]{1,0:T(8,128)(2,1)S(1)} collective-permute-done((bf16[256,128]{1,0:T(8,128)(2,1)S(1)}, bf16[256,128]{1,0:T(8,128)(2,1)S(1)}, u32[]{:S(2)}, u32[]{:S(2)}) %collective-permute-start.6) | collective-permute-done | bytes 65568 | tf_op jit(solution)/shard_map/halo/ppermute | solution.py:40
  18.6 1.4 %collective-permute-done.7.yb = bf16[256,128]{1,0:T(8,128)(2,1)S(1)} collective-permute-done((bf16[256,128]{1,0:T(8,128)(2,1)S(1)}, bf16[256,128]{1,0:T(8,128)(2,1)S(1)}, u32[]{:S(2)}, u32[]{:S(2)}) %collective-permute-start.7) | collective-permute-done | bytes 65568 | tf_op jit(solution)/shard_map/halo/ppermute | solution.py:40
  20.0 2.3 %rim.1 = (f32[32,64,128]{2,1,0:T(8,128)}, f32[2,16,16]{2,1,0:T(8,128)}) custom-call(f32[32,64,128]{2,1,0:T(8,128)S(1)} %copy-done, f32[10,64,128]{2,1,0:T(8,128)S(1)} %get-tuple-element.53.vel_halo, bf16[256,128]{1,0:T(8,128)(2,1)S(1)} %collective-permute-done.6.ya, bf16[256,128]{1,0:T(8,128)(2,1)S(1)} %collective-permute-done.7.yb, ...), custom_call_target="tpu_custom_call" | custom-call | tf_op jit(solution)/shard_map/rim/rim/pallas_call | solution.py:713
  (1 shorter events, 0.0 us)
Async XLA Ops:
  0.6 5.3 %copy-start = (f32[32,64,128]{2,1,0:T(8,128)S(1)}, f32[32,64,128]{2,1,0:T(8,128)}, u32[]{:S(2)}) copy-start(f32[32,64,128]{2,1,0:T(8,128)} %own.5) | copy-start | bytes 3145732
  2.3 5.5 %collective-permute-start = (bf16[448,128]{1,0:T(8,128)(2,1)S(1)}, bf16[448,128]{1,0:T(8,128)(2,1)S(1)}, u32[]{:S(2)}, u32[]{:S(2)}) collective-permute-start(bf16[448,128]{1,0:T(8,128)(2,1)S(1)} %get-tuple-element.46), channel_id=1, source_target_pairs={{0,24},{1,25},{2,26},{3,27},{4,28},{5,29},{6,30},{7,31},{8,16},{9,... | collective-permute-start | bytes 344072 | tf_op jit(solution)/shard_map/spectrum_edges/ppermute | solution.py:40
  3.3 4.5 %collective-permute-start.1 = (bf16[448,128]{1,0:T(8,128)(2,1)S(1)}, bf16[448,128]{1,0:T(8,128)(2,1)S(1)}, u32[]{:S(2)}, u32[]{:S(2)}) collective-permute-start(bf16[448,128]{1,0:T(8,128)(2,1)S(1)} %get-tuple-element.47), channel_id=1, source_target_pairs={{0,8},{1,9},{2,10},{3,11},{4,12},{5,13},{6,14},{7,15},{8,0},{9,1},... | collective-permute-start | bytes 344072 | tf_op jit(solution)/shard_map/spectrum_edges/ppermute | solution.py:40
  4.0 4.0 %collective-permute-start.2 = (bf16[16,1152]{1,0:T(8,128)(2,1)S(1)}, bf16[16,1152]{1,0:T(8,128)(2,1)S(1)}, u32[]{:S(2)}, u32[]{:S(2)}) collective-permute-start(bf16[16,1152]{1,0:T(8,128)(2,1)S(1)} %get-tuple-element.60), channel_id=1, source_target_pairs={{0,1},{1,0},{2,3},{3,2},{4,5},{5,4},{6,7},{7,6},{8,9},{9,8},{10,11... | collective-permute-start | bytes 110600 | tf_op jit(solution)/shard_map/spectrum_edges/ppermute | solution.py:40
  5.5 4.9 %collective-permute-start.3 = (bf16[16,1152]{1,0:T(8,128)(2,1)S(1)}, bf16[16,1152]{1,0:T(8,128)(2,1)S(1)}, u32[]{:S(2)}, u32[]{:S(2)}) collective-permute-start(bf16[16,1152]{1,0:T(8,128)(2,1)S(1)} %get-tuple-element.61), channel_id=1, source_target_pairs={{0,8},{1,2},{2,1},{3,4},{4,3},{5,6},{6,5},{7,15},{8,0},{9,10},{10,... | collective-permute-start | bytes 110600 | tf_op jit(solution)/shard_map/spectrum_edges/ppermute | solution.py:40
  10.9 3.2 %collective-permute-start.4 = (bf16[3,16,128]{2,1,0:T(8,128)(2,1)S(1)}, bf16[3,16,128]{2,1,0:T(8,128)(2,1)S(1)}, u32[]{:S(2)}, u32[]{:S(2)}) collective-permute-start(bf16[3,16,128]{2,1,0:T(8,128)(2,1)S(1)} %get-tuple-element.68), channel_id=1, source_target_pairs={{0,24},{1,25},{2,26},{3,27},{4,28},{5,29},{6,30},{7,31},{8,16},{9,... | collective-permute-start | bytes 36872 | tf_op jit(solution)/shard_map/wave/ppermute | solution.py:40
  11.0 3.1 %collective-permute-start.5 = (bf16[3,16,128]{2,1,0:T(8,128)(2,1)S(1)}, bf16[3,16,128]{2,1,0:T(8,128)(2,1)S(1)}, u32[]{:S(2)}, u32[]{:S(2)}) collective-permute-start(bf16[3,16,128]{2,1,0:T(8,128)(2,1)S(1)} %get-tuple-element.69), channel_id=1, source_target_pairs={{0,8},{1,9},{2,10},{3,11},{4,12},{5,13},{6,14},{7,15},{8,0},{9,1},... | collective-permute-start | bytes 36872 | tf_op jit(solution)/shard_map/wave/ppermute | solution.py:40
  14.3 4.3 %collective-permute-start.6 = (bf16[256,128]{1,0:T(8,128)(2,1)S(1)}, bf16[256,128]{1,0:T(8,128)(2,1)S(1)}, u32[]{:S(2)}, u32[]{:S(2)}) collective-permute-start(bf16[256,128]{1,0:T(8,128)(2,1)S(1)} %get-tuple-element.75), channel_id=1, source_target_pairs={{0,1},{1,0},{2,3},{3,2},{4,5},{5,4},{6,7},{7,6},{8,9},{9,8},{10,11... | collective-permute-start | bytes 196616 | tf_op jit(solution)/shard_map/halo/ppermute | solution.py:40
  14.8 5.2 %collective-permute-start.7 = (bf16[256,128]{1,0:T(8,128)(2,1)S(1)}, bf16[256,128]{1,0:T(8,128)(2,1)S(1)}, u32[]{:S(2)}, u32[]{:S(2)}) collective-permute-start(bf16[256,128]{1,0:T(8,128)(2,1)S(1)} %get-tuple-element.76), channel_id=1, source_target_pairs={{0,8},{1,2},{2,1},{3,4},{4,3},{5,6},{6,5},{7,15},{8,0},{9,10},{10,... | collective-permute-start | bytes 196616 | tf_op jit(solution)/shard_map/halo/ppermute | solution.py:40

commit v8 on v7

--- a/solution.py
+++ b/solution.py
@@ -82,17 +82,15 @@
 
 
 def edges_kernel(*refs):
-    (spec_far, courant_far, source_far, land_far, codes_far, weights_far, coriolis_far, vel_far, basis_far) = refs[:9]
-    (wave_codes_far, wave_weights_far) = refs[9:11]
-    (oa, ob, ya, yb, lists, spec, courant, source_t, land_t, basis, wave_codes, wave_weights) = refs[11:23]
-    (source, land, codes, weights, coriolis, vel, sems) = refs[23:]
+    (spec_far, courant_far, source_far, land_far, codes_far, weights_far, coriolis_far, vel_far) = refs[:8]
+    (oa, ob, ya, yb, lists, spec, courant, source_t, land_t) = refs[8:17]
+    (source, land, codes, weights, coriolis, vel, sems) = refs[17:]
     rows, cols, bins = spec.shape
     lanes = vel.shape[-1]
     pairs = [(spec_far, spec)]
     pairs += [(vel_far.at[pl.ds(at, HV)], vel.at[i]) for i, at in ((0, 0), (1, vel_far.shape[0] - HV))]
     pairs += [(codes_far, codes), (weights_far, weights), (coriolis_far, coriolis)]
-    pairs += [(courant_far, courant), (source_far, source), (land_far, land), (basis_far, basis)]
-    pairs += [(wave_codes_far, wave_codes), (wave_weights_far, wave_weights)]
+    pairs += [(courant_far, courant), (source_far, source), (land_far, land)]
     copies = [pltpu.make_async_copy(one, two, sems.at[i]) for i, (one, two) in enumerate(pairs)]
     for copy in copies:
         copy.start()
@@ -334,6 +332,16 @@
     return jnp.where((at % lanes) // half == to % 2, 1.0 / half, 0.0).astype(BF)
 
 
+def add_means(acc, first, values, average):
+    size, lanes = values[0].shape
+    parts = jnp.concatenate([jnp.concatenate(split(v), axis=1) for v in values], axis=0)
+    sums = jnp.dot(parts, average, preferred_element_type=F32)
+    place = iota((1, lanes), 1) // 2
+    for i in range(len(values)):
+        acc = jnp.where(place == first + i, sums[i * size : (i + 1) * size], acc)
+    return acc
+
+
 def turned(value):
     half = value.shape[-1] // 2
     sign = jnp.where(iota((1, 2 * half), 1) < half, 1.0, -1.0)
@@ -362,9 +370,15 @@
 
 
 def prepare_own_kernel(
-    own, lists, codes, weights, spin, turn, table, list_rim, wave_shares, chosen, spread, vel
+    own, lists, codes_far, weights_far, basis_far,
+    spin, turn, table, list_rim, wave_shares, chosen, spread, basis,
+    vel, codes, weights, sems,
 ):
     rows, cols, lanes = own.shape
+    pairs = ((codes_far, codes), (weights_far, weights), (basis_far, basis))
+    copies = [pltpu.make_async_copy(one, two, sems.at[i]) for i, (one, two) in enumerate(pairs)]
+    for copy in copies:
+        copy.start()
     per = lanes // 16
     blank = jnp.zeros((EDGE, lanes), F32)
 
@@ -410,6 +424,8 @@
     at, to = iota((lanes, lanes), 0), iota((lanes, lanes), 1)
     spread[...] = ((at < reach) & (at % wc == to)).astype(F32).astype(BF)
 
+    for copy in copies:
+        copy.wait()
     at, to = iota((wc, lanes), 0), iota((wc, lanes), 1)
     repeat = ((to < reach) & (to % wc == at)).astype(F32).astype(BF)
     shift = (lane // wc).astype(F32)
@@ -537,13 +553,16 @@
 
     average = averager(lanes)
     means = jnp.zeros((cols, lanes), F32)
+    ready = []
     for n in range(rows + 2):
         r = n + HL - 1
         absolute = row_of(n - 1, rows, spin_own, spin_ends, HL) + vorticity(mid, r, EDGE, cols)
         old = row_of(n - 1, rows, vel, vel_halo, HV) + mid[r, EDGE : EDGE + cols, :]
         new = 0.5 * old + (0.5 * STEP) * (absolute * drift[r])
-        sums = jnp.dot(jnp.concatenate(split(new), axis=1), average, preferred_element_type=F32)
-        means = jnp.where(lane // 2 == n, sums, means)
+        ready.append(new)
+        if len(ready) == 2 or n == rows + 1:
+            means = add_means(means, n + 1 - len(ready), ready, average)
+            ready = []
         if 1 <= n <= rows:
             out[n - 1] = new
     total[...] = means
@@ -554,8 +573,8 @@
 
 def rim_kernel(
     own, vel_halo, ya, yb, mid_rim, drift_rim, spin_rim, total, list_rim, prof_rim, wave_shares, chosen, spread, inner,
-    out, current,
-    vel, mid, prof, drift, spin, picked, means, strips, sems,
+    out, current_far,
+    vel, mid, prof, drift, spin, picked, means, strips, current, sems,
 ):
     rows, cols, lanes = own.shape
     vrow = rows + 2 * HV
@@ -651,6 +670,7 @@
 
     average = averager(lanes)
     acc = jnp.zeros((2 * EDGE, lanes), F32)
+    ready = []
     step = rows // PARTS
     begins = (EDGE - 1, EDGE + 1)
     for n in range(rows + 2):
@@ -670,10 +690,10 @@
                 kept = inner[n - 1, side * (cols - EDGE) : side * (cols - EDGE) + EDGE, :]
                 moved = pltpu.roll(new, EDGE - 1 if side == 0 else 1, 0)
                 strips[side, n - 1] = jnp.where(sub == (EDGE - 1 if side == 0 else 0), kept, moved)
-        sums = jnp.dot(
-            jnp.concatenate(split(jnp.concatenate(both, axis=0)), axis=1), average, preferred_element_type=F32
-        )
-        acc = jnp.where(lane // 2 == n, sums, acc)
+        ready.append(jnp.concatenate(both, axis=0))
+        if len(ready) == 9 or n == rows + 1:
+            acc = add_means(acc, n + 1 - len(ready), ready, average)
+            ready = []
         if n and n % step == 0:
             part = pl.ds(n - step, step)
             for side, at in ((0, 0), (1, cols - EDGE)):
@@ -689,17 +709,19 @@
 
     named = chosen[...].astype(BF)
     picked[...] = sum(
-        lax.dot_general(p, named, ROWS_DOT, preferred_element_type=F32) for p in split3(means[...])
+        lax.dot_general(p, named, ROWS_DOT, preferred_element_type=F32) for p in split(means[...])
     )
     summed = [
         sum(wave_shares[near] * picked[pl.ds(2 * near + c, wr, stride=2 * RX), :] for near in range(RX + 2))
         for c in range(2)
     ]
     sums = sum(
-        jnp.dot(p, spread[...], preferred_element_type=F32) for p in split3(jnp.concatenate(summed, axis=0))
+        jnp.dot(p, spread[...], preferred_element_type=F32) for p in split(jnp.concatenate(summed, axis=0))
     )
     current[0] = sums[0:wr, 0:wc]
     current[1] = sums[wr:, 0:wc]
+    copies.append(pltpu.make_async_copy(current, current_far, sems.at[len(copies)]))
+    copies[-1].start()
     for copy in copies:
         copy.wait()
 
@@ -734,12 +756,10 @@
         codes, weights = jnp.transpose(ocean_codes, (0, 2, 1)), jnp.transpose(ocean_weights, (0, 2, 1))
         size = sum(x_rows(cols)) + wc * bins // lanes
         outs = [((size, lanes), BF)] * 2 + [((wr, bins), BF)] * 2 + [((rows, 16, lanes), F32)]
-        outs += [(spectrum.shape, BF), (courant.shape, F32), ((wc, wr), F32), ((wc, wr), F32), (stokes_kernel.shape, BF)]
-        outs += [((wr, K, wc), wave_codes.dtype), ((wr, K, wc), F32)]
-        oa, ob, ya, yb, lists, spectrum, courant, source, land, stokes_kernel, wave_codes, wave_weights = call(
+        outs += [(spectrum.shape, BF), (courant.shape, F32), ((wc, wr), F32), ((wc, wr), F32)]
+        oa, ob, ya, yb, lists, spectrum, courant, source, land = call(
             edges_kernel, "edges", outs,
-            spectrum, courant, source, wave_land, codes, weights, coriolis, velocity, stokes_kernel,
-            jnp.transpose(wave_codes, (0, 2, 1)), jnp.transpose(wave_weights, (0, 2, 1)), any_in=range(11),
+            spectrum, courant, source, wave_land, codes, weights, coriolis, velocity, any_in=range(8),
             scratch=[
                 pltpu.VMEM(source.shape, F32),
                 pltpu.VMEM(wave_land.shape, wave_land.dtype),
@@ -747,7 +767,7 @@
                 pltpu.VMEM(weights.shape, F32),
                 pltpu.VMEM(coriolis.shape, F32),
                 pltpu.VMEM((2, HV, cols, lanes), F32),
-                pltpu.SemaphoreType.DMA((12,)),
+                pltpu.SemaphoreType.DMA((9,)),
             ],
         )
         oa, ob = exchange("gx", oa, ob)
@@ -756,13 +776,21 @@
     with jax.named_scope("prepare_own"):
         groups = -(-listed // (lanes // 16))
         level = (cols, lanes)
-        spin_own, turn_own, table_own, list_own, wave_shares, chosen, spread = call(
+        spin_own, turn_own, table_own, list_own, wave_shares, chosen, spread, stokes_kernel = call(
             prepare_own_kernel, "prepare_own",
             [
                 ((rows, *level), F32), ((rows - 4, *level), F32), ((rows, 3 * wc, lanes), BF), ((groups, 16, lanes), F32),
                 ((RX + 2, wr, lanes), F32), ((cols + 2 * RIM, lanes), F32), ((lanes, lanes), BF),
+                (stokes_kernel.shape, BF),
             ],
-            velocity, lists, wave_codes, wave_weights, scratch=[pltpu.VMEM((rows, cols + 2 * EDGE, lanes), F32)],
+            velocity, lists, jnp.transpose(wave_codes, (0, 2, 1)), jnp.transpose(wave_weights, (0, 2, 1)),
+            stokes_kernel, any_in=(2, 3, 4),
+            scratch=[
+                pltpu.VMEM((rows, cols + 2 * EDGE, lanes), F32),
+                pltpu.VMEM((wr, K, wc), wave_codes.dtype),
+                pltpu.VMEM((wr, K, wc), F32),
+                pltpu.SemaphoreType.DMA((3,)),
+            ],
         )
 
     with jax.named_scope("wave"):
@@ -834,12 +862,13 @@
             pltpu.VMEM((lanes, lanes), F32),
             pltpu.VMEM((cols + 2 * RIM, lanes), F32),
             pltpu.VMEM((2, rows, EDGE, lanes), F32),
-            pltpu.SemaphoreType.DMA((1 + 2 * PARTS,)),
+            pltpu.VMEM((2, wr, wc), F32),
+            pltpu.SemaphoreType.DMA((2 + 2 * PARTS,)),
         ]
         new_velocity, current = call(
             rim_kernel, "rim", [(velocity.shape, F32), ((2, wr, wc), F32)],
             velocity, vel_halo, ya, yb, mid_rim, drift_rim, spin_rim, total, list_rim, prof_rim, wave_shares, chosen, spread,
-            result, scratch=scratch, any_out=(0,),
+            result, scratch=scratch, any_out=(0, 1),
         )
     return new_spectrum, new_velocity, current
 

time: 22.4 us -> 22 us (0.982)
  Pallas kernels: 9.41 us -> 9.07 us
    pallas_call x9, Pallas kernels: 9.41 us -> 9.07 us  [call(): pl.pallas_call(kernel, out_shape=tuple((jax.ShapeDtypeStruct(shape, dtype...]
  transfers between devices with their start and end apart: 8 -> 8, of which waited for: 6 -> 6; matrix products, arithmetic and copies ran while one was open for 0% -> 0% of each run, Pallas kernels for 21% -> 22%
where the time goes in v8:
time: 22 us; the launch traced here: 21.9 us
  Pallas kernels  9.07 us (41%)
  waiting for transfers between devices  7.23 us (33%)
  starting transfers between devices  4.86 us (22%)
  between operations  0.71 us (3%)
    pallas_call x9, Pallas kernels, call(): pl.pallas_call(kernel, out_shape=tuple((jax.ShapeDtypeStruct(shape, dtype...  9.07 us
    ppermute x8, waiting for transfers between devices, swap(): return lax.ppermute(value, ('gx', 'gy'), pairs)  7.23 us
    ppermute x8, starting transfers between devices, swap(): return lax.ppermute(value, ('gx', 'gy'), pairs)  4.86 us
  transfers between devices with their start and end apart: 8, of which 6 were waited for; matrix products, arithmetic and copies ran while one was open for 0% of the time, Pallas kernels for 22%

profile of v8, /device:TPU:8, one launch (start us, length us, event | category | flops | bytes accessed | tf_op | source)
XLA Modules:
  0.0 21.9 jit_solution(56970227992002600)
XLA Ops:
  0.6 0.0 copy-start
  0.6 1.6 %edges.1 = (bf16[448,128]{1,0:T(8,128)(2,1)S(1)}, bf16[448,128]{1,0:T(8,128)(2,1)S(1)}, bf16[16,1152]{1,0:T(8,128)(2,1)S(1)}, bf16[16,1152]{1,0:T(8,128)(2,1)S(1...) custom-call(bf16[16,16,1152]{2,1,0:T(8,128)(2,1)} %refs_0_.1, ...), custom_call_target="tpu_custom_call" | custom-call | tf_op jit(solution)/shard_map/spectrum_edges/edges/pallas_call | solution.py:735
  2.3 1.0 %collective-permute-start = (bf16[448,128]{1,0:T(8,128)(2,1)S(1)}, bf16[448,128]{1,0:T(8,128)(2,1)S(1)}, u32[]{:S(2)}, u32[]{:S(2)}) collective-permute-start(bf16[448,128]{1,0:T(8,128)(2,1)S(1)} %get-tuple-element.44), channel_id=1, source_target_pairs={{0,24},{1,25},{2,26},{3,27},{4,28},{5,29},{6,30},{7,31},{8,16},{9,... | collective-permute-start | bytes 344072 | tf_op jit(solution)/shard_map/spectrum_edges/ppermute | solution.py:40
  3.3 0.7 %collective-permute-start.1 = (bf16[448,128]{1,0:T(8,128)(2,1)S(1)}, bf16[448,128]{1,0:T(8,128)(2,1)S(1)}, u32[]{:S(2)}, u32[]{:S(2)}) collective-permute-start(bf16[448,128]{1,0:T(8,128)(2,1)S(1)} %get-tuple-element.45), channel_id=1, source_target_pairs={{0,8},{1,9},{2,10},{3,11},{4,12},{5,13},{6,14},{7,15},{8,0},{9,1},... | collective-permute-start | bytes 344072 | tf_op jit(solution)/shard_map/spectrum_edges/ppermute | solution.py:40
  4.0 1.5 %collective-permute-start.2 = (bf16[16,1152]{1,0:T(8,128)(2,1)S(1)}, bf16[16,1152]{1,0:T(8,128)(2,1)S(1)}, u32[]{:S(2)}, u32[]{:S(2)}) collective-permute-start(bf16[16,1152]{1,0:T(8,128)(2,1)S(1)} %get-tuple-element.56), channel_id=1, source_target_pairs={{0,1},{1,0},{2,3},{3,2},{4,5},{5,4},{6,7},{7,6},{8,9},{9,8},{10,11... | collective-permute-start | bytes 110600 | tf_op jit(solution)/shard_map/spectrum_edges/ppermute | solution.py:40
  5.5 0.4 %collective-permute-start.3 = (bf16[16,1152]{1,0:T(8,128)(2,1)S(1)}, bf16[16,1152]{1,0:T(8,128)(2,1)S(1)}, u32[]{:S(2)}, u32[]{:S(2)}) collective-permute-start(bf16[16,1152]{1,0:T(8,128)(2,1)S(1)} %get-tuple-element.57), channel_id=1, source_target_pairs={{0,8},{1,2},{2,1},{3,4},{4,3},{5,6},{6,5},{7,15},{8,0},{9,10},{10,... | collective-permute-start | bytes 110600 | tf_op jit(solution)/shard_map/spectrum_edges/ppermute | solution.py:40
  5.9 0.0 copy-done
  5.9 1.6 %prepare_own.1 = (f32[32,64,128]{2,1,0:T(8,128)S(1)}, f32[28,64,128]{2,1,0:T(8,128)S(1)}, bf16[32,48,128]{2,1,0:T(8,128)(2,1)S(1)}, f32[5,16,128]{2,1,0:T(8,128)...) custom-call(f32[32,64,128]{2,1,0:T(8,128)S(1)} %copy-done, ...), custom_call_target="tpu_custom_call" | custom-call | tf_op jit(solution)/shard_map/prepare_own/prepare_own/pallas_call | solution.py:735
  7.5 0.3 %collective-permute-done.ob.xb = bf16[448,128]{1,0:T(8,128)(2,1)S(1)} collective-permute-done((bf16[448,128]{1,0:T(8,128)(2,1)S(1)}, bf16[448,128]{1,0:T(8,128)(2,1)S(1)}, u32[]{:S(2)}, u32[]{:S(2)}) %collective-permute-start) | collective-permute-done | bytes 114720 | tf_op jit(solution)/shard_map/spectrum_edges/ppermute | solution.py:40
  7.8 0.0 collective-permute-done.1.oa.xa
  7.8 0.1 collective-permute-done.2.ya
  7.9 2.4 %collective-permute-done.3.yb = bf16[16,1152]{1,0:T(8,128)(2,1)S(1)} collective-permute-done((bf16[16,1152]{1,0:T(8,128)(2,1)S(1)}, bf16[16,1152]{1,0:T(8,128)(2,1)S(1)}, u32[]{:S(2)}, u32[]{:S(2)}) %collective-permute-start.3) | collective-permute-done | bytes 36896 | tf_op jit(solution)/shard_map/spectrum_edges/ppermute | solution.py:40
  10.3 0.5 %wave_ends.1 = (bf16[6,16,1152]{2,1,0:T(8,128)(2,1)S(1)}, bf16[6,16,128]{2,1,0:T(8,128)(2,1)S(1)}, bf16[3,16,128]{2,1,0:T(8,128)(2,1)S(1)}, bf16[3,16,128]{2,1,0:T(8,128)(2,1)S(1)}) custom-call(bf16[16,16,1152]{2,1,0:T(8,128)(2,1)S(1)} %get-tuple-element.55.spec, bf16[2,16,1152]{2,1,0:T(8,128)(2,1)S(1)} %sides.1, ...), custom_call_target="tpu_custom_call" | custom-call | tf_op jit(solution)/shard_map/wave/wave_ends/pallas_call | solution.py:735
  10.8 0.1 collective-permute-start.4
  10.9 0.6 %collective-permute-start.5 = (bf16[3,16,128]{2,1,0:T(8,128)(2,1)S(1)}, bf16[3,16,128]{2,1,0:T(8,128)(2,1)S(1)}, u32[]{:S(2)}, u32[]{:S(2)}) collective-permute-start(bf16[3,16,128]{2,1,0:T(8,128)(2,1)S(1)} %get-tuple-element.65), channel_id=1, source_target_pairs={{0,8},{1,9},{2,10},{3,11},{4,12},{5,13},{6,14},{7,15},{8,0},{9,1},... | collective-permute-start | bytes 36872 | tf_op jit(solution)/shard_map/wave/ppermute | solution.py:40
  11.5 0.7 %wave_rest.1 = (bf16[10,16,1152]{2,1,0:T(8,128)(2,1)S(1)}, bf16[10,16,128]{2,1,0:T(8,128)(2,1)S(1)}) custom-call(bf16[16,16,1152]{2,1,0:T(8,128)(2,1)S(1)} %get-tuple-element.55.spec, bf16[16,1152]{1,0:T(8,128)(2,1)S(1)} %collective-permute-done.2.ya, bf16[16,1152]{1,0:T(8,128)(2,1)S(1)} %collective-permute-done.3.yb, ...), custom_call_target="tpu_custom_call" | custom-call | tf_op jit(solution)/shard_map/wave/wave_rest/pallas_call | solution.py:735
  12.2 0.5 %prepare_ends.1 = (f32[10,64,128]{2,1,0:T(8,128)S(1)}, f32[6,64,128]{2,1,0:T(8,128)S(1)}, f32[10,64,128]{2,1,0:T(8,128)S(1)}, bf16[6,48,128]{2,1,0:T(8,128)(2,1)...) custom-call(f32[32,64,128]{2,1,0:T(8,128)S(1)} %copy-done, ...), custom_call_target="tpu_custom_call" | custom-call | tf_op jit(solution)/shard_map/prepare_ends/prepare_ends/pallas_call | solution.py:735
  12.7 1.3 %collective-permute-done.4.pb = bf16[3,16,128]{2,1,0:T(8,128)(2,1)S(1)} collective-permute-done((bf16[3,16,128]{2,1,0:T(8,128)(2,1)S(1)}, bf16[3,16,128]{2,1,0:T(8,128)(2,1)S(1)}, u32[]{:S(2)}, u32[]{:S(2)}) %collective-permute-start.4) | collective-permute-done | bytes 12320 | tf_op jit(solution)/shard_map/wave/ppermute | solution.py:40
  14.0 0.0 collective-permute-done.5.pa
  14.0 0.2 halo.1
  14.2 0.6 %collective-permute-start.6 = (bf16[256,128]{1,0:T(8,128)(2,1)S(1)}, bf16[256,128]{1,0:T(8,128)(2,1)S(1)}, u32[]{:S(2)}, u32[]{:S(2)}) collective-permute-start(bf16[256,128]{1,0:T(8,128)(2,1)S(1)} %get-tuple-element.71), channel_id=1, source_target_pairs={{0,1},{1,0},{2,3},{3,2},{4,5},{5,4},{6,7},{7,6},{8,9},{9,8},{10,11... | collective-permute-start | bytes 196616 | tf_op jit(solution)/shard_map/halo/ppermute | solution.py:40
  14.8 0.0 collective-permute-start.7
  14.8 2.1 %inner.1 = (f32[32,64,128]{2,1,0:T(8,128)S(1)}, bf16[16,16,1152]{2,1,0:T(8,128)(2,1)}, f32[38,2,16,128]{3,2,1,0:T(8,128)S(1)}, f32[38,2,8,128]{3,2,1,0:T(8,128)S...) custom-call(f32[32,64,128]{2,1,0:T(8,128)S(1)} %copy-done, ...), custom_call_target="tpu_custom_call" | custom-call | tf_op jit(solution)/shard_map/inner/inner/pallas_call | solution.py:735
  16.9 1.7 %collective-permute-done.6.ya = bf16[256,128]{1,0:T(8,128)(2,1)S(1)} collective-permute-done((bf16[256,128]{1,0:T(8,128)(2,1)S(1)}, bf16[256,128]{1,0:T(8,128)(2,1)S(1)}, u32[]{:S(2)}, u32[]{:S(2)}) %collective-permute-start.6) | collective-permute-done | bytes 65568 | tf_op jit(solution)/shard_map/halo/ppermute | solution.py:40
  18.5 1.4 %collective-permute-done.7.yb = bf16[256,128]{1,0:T(8,128)(2,1)S(1)} collective-permute-done((bf16[256,128]{1,0:T(8,128)(2,1)S(1)}, bf16[256,128]{1,0:T(8,128)(2,1)S(1)}, u32[]{:S(2)}, u32[]{:S(2)}) %collective-permute-start.7) | collective-permute-done | bytes 65568 | tf_op jit(solution)/shard_map/halo/ppermute | solution.py:40
  20.0 1.9 %rim.1 = (f32[32,64,128]{2,1,0:T(8,128)}, f32[2,16,16]{2,1,0:T(8,128)}) custom-call(f32[32,64,128]{2,1,0:T(8,128)S(1)} %copy-done, f32[10,64,128]{2,1,0:T(8,128)S(1)} %get-tuple-element.49.vel_halo, bf16[256,128]{1,0:T(8,128)(2,1)S(1)} %collective-permute-done.6.ya, bf16[256,128]{1,0:T(8,128)(2,1)S(1)} %collective-permute-done.7.yb, ...), custom_call_target="tpu_custom_call" | custom-call | tf_op jit(solution)/shard_map/rim/rim/pallas_call | solution.py:735
  (1 shorter events, 0.0 us)
Async XLA Ops:
  0.6 5.3 %copy-start = (f32[32,64,128]{2,1,0:T(8,128)S(1)}, f32[32,64,128]{2,1,0:T(8,128)}, u32[]{:S(2)}) copy-start(f32[32,64,128]{2,1,0:T(8,128)} %own.5) | copy-start | bytes 3145732
  2.3 5.5 %collective-permute-start = (bf16[448,128]{1,0:T(8,128)(2,1)S(1)}, bf16[448,128]{1,0:T(8,128)(2,1)S(1)}, u32[]{:S(2)}, u32[]{:S(2)}) collective-permute-start(bf16[448,128]{1,0:T(8,128)(2,1)S(1)} %get-tuple-element.44), channel_id=1, source_target_pairs={{0,24},{1,25},{2,26},{3,27},{4,28},{5,29},{6,30},{7,31},{8,16},{9,... | collective-permute-start | bytes 344072 | tf_op jit(solution)/shard_map/spectrum_edges/ppermute | solution.py:40
  3.3 4.5 %collective-permute-start.1 = (bf16[448,128]{1,0:T(8,128)(2,1)S(1)}, bf16[448,128]{1,0:T(8,128)(2,1)S(1)}, u32[]{:S(2)}, u32[]{:S(2)}) collective-permute-start(bf16[448,128]{1,0:T(8,128)(2,1)S(1)} %get-tuple-element.45), channel_id=1, source_target_pairs={{0,8},{1,9},{2,10},{3,11},{4,12},{5,13},{6,14},{7,15},{8,0},{9,1},... | collective-permute-start | bytes 344072 | tf_op jit(solution)/shard_map/spectrum_edges/ppermute | solution.py:40
  4.0 4.0 %collective-permute-start.2 = (bf16[16,1152]{1,0:T(8,128)(2,1)S(1)}, bf16[16,1152]{1,0:T(8,128)(2,1)S(1)}, u32[]{:S(2)}, u32[]{:S(2)}) collective-permute-start(bf16[16,1152]{1,0:T(8,128)(2,1)S(1)} %get-tuple-element.56), channel_id=1, source_target_pairs={{0,1},{1,0},{2,3},{3,2},{4,5},{5,4},{6,7},{7,6},{8,9},{9,8},{10,11... | collective-permute-start | bytes 110600 | tf_op jit(solution)/shard_map/spectrum_edges/ppermute | solution.py:40
  5.5 4.9 %collective-permute-start.3 = (bf16[16,1152]{1,0:T(8,128)(2,1)S(1)}, bf16[16,1152]{1,0:T(8,128)(2,1)S(1)}, u32[]{:S(2)}, u32[]{:S(2)}) collective-permute-start(bf16[16,1152]{1,0:T(8,128)(2,1)S(1)} %get-tuple-element.57), channel_id=1, source_target_pairs={{0,8},{1,2},{2,1},{3,4},{4,3},{5,6},{6,5},{7,15},{8,0},{9,10},{10,... | collective-permute-start | bytes 110600 | tf_op jit(solution)/shard_map/spectrum_edges/ppermute | solution.py:40
  10.8 3.2 %collective-permute-start.4 = (bf16[3,16,128]{2,1,0:T(8,128)(2,1)S(1)}, bf16[3,16,128]{2,1,0:T(8,128)(2,1)S(1)}, u32[]{:S(2)}, u32[]{:S(2)}) collective-permute-start(bf16[3,16,128]{2,1,0:T(8,128)(2,1)S(1)} %get-tuple-element.64), channel_id=1, source_target_pairs={{0,24},{1,25},{2,26},{3,27},{4,28},{5,29},{6,30},{7,31},{8,16},{9,... | collective-permute-start | bytes 36872 | tf_op jit(solution)/shard_map/wave/ppermute | solution.py:40
  10.9 3.1 %collective-permute-start.5 = (bf16[3,16,128]{2,1,0:T(8,128)(2,1)S(1)}, bf16[3,16,128]{2,1,0:T(8,128)(2,1)S(1)}, u32[]{:S(2)}, u32[]{:S(2)}) collective-permute-start(bf16[3,16,128]{2,1,0:T(8,128)(2,1)S(1)} %get-tuple-element.65), channel_id=1, source_target_pairs={{0,8},{1,9},{2,10},{3,11},{4,12},{5,13},{6,14},{7,15},{8,0},{9,1},... | collective-permute-start | bytes 36872 | tf_op jit(solution)/shard_map/wave/ppermute | solution.py:40
  14.2 4.3 %collective-permute-start.6 = (bf16[256,128]{1,0:T(8,128)(2,1)S(1)}, bf16[256,128]{1,0:T(8,128)(2,1)S(1)}, u32[]{:S(2)}, u32[]{:S(2)}) collective-permute-start(bf16[256,128]{1,0:T(8,128)(2,1)S(1)} %get-tuple-element.71), channel_id=1, source_target_pairs={{0,1},{1,0},{2,3},{3,2},{4,5},{5,4},{6,7},{7,6},{8,9},{9,8},{10,11... | collective-permute-start | bytes 196616 | tf_op jit(solution)/shard_map/halo/ppermute | solution.py:40
  14.8 5.2 %collective-permute-start.7 = (bf16[256,128]{1,0:T(8,128)(2,1)S(1)}, bf16[256,128]{1,0:T(8,128)(2,1)S(1)}, u32[]{:S(2)}, u32[]{:S(2)}) collective-permute-start(bf16[256,128]{1,0:T(8,128)(2,1)S(1)} %get-tuple-element.72), channel_id=1, source_target_pairs={{0,8},{1,2},{2,1},{3,4},{4,3},{5,6},{6,5},{7,15},{8,0},{9,10},{10,... | collective-permute-start | bytes 196616 | tf_op jit(solution)/shard_map/halo/ppermute | solution.py:40

commit v9 on v8

--- a/solution.py
+++ b/solution.py
@@ -9,7 +9,7 @@
 RX = 2
 RY = 4
 STEP = 0.5
-PARTS = 4
+PARTS = 2
 TALL = 24
 RIM = 4
 HV, HL = 5, 3
@@ -173,18 +173,18 @@
             cells = []
 
 
-def sides_kernel(xb, xa, after, sides):
-    even_x = is_even("gx")
-    cols, bins = sides.shape[1], sides.shape[2]
-    lanes = xa.shape[1]
-    start = xa.shape[0] - cols * bins // lanes
-    for i in range(bins // lanes):
-        a, b = (ref[start + i * cols : start + (i + 1) * cols, :] for ref in (xa, xb))
-        part = slice(i * lanes, (i + 1) * lanes)
-        sides[0, :, part], sides[1, :, part] = pick(even_x, b, a).astype(BF), pick(even_x, a, b).astype(BF)
-
-
-def wave_ends_kernel(spec, sides, ya, yb, courant, source, land, weights, out, profile, pa, pb):
+def spectrum_of(ref, cols, bins):
+    lanes = ref.shape[1]
+    start = ref.shape[0] - cols * bins // lanes
+    blocks = [ref[start + i * cols : start + (i + 1) * cols, :] for i in range(bins // lanes)]
+    return jnp.concatenate(blocks, axis=1)
+
+
+def side_kernel(xb, after, side):
+    side[...] = spectrum_of(xb, *side.shape)
+
+
+def wave_ends_kernel(spec, side, ya, yb, xa, courant, source, land, weights, out, profile, pa, pb):
     rows, cols, bins = spec.shape
     even_x = is_even("gx")
     parts = []
@@ -195,7 +195,9 @@
         parts.append(part)
 
     ends = list(range(HX)) + list(range(rows - HX, rows))
-    advance(ends, spec, [sides[i].astype(F32) for i in range(2)], ya, yb, courant, source, land, weights, HX, put)
+    one, two = side[...], spectrum_of(xa, cols, bins)
+    sides = pick(even_x, one, two), pick(even_x, two, one)
+    advance(ends, spec, sides, ya, yb, courant, source, land, weights, HX, put)
     for i in range(HX):
         first, last = parts[i], parts[HX + i]
         pa[i] = jnp.where(even_x, last, first).astype(BF)
@@ -288,7 +290,7 @@
         put(start + tile * 16, acc[tile][0], acc[tile][1])
 
 
-def halo_kernel(fixed_a, fixed_b, ends, rest, pb, pa, ya, yb):
+def halo_kernel(fixed_a, fixed_b, columns, ends, rest, pb, pa, ya, yb):
     lanes = rest.shape[2]
     even_x, even_y = is_even("gx"), is_even("gy")
     wr, wc = rest.shape[0] + 2 * HX, rest.shape[1]
@@ -302,12 +304,7 @@
     joined = jnp.concatenate([before.astype(BF), ends[0:HX], rest[...], ends[HX:], after.astype(BF)], axis=0)
     count = (wr + 2 * HX) * wc
     slots = TALL * HY
-    at, cell = iota((2 * slots, count), 0), iota((2 * slots, count), 1)
-    side, rest = at // slots, at % slots
-    column = rest // TALL + jnp.where(side == 0, wc - HY, 0)
-    row = rest % TALL
-    chosen = ((row < wr + 2 * HX) & (cell == row * wc + column)).astype(F32).astype(BF)
-    sides = jnp.dot(chosen, joined.reshape(count, lanes), preferred_element_type=F32)
+    sides = jnp.dot(columns[...], joined.reshape(count, lanes), preferred_element_type=F32)
     put(0, sides[0:slots], sides[slots:])
     ya[slots:], yb[slots:] = fixed_a[...], fixed_b[...]
 
@@ -371,7 +368,7 @@
 
 def prepare_own_kernel(
     own, lists, codes_far, weights_far, basis_far,
-    spin, turn, table, list_rim, wave_shares, chosen, spread, basis,
+    spin, turn, table, list_rim, wave_shares, chosen, spread, basis, columns,
     vel, codes, weights, sems,
 ):
     rows, cols, lanes = own.shape
@@ -418,6 +415,13 @@
 
     wc = cols // RY
     lane = iota((1, lanes), 1)
+    slots, wr = TALL * HY, rows // RX
+    at, cell = iota(columns.shape, 0), iota(columns.shape, 1)
+    rest = at % slots
+    column = rest // TALL + jnp.where(at < slots, wc - HY, 0)
+    row = rest % TALL
+    columns[...] = ((row < wr + 2 * HX) & (cell == row * wc + column)).astype(F32).astype(BF)
+
     at, to = iota(chosen.shape, 0), iota(chosen.shape, 1)
     reach = (RY + 2) * wc
     chosen[...] = ((to < reach) & (at == RY * (to % wc) + to // wc + RIM - 1)).astype(F32)
@@ -527,10 +531,9 @@
         mid[r, 0:EDGE, :] = blank
         mid[r, EDGE + cols :, :] = blank
         mid[r, EDGE : EDGE + cols, :] = new
-        mid_rim[r, 0] = new[0 : 2 * EDGE]
-        mid_rim[r, 1] = new[cols - 2 * EDGE :]
         for where in range(2):
             begin = RIM if where == 0 else cols - RIM - EDGE
+            mid_rim[r, where] = mid[r, EDGE + begin : 2 * EDGE + begin, :]
             drift_rim[r, where] = drift[r, begin : begin + EDGE, :]
             spin_rim[r, where] = spin_ref[tk, begin : begin + EDGE, :]
 
@@ -662,8 +665,8 @@
     for r in range(listed):
         for side in range(2):
             base = RIM + side * EDGE
-            mid[side, r, 2 * EDGE * side : 2 * EDGE * side + EDGE, :] = blank
-            mid[side, r, EDGE - side * EDGE : 3 * EDGE - side * EDGE, :] = mid_rim[r, side]
+            kept = RIM + EDGE - side * EDGE
+            mid[side, r, kept : kept + EDGE, :] = mid_rim[r, side]
             absolute = spin[side, r] + vorticity(vel.at[side], r + lift, base, EDGE)
             new = vel[side, r + lift, base : base + EDGE, :] + STEP * (absolute * drift[side, r])
             mid[side, r, base : base + EDGE, :] = new
@@ -702,21 +705,25 @@
                 copies[-1].start()
     count = cols + 2 * RIM
     means[0:EDGE] = blank
-    means[count - EDGE :] = blank
+    means[count - EDGE : count] = blank
     means[RIM - 1 : RIM - 1 + EDGE] = acc[0:EDGE]
     means[RIM - 1 + EDGE : count - RIM + 1 - EDGE] = total[EDGE - 1 : cols - EDGE + 1, :]
     means[count - RIM + 1 - EDGE : count - RIM + 1] = acc[EDGE:]
 
+    means[count:] = jnp.zeros((means.shape[0] - count, lanes), F32)
     named = chosen[...].astype(BF)
-    picked[...] = sum(
-        lax.dot_general(p, named, ROWS_DOT, preferred_element_type=F32) for p in split(means[...])
+    picked[...] = lax.dot_general(
+        jnp.concatenate(split(means[...]), axis=0), jnp.concatenate([named] * 2, axis=0), ROWS_DOT,
+        preferred_element_type=F32,
     )
     summed = [
         sum(wave_shares[near] * picked[pl.ds(2 * near + c, wr, stride=2 * RX), :] for near in range(RX + 2))
         for c in range(2)
     ]
-    sums = sum(
-        jnp.dot(p, spread[...], preferred_element_type=F32) for p in split(jnp.concatenate(summed, axis=0))
+    sums = jnp.dot(
+        jnp.concatenate(split(jnp.concatenate(summed, axis=0)), axis=1),
+        jnp.concatenate([spread[...]] * 2, axis=0),
+        preferred_element_type=F32,
     )
     current[0] = sums[0:wr, 0:wc]
     current[1] = sums[wr:, 0:wc]
@@ -776,12 +783,13 @@
     with jax.named_scope("prepare_own"):
         groups = -(-listed // (lanes // 16))
         level = (cols, lanes)
-        spin_own, turn_own, table_own, list_own, wave_shares, chosen, spread, stokes_kernel = call(
+        named = -(-(cols + 2 * RIM) // 16) * 16
+        spin_own, turn_own, table_own, list_own, wave_shares, chosen, spread, stokes_kernel, columns = call(
             prepare_own_kernel, "prepare_own",
             [
                 ((rows, *level), F32), ((rows - 4, *level), F32), ((rows, 3 * wc, lanes), BF), ((groups, 16, lanes), F32),
-                ((RX + 2, wr, lanes), F32), ((cols + 2 * RIM, lanes), F32), ((lanes, lanes), BF),
-                (stokes_kernel.shape, BF),
+                ((RX + 2, wr, lanes), F32), ((named, lanes), F32), ((lanes, lanes), BF),
+                (stokes_kernel.shape, BF), ((2 * TALL * HY, prow * wc), BF),
             ],
             velocity, lists, jnp.transpose(wave_codes, (0, 2, 1)), jnp.transpose(wave_weights, (0, 2, 1)),
             stokes_kernel, any_in=(2, 3, 4),
@@ -795,11 +803,11 @@
 
     with jax.named_scope("wave"):
         edge = (HX, wc, lanes)
-        sides = call(sides_kernel, "sides", [((2, wc, bins), BF)], ob, oa, list_own)[0]
+        side = call(side_kernel, "side", [((wc, bins), BF)], ob, list_own)[0]
         cells_ends, ends, pa, pb = call(
             wave_ends_kernel, "wave_ends",
             [((2 * HX, wc, bins), BF), ((2 * HX, wc, lanes), BF), (edge, BF), (edge, BF)],
-            spectrum, sides, ya, yb, courant, source, land, stokes_kernel,
+            spectrum, side, ya, yb, oa, courant, source, land, stokes_kernel,
         )
         pa, pb = exchange("gx", pa, pb)
         cells_rest, rest = call(
@@ -824,7 +832,7 @@
     with jax.named_scope("halo"):
         size += y_rows(rows)[0]
         ya, yb = call(
-            halo_kernel, "halo", [((size, lanes), BF)] * 2, fixed_a, fixed_b, ends, rest, pb, pa
+            halo_kernel, "halo", [((size, lanes), BF)] * 2, fixed_a, fixed_b, columns, ends, rest, pb, pa
         )
         ya, yb = exchange("gy", ya, yb)
 
@@ -841,7 +849,7 @@
             [
                 (velocity.shape, F32),
                 (spectrum.shape, BF),
-                ((listed, 2, 2 * EDGE, lanes), F32),
+                ((listed, 2, EDGE, lanes), F32),
                 ((listed, 2, EDGE, lanes), F32),
                 ((listed, 2, EDGE, lanes), F32),
                 ((cols, lanes), F32),
@@ -860,7 +868,7 @@
             pltpu.VMEM((2, listed, EDGE, lanes), F32),
             pltpu.VMEM((2, listed, EDGE, lanes), F32),
             pltpu.VMEM((lanes, lanes), F32),
-            pltpu.VMEM((cols + 2 * RIM, lanes), F32),
+            pltpu.VMEM((named, lanes), F32),
             pltpu.VMEM((2, rows, EDGE, lanes), F32),
             pltpu.VMEM((2, wr, wc), F32),
             pltpu.SemaphoreType.DMA((2 + 2 * PARTS,)),

time: 22 us -> 22 us (level)
  transfers between devices with their start and end apart: 8 -> 8, of which waited for: 6 -> 6; matrix products, arithmetic and copies ran while one was open for 0% -> 0% of each run, Pallas kernels for 22% -> 23%
where the time goes in v9:
time: 22 us; the launch traced here: 21.8 us
  Pallas kernels  9.1 us (41%)
  waiting for transfers between devices  7.14 us (32%)
  starting transfers between devices  4.87 us (22%)
  between operations  0.71 us (3%)
    pallas_call x9, Pallas kernels, call(): pl.pallas_call(kernel, out_shape=tuple((jax.ShapeDtypeStruct(shape, dtype...  9.1 us
    ppermute x8, waiting for transfers between devices, swap(): return lax.ppermute(value, ('gx', 'gy'), pairs)  7.14 us
    ppermute x8, starting transfers between devices, swap(): return lax.ppermute(value, ('gx', 'gy'), pairs)  4.87 us
  transfers between devices with their start and end apart: 8, of which 6 were waited for; matrix products, arithmetic and copies ran while one was open for 0% of the time, Pallas kernels for 23%

profile of v9, /device:TPU:8, one launch (start us, length us, event | category | flops | bytes accessed | tf_op | source)
XLA Modules:
  0.0 21.8 jit_solution(9814365620271004307)
XLA Ops:
  0.6 0.0 copy-start
  0.6 1.6 %edges.1 = (bf16[448,128]{1,0:T(8,128)(2,1)S(1)}, bf16[448,128]{1,0:T(8,128)(2,1)S(1)}, bf16[16,1152]{1,0:T(8,128)(2,1)S(1)}, bf16[16,1152]{1,0:T(8,128)(2,1)S(1...) custom-call(bf16[16,16,1152]{2,1,0:T(8,128)(2,1)} %refs_0_.1, ...), custom_call_target="tpu_custom_call" | custom-call | tf_op jit(solution)/shard_map/spectrum_edges/edges/pallas_call | solution.py:742
  2.3 1.0 %collective-permute-start = (bf16[448,128]{1,0:T(8,128)(2,1)S(1)}, bf16[448,128]{1,0:T(8,128)(2,1)S(1)}, u32[]{:S(2)}, u32[]{:S(2)}) collective-permute-start(bf16[448,128]{1,0:T(8,128)(2,1)S(1)} %get-tuple-element.45), channel_id=1, source_target_pairs={{0,24},{1,25},{2,26},{3,27},{4,28},{5,29},{6,30},{7,31},{8,16},{9,... | collective-permute-start | bytes 344072 | tf_op jit(solution)/shard_map/spectrum_edges/ppermute | solution.py:40
  3.3 0.7 %collective-permute-start.1 = (bf16[448,128]{1,0:T(8,128)(2,1)S(1)}, bf16[448,128]{1,0:T(8,128)(2,1)S(1)}, u32[]{:S(2)}, u32[]{:S(2)}) collective-permute-start(bf16[448,128]{1,0:T(8,128)(2,1)S(1)} %get-tuple-element.46), channel_id=1, source_target_pairs={{0,8},{1,9},{2,10},{3,11},{4,12},{5,13},{6,14},{7,15},{8,0},{9,1},... | collective-permute-start | bytes 344072 | tf_op jit(solution)/shard_map/spectrum_edges/ppermute | solution.py:40
  4.0 1.5 %collective-permute-start.2 = (bf16[16,1152]{1,0:T(8,128)(2,1)S(1)}, bf16[16,1152]{1,0:T(8,128)(2,1)S(1)}, u32[]{:S(2)}, u32[]{:S(2)}) collective-permute-start(bf16[16,1152]{1,0:T(8,128)(2,1)S(1)} %get-tuple-element.57), channel_id=1, source_target_pairs={{0,1},{1,0},{2,3},{3,2},{4,5},{5,4},{6,7},{7,6},{8,9},{9,8},{10,11... | collective-permute-start | bytes 110600 | tf_op jit(solution)/shard_map/spectrum_edges/ppermute | solution.py:40
  5.5 0.4 %collective-permute-start.3 = (bf16[16,1152]{1,0:T(8,128)(2,1)S(1)}, bf16[16,1152]{1,0:T(8,128)(2,1)S(1)}, u32[]{:S(2)}, u32[]{:S(2)}) collective-permute-start(bf16[16,1152]{1,0:T(8,128)(2,1)S(1)} %get-tuple-element.58), channel_id=1, source_target_pairs={{0,8},{1,2},{2,1},{3,4},{4,3},{5,6},{6,5},{7,15},{8,0},{9,10},{10,... | collective-permute-start | bytes 110600 | tf_op jit(solution)/shard_map/spectrum_edges/ppermute | solution.py:40
  5.9 0.0 copy-done
  5.9 1.7 %prepare_own.1 = (f32[32,64,128]{2,1,0:T(8,128)S(1)}, f32[28,64,128]{2,1,0:T(8,128)S(1)}, bf16[32,48,128]{2,1,0:T(8,128)(2,1)S(1)}, f32[5,16,128]{2,1,0:T(8,128)...) custom-call(f32[32,64,128]{2,1,0:T(8,128)S(1)} %copy-done, ...), custom_call_target="tpu_custom_call" | custom-call | tf_op jit(solution)/shard_map/prepare_own/prepare_own/pallas_call | solution.py:742
  7.6 0.2 collective-permute-done.ob.xb
  7.8 0.2 collective-permute-done.2.ya
  7.9 2.4 %collective-permute-done.3.yb = bf16[16,1152]{1,0:T(8,128)(2,1)S(1)} collective-permute-done((bf16[16,1152]{1,0:T(8,128)(2,1)S(1)}, bf16[16,1152]{1,0:T(8,128)(2,1)S(1)}, u32[]{:S(2)}, u32[]{:S(2)}) %collective-permute-start.3) | collective-permute-done | bytes 36896 | tf_op jit(solution)/shard_map/spectrum_edges/ppermute | solution.py:40
  10.3 0.0 collective-permute-done.1.oa.xa
  10.4 0.5 %wave_ends.1 = (bf16[6,16,1152]{2,1,0:T(8,128)(2,1)S(1)}, bf16[6,16,128]{2,1,0:T(8,128)(2,1)S(1)}, bf16[3,16,128]{2,1,0:T(8,128)(2,1)S(1)}, bf16[3,16,128]{2,1,0:T(8,128)(2,1)S(1)}) custom-call(bf16[16,16,1152]{2,1,0:T(8,128)(2,1)S(1)} %get-tuple-element.56.spec, bf16[16,1152]{1,0:T(8,128)(2,1)S(1)} %side.1, bf16[16,1152]{1,0:T(8,128)(2,1)S(1)} %collective-permute-done.2.ya, ...), custom_call_target="tpu_custom_call" | custom-call | tf_op jit(solution)/shard_map/wave/wave_ends/pallas_call | solution.py:742
  10.8 0.1 collective-permute-start.4
  10.9 0.6 %collective-permute-start.5 = (bf16[3,16,128]{2,1,0:T(8,128)(2,1)S(1)}, bf16[3,16,128]{2,1,0:T(8,128)(2,1)S(1)}, u32[]{:S(2)}, u32[]{:S(2)}) collective-permute-start(bf16[3,16,128]{2,1,0:T(8,128)(2,1)S(1)} %get-tuple-element.66), channel_id=1, source_target_pairs={{0,8},{1,9},{2,10},{3,11},{4,12},{5,13},{6,14},{7,15},{8,0},{9,1},... | collective-permute-start | bytes 36872 | tf_op jit(solution)/shard_map/wave/ppermute | solution.py:40
  11.6 0.7 %wave_rest.1 = (bf16[10,16,1152]{2,1,0:T(8,128)(2,1)S(1)}, bf16[10,16,128]{2,1,0:T(8,128)(2,1)S(1)}) custom-call(bf16[16,16,1152]{2,1,0:T(8,128)(2,1)S(1)} %get-tuple-element.56.spec, bf16[16,1152]{1,0:T(8,128)(2,1)S(1)} %collective-permute-done.2.ya, bf16[16,1152]{1,0:T(8,128)(2,1)S(1)} %collective-permute-done.3.yb, ...), custom_call_target="tpu_custom_call" | custom-call | tf_op jit(solution)/shard_map/wave/wave_rest/pallas_call | solution.py:742
  12.2 0.5 %prepare_ends.1 = (f32[10,64,128]{2,1,0:T(8,128)S(1)}, f32[6,64,128]{2,1,0:T(8,128)S(1)}, f32[10,64,128]{2,1,0:T(8,128)S(1)}, bf16[6,48,128]{2,1,0:T(8,128)(2,1)...) custom-call(f32[32,64,128]{2,1,0:T(8,128)S(1)} %copy-done, ...), custom_call_target="tpu_custom_call" | custom-call | tf_op jit(solution)/shard_map/prepare_ends/prepare_ends/pallas_call | solution.py:742
  12.7 1.3 %collective-permute-done.4.pb = bf16[3,16,128]{2,1,0:T(8,128)(2,1)S(1)} collective-permute-done((bf16[3,16,128]{2,1,0:T(8,128)(2,1)S(1)}, bf16[3,16,128]{2,1,0:T(8,128)(2,1)S(1)}, u32[]{:S(2)}, u32[]{:S(2)}) %collective-permute-start.4) | collective-permute-done | bytes 12320 | tf_op jit(solution)/shard_map/wave/ppermute | solution.py:40
  14.0 0.0 collective-permute-done.5.pa
  14.0 0.2 halo.1
  14.2 0.6 %collective-permute-start.6 = (bf16[256,128]{1,0:T(8,128)(2,1)S(1)}, bf16[256,128]{1,0:T(8,128)(2,1)S(1)}, u32[]{:S(2)}, u32[]{:S(2)}) collective-permute-start(bf16[256,128]{1,0:T(8,128)(2,1)S(1)} %get-tuple-element.73), channel_id=1, source_target_pairs={{0,1},{1,0},{2,3},{3,2},{4,5},{5,4},{6,7},{7,6},{8,9},{9,8},{10,11... | collective-permute-start | bytes 196616 | tf_op jit(solution)/shard_map/halo/ppermute | solution.py:40
  14.8 0.0 collective-permute-start.7
  14.8 2.1 %inner.1 = (f32[32,64,128]{2,1,0:T(8,128)S(1)}, bf16[16,16,1152]{2,1,0:T(8,128)(2,1)}, f32[38,2,8,128]{3,2,1,0:T(8,128)S(1)}, f32[38,2,8,128]{3,2,1,0:T(8,128)S(...) custom-call(f32[32,64,128]{2,1,0:T(8,128)S(1)} %copy-done, ...), custom_call_target="tpu_custom_call" | custom-call | tf_op jit(solution)/shard_map/inner/inner/pallas_call | solution.py:742
  16.9 1.7 %collective-permute-done.6.ya = bf16[256,128]{1,0:T(8,128)(2,1)S(1)} collective-permute-done((bf16[256,128]{1,0:T(8,128)(2,1)S(1)}, bf16[256,128]{1,0:T(8,128)(2,1)S(1)}, u32[]{:S(2)}, u32[]{:S(2)}) %collective-permute-start.6) | collective-permute-done | bytes 65568 | tf_op jit(solution)/shard_map/halo/ppermute | solution.py:40
  18.5 1.4 %collective-permute-done.7.yb = bf16[256,128]{1,0:T(8,128)(2,1)S(1)} collective-permute-done((bf16[256,128]{1,0:T(8,128)(2,1)S(1)}, bf16[256,128]{1,0:T(8,128)(2,1)S(1)}, u32[]{:S(2)}, u32[]{:S(2)}) %collective-permute-start.7) | collective-permute-done | bytes 65568 | tf_op jit(solution)/shard_map/halo/ppermute | solution.py:40
  20.0 1.9 %rim.1 = (f32[32,64,128]{2,1,0:T(8,128)}, f32[2,16,16]{2,1,0:T(8,128)}) custom-call(f32[32,64,128]{2,1,0:T(8,128)S(1)} %copy-done, f32[10,64,128]{2,1,0:T(8,128)S(1)} %get-tuple-element.50.vel_halo, bf16[256,128]{1,0:T(8,128)(2,1)S(1)} %collective-permute-done.6.ya, bf16[256,128]{1,0:T(8,128)(2,1)S(1)} %collective-permute-done.7.yb, ...), custom_call_target="tpu_custom_call" | custom-call | tf_op jit(solution)/shard_map/rim/rim/pallas_call | solution.py:742
  (1 shorter events, 0.0 us)
Async XLA Ops:
  0.6 5.3 %copy-start = (f32[32,64,128]{2,1,0:T(8,128)S(1)}, f32[32,64,128]{2,1,0:T(8,128)}, u32[]{:S(2)}) copy-start(f32[32,64,128]{2,1,0:T(8,128)} %own.5) | copy-start | bytes 3145732
  2.3 5.5 %collective-permute-start = (bf16[448,128]{1,0:T(8,128)(2,1)S(1)}, bf16[448,128]{1,0:T(8,128)(2,1)S(1)}, u32[]{:S(2)}, u32[]{:S(2)}) collective-permute-start(bf16[448,128]{1,0:T(8,128)(2,1)S(1)} %get-tuple-element.45), channel_id=1, source_target_pairs={{0,24},{1,25},{2,26},{3,27},{4,28},{5,29},{6,30},{7,31},{8,16},{9,... | collective-permute-start | bytes 344072 | tf_op jit(solution)/shard_map/spectrum_edges/ppermute | solution.py:40
  3.3 7.1 %collective-permute-start.1 = (bf16[448,128]{1,0:T(8,128)(2,1)S(1)}, bf16[448,128]{1,0:T(8,128)(2,1)S(1)}, u32[]{:S(2)}, u32[]{:S(2)}) collective-permute-start(bf16[448,128]{1,0:T(8,128)(2,1)S(1)} %get-tuple-element.46), channel_id=1, source_target_pairs={{0,8},{1,9},{2,10},{3,11},{4,12},{5,13},{6,14},{7,15},{8,0},{9,1},... | collective-permute-start | bytes 344072 | tf_op jit(solution)/shard_map/spectrum_edges/ppermute | solution.py:40
  4.0 4.0 %collective-permute-start.2 = (bf16[16,1152]{1,0:T(8,128)(2,1)S(1)}, bf16[16,1152]{1,0:T(8,128)(2,1)S(1)}, u32[]{:S(2)}, u32[]{:S(2)}) collective-permute-start(bf16[16,1152]{1,0:T(8,128)(2,1)S(1)} %get-tuple-element.57), channel_id=1, source_target_pairs={{0,1},{1,0},{2,3},{3,2},{4,5},{5,4},{6,7},{7,6},{8,9},{9,8},{10,11... | collective-permute-start | bytes 110600 | tf_op jit(solution)/shard_map/spectrum_edges/ppermute | solution.py:40
  5.5 4.9 %collective-permute-start.3 = (bf16[16,1152]{1,0:T(8,128)(2,1)S(1)}, bf16[16,1152]{1,0:T(8,128)(2,1)S(1)}, u32[]{:S(2)}, u32[]{:S(2)}) collective-permute-start(bf16[16,1152]{1,0:T(8,128)(2,1)S(1)} %get-tuple-element.58), channel_id=1, source_target_pairs={{0,8},{1,2},{2,1},{3,4},{4,3},{5,6},{6,5},{7,15},{8,0},{9,10},{10,... | collective-permute-start | bytes 110600 | tf_op jit(solution)/shard_map/spectrum_edges/ppermute | solution.py:40
  10.8 3.2 %collective-permute-start.4 = (bf16[3,16,128]{2,1,0:T(8,128)(2,1)S(1)}, bf16[3,16,128]{2,1,0:T(8,128)(2,1)S(1)}, u32[]{:S(2)}, u32[]{:S(2)}) collective-permute-start(bf16[3,16,128]{2,1,0:T(8,128)(2,1)S(1)} %get-tuple-element.65), channel_id=1, source_target_pairs={{0,24},{1,25},{2,26},{3,27},{4,28},{5,29},{6,30},{7,31},{8,16},{9,... | collective-permute-start | bytes 36872 | tf_op jit(solution)/shard_map/wave/ppermute | solution.py:40
  10.9 3.1 %collective-permute-start.5 = (bf16[3,16,128]{2,1,0:T(8,128)(2,1)S(1)}, bf16[3,16,128]{2,1,0:T(8,128)(2,1)S(1)}, u32[]{:S(2)}, u32[]{:S(2)}) collective-permute-start(bf16[3,16,128]{2,1,0:T(8,128)(2,1)S(1)} %get-tuple-element.66), channel_id=1, source_target_pairs={{0,8},{1,9},{2,10},{3,11},{4,12},{5,13},{6,14},{7,15},{8,0},{9,1},... | collective-permute-start | bytes 36872 | tf_op jit(solution)/shard_map/wave/ppermute | solution.py:40
  14.2 4.3 %collective-permute-start.6 = (bf16[256,128]{1,0:T(8,128)(2,1)S(1)}, bf16[256,128]{1,0:T(8,128)(2,1)S(1)}, u32[]{:S(2)}, u32[]{:S(2)}) collective-permute-start(bf16[256,128]{1,0:T(8,128)(2,1)S(1)} %get-tuple-element.73), channel_id=1, source_target_pairs={{0,1},{1,0},{2,3},{3,2},{4,5},{5,4},{6,7},{7,6},{8,9},{9,8},{10,11... | collective-permute-start | bytes 196616 | tf_op jit(solution)/shard_map/halo/ppermute | solution.py:40
  14.8 5.2 %collective-permute-start.7 = (bf16[256,128]{1,0:T(8,128)(2,1)S(1)}, bf16[256,128]{1,0:T(8,128)(2,1)S(1)}, u32[]{:S(2)}, u32[]{:S(2)}) collective-permute-start(bf16[256,128]{1,0:T(8,128)(2,1)S(1)} %get-tuple-element.74), channel_id=1, source_target_pairs={{0,8},{1,2},{2,1},{3,4},{4,3},{5,6},{6,5},{7,15},{8,0},{9,10},{10,... | collective-permute-start | bytes 196616 | tf_op jit(solution)/shard_map/halo/ppermute | solution.py:40

commit v10 on v9

--- a/solution.py
+++ b/solution.py
@@ -600,8 +600,6 @@
 
     blank = jnp.zeros((EDGE, lanes), F32)
     for r in range(vrow):
-        vel[0, r, 0:EDGE, :] = blank
-        vel[1, r, 2 * EDGE :, :] = blank
         ref, k = (own, r - HV) if HV <= r < HV + rows else (vel_halo, r if r < HV else r - rows)
         vel[0, r, EDGE:, :] = ref[k, 0 : 2 * EDGE, :]
         vel[1, r, 0 : 2 * EDGE, :] = ref[k, cols - 2 * EDGE : cols, :]
@@ -614,11 +612,12 @@
             for j in range(2):
                 r = (start + i * EDGE) // RIM + j
                 if r < vrow:
-                    at = j * RIM
-                    vel[0, r, EDGE - RIM : EDGE, :] = low_in[at : at + RIM]
-                    vel[0, r, EDGE - RIM - 1 : EDGE - RIM, :] = low[at : at + 1]
-                    vel[1, r, 2 * EDGE : 2 * EDGE + RIM, :] = high[at : at + RIM]
-                    vel[1, r, 2 * EDGE + RIM : 2 * EDGE + RIM + 1, :] = high_moved[at + RIM - 1 : at + RIM]
+                    near = low_in if j else pltpu.roll(low_in, RIM, 0)
+                    far = pltpu.roll(low, EDGE - 1 if j else RIM - 1, 0)
+                    vel[0, r, 0:EDGE, :] = jnp.where(sub >= RIM, near, jnp.where(sub == RIM - 1, far, 0.0))
+                    near = pltpu.roll(high, RIM, 0) if j else high
+                    far = pltpu.roll(high_moved, RIM + 1 if j else 1, 0)
+                    vel[1, r, 2 * EDGE :, :] = jnp.where(sub < RIM, near, jnp.where(sub == RIM, far, 0.0))
 
     prof[...] = prof_rim[...]
     south, north = from_y(0, slots)

time: 22 us -> 22 us (level)
  transfers between devices with their start and end apart: 8 -> 8, of which waited for: 6 -> 6; matrix products, arithmetic and copies ran while one was open for 0% -> 0% of each run, Pallas kernels for 23% -> 22%
where the time goes in v10:
time: 22 us; the launch traced here: 21.9 us
  Pallas kernels  9.14 us (42%)
  waiting for transfers between devices  7.14 us (32%)
  starting transfers between devices  4.87 us (22%)
  between operations  0.71 us (3%)
    pallas_call x9, Pallas kernels, call(): pl.pallas_call(kernel, out_shape=tuple((jax.ShapeDtypeStruct(shape, dtype...  9.14 us
    ppermute x8, waiting for transfers between devices, swap(): return lax.ppermute(value, ('gx', 'gy'), pairs)  7.14 us
    ppermute x8, starting transfers between devices, swap(): return lax.ppermute(value, ('gx', 'gy'), pairs)  4.87 us
  transfers between devices with their start and end apart: 8, of which 6 were waited for; matrix products, arithmetic and copies ran while one was open for 0% of the time, Pallas kernels for 22%

profile of v10, /device:TPU:8, one launch (start us, length us, event | category | flops | bytes accessed | tf_op | source)
XLA Modules:
  0.0 21.9 jit_solution(14610901242250436945)
XLA Ops:
  0.6 0.0 copy-start
  0.6 1.6 %edges.1 = (bf16[448,128]{1,0:T(8,128)(2,1)S(1)}, bf16[448,128]{1,0:T(8,128)(2,1)S(1)}, bf16[16,1152]{1,0:T(8,128)(2,1)S(1)}, bf16[16,1152]{1,0:T(8,128)(2,1)S(1...) custom-call(bf16[16,16,1152]{2,1,0:T(8,128)(2,1)} %refs_0_.1, ...), custom_call_target="tpu_custom_call" | custom-call | tf_op jit(solution)/shard_map/spectrum_edges/edges/pallas_call | solution.py:741
  2.3 1.0 %collective-permute-start = (bf16[448,128]{1,0:T(8,128)(2,1)S(1)}, bf16[448,128]{1,0:T(8,128)(2,1)S(1)}, u32[]{:S(2)}, u32[]{:S(2)}) collective-permute-start(bf16[448,128]{1,0:T(8,128)(2,1)S(1)} %get-tuple-element.45), channel_id=1, source_target_pairs={{0,24},{1,25},{2,26},{3,27},{4,28},{5,29},{6,30},{7,31},{8,16},{9,... | collective-permute-start | bytes 344072 | tf_op jit(solution)/shard_map/spectrum_edges/ppermute | solution.py:40
  3.3 0.7 %collective-permute-start.1 = (bf16[448,128]{1,0:T(8,128)(2,1)S(1)}, bf16[448,128]{1,0:T(8,128)(2,1)S(1)}, u32[]{:S(2)}, u32[]{:S(2)}) collective-permute-start(bf16[448,128]{1,0:T(8,128)(2,1)S(1)} %get-tuple-element.46), channel_id=1, source_target_pairs={{0,8},{1,9},{2,10},{3,11},{4,12},{5,13},{6,14},{7,15},{8,0},{9,1},... | collective-permute-start | bytes 344072 | tf_op jit(solution)/shard_map/spectrum_edges/ppermute | solution.py:40
  4.0 1.5 %collective-permute-start.2 = (bf16[16,1152]{1,0:T(8,128)(2,1)S(1)}, bf16[16,1152]{1,0:T(8,128)(2,1)S(1)}, u32[]{:S(2)}, u32[]{:S(2)}) collective-permute-start(bf16[16,1152]{1,0:T(8,128)(2,1)S(1)} %get-tuple-element.57), channel_id=1, source_target_pairs={{0,1},{1,0},{2,3},{3,2},{4,5},{5,4},{6,7},{7,6},{8,9},{9,8},{10,11... | collective-permute-start | bytes 110600 | tf_op jit(solution)/shard_map/spectrum_edges/ppermute | solution.py:40
  5.5 0.4 %collective-permute-start.3 = (bf16[16,1152]{1,0:T(8,128)(2,1)S(1)}, bf16[16,1152]{1,0:T(8,128)(2,1)S(1)}, u32[]{:S(2)}, u32[]{:S(2)}) collective-permute-start(bf16[16,1152]{1,0:T(8,128)(2,1)S(1)} %get-tuple-element.58), channel_id=1, source_target_pairs={{0,8},{1,2},{2,1},{3,4},{4,3},{5,6},{6,5},{7,15},{8,0},{9,10},{10,... | collective-permute-start | bytes 110600 | tf_op jit(solution)/shard_map/spectrum_edges/ppermute | solution.py:40
  5.9 0.0 copy-done
  5.9 1.7 %prepare_own.1 = (f32[32,64,128]{2,1,0:T(8,128)S(1)}, f32[28,64,128]{2,1,0:T(8,128)S(1)}, bf16[32,48,128]{2,1,0:T(8,128)(2,1)S(1)}, f32[5,16,128]{2,1,0:T(8,128)...) custom-call(f32[32,64,128]{2,1,0:T(8,128)S(1)} %copy-done, ...), custom_call_target="tpu_custom_call" | custom-call | tf_op jit(solution)/shard_map/prepare_own/prepare_own/pallas_call | solution.py:741
  7.6 0.2 collective-permute-done.ob.xb
  7.8 0.2 collective-permute-done.2.ya
  7.9 2.4 %collective-permute-done.3.yb = bf16[16,1152]{1,0:T(8,128)(2,1)S(1)} collective-permute-done((bf16[16,1152]{1,0:T(8,128)(2,1)S(1)}, bf16[16,1152]{1,0:T(8,128)(2,1)S(1)}, u32[]{:S(2)}, u32[]{:S(2)}) %collective-permute-start.3) | collective-permute-done | bytes 36896 | tf_op jit(solution)/shard_map/spectrum_edges/ppermute | solution.py:40
  10.3 0.0 collective-permute-done.1.oa.xa
  10.4 0.5 %wave_ends.1 = (bf16[6,16,1152]{2,1,0:T(8,128)(2,1)S(1)}, bf16[6,16,128]{2,1,0:T(8,128)(2,1)S(1)}, bf16[3,16,128]{2,1,0:T(8,128)(2,1)S(1)}, bf16[3,16,128]{2,1,0:T(8,128)(2,1)S(1)}) custom-call(bf16[16,16,1152]{2,1,0:T(8,128)(2,1)S(1)} %get-tuple-element.56.spec, bf16[16,1152]{1,0:T(8,128)(2,1)S(1)} %side.1, bf16[16,1152]{1,0:T(8,128)(2,1)S(1)} %collective-permute-done.2.ya, ...), custom_call_target="tpu_custom_call" | custom-call | tf_op jit(solution)/shard_map/wave/wave_ends/pallas_call | solution.py:741
  10.8 0.1 collective-permute-start.4
  10.9 0.6 %collective-permute-start.5 = (bf16[3,16,128]{2,1,0:T(8,128)(2,1)S(1)}, bf16[3,16,128]{2,1,0:T(8,128)(2,1)S(1)}, u32[]{:S(2)}, u32[]{:S(2)}) collective-permute-start(bf16[3,16,128]{2,1,0:T(8,128)(2,1)S(1)} %get-tuple-element.66), channel_id=1, source_target_pairs={{0,8},{1,9},{2,10},{3,11},{4,12},{5,13},{6,14},{7,15},{8,0},{9,1},... | collective-permute-start | bytes 36872 | tf_op jit(solution)/shard_map/wave/ppermute | solution.py:40
  11.6 0.7 %wave_rest.1 = (bf16[10,16,1152]{2,1,0:T(8,128)(2,1)S(1)}, bf16[10,16,128]{2,1,0:T(8,128)(2,1)S(1)}) custom-call(bf16[16,16,1152]{2,1,0:T(8,128)(2,1)S(1)} %get-tuple-element.56.spec, bf16[16,1152]{1,0:T(8,128)(2,1)S(1)} %collective-permute-done.2.ya, bf16[16,1152]{1,0:T(8,128)(2,1)S(1)} %collective-permute-done.3.yb, ...), custom_call_target="tpu_custom_call" | custom-call | tf_op jit(solution)/shard_map/wave/wave_rest/pallas_call | solution.py:741
  12.2 0.5 %prepare_ends.1 = (f32[10,64,128]{2,1,0:T(8,128)S(1)}, f32[6,64,128]{2,1,0:T(8,128)S(1)}, f32[10,64,128]{2,1,0:T(8,128)S(1)}, bf16[6,48,128]{2,1,0:T(8,128)(2,1)...) custom-call(f32[32,64,128]{2,1,0:T(8,128)S(1)} %copy-done, ...), custom_call_target="tpu_custom_call" | custom-call | tf_op jit(solution)/shard_map/prepare_ends/prepare_ends/pallas_call | solution.py:741
  12.7 1.3 %collective-permute-done.4.pb = bf16[3,16,128]{2,1,0:T(8,128)(2,1)S(1)} collective-permute-done((bf16[3,16,128]{2,1,0:T(8,128)(2,1)S(1)}, bf16[3,16,128]{2,1,0:T(8,128)(2,1)S(1)}, u32[]{:S(2)}, u32[]{:S(2)}) %collective-permute-start.4) | collective-permute-done | bytes 12320 | tf_op jit(solution)/shard_map/wave/ppermute | solution.py:40
  14.0 0.0 collective-permute-done.5.pa
  14.0 0.2 halo.1
  14.2 0.6 %collective-permute-start.6 = (bf16[256,128]{1,0:T(8,128)(2,1)S(1)}, bf16[256,128]{1,0:T(8,128)(2,1)S(1)}, u32[]{:S(2)}, u32[]{:S(2)}) collective-permute-start(bf16[256,128]{1,0:T(8,128)(2,1)S(1)} %get-tuple-element.73), channel_id=1, source_target_pairs={{0,1},{1,0},{2,3},{3,2},{4,5},{5,4},{6,7},{7,6},{8,9},{9,8},{10,11... | collective-permute-start | bytes 196616 | tf_op jit(solution)/shard_map/halo/ppermute | solution.py:40
  14.8 0.0 collective-permute-start.7
  14.8 2.1 %inner.1 = (f32[32,64,128]{2,1,0:T(8,128)S(1)}, bf16[16,16,1152]{2,1,0:T(8,128)(2,1)}, f32[38,2,8,128]{3,2,1,0:T(8,128)S(1)}, f32[38,2,8,128]{3,2,1,0:T(8,128)S(...) custom-call(f32[32,64,128]{2,1,0:T(8,128)S(1)} %copy-done, ...), custom_call_target="tpu_custom_call" | custom-call | tf_op jit(solution)/shard_map/inner/inner/pallas_call | solution.py:741
  16.9 1.7 %collective-permute-done.6.ya = bf16[256,128]{1,0:T(8,128)(2,1)S(1)} collective-permute-done((bf16[256,128]{1,0:T(8,128)(2,1)S(1)}, bf16[256,128]{1,0:T(8,128)(2,1)S(1)}, u32[]{:S(2)}, u32[]{:S(2)}) %collective-permute-start.6) | collective-permute-done | bytes 65568 | tf_op jit(solution)/shard_map/halo/ppermute | solution.py:40
  18.5 1.4 %collective-permute-done.7.yb = bf16[256,128]{1,0:T(8,128)(2,1)S(1)} collective-permute-done((bf16[256,128]{1,0:T(8,128)(2,1)S(1)}, bf16[256,128]{1,0:T(8,128)(2,1)S(1)}, u32[]{:S(2)}, u32[]{:S(2)}) %collective-permute-start.7) | collective-permute-done | bytes 65568 | tf_op jit(solution)/shard_map/halo/ppermute | solution.py:40
  20.0 1.9 %rim.1 = (f32[32,64,128]{2,1,0:T(8,128)}, f32[2,16,16]{2,1,0:T(8,128)}) custom-call(f32[32,64,128]{2,1,0:T(8,128)S(1)} %copy-done, f32[10,64,128]{2,1,0:T(8,128)S(1)} %get-tuple-element.50.vel_halo, bf16[256,128]{1,0:T(8,128)(2,1)S(1)} %collective-permute-done.6.ya, bf16[256,128]{1,0:T(8,128)(2,1)S(1)} %collective-permute-done.7.yb, ...), custom_call_target="tpu_custom_call" | custom-call | tf_op jit(solution)/shard_map/rim/rim/pallas_call | solution.py:741
  (1 shorter events, 0.0 us)
Async XLA Ops:
  0.6 5.3 %copy-start = (f32[32,64,128]{2,1,0:T(8,128)S(1)}, f32[32,64,128]{2,1,0:T(8,128)}, u32[]{:S(2)}) copy-start(f32[32,64,128]{2,1,0:T(8,128)} %own.5) | copy-start | bytes 3145732
  2.3 5.5 %collective-permute-start = (bf16[448,128]{1,0:T(8,128)(2,1)S(1)}, bf16[448,128]{1,0:T(8,128)(2,1)S(1)}, u32[]{:S(2)}, u32[]{:S(2)}) collective-permute-start(bf16[448,128]{1,0:T(8,128)(2,1)S(1)} %get-tuple-element.45), channel_id=1, source_target_pairs={{0,24},{1,25},{2,26},{3,27},{4,28},{5,29},{6,30},{7,31},{8,16},{9,... | collective-permute-start | bytes 344072 | tf_op jit(solution)/shard_map/spectrum_edges/ppermute | solution.py:40
  3.3 7.1 %collective-permute-start.1 = (bf16[448,128]{1,0:T(8,128)(2,1)S(1)}, bf16[448,128]{1,0:T(8,128)(2,1)S(1)}, u32[]{:S(2)}, u32[]{:S(2)}) collective-permute-start(bf16[448,128]{1,0:T(8,128)(2,1)S(1)} %get-tuple-element.46), channel_id=1, source_target_pairs={{0,8},{1,9},{2,10},{3,11},{4,12},{5,13},{6,14},{7,15},{8,0},{9,1},... | collective-permute-start | bytes 344072 | tf_op jit(solution)/shard_map/spectrum_edges/ppermute | solution.py:40
  4.0 4.0 %collective-permute-start.2 = (bf16[16,1152]{1,0:T(8,128)(2,1)S(1)}, bf16[16,1152]{1,0:T(8,128)(2,1)S(1)}, u32[]{:S(2)}, u32[]{:S(2)}) collective-permute-start(bf16[16,1152]{1,0:T(8,128)(2,1)S(1)} %get-tuple-element.57), channel_id=1, source_target_pairs={{0,1},{1,0},{2,3},{3,2},{4,5},{5,4},{6,7},{7,6},{8,9},{9,8},{10,11... | collective-permute-start | bytes 110600 | tf_op jit(solution)/shard_map/spectrum_edges/ppermute | solution.py:40
  5.5 4.9 %collective-permute-start.3 = (bf16[16,1152]{1,0:T(8,128)(2,1)S(1)}, bf16[16,1152]{1,0:T(8,128)(2,1)S(1)}, u32[]{:S(2)}, u32[]{:S(2)}) collective-permute-start(bf16[16,1152]{1,0:T(8,128)(2,1)S(1)} %get-tuple-element.58), channel_id=1, source_target_pairs={{0,8},{1,2},{2,1},{3,4},{4,3},{5,6},{6,5},{7,15},{8,0},{9,10},{10,... | collective-permute-start | bytes 110600 | tf_op jit(solution)/shard_map/spectrum_edges/ppermute | solution.py:40
  10.8 3.2 %collective-permute-start.4 = (bf16[3,16,128]{2,1,0:T(8,128)(2,1)S(1)}, bf16[3,16,128]{2,1,0:T(8,128)(2,1)S(1)}, u32[]{:S(2)}, u32[]{:S(2)}) collective-permute-start(bf16[3,16,128]{2,1,0:T(8,128)(2,1)S(1)} %get-tuple-element.65), channel_id=1, source_target_pairs={{0,24},{1,25},{2,26},{3,27},{4,28},{5,29},{6,30},{7,31},{8,16},{9,... | collective-permute-start | bytes 36872 | tf_op jit(solution)/shard_map/wave/ppermute | solution.py:40
  10.9 3.1 %collective-permute-start.5 = (bf16[3,16,128]{2,1,0:T(8,128)(2,1)S(1)}, bf16[3,16,128]{2,1,0:T(8,128)(2,1)S(1)}, u32[]{:S(2)}, u32[]{:S(2)}) collective-permute-start(bf16[3,16,128]{2,1,0:T(8,128)(2,1)S(1)} %get-tuple-element.66), channel_id=1, source_target_pairs={{0,8},{1,9},{2,10},{3,11},{4,12},{5,13},{6,14},{7,15},{8,0},{9,1},... | collective-permute-start | bytes 36872 | tf_op jit(solution)/shard_map/wave/ppermute | solution.py:40
  14.2 4.3 %collective-permute-start.6 = (bf16[256,128]{1,0:T(8,128)(2,1)S(1)}, bf16[256,128]{1,0:T(8,128)(2,1)S(1)}, u32[]{:S(2)}, u32[]{:S(2)}) collective-permute-start(bf16[256,128]{1,0:T(8,128)(2,1)S(1)} %get-tuple-element.73), channel_id=1, source_target_pairs={{0,1},{1,0},{2,3},{3,2},{4,5},{5,4},{6,7},{7,6},{8,9},{9,8},{10,11... | collective-permute-start | bytes 196616 | tf_op jit(solution)/shard_map/halo/ppermute | solution.py:40
  14.8 5.2 %collective-permute-start.7 = (bf16[256,128]{1,0:T(8,128)(2,1)S(1)}, bf16[256,128]{1,0:T(8,128)(2,1)S(1)}, u32[]{:S(2)}, u32[]{:S(2)}) collective-permute-start(bf16[256,128]{1,0:T(8,128)(2,1)S(1)} %get-tuple-element.74), channel_id=1, source_target_pairs={{0,8},{1,2},{2,1},{3,4},{4,3},{5,6},{6,5},{7,15},{8,0},{9,10},{10,... | collective-permute-start | bytes 196616 | tf_op jit(solution)/shard_map/halo/ppermute | solution.py:40
